TPU v7x, 256 devices: a whole 4x4x8 slice. The times are simulated.
256 devices in a mesh: dp: 2 (over x_hi), expert: 8 (over y, core), tensor: 16 (over z, x_lo).
Axes of the slice: x: 4 (x_hi: 2, x_lo: 2; x = x_hi * 2 + x_lo), y: 4, z: 8, core: 2. Of those that a mesh axis runs over, the one named last changes fastest.
Arguments:
- tokens: bfloat16 [4, 2048, 3072], P(None, ('dp', 'expert'), 'tensor'), parts along dimension 1, may hold values from -6 to 6
- expert_ids: int32 [4, 2048, 2], P(None, ('dp', 'expert')), parts along dimension 1, may hold values from 0 to 3, all different within a row; in each aligned block of 128 rows (0 to 127, 128 to 255, ..., all dimensions but the last counted through in order) at most 80 rows name the same one
- route_weights: float32 [4, 2048, 2], P(None, ('dp', 'expert')), parts along dimension 1, may hold values from 0.2 to 1
- gate_train: bfloat16 [8, 3072, 4096], P('expert', 'tensor'), may hold values from -0.109375 to 0.109375
- up_train: bfloat16 [8, 3072, 4096], P('expert', 'tensor'), may hold values from -0.109375 to 0.109375
Outputs:
- hidden: bfloat16 [4, 2048, 2, 2, 4096], P(None, ('dp', 'expert'), None, None, 'tensor'), parts along dimension 1
There are 2 independent parts, one for each index of `dp`. A program takes and returns all parts, laid end to end along the dimension named above; an argument that names none is the same for every part. Nothing has to cross between parts.
Inputs may be any that keep to these rules, and one draw needn't show every extreme that they name: `expert_ids`: each token names 2 different experts; within one step, in each aligned block of 128 tokens (the tokens of one index of expert) no expert is named by more than 80 tokens, a bound that some block reaches.
All inputs are finite; a program needn't handle non-finite values.
Results may differ from a plain program's by a relative error of at most 0.001.
Values may be sent and summed in bfloat16 or wider, within the bound.
No kernel may reach another device: no remote copies, remote signals or barrier semaphores. Data moves between devices by JAX's collectives and lax.ppermute only.
A program may use at most 128 MiB of HBM per device.

v0:
```python
import jax
import jax.numpy as jnp
from jax import lax
from jax.sharding import PartitionSpec as P


def activate(features, gate_cols, up_cols):
    gate_val = jnp.einsum("snd,odw->snow", features, gate_cols, preferred_element_type=jnp.float32)
    up_val = jnp.einsum("snd,odw->snow", features, up_cols, preferred_element_type=jnp.float32)
    return jax.nn.silu(gate_val) * up_val


def select_slots(activation, expert_ids, route_weights):
    expert_count = activation.shape[2]
    chosen = expert_ids[..., None] == jnp.arange(expert_count, dtype=jnp.int32)
    picked = jnp.sum(jnp.where(chosen[..., None, None], activation[:, :, None], 0.0), axis=3)
    return (route_weights[..., None, None] * picked).astype(jnp.bfloat16)


def body(tokens, expert_ids, route_weights, gate_train, up_train):
    gate_cols, up_cols = (
        lax.all_to_all(gate_train, "tensor", split_axis=2, concat_axis=1, tiled=True),
        lax.all_to_all(up_train, "tensor", split_axis=2, concat_axis=1, tiled=True),
    )
    features = lax.all_gather(tokens, "tensor", axis=2, tiled=True)
    step_count, row_count, model_width = features.shape
    gate_all, up_all = (
        lax.all_gather(gate_cols, "expert", axis=0, tiled=True),
        lax.all_gather(up_cols, "expert", axis=0, tiled=True),
    )
    activation = activate(features, gate_all, up_all)
    owner_count, unit_width = (activation.shape[2], activation.shape[3])
    activation = activation.reshape(step_count, row_count, owner_count // 2, 2, unit_width)
    return select_slots(activation, expert_ids, route_weights)


def solution(mesh):
    in_specs = (
        P(None, ("dp", "expert"), "tensor"),
        P(None, ("dp", "expert"), None),
        P(None, ("dp", "expert"), None),
        P("expert", "tensor", None),
        P("expert", "tensor", None),
    )
    out_specs = P(None, ("dp", "expert"), None, None, "tensor")
    return jax.shard_map(body, mesh=mesh, in_specs=in_specs, out_specs=out_specs, check_vma=False)
```

profile of v0, /device:TPU:1, one launch (start us, length us, event | category | flops | bytes accessed | tf_op | source)
XLA Modules:
  0.0 314.1 jit_solution(16593431012892751783)
XLA Ops:
  6.5 0.0 all-gather.4.cloned.1.call-start
  6.5 0.7 all-gather.4.cloned.1.call-update
  7.3 0.0 all-gather.8.cloned.1.call-start
  7.3 9.9 %copy.37 = bf16[1,192,4096]{1,0,2:T(2,128)(2,1)} copy(bf16[1,192,4096]{2,1,0:T(8,128)(2,1)} %param.9) | data formatting | bytes 3145728 | tf_op args[4]
  17.2 0.5 broadcast.9
  17.7 23.6 %reduce = bf16[4096,192]{1,0:T(8,128)(2,1)S(1)} reduce(bf16[4096,1,192]{2,1,0:T(2,128)(2,1)} %bitcast.40, bf16[]{:T(256)} %broadcast.9), dimensions={1}, to_apply=%bitcast.34.reduce_sub_computation | reduce | bytes 3145730
  41.4 3.3 %reshape.9 = bf16[16,2,24576]{2,1,0:T(2,128)(2,1)} reshape(bf16[4096,192]{1,0:T(8,128)(2,1)S(1)} %reduce) | data formatting | bytes 3145728
  44.6 61.2 %all_to_all.36 = bf16[16,2,24576]{2,1,0:T(2,128)(2,1)S(1)} all-to-all(bf16[16,2,24576]{2,1,0:T(2,128)(2,1)} %reshape.9), channel_id=1, replica_groups=mesh['dp'=2,'expert'=8,'tensor'=16] {'tensor'}, dimensions={0} | all-to-all | bytes 3145728 | tf_op jit(solution)/shard_map/all_to_all | solution.py:23
  105.8 7.2 %reshape.10 = bf16[4096,1,192]{2,1,0:T(2,128)(2,1)} reshape(bf16[16,2,24576]{2,1,0:T(2,128)(2,1)S(1)} %all_to_all.36) | data formatting | bytes 3145728
  113.1 9.9 %copy.38 = bf16[1,192,4096]{2,1,0:T(8,128)(2,1)S(1)} copy(bf16[1,192,4096]{1,0,2:T(2,128)(2,1)} %bitcast.41) | data formatting | bytes 3145728 | tf_op jit(solution)/shard_map/all_to_all | solution.py:23
  123.0 0.4 copy.43
  123.4 0.1 bitcast_bitcast_fusion
  123.5 0.0 copy-start
  123.5 1.8 copy.39
  125.3 0.0 all-gather.8.cloned.1.call-update
  125.3 0.0 all-gather.6.cloned.1.call-start
  125.4 0.0 copy-done
  125.4 8.5 %copy.34 = bf16[1,192,4096]{1,0,2:T(2,128)(2,1)} copy(bf16[1,192,4096]{2,1,0:T(8,128)(2,1)S(1)} %copy-done) | data formatting | bytes 3145728 | tf_op args[3]
  133.9 23.6 %reduce.1 = bf16[4096,192]{1,0:T(8,128)(2,1)S(1)} reduce(bf16[4096,1,192]{2,1,0:T(2,128)(2,1)} %bitcast.42, bf16[]{:T(256)} %broadcast.9), dimensions={1}, to_apply=%bitcast.36.reduce_sub_computation | reduce | bytes 3145730
  157.5 3.3 %reshape.11 = bf16[16,2,24576]{2,1,0:T(2,128)(2,1)} reshape(bf16[4096,192]{1,0:T(8,128)(2,1)S(1)} %reduce.1) | data formatting | bytes 3145728
  160.8 44.1 %all_to_all.37 = bf16[16,2,24576]{2,1,0:T(2,128)(2,1)S(1)} all-to-all(bf16[16,2,24576]{2,1,0:T(2,128)(2,1)} %reshape.11), channel_id=1, replica_groups=mesh['dp'=2,'expert'=8,'tensor'=16] {'tensor'}, dimensions={0} | all-to-all | bytes 3145728 | tf_op jit(solution)/shard_map/all_to_all | solution.py:22
  204.9 7.3 %reshape.12 = bf16[4096,1,192]{2,1,0:T(2,128)(2,1)} reshape(bf16[16,2,24576]{2,1,0:T(2,128)(2,1)S(1)} %all_to_all.37) | data formatting | bytes 3145728
  212.2 9.9 %copy.35 = bf16[1,192,4096]{2,1,0:T(8,128)(2,1)S(1)} copy(bf16[1,192,4096]{1,0,2:T(2,128)(2,1)} %bitcast.43) | data formatting | bytes 3145728 | tf_op jit(solution)/shard_map/all_to_all | solution.py:22
  222.1 0.4 copy.42
  222.5 0.1 bitcast_bitcast_fusion.1
  222.6 0.0 copy-start.2
  222.6 1.7 copy.36
  224.4 0.0 all-gather.6.cloned.1.call-update
  224.4 0.0 copy-done.2
  224.4 0.0 all-gather.4.cloned.1.call-done
  224.4 0.0 copy-start.3
  224.4 0.0 all-gather.8.cloned.1.call-done
  224.5 13.6 %fusion = f32[4,128,8,256]{3,1,2,0:T(8,128)} fusion(bf16[8,3072,256]{2,1,0:T(8,128)(2,1)} %all-gather.8.cloned.1.call-done, bf16[4,128,3072]{1,2,0:T(8,128)(2,1)} %all-gather.4.cloned.1.call-done), kind=kOutput, calls=%fused_computation | convolution fusion | flops 6442450944 | bytes 19922944 | tf_op jit(solution)/shard_map/snd,odw->snow/dot_general | solution.py:9
  238.1 55.3 %all-gather.6.cloned.1.call-done = bf16[8,3072,256]{2,1,0:T(8,128)(2,1)} async-done(((bf16[1,3072,256]{2,1,0:T(8,128)(2,1)}), bf16[8,3072,256]{2,1,0:T(8,128)(2,1)}) %all-gather.6.cloned.1.call-update) | async-done | bytes 12582928 | tf_op jit(solution)/shard_map/all_gather | solution.py:28
  293.4 0.0 copy-done.3
  293.4 10.9 %multiply_multiply_fusion = f32[4,128,8,256]{3,1,2,0:T(8,128)S(1)} fusion(f32[4,128,8,256]{3,1,2,0:T(8,128)} %fusion, bf16[8,3072,256]{2,1,0:T(8,128)(2,1)} %all-gather.6.cloned.1.call-done, bf16[4,128,3072]{1,2,0:T(8,128)(2,1)S(1)} %copy-done.3), kind=kOutput, calls=%fused_computation.5 | convolution fusion | flops 6447693824 | bytes 24117248 | tf_op jit(solution)/shard_map/snd,odw->snow/dot_general | solution.py:8
  304.3 0.0 copy-start.1
  304.3 1.0 select_reduce_fusion
  305.3 0.0 copy-done.1
  305.3 0.2 multiply_convert_fusion
  305.5 2.0 copy.40
  (1 shorter events, 0.0 us)
Async XLA Ops:
  6.5 217.9 %all-gather.4.cloned.1.call-start = ((), (), s32[]{:S(2)}) async-start(), calls=%async_computation.2 | async-start | bytes 3342336 | tf_op jit(solution)/shard_map/all_gather | solution.py:25
  7.3 217.2 %all-gather.8.cloned.1.call-start = ((), (), s32[]{:S(2)}) async-start(), calls=%async_computation.4 | async-start | bytes 14155776 | tf_op jit(solution)/shard_map/all_gather | solution.py:29
  123.5 1.9 copy-start
  125.3 168.0 %all-gather.6.cloned.1.call-start = ((), (), s32[]{:S(2)}) async-start(), calls=%async_computation.3 | async-start | bytes 14155776 | tf_op jit(solution)/shard_map/all_gather | solution.py:28
  222.6 1.8 copy-start.2
  224.4 68.9 %copy-start.3 = (bf16[4,128,3072]{1,2,0:T(8,128)(2,1)S(1)}, bf16[4,128,3072]{1,2,0:T(8,128)(2,1)}, u32[]{:S(2)}) copy-start(bf16[4,128,3072]{1,2,0:T(8,128)(2,1)} %all-gather.4.cloned.1.call-done) | copy-start | bytes 9437188
  304.3 1.0 copy-start.1
Sparse Core Ops, SparseCore 0:
  9.1 101.2 all-gather.3
  125.5 70.8 all-gather.7
  224.5 68.8 all-gather.5
where the time goes:
time: 315 us; the launch traced here: 314 us
  blocking collectives  105 us (33%)
  local copies, waits for them, and re-layouts  66.4 us (21%)
  waiting for transfers between devices  56.1 us (18%)
  other arithmetic  48.5 us (15%)
  matrix products  24.5 us (8%)
  between operations  13.3 us (4%)
    all_to_all x1, blocking collectives, body(): lax.all_to_all(up_train, 'tensor', split_axis=2, concat_axis=1, tiled=True)  61.2 us
    all_gather x1, waiting for transfers between devices, body(): lax.all_gather(gate_cols, 'expert', axis=0, tiled=True)  55.3 us
    unnamed x2, other arithmetic  47.3 us
    all_to_all x1, blocking collectives, body(): lax.all_to_all(gate_train, 'tensor', split_axis=2, concat_axis=1, tiled=T...  44.1 us
    unnamed x17, local copies, waits for them, and re-layouts  40.9 us
    dot_general x1, matrix products, activate(): jnp.einsum('snd,odw->snow', features, up_cols, preferred_element_type=jnp...  13.6 us
    all_to_all x3, local copies, waits for them, and re-layouts, body(): lax.all_to_all(up_train, 'tensor', split_axis=2, concat_axis=1, tiled=True)  11.8 us
    all_to_all x3, local copies, waits for them, and re-layouts, body(): lax.all_to_all(gate_train, 'tensor', split_axis=2, concat_axis=1, tiled=T...  11.7 us
  transfers between devices with their start and end apart: 3, of which 1 were waited for; matrix products, arithmetic and copies ran while one was open for 40% of the time, Pallas kernels for 0%

commit v1 on v0

v1 whole, which is shorter than its diff:
```python
import functools

import jax
import jax.numpy as jnp
from jax import lax
from jax.experimental import pallas as pl
from jax.experimental.pallas import tpu as pltpu
from jax.sharding import Mesh, PartitionSpec as P

MOST = 80
X = ("dp", "xl")
BF, F32 = jnp.bfloat16, jnp.float32
ANY = pl.BlockSpec(memory_space=pl.ANY)
VM = pl.BlockSpec(memory_space=pltpu.VMEM)
SM = pl.BlockSpec(memory_space=pltpu.SMEM)


def ring(x, axis, size, step):
    return lax.ppermute(x, axis, [(i, (i + step) % size) for i in range(size)])


def ranks(member):
    n = member.shape[1]
    before = lax.broadcasted_iota(jnp.int32, (n, n), 0) < lax.broadcasted_iota(jnp.int32, (n, n), 1)
    return jnp.dot(member.astype(BF), before.astype(BF), preferred_element_type=F32)


def slots(rank, member):
    row = lax.broadcasted_iota(jnp.int32, (MOST, rank.shape[1]), 0).astype(F32)
    return (row == rank) & (member > 0)


def dispatch_kernel(pos, meta, feats, *outs):
    y, xl = pos[0], pos[2]
    zs, ss, width, n = feats.shape
    for s in range(ss):
        own = meta[2 * xl + s]
        rows = []
        members = []
        for d in range(4):
            e = lax.rem(y + d, 4).astype(F32)
            members.append(((own[0:1] == e) | (own[1:2] == e)).astype(F32))
        rank = ranks(jnp.concatenate(members, axis=0))
        for d in range(4):
            rows.append(slots(rank[d : d + 1], members[d]).astype(BF))
        onehot = jnp.concatenate(rows, axis=0)
        for z in range(zs):
            picked = lax.dot_general(onehot, feats[z, s], (((1,), (1,)), ((), ())), preferred_element_type=F32).astype(BF)
            for d in range(4):
                outs[d][s * MOST : (s + 1) * MOST, z * width : (z + 1) * width] = picked[d * MOST : (d + 1) * MOST]


def expert_kernel(chunks, pos, meta, *refs):
    xs, refs = refs[:8], refs[8:]
    ws, refs = refs[: 5 * chunks], refs[5 * chunks :]
    out, xbuf, wbuf, rwbuf, xsem, wsem = refs
    y, c, xl, dp = pos[0], pos[1], pos[2], pos[3]
    rows = xs[0].shape[0]
    depth = ws[0].shape[1]
    copies = []
    for g in range(8):
        copies.append(pltpu.make_async_copy(xs[g], xbuf.at[pl.ds(g * rows, rows)], xsem.at[g]))
    here = dp * 2 + xl
    for ch in range(chunks):
        own, left, right, far_a, far_b = ws[5 * ch : 5 * ch + 5]
        span = pl.ds(ch * depth, depth)
        for i, (src, off, zlo, zn) in enumerate(((own, 0, 0, 8), (left, 3, 0, 8), (right, 1, 0, 8), (far_a, 2, 0, 4), (far_b, 2, 4, 4))):
            j = lax.rem(here + off, 4)
            dst = wbuf.at[lax.div(j, 2), pl.ds(zlo, zn), lax.rem(j, 2), span]
            copies.append(pltpu.make_async_copy(src, dst, wsem.at[ch * 5 + i]))
    for cp in copies:
        cp.start()
    e = y.astype(F32)
    infos = []
    for cc in range(2):
        for d in range(4):
            for s in range(2):
                infos.append(meta[lax.rem(y + 4 - d, 4), c + cc - 2 * c * cc, 2 * xl + s])
    members = [((o[0:1] == e) | (o[1:2] == e)).astype(F32) for o in infos]
    rank = ranks(jnp.concatenate(members, axis=0))
    for i, o in enumerate(infos):
        weight = jnp.where(o[0:1] == e, o[2:3], o[3:4])
        value = jnp.sum(jnp.where(slots(rank[i : i + 1], members[i]), weight, 0.0), axis=1, keepdims=True)
        rwbuf[i * MOST : (i + 1) * MOST, :] = jnp.broadcast_to(value, (MOST, 128))
    for cp in copies:
        cp.wait()
    half = 4 * rows
    for m in range(2):
        data = xbuf[m * half : (m + 1) * half]
        rw = rwbuf[m * half : (m + 1) * half]
        rw = jnp.concatenate([rw, rw], axis=1)
        for t in range(2):
            gate = jnp.dot(data, wbuf[0, :, :, :, t * 256 : (t + 1) * 256].reshape(-1, 256), preferred_element_type=F32)
            up = jnp.dot(data, wbuf[1, :, :, :, t * 256 : (t + 1) * 256].reshape(-1, 256), preferred_element_type=F32)
            act = (rw * (gate / (1.0 + jnp.exp(-gate)) * up)).astype(BF)
            for d in range(4):
                out[lax.rem(y + 4 - d, 4), c + m - 2 * c * m, t] = act[d * rows : (d + 1) * rows]


def combine_kernel(meta, recv, out):
    steps = meta.shape[0]
    for s in range(steps):
        own = meta[s]
        members = [((own[0:1] == e) | (own[1:2] == e)).astype(F32) for e in range(4)]
        rank = ranks(jnp.concatenate(members, axis=0))
        left, right = [], []
        for e in range(4):
            place = slots(rank[e : e + 1], members[e])
            left.append(jnp.concatenate([(place & (own[k : k + 1] == e)).astype(BF) for k in range(2)], axis=1))
            part = pl.ds((s % 2) * MOST, MOST)
            right.append(jnp.concatenate([recv[e, h, s // 2, part] for h in range(2)], axis=1))
        picked = lax.dot_general(
            jnp.concatenate(left, axis=0), jnp.concatenate(right, axis=0), (((0,), (0,)), ((), ())), preferred_element_type=F32
        ).astype(BF)
        n = picked.shape[0] // 2
        out[s] = jnp.concatenate([picked[:n], picked[n:]], axis=1)


def body(tokens, expert_ids, route_weights, gate_train, up_train):
    chunks = 2
    dp, y, c, z, xl = (lax.axis_index(a) for a in ("dp", "y", "c", "z", "xl"))
    pos = jnp.stack([y, c, xl, dp]).astype(jnp.int32)
    steps, n, width = tokens.shape
    meta = jnp.concatenate([expert_ids.astype(F32), route_weights], axis=2).transpose(0, 2, 1)
    meta_all = lax.all_gather(meta, ("y", "c"), axis=0, tiled=False).reshape(4, 2, steps, 4, n)
    turned = tokens.transpose(0, 2, 1).reshape(2, steps // 2, width, n)
    mine = lax.dynamic_index_in_dim(turned, xl, 0, keepdims=False)
    theirs = lax.dynamic_index_in_dim(turned, 1 - xl, 0, keepdims=False)
    got = ring(theirs, "xl", 2, 1)
    pair = jnp.concatenate([jnp.where(xl == 0, mine, got), jnp.where(xl == 0, got, mine)], axis=1)
    feats = lax.all_gather(pair, "z", axis=0, tiled=False)
    sent = pl.pallas_call(
        dispatch_kernel,
        out_shape=[jax.ShapeDtypeStruct((2 * MOST, 16 * width), BF)] * 4,
        in_specs=[SM, VM, VM],
        out_specs=[VM] * 4,
        compiler_params=pltpu.CompilerParams(vmem_limit_bytes=32 << 20),
        name="dispatch",
    )(pos, meta, feats)
    held = [sent[0]] + [ring(sent[d], "y", 4, d) for d in (1, 2, 3)]
    other = [ring(h, "c", 2, 1) for h in held]
    source = jnp.where(dp == 0, gate_train[0], up_train[0])
    rows, units = source.shape
    blocks = source.reshape(rows, 8, units // 8).transpose(1, 0, 2)
    pieces = []
    for ch in range(chunks):
        depth = rows // chunks
        own = lax.all_to_all(blocks[:, ch * depth : (ch + 1) * depth], "z", split_axis=0, concat_axis=0, tiled=True)
        left, right = ring(own, X, 4, 1), ring(own, X, 4, -1)
        far_a, far_b = ring(left[:4], X, 4, 1), ring(right[4:], X, 4, -1)
        pieces += [own, left, right, far_a, far_b]
    act = pl.pallas_call(
        functools.partial(expert_kernel, chunks),
        out_shape=jax.ShapeDtypeStruct((4, 2, 2, 2 * MOST, 256), BF),
        in_specs=[SM, VM] + [ANY] * (8 + 5 * chunks),
        out_specs=VM,
        scratch_shapes=[
            pltpu.VMEM((16 * MOST, 16 * width), BF),
            pltpu.VMEM((2, 8, 2, rows, units // 8), BF),
            pltpu.VMEM((16 * MOST, 128), F32),
            pltpu.SemaphoreType.DMA((8,)),
            pltpu.SemaphoreType.DMA((5 * chunks,)),
        ],
        compiler_params=pltpu.CompilerParams(vmem_limit_bytes=44 << 20),
        cost_estimate=pl.CostEstimate(flops=16 * MOST * 16 * width * 1024 * 2, bytes_accessed=15 << 20, transcendentals=16 * MOST * 512),
        name="expert",
    )(pos, meta_all, *held, *other, *pieces)
    back = lax.all_to_all(act.reshape(16, 2 * MOST, 256), ("y", "c", "xl"), split_axis=0, concat_axis=0, tiled=True)
    out = pl.pallas_call(
        combine_kernel,
        out_shape=jax.ShapeDtypeStruct((steps, n, 1024), BF),
        in_specs=[VM, VM],
        out_specs=VM,
        compiler_params=pltpu.CompilerParams(vmem_limit_bytes=32 << 20),
        name="combine",
    )(meta, back.reshape(4, 2, 2, 2 * MOST, 256))
    return out.reshape(steps, n, 2, 2, 256)


def solution(mesh):
    fine = Mesh(mesh.devices.reshape(2, 4, 2, 8, 2), ("dp", "y", "c", "z", "xl"))
    group, tensor = ("dp", "y", "c"), ("z", "xl")
    in_specs = (
        P(None, group, tensor),
        P(None, group, None),
        P(None, group, None),
        P(("y", "c"), tensor, None),
        P(("y", "c"), tensor, None),
    )
    out_specs = P(None, group, None, None, tensor)
    return jax.shard_map(body, mesh=fine, in_specs=in_specs, out_specs=out_specs, check_vma=False)
```

time: 315 us -> 207 us (0.66)
  blocking collectives: 105 us -> 37.6 us
  local copies, waits for them, and re-layouts: 66.4 us -> 10.3 us
  other arithmetic: 48.5 us -> 2.39 us
  starting transfers between devices: 0.08 us -> 37.1 us
  waiting for transfers between devices: 56.1 us -> 88.1 us
  matrix products: 24.5 us -> 0 us
  Pallas kernels: 0 us -> 17.6 us
    all_to_all x2 -> x1, blocking collectives: 105 us -> 23.5 us  [body(): lax.all_to_all(act.reshape(16, 2 * MOST, 256), ('y', 'c', 'xl'), split_ax...]
    all_gather x3 -> x1, waiting for transfers between devices: 55.3 us -> 0.02 us  [body(): feats = lax.all_gather(pair, 'z', axis=0, tiled=False)]
    all_to_all x0 -> x2, waiting for transfers between devices: none -> 49.7 us  [body(): lax.all_to_all(blocks[:, ch * depth:(ch + 1) * depth], 'z', split_axis=0,...]
    unnamed x2 -> x0, other arithmetic: 47.3 us -> none
    ppermute x0 -> x16, waiting for transfers between devices: none -> 38.4 us  [ring(): return lax.ppermute(x, axis, [(i, (i + step) % size) for i in range(size)])]
    unnamed x17, local copies, waits for them, and re-layouts: 40.9 us -> 3.94 us
    ppermute x0 -> x16, starting transfers between devices: none -> 25.2 us  [ring(): return lax.ppermute(x, axis, [(i, (i + step) % size) for i in range(size)])]
    dot_general x2 -> x0, matrix products: 24.5 us -> none  [the longest x1 13.6 us: activate(): jnp.einsum('snd,odw->snow', features, up_cols, preferred_element_type=jnp...]
  transfers between devices with their start and end apart: 3 -> 19, of which waited for: 1 -> 6; matrix products, arithmetic and copies ran while one was open for 40% -> 3% of each run, Pallas kernels for 0% -> 1%
where the time goes in v1:
time: 207 us
  waiting for transfers between devices  88.1 us (43%)
  blocking collectives  37.6 us (18%)
  starting transfers between devices  37.1 us (18%)
  Pallas kernels  17.6 us (9%)
  between operations  13.6 us (7%)
  local copies, waits for them, and re-layouts  10.3 us (5%)
  other arithmetic  2.39 us (1%)
    all_to_all x2, waiting for transfers between devices, body(): lax.all_to_all(blocks[:, ch * depth:(ch + 1) * depth], 'z', split_axis=0,...  49.7 us
    ppermute x16, waiting for transfers between devices, ring(): return lax.ppermute(x, axis, [(i, (i + step) % size) for i in range(size)])  38.4 us
    ppermute x16, starting transfers between devices, ring(): return lax.ppermute(x, axis, [(i, (i + step) % size) for i in range(size)])  25.2 us
    all_to_all x1, blocking collectives, body(): lax.all_to_all(act.reshape(16, 2 * MOST, 256), ('y', 'c', 'xl'), split_ax...  23.5 us
    all_gather x1, blocking collectives, body(): lax.all_gather(meta, ('y', 'c'), axis=0, tiled=False)  14.2 us
    pallas_call x1, Pallas kernels, body(): pl.pallas_call(functools.partial(expert_kernel, chunks), out_shape=jax.Sh...  14.1 us
    all_to_all x2, starting transfers between devices, body(): lax.all_to_all(blocks[:, ch * depth:(ch + 1) * depth], 'z', split_axis=0,...  11.9 us
  transfers between devices with their start and end apart: 19, of which 6 were waited for; matrix products, arithmetic and copies ran while one was open for 3% of the time, Pallas kernels for 1%

profile of v1, /device:TPU:1, one launch (start us, length us, event | category | flops | bytes accessed | tf_op | source)
XLA Modules:
  0.0 206.7 jit_solution(5704715016687377913)
XLA Ops:
  6.5 0.9 dynamic-slice_bitcast_fusion
  7.4 2.0 collective-permute-start
  9.5 1.6 broadcast_select_fusion
  11.1 0.6 copy.8
  11.7 0.5 copy.10
  12.2 1.3 fusion
  13.5 8.3 %all-to-all-start = ((bf16[8,96,512]{2,1,0:T(8,128)(2,1)}), bf16[8,96,512]{2,1,0:T(8,128)(2,1)S(1)}, u32[]{:S(2)}, u32[]{:S(2)}) async-start(bf16[8,96,512]{2,1,0:T(8,128)(2,1)} %get-tuple-element.14), calls=%async_computation | async-start | bytes 1572864 | tf_op jit(solution)/shard_map/all_to_all | solution.py:148
  21.8 0.0 copy-start.3
  21.8 0.0 all-gather.4.cloned.1.call-start
  21.9 0.7 pad_maximum_fusion
  22.6 0.0 all-gather.4.cloned.1.call-update
  22.6 21.7 %all-to-all-done.refs_8_ = bf16[8,96,512]{2,1,0:T(8,128)(2,1)S(1)} async-done(((bf16[8,96,512]{2,1,0:T(8,128)(2,1)}), bf16[8,96,512]{2,1,0:T(8,128)(2,1)S(1)}, u32[]{:S(2)}, u32[]{:S(2)}) %all-to-all-start) | async-done | bytes 786464 | tf_op jit(solution)/shard_map/all_to_all | solution.py:148
  44.3 3.6 %all-to-all-start.1 = ((bf16[8,96,512]{2,1,0:T(8,128)(2,1)}), bf16[8,96,512]{2,1,0:T(8,128)(2,1)S(1)}, u32[]{:S(2)}, u32[]{:S(2)}) async-start(bf16[8,96,512]{2,1,0:T(8,128)(2,1)} %get-tuple-element.13), calls=%async_computation.1 | async-start | bytes 1572864 | tf_op jit(solution)/shard_map/all_to_all | solution.py:148
  47.9 2.4 %collective-permute-start.9 = (bf16[8,96,512]{2,1,0:T(8,128)(2,1)S(1)}, bf16[8,96,512]{2,1,0:T(8,128)(2,1)S(1)}, u32[]{:S(2)}, u32[]{:S(2)}) collective-permute-start(bf16[8,96,512]{2,1,0:T(8,128)(2,1)S(1)} %all-to-all-done.refs_8_), channel_id=1, source_target_pairs={{0,129},{1,0},{128,1},{129,128},{2,131},{3,2},{130,3},{131,130},{4... | collective-permute-start | bytes 2359304 | tf_op jit(solution)/shard_map/ppermute | solution.py:19
  50.3 0.0 collective-permute-start.8
  50.3 28.0 %all-to-all-done.1.refs_13_ = bf16[8,96,512]{2,1,0:T(8,128)(2,1)S(1)} async-done(((bf16[8,96,512]{2,1,0:T(8,128)(2,1)}), bf16[8,96,512]{2,1,0:T(8,128)(2,1)S(1)}, u32[]{:S(2)}, u32[]{:S(2)}) %all-to-all-start.1) | async-done | bytes 786464 | tf_op jit(solution)/shard_map/all_to_all | solution.py:148
  78.3 1.7 collective-permute-start.13
  80.0 0.1 pad_add_fusion.pos
  80.1 0.1 collective-permute-start.12
  80.2 0.0 all-gather.4.cloned.1.call-done
  80.3 1.4 copy-done
  81.7 2.0 dispatch.1
  83.6 1.5 collective-permute-start.1
  85.1 0.0 collective-permute-done.9.refs_10_
  85.1 2.5 %collective-permute-start.2 = (bf16[160,3072]{1,0:T(8,128)(2,1)S(1)}, bf16[160,3072]{1,0:T(8,128)(2,1)S(1)}, u32[]{:S(2)}, u32[]{:S(2)}) collective-permute-start(bf16[160,3072]{1,0:T(8,128)(2,1)S(1)} %get-tuple-element.11), channel_id=1, source_target_pairs={{0,64},{32,96},{64,0},{96,32},{1,65},{33,97},{65,1},{97,33},{2,66}... | collective-permute-start | bytes 2949128 | tf_op jit(solution)/shard_map/ppermute | solution.py:19
  87.6 1.1 collective-permute-start.3
  88.8 7.2 %collective-permute-done.13.refs_15_ = bf16[8,96,512]{2,1,0:T(8,128)(2,1)} collective-permute-done((bf16[8,96,512]{2,1,0:T(8,128)(2,1)S(1)}, bf16[8,96,512]{2,1,0:T(8,128)(2,1)}, u32[]{:S(2)}, u32[]{:S(2)}) %collective-permute-start.13) | collective-permute-done | bytes 786464 | tf_op jit(solution)/shard_map/ppermute | solution.py:19
  95.9 3.5 %collective-permute-start.11 = (bf16[4,96,512]{2,1,0:T(8,128)(2,1)S(1)}, bf16[4,96,512]{2,1,0:T(8,128)(2,1)S(1)}, u32[]{:S(2)}, u32[]{:S(2)}) collective-permute-start(bf16[4,96,512]{2,1,0:T(8,128)(2,1)S(1)} %slice.26), channel_id=1, source_target_pairs={{0,129},{1,0},{128,1},{129,128},{2,131},{3,2},{130,3},{131,130},{4... | collective-permute-start | bytes 1179656 | tf_op jit(solution)/shard_map/ppermute | solution.py:19
  99.4 0.1 collective-permute-start.10
  99.5 6.4 %collective-permute-done.11.refs_12_ = bf16[4,96,512]{2,1,0:T(8,128)(2,1)S(1)} collective-permute-done((bf16[4,96,512]{2,1,0:T(8,128)(2,1)S(1)}, bf16[4,96,512]{2,1,0:T(8,128)(2,1)S(1)}, u32[]{:S(2)}, u32[]{:S(2)}) %collective-permute-start.11) | collective-permute-done | bytes 393248 | tf_op jit(solution)/shard_map/ppermute | solution.py:19
  105.9 2.8 %collective-permute-start.4 = (bf16[160,3072]{1,0:T(8,128)(2,1)S(1)}, bf16[160,3072]{1,0:T(8,128)(2,1)S(1)}, u32[]{:S(2)}, u32[]{:S(2)}) collective-permute-start(bf16[160,3072]{1,0:T(8,128)(2,1)S(1)} %get-tuple-element.9.refs_0_), channel_id=1, source_target_pairs={{0,16},{16,0},{1,17},{17,1},{2,18},{18,2},{3,19},{19,3},{4,20},{20... | collective-permute-start | bytes 2949128 | tf_op jit(solution)/shard_map/ppermute | solution.py:19
  108.7 1.8 collective-permute-start.5
  110.5 17.9 %collective-permute-done.2.refs_2_ = bf16[160,3072]{1,0:T(8,128)(2,1)S(1)} collective-permute-done((bf16[160,3072]{1,0:T(8,128)(2,1)S(1)}, bf16[160,3072]{1,0:T(8,128)(2,1)S(1)}, u32[]{:S(2)}, u32[]{:S(2)}) %collective-permute-start.2) | collective-permute-done | bytes 983072 | tf_op jit(solution)/shard_map/ppermute | solution.py:19
  128.4 3.0 %collective-permute-start.6 = (bf16[160,3072]{1,0:T(8,128)(2,1)S(1)}, bf16[160,3072]{1,0:T(8,128)(2,1)S(1)}, u32[]{:S(2)}, u32[]{:S(2)}) collective-permute-start(bf16[160,3072]{1,0:T(8,128)(2,1)S(1)} %collective-permute-done.2.refs_2_), channel_id=1, source_target_pairs={{0,16},{16,0},{1,17},{17,1},{2,18},{18,2},{3,19},{19,3},{4,20},{20... | collective-permute-start | bytes 2949128 | tf_op jit(solution)/shard_map/ppermute | solution.py:19
  131.4 0.0 collective-permute-start.7
  131.4 1.0 slice.29
  132.4 2.7 %collective-permute-start.15 = (bf16[4,96,512]{2,1,0:T(8,128)(2,1)S(1)}, bf16[4,96,512]{2,1,0:T(8,128)(2,1)S(1)}, u32[]{:S(2)}, u32[]{:S(2)}) collective-permute-start(bf16[4,96,512]{2,1,0:T(8,128)(2,1)S(1)} %slice.29), channel_id=1, source_target_pairs={{0,129},{1,0},{128,1},{129,128},{2,131},{3,2},{130,3},{131,130},{4... | collective-permute-start | bytes 1179656 | tf_op jit(solution)/shard_map/ppermute | solution.py:19
  135.1 1.0 slice.28
  136.2 6.9 %collective-permute-done.15.refs_17_ = bf16[4,96,512]{2,1,0:T(8,128)(2,1)S(1)} collective-permute-done((bf16[4,96,512]{2,1,0:T(8,128)(2,1)S(1)}, bf16[4,96,512]{2,1,0:T(8,128)(2,1)S(1)}, u32[]{:S(2)}, u32[]{:S(2)}) %collective-permute-start.15) | collective-permute-done | bytes 393248 | tf_op jit(solution)/shard_map/ppermute | solution.py:19
  143.1 14.2 %all-gather = f32[32,4,128]{2,1,0:T(4,128)S(1)} all-gather(f32[4,4,128]{2,1,0:T(4,128)S(1)} %maximum_bitcast_fusion.meta), channel_id=2, replica_groups=mesh['dp'=2,'y'=4,'c'=2,'z'=8,'xl'=2] {'y','c'}, dimensions={0}, use_global_device_ids=true | all-gather | bytes 73728 | tf_op jit(solution)/shard_map/all_gather | solution.py:125
  157.3 0.9 copy-done.4
  158.2 0.3 copy-done.5
  158.6 0.3 copy-done.6
  158.9 0.3 copy-done.7
  159.2 14.1 %expert.1 = bf16[4,2,2,160,256]{4,3,2,1,0:T(8,128)(2,1)} custom-call(s32[4]{0:T(128)S(1)} %pad_add_fusion.pos, f32[4,2,4,4,128]{4,3,2,1,0:T(4,128)S(1)} %bitcast.26, bf16[160,3072]{1,0:T(8,128)(2,1)S(1)} %get-tuple-element.9.refs_0_, bf16[160,3072]{1,0:T(8,128)(2,1)S(1)} %collective-permute-done.1.refs_1_, ...), custom_call_target="tpu_custom_call" | custom-call | flops 8053063680 | bytes 15728640 | tf_op jit(solution)/shard_map/expert/pallas_call | solution.py:152
  173.4 23.5 %all_to_all.15 = bf16[16,160,256]{2,1,0:T(8,128)(2,1)S(1)} all-to-all(bf16[16,160,256]{2,1,0:T(8,128)(2,1)} %bitcast.30), channel_id=1, replica_groups=mesh['dp'=2,'y'=4,'c'=2,'z'=8,'xl'=2] {'y','c','xl'}, dimensions={0} | all-to-all | bytes 2621440 | tf_op jit(solution)/shard_map/all_to_all | solution.py:168
  196.8 1.4 combine.1
  198.3 1.6 reshape.24
  (27 shorter events, 0.1 us)
Async XLA Ops:
  7.4 14.4 %collective-permute-start = (bf16[2,192,128]{2,1,0:T(8,128)(2,1)S(1)}, bf16[2,192,128]{2,1,0:T(8,128)(2,1)S(1)}, u32[]{:S(2)}, u32[]{:S(2)}) collective-permute-start(bf16[2,192,128]{2,1,0:T(8,128)(2,1)S(1)} %dynamic-slice_bitcast_fusion), channel_id=1, source_target_pairs={{0,1},{1,0},{2,3},{3,2},{4,5},{5,4},{6,7},{7,6},{8,9},{9,8},{10,11... | collective-permute-start | bytes 294920 | tf_op jit(solution)/shard_map/ppermute | solution.py:19
  13.5 8.4 %copy-start.1 = (bf16[4,128,192]{1,2,0:T(8,128)(2,1)S(1)}, bf16[4,128,192]{1,2,0:T(8,128)(2,1)}, u32[]{:S(2)}) copy-start(bf16[4,128,192]{1,2,0:T(8,128)(2,1)} %param.5) | copy-start | bytes 589828
  13.5 30.8 %all-to-all-start = ((bf16[8,96,512]{2,1,0:T(8,128)(2,1)}), bf16[8,96,512]{2,1,0:T(8,128)(2,1)S(1)}, u32[]{:S(2)}, u32[]{:S(2)}) async-start(bf16[8,96,512]{2,1,0:T(8,128)(2,1)} %get-tuple-element.14), calls=%async_computation | async-start | bytes 1572864 | tf_op jit(solution)/shard_map/all_to_all | solution.py:148
  21.8 28.5 %copy-start.2 = (s32[4,128,2]{1,2,0:T(2,128)S(1)}, s32[4,128,2]{1,2,0:T(2,128)}, u32[]{:S(2)}) copy-start(s32[4,128,2]{1,2,0:T(2,128)} %param.6) | copy-start | bytes 12292
  21.8 58.3 %copy-start.3 = (f32[4,128,2]{1,2,0:T(2,128)S(1)}, f32[4,128,2]{1,2,0:T(2,128)}, u32[]{:S(2)}) copy-start(f32[4,128,2]{1,2,0:T(2,128)} %param.7) | copy-start | bytes 12292
  21.8 58.4 %all-gather.4.cloned.1.call-start = ((), (), s32[]{:S(2)}) async-start(), calls=%async_computation.3 | async-start | bytes 1769472 | tf_op jit(solution)/shard_map/all_gather | solution.py:131
  44.3 34.0 %all-to-all-start.1 = ((bf16[8,96,512]{2,1,0:T(8,128)(2,1)}), bf16[8,96,512]{2,1,0:T(8,128)(2,1)S(1)}, u32[]{:S(2)}, u32[]{:S(2)}) async-start(bf16[8,96,512]{2,1,0:T(8,128)(2,1)} %get-tuple-element.13), calls=%async_computation.1 | async-start | bytes 1572864 | tf_op jit(solution)/shard_map/all_to_all | solution.py:148
  47.9 37.2 %collective-permute-start.9 = (bf16[8,96,512]{2,1,0:T(8,128)(2,1)S(1)}, bf16[8,96,512]{2,1,0:T(8,128)(2,1)S(1)}, u32[]{:S(2)}, u32[]{:S(2)}) collective-permute-start(bf16[8,96,512]{2,1,0:T(8,128)(2,1)S(1)} %all-to-all-done.refs_8_), channel_id=1, source_target_pairs={{0,129},{1,0},{128,1},{129,128},{2,131},{3,2},{130,3},{131,130},{4... | collective-permute-start | bytes 2359304 | tf_op jit(solution)/shard_map/ppermute | solution.py:19
  50.3 37.3 %collective-permute-start.8 = (bf16[8,96,512]{2,1,0:T(8,128)(2,1)S(1)}, bf16[8,96,512]{2,1,0:T(8,128)(2,1)S(1)}, u32[]{:S(2)}, u32[]{:S(2)}) collective-permute-start(bf16[8,96,512]{2,1,0:T(8,128)(2,1)S(1)} %all-to-all-done.refs_8_), channel_id=1, source_target_pairs={{0,1},{1,128},{128,129},{129,0},{2,3},{3,130},{130,131},{131,2},{4... | collective-permute-start | bytes 2359304 | tf_op jit(solution)/shard_map/ppermute | solution.py:19
  78.3 17.6 %collective-permute-start.13 = (bf16[8,96,512]{2,1,0:T(8,128)(2,1)S(1)}, bf16[8,96,512]{2,1,0:T(8,128)(2,1)}, u32[]{:S(2)}, u32[]{:S(2)}) collective-permute-start(bf16[8,96,512]{2,1,0:T(8,128)(2,1)S(1)} %all-to-all-done.1.refs_13_), channel_id=1, source_target_pairs={{0,129},{1,0},{128,1},{129,128},{2,131},{3,2},{130,3},{131,130},{4... | collective-permute-start | bytes 2359304 | tf_op jit(solution)/shard_map/ppermute | solution.py:19
  80.1 19.3 %collective-permute-start.12 = (bf16[8,96,512]{2,1,0:T(8,128)(2,1)S(1)}, bf16[8,96,512]{2,1,0:T(8,128)(2,1)}, u32[]{:S(2)}, u32[]{:S(2)}) collective-permute-start(bf16[8,96,512]{2,1,0:T(8,128)(2,1)S(1)} %all-to-all-done.1.refs_13_), channel_id=1, source_target_pairs={{0,1},{1,128},{128,129},{129,0},{2,3},{3,130},{130,131},{131,2},{4... | collective-permute-start | bytes 2359304 | tf_op jit(solution)/shard_map/ppermute | solution.py:19
  80.3 1.4 copy-start
  83.6 25.1 %collective-permute-start.1 = (bf16[160,3072]{1,0:T(8,128)(2,1)S(1)}, bf16[160,3072]{1,0:T(8,128)(2,1)S(1)}, u32[]{:S(2)}, u32[]{:S(2)}) collective-permute-start(bf16[160,3072]{1,0:T(8,128)(2,1)S(1)} %get-tuple-element.10), channel_id=1, source_target_pairs={{0,32},{32,64},{64,96},{96,0},{1,33},{33,65},{65,97},{97,1},{2,34}... | collective-permute-start | bytes 2949128 | tf_op jit(solution)/shard_map/ppermute | solution.py:19
  85.1 43.3 %collective-permute-start.2 = (bf16[160,3072]{1,0:T(8,128)(2,1)S(1)}, bf16[160,3072]{1,0:T(8,128)(2,1)S(1)}, u32[]{:S(2)}, u32[]{:S(2)}) collective-permute-start(bf16[160,3072]{1,0:T(8,128)(2,1)S(1)} %get-tuple-element.11), channel_id=1, source_target_pairs={{0,64},{32,96},{64,0},{96,32},{1,65},{33,97},{65,1},{97,33},{2,66}... | collective-permute-start | bytes 2949128 | tf_op jit(solution)/shard_map/ppermute | solution.py:19
  87.6 43.8 %collective-permute-start.3 = (bf16[160,3072]{1,0:T(8,128)(2,1)S(1)}, bf16[160,3072]{1,0:T(8,128)(2,1)S(1)}, u32[]{:S(2)}, u32[]{:S(2)}) collective-permute-start(bf16[160,3072]{1,0:T(8,128)(2,1)S(1)} %get-tuple-element.12), channel_id=1, source_target_pairs={{0,96},{32,0},{64,32},{96,64},{1,97},{33,1},{65,33},{97,65},{2,98}... | collective-permute-start | bytes 2949128 | tf_op jit(solution)/shard_map/ppermute | solution.py:19
  95.9 10.0 %collective-permute-start.11 = (bf16[4,96,512]{2,1,0:T(8,128)(2,1)S(1)}, bf16[4,96,512]{2,1,0:T(8,128)(2,1)S(1)}, u32[]{:S(2)}, u32[]{:S(2)}) collective-permute-start(bf16[4,96,512]{2,1,0:T(8,128)(2,1)S(1)} %slice.26), channel_id=1, source_target_pairs={{0,129},{1,0},{128,1},{129,128},{2,131},{3,2},{130,3},{131,130},{4... | collective-permute-start | bytes 1179656 | tf_op jit(solution)/shard_map/ppermute | solution.py:19
  99.4 33.0 %collective-permute-start.10 = (bf16[4,96,512]{2,1,0:T(8,128)(2,1)S(1)}, bf16[4,96,512]{2,1,0:T(8,128)(2,1)S(1)}, u32[]{:S(2)}, u32[]{:S(2)}) collective-permute-start(bf16[4,96,512]{2,1,0:T(8,128)(2,1)S(1)} %slice.25), channel_id=1, source_target_pairs={{0,1},{1,128},{128,129},{129,0},{2,3},{3,130},{130,131},{131,2},{4... | collective-permute-start | bytes 1179656 | tf_op jit(solution)/shard_map/ppermute | solution.py:19
  105.9 51.4 %collective-permute-start.4 = (bf16[160,3072]{1,0:T(8,128)(2,1)S(1)}, bf16[160,3072]{1,0:T(8,128)(2,1)S(1)}, u32[]{:S(2)}, u32[]{:S(2)}) collective-permute-start(bf16[160,3072]{1,0:T(8,128)(2,1)S(1)} %get-tuple-element.9.refs_0_), channel_id=1, source_target_pairs={{0,16},{16,0},{1,17},{17,1},{2,18},{18,2},{3,19},{19,3},{4,20},{20... | collective-permute-start | bytes 2949128 | tf_op jit(solution)/shard_map/ppermute | solution.py:19
  108.7 48.5 %collective-permute-start.5 = (bf16[160,3072]{1,0:T(8,128)(2,1)S(1)}, bf16[160,3072]{1,0:T(8,128)(2,1)S(1)}, u32[]{:S(2)}, u32[]{:S(2)}) collective-permute-start(bf16[160,3072]{1,0:T(8,128)(2,1)S(1)} %collective-permute-done.1.refs_1_), channel_id=1, source_target_pairs={{0,16},{16,0},{1,17},{17,1},{2,18},{18,2},{3,19},{19,3},{4,20},{20... | collective-permute-start | bytes 2949128 | tf_op jit(solution)/shard_map/ppermute | solution.py:19
  128.4 28.9 %collective-permute-start.6 = (bf16[160,3072]{1,0:T(8,128)(2,1)S(1)}, bf16[160,3072]{1,0:T(8,128)(2,1)S(1)}, u32[]{:S(2)}, u32[]{:S(2)}) collective-permute-start(bf16[160,3072]{1,0:T(8,128)(2,1)S(1)} %collective-permute-done.2.refs_2_), channel_id=1, source_target_pairs={{0,16},{16,0},{1,17},{17,1},{2,18},{18,2},{3,19},{19,3},{4,20},{20... | collective-permute-start | bytes 2949128 | tf_op jit(solution)/shard_map/ppermute | solution.py:19
  131.4 25.9 %collective-permute-start.7 = (bf16[160,3072]{1,0:T(8,128)(2,1)S(1)}, bf16[160,3072]{1,0:T(8,128)(2,1)S(1)}, u32[]{:S(2)}, u32[]{:S(2)}) collective-permute-start(bf16[160,3072]{1,0:T(8,128)(2,1)S(1)} %collective-permute-done.3.refs_3_), channel_id=1, source_target_pairs={{0,16},{16,0},{1,17},{17,1},{2,18},{18,2},{3,19},{19,3},{4,20},{20... | collective-permute-start | bytes 2949128 | tf_op jit(solution)/shard_map/ppermute | solution.py:19
  132.4 10.7 %collective-permute-start.15 = (bf16[4,96,512]{2,1,0:T(8,128)(2,1)S(1)}, bf16[4,96,512]{2,1,0:T(8,128)(2,1)S(1)}, u32[]{:S(2)}, u32[]{:S(2)}) collective-permute-start(bf16[4,96,512]{2,1,0:T(8,128)(2,1)S(1)} %slice.29), channel_id=1, source_target_pairs={{0,129},{1,0},{128,1},{129,128},{2,131},{3,2},{130,3},{131,130},{4... | collective-permute-start | bytes 1179656 | tf_op jit(solution)/shard_map/ppermute | solution.py:19
  143.1 14.2 %collective-permute-start.14 = (bf16[4,96,512]{2,1,0:T(8,128)(2,1)S(1)}, bf16[4,96,512]{2,1,0:T(8,128)(2,1)S(1)}, u32[]{:S(2)}, u32[]{:S(2)}) collective-permute-start(bf16[4,96,512]{2,1,0:T(8,128)(2,1)S(1)} %slice.28), channel_id=1, source_target_pairs={{0,1},{1,128},{128,129},{129,0},{2,3},{3,130},{130,131},{131,2},{4... | collective-permute-start | bytes 1179656 | tf_op jit(solution)/shard_map/ppermute | solution.py:19
  157.3 0.9 copy-start.4
  157.3 1.3 copy-start.5
  157.3 1.6 copy-start.6
  157.3 1.9 copy-start.7
Sparse Core Ops, SparseCore 0:
  24.4 52.1 all-gather.3

commit v2 on v1

v2 whole, which is shorter than its diff:
```python
import functools

import jax
import jax.numpy as jnp
from jax import lax
from jax.experimental import pallas as pl
from jax.experimental.pallas import tpu as pltpu
from jax.sharding import Mesh, PartitionSpec as P

MOST = 80
X = ("dp", "xl")
BF, F32 = jnp.bfloat16, jnp.float32
ANY = pl.BlockSpec(memory_space=pl.ANY)
VM = pl.BlockSpec(memory_space=pltpu.VMEM)
SM = pl.BlockSpec(memory_space=pltpu.SMEM)


def ring(x, axis, size, step):
    return lax.ppermute(x, axis, [(i, (i + step) % size) for i in range(size)])


def ranks(member):
    n = member.shape[1]
    before = lax.broadcasted_iota(jnp.int32, (n, n), 0) < lax.broadcasted_iota(jnp.int32, (n, n), 1)
    return jnp.dot(member.astype(BF), before.astype(BF), preferred_element_type=F32)


def slots(rank, member):
    row = lax.broadcasted_iota(jnp.int32, (MOST, rank.shape[1]), 0).astype(F32)
    return (row == rank) & (member > 0)


def dispatch_kernel(pos, meta, *refs):
    y, xl = pos[0], pos[2]
    feats, outs = refs[:8], refs[8:]
    ss, width, n = feats[0].shape
    lane = lax.broadcasted_iota(jnp.int32, (MOST, 128), 1)
    for s in range(ss):
        own = meta[2 * xl + s]
        rows = []
        members = []
        for d in range(4):
            e = lax.rem(y + d, 4).astype(F32)
            members.append(((own[0:1] == e) | (own[1:2] == e)).astype(F32))
        rank = ranks(jnp.concatenate(members, axis=0))
        for d in range(4):
            place = slots(rank[d : d + 1], members[d])
            rows.append(place.astype(BF))
            e = lax.rem(y + d, 4).astype(F32)
            weight = jnp.where(own[0:1] == e, own[2:3], own[3:4])
            whole = jnp.broadcast_to(jnp.sum(jnp.where(place, weight, 0.0), axis=1, keepdims=True), (MOST, 128))
            high = whole.astype(BF)
            rest = whole - high.astype(F32)
            mid = rest.astype(BF)
            low = (rest - mid.astype(F32)).astype(BF)
            terms = jnp.where(lane == 0, high.astype(F32), jnp.where(lane == 1, mid.astype(F32), jnp.where(lane == 2, low.astype(F32), 0.0)))
            outs[d][s * MOST : (s + 1) * MOST, 8 * width :] = terms.astype(BF)
        onehot = jnp.concatenate(rows, axis=0)
        for k in range(8):
            picked = lax.dot_general(onehot, feats[k][s], (((1,), (1,)), ((), ())), preferred_element_type=F32).astype(BF)
            for d in range(4):
                outs[d][s * MOST : (s + 1) * MOST, k * width : (k + 1) * width] = picked[d * MOST : (d + 1) * MOST]


def expert_kernel(chunks, pos, *refs):
    xs, refs = refs[:8], refs[8:]
    ws, refs = refs[: 5 * chunks], refs[5 * chunks :]
    out, xbuf, wbuf, xsem, wsem = refs
    y, c, xl, dp = pos[0], pos[1], pos[2], pos[3]
    rows = xs[0].shape[0]
    depth = ws[0].shape[1]
    width = 2 * 8 * depth * chunks
    xcopies, wcopies = [], []
    for g in range(8):
        xcopies.append(pltpu.make_async_copy(xs[g], xbuf.at[pl.ds(g * rows, rows)], xsem.at[g]))
    here = dp * 2 + xl
    for ch in range(chunks):
        own, left, right, far_a, far_b = ws[5 * ch : 5 * ch + 5]
        span = pl.ds(ch * depth, depth)
        for i, (src, off, zlo, zn) in enumerate(((own, 0, 0, 8), (left, 3, 0, 8), (right, 1, 0, 8), (far_a, 2, 0, 4), (far_b, 2, 4, 4))):
            j = lax.rem(here + off, 4)
            for k in range(zn):
                dst = wbuf.at[lax.div(j, 2), lax.rem(zlo + k + 8 - pos[4], 8), lax.rem(j, 2), span]
                wcopies.append(pltpu.make_async_copy(src.at[k], dst, wsem.at[ch * 5 + i, k]))
    for cp in wcopies + xcopies:
        cp.start()
    for cp in wcopies:
        cp.wait()
    half = 4 * rows
    for m in range(2):
        for cp in xcopies[4 * m : 4 * m + 4]:
            cp.wait()
        part = slice(m * half, (m + 1) * half)
        data = xbuf[part, :width]
        rw = jnp.sum(xbuf[part, width:].astype(F32), axis=1, keepdims=True)
        gate = jnp.dot(data, wbuf[0].reshape(width, 256), preferred_element_type=F32)
        up = jnp.dot(data, wbuf[1].reshape(width, 256), preferred_element_type=F32)
        act = (rw * (gate / (1.0 + jnp.exp(-gate)) * up)).astype(BF)
        for d in range(4):
            for t in range(2):
                out[lax.rem(y + 4 - d, 4), c + m - 2 * c * m, t] = act[d * rows : (d + 1) * rows, t * 128 : (t + 1) * 128]


def combine_kernel(meta, recv_a, recv_b, out):
    steps = meta.shape[0]
    for s in range(steps):
        own = meta[s]
        members = [((own[0:1] == e) | (own[1:2] == e)).astype(F32) for e in range(4)]
        rank = ranks(jnp.concatenate(members, axis=0))
        left, right = [], []
        for e in range(4):
            place = slots(rank[e : e + 1], members[e])
            left.append(jnp.concatenate([(place & (own[k : k + 1] == e)).astype(BF) for k in range(2)], axis=1))
            part = pl.ds((s % 2) * MOST, MOST)
            right.append(jnp.concatenate([r[e, h, s // 2, part] for h in range(2) for r in (recv_a, recv_b)], axis=1))
        picked = lax.dot_general(
            jnp.concatenate(left, axis=0), jnp.concatenate(right, axis=0), (((0,), (0,)), ((), ())), preferred_element_type=F32
        ).astype(BF)
        n = picked.shape[0] // 2
        out[s] = jnp.concatenate([picked[:n], picked[n:]], axis=1)


def body(tokens, expert_ids, route_weights, gate_train, up_train):
    chunks, rounds = 1, 2
    dp, y, c, z, xl = (lax.axis_index(a) for a in ("dp", "y", "c", "z", "xl"))
    pos = jnp.stack([y, c, xl, dp, z]).astype(jnp.int32)
    steps, n, width = tokens.shape
    meta = jnp.concatenate([expert_ids.astype(F32), route_weights], axis=2).transpose(0, 2, 1)
    turned = tokens.transpose(0, 2, 1).reshape(2, steps // 2, width, n)
    mine = lax.dynamic_index_in_dim(turned, xl, 0, keepdims=False)
    theirs = lax.dynamic_index_in_dim(turned, 1 - xl, 0, keepdims=False)
    got = ring(theirs, "xl", 2, 1)
    pair = jnp.concatenate([jnp.where(xl == 0, mine, got), jnp.where(xl == 0, got, mine)], axis=1)
    source = jnp.where(dp == 0, gate_train[0], up_train[0])
    rows, units = source.shape
    depth = rows // chunks
    wide = units // 8 // 2 // rounds
    blocks = source.reshape(rows, 8, 2, rounds, wide).transpose(3, 1, 0, 2, 4).reshape(rounds, 8, rows, 2 * wide)
    below, above = [pair], [pair]
    for k in range(2):
        below.append(ring(below[-1], "z", 8, 1))
        above.append(ring(above[-1], "z", 8, -1))
    part = blocks[0, :, :depth]
    part, below[2], above[2] = lax.optimization_barrier((part, below[2], above[2]))
    first = lax.all_to_all(part, "z", split_axis=0, concat_axis=0, tiled=True)
    for k in range(2, 3):
        below.append(ring(below[-1], "z", 8, 1))
        above.append(ring(above[-1], "z", 8, -1))
    opposite = jnp.concatenate([ring(below[3][:1], "z", 8, 1), ring(above[3][1:], "z", 8, -1)], axis=0)
    feats = [pair] + above[1:] + [opposite] + below[:0:-1]
    pieces = []
    for r in range(rounds):
        for ch in range(chunks):
            own = first
            if r + ch > 0:
                part = blocks[r, :, ch * depth : (ch + 1) * depth]
                part, opposite, first = lax.optimization_barrier((part, opposite, first))
                pieces[-1][0] = first
                own = lax.all_to_all(part, "z", split_axis=0, concat_axis=0, tiled=True)
                first = own
                own, far_a, far_b = lax.optimization_barrier((own, pieces[-1][3], pieces[-1][4]))
                pieces[-1][3:] = far_a, far_b
            left, right = ring(own, X, 4, 1), ring(own, X, 4, -1)
            far_a, far_b = ring(left[:4], X, 4, 1), ring(right[4:], X, 4, -1)
            pieces.append([own, left, right, far_a, far_b])
    feats[4] = opposite
    sent = pl.pallas_call(
        dispatch_kernel,
        out_shape=[jax.ShapeDtypeStruct((2 * MOST, 16 * width + 128), BF)] * 4,
        in_specs=[SM] + [VM] * 9,
        out_specs=[VM] * 4,
        compiler_params=pltpu.CompilerParams(vmem_limit_bytes=32 << 20),
        name="dispatch",
    )(pos, meta, *feats)
    held = [sent[0]] + [ring(sent[d], "y", 4, d) for d in (1, 2, 3)]
    other = [ring(h, "c", 2, 1) for h in held]
    backs = []
    for r in range(rounds):
        ws = [w for ch in range(chunks) for w in pieces[r * chunks + ch]]
        act = pl.pallas_call(
            functools.partial(expert_kernel, chunks),
            out_shape=jax.ShapeDtypeStruct((4, 2, 2, 2 * MOST, wide), BF),
            in_specs=[SM] + [ANY] * (8 + 5 * chunks),
            out_specs=VM,
            scratch_shapes=[
                pltpu.VMEM((16 * MOST, 16 * width + 128), BF),
                pltpu.VMEM((2, 8, 2, rows, 2 * wide), BF),
                pltpu.SemaphoreType.DMA((8,)),
                pltpu.SemaphoreType.DMA((5 * chunks, 8)),
            ],
            compiler_params=pltpu.CompilerParams(vmem_limit_bytes=58 << 20),
            cost_estimate=pl.CostEstimate(
                flops=16 * MOST * 16 * width * 8 * wide, bytes_accessed=12 << 20, transcendentals=16 * MOST * 2 * wide
            ),
            name="expert",
        )(pos, *held, *other, *ws)
        back = lax.all_to_all(act.reshape(16, 2 * MOST, wide), ("y", "c", "xl"), split_axis=0, concat_axis=0, tiled=True)
        backs.append(back.reshape(4, 2, 2, 2 * MOST, wide))
    out = pl.pallas_call(
        combine_kernel,
        out_shape=jax.ShapeDtypeStruct((steps, n, 1024), BF),
        in_specs=[VM] * 3,
        out_specs=VM,
        compiler_params=pltpu.CompilerParams(vmem_limit_bytes=32 << 20),
        name="combine",
    )(meta, *backs)
    return out.reshape(steps, n, 2, 2, 256)


def solution(mesh):
    fine = Mesh(mesh.devices.reshape(2, 4, 2, 8, 2), ("dp", "y", "c", "z", "xl"))
    group, tensor = ("dp", "y", "c"), ("z", "xl")
    in_specs = (
        P(None, group, tensor),
        P(None, group, None),
        P(None, group, None),
        P(("y", "c"), tensor, None),
        P(("y", "c"), tensor, None),
    )
    out_specs = P(None, group, None, None, tensor)
    return jax.shard_map(body, mesh=fine, in_specs=in_specs, out_specs=out_specs, check_vma=False)
```

time: 207 us -> 191 us (0.923)
  starting transfers between devices: 37.1 us -> 66.8 us
  waiting for transfers between devices: 88.1 us -> 58.6 us
  blocking collectives: 37.6 us -> 17.6 us
  between operations: 13.6 us -> 0.29 us
  Pallas kernels: 17.6 us -> 25.5 us
  local copies, waits for them, and re-layouts: 10.3 us -> 17.5 us
    all_to_all x2 -> x3, waiting for transfers between devices: 49.7 us -> 0.01 us  [the longest x1 0.01 us: body(): first = lax.all_to_all(part, 'z', split_axis=0, concat_axis=0, tiled=True)]
    ppermute x16 -> x24, starting transfers between devices: 25.2 us -> 50.8 us  [ring(): return lax.ppermute(x, axis, [(i, (i + step) % size) for i in range(size)])]
    ppermute x16 -> x24, waiting for transfers between devices: 38.4 us -> 58.6 us  [ring(): return lax.ppermute(x, axis, [(i, (i + step) % size) for i in range(size)])]
    all_gather x1 -> x0, blocking collectives: 14.2 us -> none  [body(): lax.all_gather(meta, ('y', 'c'), axis=0, tiled=False)]
    pallas_call x1 -> x2, Pallas kernels: 14.1 us -> 20.4 us  [body(): pl.pallas_call(functools.partial(expert_kernel, chunks), out_shape=jax.Sh...]
    all_to_all x1, blocking collectives: 23.5 us -> 17.6 us  [body(): lax.all_to_all(act.reshape(16, 2 * MOST, wide), ('y', 'c', 'xl'), split_a...]
    select_n x1 -> x2, local copies, waits for them, and re-layouts: 0.5 us -> 4.95 us  [body(): source = jnp.where(dp == 0, gate_train[0], up_train[0])]
    all_to_all x2 -> x3, starting transfers between devices: 11.9 us -> 16 us  [the longest x1 6.05 us: body(): own = lax.all_to_all(part, 'z', split_axis=0, concat_axis=0, tiled=True)]
  transfers between devices with their start and end apart: 19 -> 27, of which waited for: 6 -> 10; matrix products, arithmetic and copies ran while one was open for 3% -> 7% of each run, Pallas kernels for 1% -> 13%
where the time goes in v2:
time: 191 us; the launch traced here: 190 us
  starting transfers between devices  66.8 us (35%)
  waiting for transfers between devices  58.6 us (31%)
  Pallas kernels  25.5 us (13%)
  blocking collectives  17.6 us (9%)
  local copies, waits for them, and re-layouts  17.5 us (9%)
  other arithmetic  3.42 us (2%)
    ppermute x24, waiting for transfers between devices, ring(): return lax.ppermute(x, axis, [(i, (i + step) % size) for i in range(size)])  58.6 us
    ppermute x24, starting transfers between devices, ring(): return lax.ppermute(x, axis, [(i, (i + step) % size) for i in range(size)])  50.8 us
    pallas_call x2, Pallas kernels, body(): pl.pallas_call(functools.partial(expert_kernel, chunks), out_shape=jax.Sh...  20.4 us
    all_to_all x1, blocking collectives, body(): lax.all_to_all(act.reshape(16, 2 * MOST, wide), ('y', 'c', 'xl'), split_a...  17.6 us
    all_to_all x1, starting transfers between devices, body(): own = lax.all_to_all(part, 'z', split_axis=0, concat_axis=0, tiled=True)  6.05 us
    all_to_all x1, starting transfers between devices, body(): lax.all_to_all(act.reshape(16, 2 * MOST, wide), ('y', 'c', 'xl'), split_a...  5.62 us
    select_n x2, local copies, waits for them, and re-layouts, body(): source = jnp.where(dp == 0, gate_train[0], up_train[0])  4.95 us
    all_to_all x1, starting transfers between devices, body(): first = lax.all_to_all(part, 'z', split_axis=0, concat_axis=0, tiled=True)  4.36 us
  transfers between devices with their start and end apart: 27, of which 10 were waited for; matrix products, arithmetic and copies ran while one was open for 7% of the time, Pallas kernels for 13%

profile of v2, /device:TPU:1, one launch (start us, length us, event | category | flops | bytes accessed | tf_op | source)
XLA Modules:
  0.0 189.8 jit_solution(3909825448055103752)
XLA Ops:
  0.0 0.9 dynamic-slice_bitcast_fusion
  0.9 2.0 %collective-permute-start = (bf16[2,192,128]{2,1,0:T(8,128)(2,1)S(1)}, bf16[2,192,128]{2,1,0:T(8,128)(2,1)S(1)}, u32[]{:S(2)}, u32[]{:S(2)}) collective-permute-start(bf16[2,192,128]{2,1,0:T(8,128)(2,1)S(1)} %dynamic-slice_bitcast_fusion), channel_id=1, source_target_pairs={{0,1},{1,0},{2,3},{3,2},{4,5},{5,4},{6,7},{7,6},{8,9},{9,8},{10,11... | collective-permute-start | bytes 294920 | tf_op jit(solution)/shard_map/ppermute | solution.py:19
  2.9 2.0 %collective-permute-done = bf16[2,192,128]{2,1,0:T(8,128)(2,1)S(1)} collective-permute-done((bf16[2,192,128]{2,1,0:T(8,128)(2,1)S(1)}, bf16[2,192,128]{2,1,0:T(8,128)(2,1)S(1)}, u32[]{:S(2)}, u32[]{:S(2)}) %collective-permute-start) | collective-permute-done | bytes 98336 | tf_op jit(solution)/shard_map/ppermute | solution.py:19
  4.9 0.9 bitcast_select_fusion.1
  5.9 5.9 %collective-permute-start.1 = (bf16[2,384,128]{2,1,0:T(8,128)(2,1)S(1)}, bf16[2,384,128]{2,1,0:T(8,128)(2,1)S(1)}, u32[]{:S(2)}, u32[]{:S(2)}) collective-permute-start(bf16[2,384,128]{2,1,0:T(8,128)(2,1)S(1)} %pad_maximum_fusion.refs_0_), channel_id=1, source_target_pairs={{0,14},{2,0},{4,2},{6,4},{8,6},{10,8},{12,10},{14,12},{1,15},{3,1}... | collective-permute-start | bytes 589832 | tf_op jit(solution)/shard_map/ppermute | solution.py:19
  11.8 1.6 broadcast_select_fusion
  13.4 2.3 %select_n.38 = bf16[192,8,2,2,128]{4,3,2,1,0:T(2,128)(2,1)} reshape(bf16[1,192,4096]{2,1,0:T(8,128)(2,1)S(1)} %broadcast_select_fusion) | data formatting | bytes 3145728 | tf_op jit(solution)/shard_map/jit(_where)/select_n | solution.py:134
  15.7 2.6 %copy.8 = bf16[192,8,2,2,128]{4,2,0,1,3:T(2,128)(2,1)S(1)} copy(bf16[192,8,2,2,128]{4,3,2,1,0:T(2,128)(2,1)} %select_n.38) | data formatting | bytes 3145728 | tf_op jit(solution)/shard_map/jit(_where)/select_n | solution.py:134
  18.4 2.7 %collective-permute-start.4 = (bf16[2,384,128]{2,1,0:T(8,128)(2,1)S(1)}, bf16[2,384,128]{2,1,0:T(8,128)(2,1)S(1)}, u32[]{:S(2)}, u32[]{:S(2)}) collective-permute-start(bf16[2,384,128]{2,1,0:T(8,128)(2,1)S(1)} %collective-permute-done.1.refs_1_), channel_id=1, source_target_pairs={{0,14},{2,0},{4,2},{6,4},{8,6},{10,8},{12,10},{14,12},{1,15},{3,1}... | collective-permute-start | bytes 589832 | tf_op jit(solution)/shard_map/ppermute | solution.py:19
  21.2 1.2 fusion
  22.4 1.4 squeeze.17
  24.2 4.4 %all-to-all-start = ((bf16[8,192,256]{2,1,0:T(8,128)(2,1)}), bf16[8,192,256]{2,1,0:T(8,128)(2,1)S(1)}, u32[]{:S(2)}, u32[]{:S(2)}) async-start(bf16[8,192,256]{2,1,0:T(8,128)(2,1)} %squeeze.17), calls=%async_computation | async-start | bytes 1572864 | tf_op jit(solution)/shard_map/all_to_all | solution.py:145
  28.5 2.7 %collective-permute-start.5 = (bf16[2,384,128]{2,1,0:T(8,128)(2,1)S(1)}, bf16[2,384,128]{2,1,0:T(8,128)(2,1)S(1)}, u32[]{:S(2)}, u32[]{:S(2)}) collective-permute-start(bf16[2,384,128]{2,1,0:T(8,128)(2,1)S(1)} %collective-permute-done.4.refs_2_), channel_id=1, source_target_pairs={{0,14},{2,0},{4,2},{6,4},{8,6},{10,8},{12,10},{14,12},{1,15},{3,1}... | collective-permute-start | bytes 589832 | tf_op jit(solution)/shard_map/ppermute | solution.py:19
  31.2 17.1 %collective-permute-done.5.refs_3_ = bf16[2,384,128]{2,1,0:T(8,128)(2,1)S(1)} collective-permute-done((bf16[2,384,128]{2,1,0:T(8,128)(2,1)S(1)}, bf16[2,384,128]{2,1,0:T(8,128)(2,1)S(1)}, u32[]{:S(2)}, u32[]{:S(2)}) %collective-permute-start.5) | collective-permute-done | bytes 196640 | tf_op jit(solution)/shard_map/ppermute | solution.py:19
  48.3 1.5 collective-permute-start.8
  50.5 1.4 squeeze.18
  51.8 1.4 collective-permute-done.8
  53.2 2.0 %collective-permute-done.7 = bf16[1,384,128]{2,1,0:T(8,128)(2,1)} collective-permute-done((bf16[1,384,128]{2,1,0:T(8,128)(2,1)S(1)}, bf16[1,384,128]{2,1,0:T(8,128)(2,1)}, u32[]{:S(2)}, u32[]{:S(2)}) %collective-permute-start.7) | collective-permute-done | bytes 98336 | tf_op jit(solution)/shard_map/ppermute | solution.py:19
  55.3 0.9 pad_maximum_fusion.1.refs_4_
  56.2 6.0 %all-to-all-start.1 = ((bf16[8,192,256]{2,1,0:T(8,128)(2,1)}), bf16[8,192,256]{2,1,0:T(8,128)(2,1)}, u32[]{:S(2)}, u32[]{:S(2)}) async-start(bf16[8,192,256]{2,1,0:T(8,128)(2,1)} %squeeze.18), calls=%async_computation.1 | async-start | bytes 1572864 | tf_op jit(solution)/shard_map/all_to_all | solution.py:159
  62.3 1.2 collective-permute-start.16
  63.5 1.5 collective-permute-start.17
  65.1 3.7 %dispatch.1 = (bf16[160,3200]{1,0:T(8,128)(2,1)S(1)}, bf16[160,3200]{1,0:T(8,128)(2,1)}, bf16[160,3200]{1,0:T(8,128)(2,1)}, bf16[160,3200]{1,0:T(8,128)(2,1)}) custom-call(s32[5]{0:T(128)S(1)} %stack.23.pos, f32[4,4,128]{2,1,0:T(4,128)S(1)} %maximum_bitcast_fusion.meta, bf16[2,384,128]{2,1,0:T(8,128)(2,1)S(1)} %pad_maximum_fusion.refs_0_, ...), custom_call_target="tpu_custom_call" | custom-call | tf_op jit(solution)/shard_map/dispatch/pallas_call | solution.py:167
  68.8 1.3 collective-permute-start.9
  70.1 2.6 %collective-permute-start.10 = (bf16[160,3200]{1,0:T(8,128)(2,1)}, bf16[160,3200]{1,0:T(8,128)(2,1)}, u32[]{:S(2)}, u32[]{:S(2)}) collective-permute-start(bf16[160,3200]{1,0:T(8,128)(2,1)} %get-tuple-element.24), channel_id=1, source_target_pairs={{0,64},{32,96},{64,0},{96,32},{1,65},{33,97},{65,1},{97,33},{2,66}... | collective-permute-start | bytes 3072008 | tf_op jit(solution)/shard_map/ppermute | solution.py:19
  72.7 1.1 collective-permute-start.11
  73.8 2.2 %collective-permute-done.16.refs_9_ = bf16[8,192,256]{2,1,0:T(8,128)(2,1)} collective-permute-done((bf16[8,192,256]{2,1,0:T(8,128)(2,1)S(1)}, bf16[8,192,256]{2,1,0:T(8,128)(2,1)}, u32[]{:S(2)}, u32[]{:S(2)}) %collective-permute-start.16) | collective-permute-done | bytes 786464 | tf_op jit(solution)/shard_map/ppermute | solution.py:19
  76.0 1.0 slice.38
  77.1 1.0 slice.39
  78.2 2.7 %collective-permute-start.19 = (bf16[4,192,256]{2,1,0:T(8,128)(2,1)S(1)}, bf16[4,192,256]{2,1,0:T(8,128)(2,1)S(1)}, u32[]{:S(2)}, u32[]{:S(2)}) collective-permute-start(bf16[4,192,256]{2,1,0:T(8,128)(2,1)S(1)} %slice.39), channel_id=1, source_target_pairs={{0,129},{1,0},{128,1},{129,128},{2,131},{3,2},{130,3},{131,130},{4... | collective-permute-start | bytes 1179656 | tf_op jit(solution)/shard_map/ppermute | solution.py:19
  80.9 6.4 %collective-permute-done.18.refs_11_ = bf16[4,192,256]{2,1,0:T(8,128)(2,1)S(1)} collective-permute-done((bf16[4,192,256]{2,1,0:T(8,128)(2,1)S(1)}, bf16[4,192,256]{2,1,0:T(8,128)(2,1)S(1)}, u32[]{:S(2)}, u32[]{:S(2)}) %collective-permute-start.18) | collective-permute-done | bytes 393248 | tf_op jit(solution)/shard_map/ppermute | solution.py:19
  87.4 0.8 copy-done.9
  88.1 0.7 copy-done.10
  89.3 10.9 %collective-permute-start.12 = (bf16[160,3200]{1,0:T(8,128)(2,1)S(1)}, bf16[160,3200]{1,0:T(8,128)(2,1)S(1)}, u32[]{:S(2)}, u32[]{:S(2)}) collective-permute-start(bf16[160,3200]{1,0:T(8,128)(2,1)S(1)} %get-tuple-element.22.refs_0_), channel_id=1, source_target_pairs={{0,16},{16,0},{1,17},{17,1},{2,18},{18,2},{3,19},{19,3},{4,20},{20... | collective-permute-start | bytes 3072008 | tf_op jit(solution)/shard_map/ppermute | solution.py:19
  100.2 1.7 collective-permute-start.13
  101.9 8.7 %collective-permute-done.10.refs_2_ = bf16[160,3200]{1,0:T(8,128)(2,1)} collective-permute-done((bf16[160,3200]{1,0:T(8,128)(2,1)}, bf16[160,3200]{1,0:T(8,128)(2,1)}, u32[]{:S(2)}, u32[]{:S(2)}) %collective-permute-start.10) | collective-permute-done | bytes 1024032 | tf_op jit(solution)/shard_map/ppermute | solution.py:19
  110.6 8.0 %collective-permute-start.14 = (bf16[160,3200]{1,0:T(8,128)(2,1)}, bf16[160,3200]{1,0:T(8,128)(2,1)}, u32[]{:S(2)}, u32[]{:S(2)}) collective-permute-start(bf16[160,3200]{1,0:T(8,128)(2,1)} %collective-permute-done.10.refs_2_), channel_id=1, source_target_pairs={{0,16},{16,0},{1,17},{17,1},{2,18},{18,2},{3,19},{19,3},{4,20},{20... | collective-permute-start | bytes 3072008 | tf_op jit(solution)/shard_map/ppermute | solution.py:19
  118.6 1.3 collective-permute-start.21
  119.9 17.7 %collective-permute-done.21.refs_10_ = bf16[8,192,256]{2,1,0:T(8,128)(2,1)S(1)} collective-permute-done((bf16[8,192,256]{2,1,0:T(8,128)(2,1)}, bf16[8,192,256]{2,1,0:T(8,128)(2,1)S(1)}, u32[]{:S(2)}, u32[]{:S(2)}) %collective-permute-start.21) | collective-permute-done | bytes 786464 | tf_op jit(solution)/shard_map/ppermute | solution.py:19
  137.6 3.0 %collective-permute-start.23 = (bf16[4,192,256]{2,1,0:T(8,128)(2,1)S(1)}, bf16[4,192,256]{2,1,0:T(8,128)(2,1)S(1)}, u32[]{:S(2)}, u32[]{:S(2)}) collective-permute-start(bf16[4,192,256]{2,1,0:T(8,128)(2,1)S(1)} %slice.41), channel_id=1, source_target_pairs={{0,129},{1,0},{128,1},{129,128},{2,131},{3,2},{130,3},{131,130},{4... | collective-permute-start | bytes 1179656 | tf_op jit(solution)/shard_map/ppermute | solution.py:19
  140.6 1.0 copy-done.8
  141.6 10.2 %expert.2 = bf16[4,2,2,160,128]{4,3,2,1,0:T(8,128)(2,1)} custom-call(s32[5]{0:T(128)} %copy-done, bf16[160,3200]{1,0:T(8,128)(2,1)} %copy-done.1, bf16[160,3200]{1,0:T(8,128)(2,1)} %collective-permute-done.9.refs_1_, bf16[160,3200]{1,0:T(8,128)(2,1)} %collective-permute-done.10.refs_2_, bf16[160,3200]{1,0:T(8,128)(2,1)} %collective-permute-done.11.refs_3_, ...), custom_call_target="tpu_custom_call" | custom-call | flops 4026531840 | bytes 12582912 | tf_op jit(solution)/shard_map/expert/pallas_call | solution.py:180
  151.8 5.6 %all-to-all-start.2 = ((bf16[16,160,128]{2,1,0:T(8,128)(2,1)}), bf16[16,160,128]{2,1,0:T(8,128)(2,1)S(1)}, u32[]{:S(2)}, u32[]{:S(2)}) async-start(bf16[16,160,128]{2,1,0:T(8,128)(2,1)} %bitcast.25), calls=%async_computation.2 | async-start | bytes 1310720 | tf_op jit(solution)/shard_map/all_to_all | solution.py:197
  158.2 0.7 copy-done.12
  158.9 10.2 %expert.3 = bf16[4,2,2,160,128]{4,3,2,1,0:T(8,128)(2,1)} custom-call(s32[5]{0:T(128)} %copy-done, bf16[160,3200]{1,0:T(8,128)(2,1)} %copy-done.1, bf16[160,3200]{1,0:T(8,128)(2,1)} %collective-permute-done.9.refs_1_, bf16[160,3200]{1,0:T(8,128)(2,1)} %collective-permute-done.10.refs_2_, bf16[160,3200]{1,0:T(8,128)(2,1)} %collective-permute-done.11.refs_3_, ...), custom_call_target="tpu_custom_call" | custom-call | flops 4026531840 | bytes 12582912 | tf_op jit(solution)/shard_map/expert/pallas_call | solution.py:180
  169.2 17.6 %all_to_all.20 = bf16[16,160,128]{2,1,0:T(8,128)(2,1)S(1)} all-to-all(bf16[16,160,128]{2,1,0:T(8,128)(2,1)} %bitcast.26), channel_id=1, replica_groups=mesh['dp'=2,'y'=4,'c'=2,'z'=8,'xl'=2] {'y','c','xl'}, dimensions={0} | all-to-all | bytes 1310720 | tf_op jit(solution)/shard_map/all_to_all | solution.py:197
  186.8 1.4 combine.1
  188.3 1.6 reshape.33
  (57 shorter events, 2.7 us)
Async XLA Ops:
  0.9 4.0 %collective-permute-start = (bf16[2,192,128]{2,1,0:T(8,128)(2,1)S(1)}, bf16[2,192,128]{2,1,0:T(8,128)(2,1)S(1)}, u32[]{:S(2)}, u32[]{:S(2)}) collective-permute-start(bf16[2,192,128]{2,1,0:T(8,128)(2,1)S(1)} %dynamic-slice_bitcast_fusion), channel_id=1, source_target_pairs={{0,1},{1,0},{2,3},{3,2},{4,5},{5,4},{6,7},{7,6},{8,9},{9,8},{10,11... | collective-permute-start | bytes 294920 | tf_op jit(solution)/shard_map/ppermute | solution.py:19
  5.9 12.6 %collective-permute-start.1 = (bf16[2,384,128]{2,1,0:T(8,128)(2,1)S(1)}, bf16[2,384,128]{2,1,0:T(8,128)(2,1)S(1)}, u32[]{:S(2)}, u32[]{:S(2)}) collective-permute-start(bf16[2,384,128]{2,1,0:T(8,128)(2,1)S(1)} %pad_maximum_fusion.refs_0_), channel_id=1, source_target_pairs={{0,14},{2,0},{4,2},{6,4},{8,6},{10,8},{12,10},{14,12},{1,15},{3,1}... | collective-permute-start | bytes 589832 | tf_op jit(solution)/shard_map/ppermute | solution.py:19
  11.8 6.5 %collective-permute-start.2 = (bf16[2,384,128]{2,1,0:T(8,128)(2,1)S(1)}, bf16[2,384,128]{2,1,0:T(8,128)(2,1)S(1)}, u32[]{:S(2)}, u32[]{:S(2)}) collective-permute-start(bf16[2,384,128]{2,1,0:T(8,128)(2,1)S(1)} %pad_maximum_fusion.refs_0_), channel_id=1, source_target_pairs={{0,2},{2,4},{4,6},{6,8},{8,10},{10,12},{12,14},{14,0},{1,3},{3,5},... | collective-permute-start | bytes 589832 | tf_op jit(solution)/shard_map/ppermute | solution.py:19
  18.3 5.8 %collective-permute-start.3 = (bf16[2,384,128]{2,1,0:T(8,128)(2,1)S(1)}, bf16[2,384,128]{2,1,0:T(8,128)(2,1)S(1)}, u32[]{:S(2)}, u32[]{:S(2)}) collective-permute-start(bf16[2,384,128]{2,1,0:T(8,128)(2,1)S(1)} %collective-permute-done.2.refs_7_), channel_id=1, source_target_pairs={{0,2},{2,4},{4,6},{6,8},{8,10},{10,12},{12,14},{14,0},{1,3},{3,5},... | collective-permute-start | bytes 589832 | tf_op jit(solution)/shard_map/ppermute | solution.py:19
  18.4 5.7 %collective-permute-start.4 = (bf16[2,384,128]{2,1,0:T(8,128)(2,1)S(1)}, bf16[2,384,128]{2,1,0:T(8,128)(2,1)S(1)}, u32[]{:S(2)}, u32[]{:S(2)}) collective-permute-start(bf16[2,384,128]{2,1,0:T(8,128)(2,1)S(1)} %collective-permute-done.1.refs_1_), channel_id=1, source_target_pairs={{0,14},{2,0},{4,2},{6,4},{8,6},{10,8},{12,10},{14,12},{1,15},{3,1}... | collective-permute-start | bytes 589832 | tf_op jit(solution)/shard_map/ppermute | solution.py:19
  24.2 32.0 %all-to-all-start = ((bf16[8,192,256]{2,1,0:T(8,128)(2,1)}), bf16[8,192,256]{2,1,0:T(8,128)(2,1)S(1)}, u32[]{:S(2)}, u32[]{:S(2)}) async-start(bf16[8,192,256]{2,1,0:T(8,128)(2,1)} %squeeze.17), calls=%async_computation | async-start | bytes 1572864 | tf_op jit(solution)/shard_map/all_to_all | solution.py:145
  28.5 19.7 %collective-permute-start.5 = (bf16[2,384,128]{2,1,0:T(8,128)(2,1)S(1)}, bf16[2,384,128]{2,1,0:T(8,128)(2,1)S(1)}, u32[]{:S(2)}, u32[]{:S(2)}) collective-permute-start(bf16[2,384,128]{2,1,0:T(8,128)(2,1)S(1)} %collective-permute-done.4.refs_2_), channel_id=1, source_target_pairs={{0,14},{2,0},{4,2},{6,4},{8,6},{10,8},{12,10},{14,12},{1,15},{3,1}... | collective-permute-start | bytes 589832 | tf_op jit(solution)/shard_map/ppermute | solution.py:19
  31.2 19.2 %collective-permute-start.6 = (bf16[2,384,128]{2,1,0:T(8,128)(2,1)S(1)}, bf16[2,384,128]{2,1,0:T(8,128)(2,1)S(1)}, u32[]{:S(2)}, u32[]{:S(2)}) collective-permute-start(bf16[2,384,128]{2,1,0:T(8,128)(2,1)S(1)} %collective-permute-done.3.refs_6_), channel_id=1, source_target_pairs={{0,2},{2,4},{4,6},{6,8},{8,10},{10,12},{12,14},{14,0},{1,3},{3,5},... | collective-permute-start | bytes 589832 | tf_op jit(solution)/shard_map/ppermute | solution.py:19
  48.3 5.0 %collective-permute-start.8 = (bf16[1,384,128]{2,1,0:T(8,128)(2,1)S(1)}, bf16[1,384,128]{2,1,0:T(8,128)(2,1)S(1)}, u32[]{:S(2)}, u32[]{:S(2)}) collective-permute-start(bf16[1,384,128]{2,1,0:T(8,128)(2,1)S(1)} %slice.37), channel_id=1, source_target_pairs={{0,14},{2,0},{4,2},{6,4},{8,6},{10,8},{12,10},{14,12},{1,15},{3,1}... | collective-permute-start | bytes 294920 | tf_op jit(solution)/shard_map/ppermute | solution.py:19
  50.4 4.9 %collective-permute-start.7 = (bf16[1,384,128]{2,1,0:T(8,128)(2,1)S(1)}, bf16[1,384,128]{2,1,0:T(8,128)(2,1)}, u32[]{:S(2)}, u32[]{:S(2)}) collective-permute-start(bf16[1,384,128]{2,1,0:T(8,128)(2,1)S(1)} %slice.36), channel_id=1, source_target_pairs={{0,2},{2,4},{4,6},{6,8},{8,10},{10,12},{12,14},{14,0},{1,3},{3,5},... | collective-permute-start | bytes 294920 | tf_op jit(solution)/shard_map/ppermute | solution.py:19
  50.5 14.6 %copy-start.5 = (s32[4,128,2]{1,2,0:T(2,128)S(1)}, s32[4,128,2]{1,2,0:T(2,128)}, u32[]{:S(2)}) copy-start(s32[4,128,2]{1,2,0:T(2,128)} %param.6) | copy-start | bytes 12292
  50.5 14.6 %copy-start.6 = (f32[4,128,2]{1,2,0:T(2,128)S(1)}, f32[4,128,2]{1,2,0:T(2,128)}, u32[]{:S(2)}) copy-start(f32[4,128,2]{1,2,0:T(2,128)} %param.7) | copy-start | bytes 12292
  56.2 12.6 %copy-start.2 = (bf16[8,192,256]{2,1,0:T(8,128)(2,1)}, bf16[8,192,256]{2,1,0:T(8,128)(2,1)S(1)}, u32[]{:S(2)}) copy-start(bf16[8,192,256]{2,1,0:T(8,128)(2,1)S(1)} %all-to-all-done.refs_8_) | copy-start | bytes 2359300
  56.2 32.6 %all-to-all-start.1 = ((bf16[8,192,256]{2,1,0:T(8,128)(2,1)}), bf16[8,192,256]{2,1,0:T(8,128)(2,1)}, u32[]{:S(2)}, u32[]{:S(2)}) async-start(bf16[8,192,256]{2,1,0:T(8,128)(2,1)} %squeeze.18), calls=%async_computation.1 | async-start | bytes 1572864 | tf_op jit(solution)/shard_map/all_to_all | solution.py:159
  62.3 13.8 %collective-permute-start.16 = (bf16[8,192,256]{2,1,0:T(8,128)(2,1)S(1)}, bf16[8,192,256]{2,1,0:T(8,128)(2,1)}, u32[]{:S(2)}, u32[]{:S(2)}) collective-permute-start(bf16[8,192,256]{2,1,0:T(8,128)(2,1)S(1)} %all-to-all-done.refs_8_), channel_id=1, source_target_pairs={{0,1},{1,128},{128,129},{129,0},{2,3},{3,130},{130,131},{131,2},{4... | collective-permute-start | bytes 2359304 | tf_op jit(solution)/shard_map/ppermute | solution.py:19
  63.5 13.7 %collective-permute-start.17 = (bf16[8,192,256]{2,1,0:T(8,128)(2,1)S(1)}, bf16[8,192,256]{2,1,0:T(8,128)(2,1)}, u32[]{:S(2)}, u32[]{:S(2)}) collective-permute-start(bf16[8,192,256]{2,1,0:T(8,128)(2,1)S(1)} %all-to-all-done.refs_8_), channel_id=1, source_target_pairs={{0,129},{1,0},{128,1},{129,128},{2,131},{3,2},{130,3},{131,130},{4... | collective-permute-start | bytes 2359304 | tf_op jit(solution)/shard_map/ppermute | solution.py:19
  65.1 13.1 %copy-start = (s32[5]{0:T(128)}, s32[5]{0:T(128)S(1)}, u32[]{:S(2)}) copy-start(s32[5]{0:T(128)S(1)} %stack.23.pos) | copy-start | bytes 64
  68.8 68.8 %copy-start.1 = (bf16[160,3200]{1,0:T(8,128)(2,1)}, bf16[160,3200]{1,0:T(8,128)(2,1)S(1)}, u32[]{:S(2)}) copy-start(bf16[160,3200]{1,0:T(8,128)(2,1)S(1)} %get-tuple-element.22.refs_0_) | copy-start | bytes 3072004
  68.8 31.4 %collective-permute-start.9 = (bf16[160,3200]{1,0:T(8,128)(2,1)}, bf16[160,3200]{1,0:T(8,128)(2,1)}, u32[]{:S(2)}, u32[]{:S(2)}) collective-permute-start(bf16[160,3200]{1,0:T(8,128)(2,1)} %get-tuple-element.23), channel_id=1, source_target_pairs={{0,32},{32,64},{64,96},{96,0},{1,33},{33,65},{65,97},{97,1},{2,34}... | collective-permute-start | bytes 3072008 | tf_op jit(solution)/shard_map/ppermute | solution.py:19
  70.1 40.5 %collective-permute-start.10 = (bf16[160,3200]{1,0:T(8,128)(2,1)}, bf16[160,3200]{1,0:T(8,128)(2,1)}, u32[]{:S(2)}, u32[]{:S(2)}) collective-permute-start(bf16[160,3200]{1,0:T(8,128)(2,1)} %get-tuple-element.24), channel_id=1, source_target_pairs={{0,64},{32,96},{64,0},{96,32},{1,65},{33,97},{65,1},{97,33},{2,66}... | collective-permute-start | bytes 3072008 | tf_op jit(solution)/shard_map/ppermute | solution.py:19
  72.7 45.8 %collective-permute-start.11 = (bf16[160,3200]{1,0:T(8,128)(2,1)}, bf16[160,3200]{1,0:T(8,128)(2,1)}, u32[]{:S(2)}, u32[]{:S(2)}) collective-permute-start(bf16[160,3200]{1,0:T(8,128)(2,1)} %get-tuple-element.25), channel_id=1, source_target_pairs={{0,96},{32,0},{64,32},{96,64},{1,97},{33,1},{65,33},{97,65},{2,98}... | collective-permute-start | bytes 3072008 | tf_op jit(solution)/shard_map/ppermute | solution.py:19
  77.0 10.3 %collective-permute-start.18 = (bf16[4,192,256]{2,1,0:T(8,128)(2,1)S(1)}, bf16[4,192,256]{2,1,0:T(8,128)(2,1)S(1)}, u32[]{:S(2)}, u32[]{:S(2)}) collective-permute-start(bf16[4,192,256]{2,1,0:T(8,128)(2,1)S(1)} %slice.38), channel_id=1, source_target_pairs={{0,1},{1,128},{128,129},{129,0},{2,3},{3,130},{130,131},{131,2},{4... | collective-permute-start | bytes 1179656 | tf_op jit(solution)/shard_map/ppermute | solution.py:19
  78.2 9.9 %collective-permute-start.19 = (bf16[4,192,256]{2,1,0:T(8,128)(2,1)S(1)}, bf16[4,192,256]{2,1,0:T(8,128)(2,1)S(1)}, u32[]{:S(2)}, u32[]{:S(2)}) collective-permute-start(bf16[4,192,256]{2,1,0:T(8,128)(2,1)S(1)} %slice.39), channel_id=1, source_target_pairs={{0,129},{1,0},{128,1},{129,128},{2,131},{3,2},{130,3},{131,130},{4... | collective-permute-start | bytes 1179656 | tf_op jit(solution)/shard_map/ppermute | solution.py:19
  87.4 0.8 copy-start.9
  88.1 0.7 copy-start.10
  88.9 29.7 %collective-permute-start.20 = (bf16[8,192,256]{2,1,0:T(8,128)(2,1)}, bf16[8,192,256]{2,1,0:T(8,128)(2,1)S(1)}, u32[]{:S(2)}, u32[]{:S(2)}) collective-permute-start(bf16[8,192,256]{2,1,0:T(8,128)(2,1)} %all-to-all-done.1.refs_8_), channel_id=1, source_target_pairs={{0,1},{1,128},{128,129},{129,0},{2,3},{3,130},{130,131},{131,2},{4... | collective-permute-start | bytes 2359304 | tf_op jit(solution)/shard_map/ppermute | solution.py:19
  89.3 48.3 %collective-permute-start.12 = (bf16[160,3200]{1,0:T(8,128)(2,1)S(1)}, bf16[160,3200]{1,0:T(8,128)(2,1)S(1)}, u32[]{:S(2)}, u32[]{:S(2)}) collective-permute-start(bf16[160,3200]{1,0:T(8,128)(2,1)S(1)} %get-tuple-element.22.refs_0_), channel_id=1, source_target_pairs={{0,16},{16,0},{1,17},{17,1},{2,18},{18,2},{3,19},{19,3},{4,20},{20... | collective-permute-start | bytes 3072008 | tf_op jit(solution)/shard_map/ppermute | solution.py:19
  100.2 40.4 %collective-permute-start.13 = (bf16[160,3200]{1,0:T(8,128)(2,1)}, bf16[160,3200]{1,0:T(8,128)(2,1)S(1)}, u32[]{:S(2)}, u32[]{:S(2)}) collective-permute-start(bf16[160,3200]{1,0:T(8,128)(2,1)} %collective-permute-done.9.refs_1_), channel_id=1, source_target_pairs={{0,16},{16,0},{1,17},{17,1},{2,18},{18,2},{3,19},{19,3},{4,20},{20... | collective-permute-start | bytes 3072008 | tf_op jit(solution)/shard_map/ppermute | solution.py:19
  110.6 30.1 %collective-permute-start.14 = (bf16[160,3200]{1,0:T(8,128)(2,1)}, bf16[160,3200]{1,0:T(8,128)(2,1)}, u32[]{:S(2)}, u32[]{:S(2)}) collective-permute-start(bf16[160,3200]{1,0:T(8,128)(2,1)} %collective-permute-done.10.refs_2_), channel_id=1, source_target_pairs={{0,16},{16,0},{1,17},{17,1},{2,18},{18,2},{3,19},{19,3},{4,20},{20... | collective-permute-start | bytes 3072008 | tf_op jit(solution)/shard_map/ppermute | solution.py:19
  118.6 22.1 %collective-permute-start.15 = (bf16[160,3200]{1,0:T(8,128)(2,1)}, bf16[160,3200]{1,0:T(8,128)(2,1)}, u32[]{:S(2)}, u32[]{:S(2)}) collective-permute-start(bf16[160,3200]{1,0:T(8,128)(2,1)} %collective-permute-done.11.refs_3_), channel_id=1, source_target_pairs={{0,16},{16,0},{1,17},{17,1},{2,18},{18,2},{3,19},{19,3},{4,20},{20... | collective-permute-start | bytes 3072008 | tf_op jit(solution)/shard_map/ppermute | solution.py:19
  118.6 19.0 %copy-start.3 = (bf16[8,192,256]{2,1,0:T(8,128)(2,1)}, bf16[8,192,256]{2,1,0:T(8,128)(2,1)S(1)}, u32[]{:S(2)}) copy-start(bf16[8,192,256]{2,1,0:T(8,128)(2,1)S(1)} %collective-permute-done.20.refs_9_) | copy-start | bytes 2359300
  118.6 19.0 %collective-permute-start.21 = (bf16[8,192,256]{2,1,0:T(8,128)(2,1)}, bf16[8,192,256]{2,1,0:T(8,128)(2,1)S(1)}, u32[]{:S(2)}, u32[]{:S(2)}) collective-permute-start(bf16[8,192,256]{2,1,0:T(8,128)(2,1)} %all-to-all-done.1.refs_8_), channel_id=1, source_target_pairs={{0,129},{1,0},{128,1},{129,128},{2,131},{3,2},{130,3},{131,130},{4... | collective-permute-start | bytes 2359304 | tf_op jit(solution)/shard_map/ppermute | solution.py:19
  137.6 3.0 %copy-start.4 = (bf16[8,192,256]{2,1,0:T(8,128)(2,1)}, bf16[8,192,256]{2,1,0:T(8,128)(2,1)S(1)}, u32[]{:S(2)}) copy-start(bf16[8,192,256]{2,1,0:T(8,128)(2,1)S(1)} %collective-permute-done.21.refs_10_) | copy-start | bytes 2359300
  137.6 19.8 %collective-permute-start.22 = (bf16[4,192,256]{2,1,0:T(8,128)(2,1)S(1)}, bf16[4,192,256]{2,1,0:T(8,128)(2,1)S(1)}, u32[]{:S(2)}, u32[]{:S(2)}) collective-permute-start(bf16[4,192,256]{2,1,0:T(8,128)(2,1)S(1)} %slice.40), channel_id=1, source_target_pairs={{0,1},{1,128},{128,129},{129,0},{2,3},{3,130},{130,131},{131,2},{4... | collective-permute-start | bytes 1179656 | tf_op jit(solution)/shard_map/ppermute | solution.py:19
  137.6 3.0 %copy-start.7 = (bf16[160,3200]{1,0:T(8,128)(2,1)}, bf16[160,3200]{1,0:T(8,128)(2,1)S(1)}, u32[]{:S(2)}) copy-start(bf16[160,3200]{1,0:T(8,128)(2,1)S(1)} %collective-permute-done.12.refs_4_) | copy-start | bytes 3072004
  137.6 19.8 %collective-permute-start.23 = (bf16[4,192,256]{2,1,0:T(8,128)(2,1)S(1)}, bf16[4,192,256]{2,1,0:T(8,128)(2,1)S(1)}, u32[]{:S(2)}, u32[]{:S(2)}) collective-permute-start(bf16[4,192,256]{2,1,0:T(8,128)(2,1)S(1)} %slice.41), channel_id=1, source_target_pairs={{0,129},{1,0},{128,1},{129,128},{2,131},{3,2},{130,3},{131,130},{4... | collective-permute-start | bytes 1179656 | tf_op jit(solution)/shard_map/ppermute | solution.py:19
  140.6 1.0 copy-start.8
  151.8 17.4 %all-to-all-start.2 = ((bf16[16,160,128]{2,1,0:T(8,128)(2,1)}), bf16[16,160,128]{2,1,0:T(8,128)(2,1)S(1)}, u32[]{:S(2)}, u32[]{:S(2)}) async-start(bf16[16,160,128]{2,1,0:T(8,128)(2,1)} %bitcast.25), calls=%async_computation.2 | async-start | bytes 1310720 | tf_op jit(solution)/shard_map/all_to_all | solution.py:197
  157.4 0.7 copy-start.11
  158.2 0.8 copy-start.12

commit v3 on v2

--- a/solution.py
+++ b/solution.py
@@ -60,6 +60,25 @@
             picked = lax.dot_general(onehot, feats[k][s], (((1,), (1,)), ((), ())), preferred_element_type=F32).astype(BF)
             for d in range(4):
                 outs[d][s * MOST : (s + 1) * MOST, k * width : (k + 1) * width] = picked[d * MOST : (d + 1) * MOST]
+
+
+def columns_kernel(pos, gate, up, out_a, out_b, sem):
+    for flag, src in ((0, gate), (1, up)):
+
+        @pl.when(pos[3] == flag)
+        def _(src=src):
+            copies = []
+            for r, out in enumerate((out_a, out_b)):
+                for z in range(8):
+                    for t in range(2):
+                        columns = pl.ds(z * 512 + t * 256 + r * 128, 128)
+                        copies.append(
+                            pltpu.make_async_copy(src.at[0, :, columns], out.at[z, :, pl.ds(t * 128, 128)], sem.at[len(copies)])
+                        )
+            for cp in copies:
+                cp.start()
+            for cp in copies:
+                cp.wait()
 
 
 def expert_kernel(chunks, pos, *refs):
@@ -121,7 +140,7 @@
 
 
 def body(tokens, expert_ids, route_weights, gate_train, up_train):
-    chunks, rounds = 1, 2
+    barrier = lax.optimization_barrier
     dp, y, c, z, xl = (lax.axis_index(a) for a in ("dp", "y", "c", "z", "xl"))
     pos = jnp.stack([y, c, xl, dp, z]).astype(jnp.int32)
     steps, n, width = tokens.shape
@@ -131,64 +150,64 @@
     theirs = lax.dynamic_index_in_dim(turned, 1 - xl, 0, keepdims=False)
     got = ring(theirs, "xl", 2, 1)
     pair = jnp.concatenate([jnp.where(xl == 0, mine, got), jnp.where(xl == 0, got, mine)], axis=1)
-    source = jnp.where(dp == 0, gate_train[0], up_train[0])
-    rows, units = source.shape
-    depth = rows // chunks
-    wide = units // 8 // 2 // rounds
-    blocks = source.reshape(rows, 8, 2, rounds, wide).transpose(3, 1, 0, 2, 4).reshape(rounds, 8, rows, 2 * wide)
+    rows, units = gate_train.shape[1:]
+    wide = units // 32
+    blocks = pl.pallas_call(
+        columns_kernel,
+        out_shape=[jax.ShapeDtypeStruct((8, rows, 2 * wide), BF)] * 2,
+        in_specs=[SM, ANY, ANY],
+        out_specs=[ANY] * 2,
+        scratch_shapes=[pltpu.SemaphoreType.DMA((32,))],
+        name="columns",
+    )(pos, gate_train, up_train)
+
+    def exchange(x):
+        return lax.all_to_all(x, "z", split_axis=0, concat_axis=0, tiled=True)
+
     below, above = [pair], [pair]
-    for k in range(2):
+    for k in range(3):
         below.append(ring(below[-1], "z", 8, 1))
         above.append(ring(above[-1], "z", 8, -1))
-    part = blocks[0, :, :depth]
-    part, below[2], above[2] = lax.optimization_barrier((part, below[2], above[2]))
-    first = lax.all_to_all(part, "z", split_axis=0, concat_axis=0, tiled=True)
-    for k in range(2, 3):
-        below.append(ring(below[-1], "z", 8, 1))
-        above.append(ring(above[-1], "z", 8, -1))
+    own_a, below[3], above[3] = barrier((blocks[0], below[3], above[3]))
+    own_a = exchange(own_a)
     opposite = jnp.concatenate([ring(below[3][:1], "z", 8, 1), ring(above[3][1:], "z", 8, -1)], axis=0)
     feats = [pair] + above[1:] + [opposite] + below[:0:-1]
-    pieces = []
-    for r in range(rounds):
-        for ch in range(chunks):
-            own = first
-            if r + ch > 0:
-                part = blocks[r, :, ch * depth : (ch + 1) * depth]
-                part, opposite, first = lax.optimization_barrier((part, opposite, first))
-                pieces[-1][0] = first
-                own = lax.all_to_all(part, "z", split_axis=0, concat_axis=0, tiled=True)
-                first = own
-                own, far_a, far_b = lax.optimization_barrier((own, pieces[-1][3], pieces[-1][4]))
-                pieces[-1][3:] = far_a, far_b
-            left, right = ring(own, X, 4, 1), ring(own, X, 4, -1)
-            far_a, far_b = ring(left[:4], X, 4, 1), ring(right[4:], X, 4, -1)
-            pieces.append([own, left, right, far_a, far_b])
-    feats[4] = opposite
     sent = pl.pallas_call(
         dispatch_kernel,
         out_shape=[jax.ShapeDtypeStruct((2 * MOST, 16 * width + 128), BF)] * 4,
         in_specs=[SM] + [VM] * 9,
         out_specs=[VM] * 4,
-        compiler_params=pltpu.CompilerParams(vmem_limit_bytes=32 << 20),
+        compiler_params=pltpu.CompilerParams(vmem_limit_bytes=24 << 20),
         name="dispatch",
     )(pos, meta, *feats)
     held = [sent[0]] + [ring(sent[d], "y", 4, d) for d in (1, 2, 3)]
-    other = [ring(h, "c", 2, 1) for h in held]
+    other = [ring(sent[0], "c", 2, 1)]
+    own_a, other[0] = barrier((own_a, other[0]))
+    own_b, own_a = barrier((blocks[1], own_a))
+    own_b = exchange(own_b)
+    pieces = []
+    for own in (own_a, own_b):
+        if pieces:
+            own, *pieces[0] = barrier((own, *pieces[0]))
+        left, right = ring(own, X, 4, 1), ring(own, X, 4, -1)
+        far_a, far_b = ring(left[:4], X, 4, 1), ring(right[4:], X, 4, -1)
+        pieces.append([own, left, right, far_a, far_b])
+    held[1:] = barrier(tuple(held[1:]))
+    other += [ring(h, "c", 2, 1) for h in held[1:]]
     backs = []
-    for r in range(rounds):
-        ws = [w for ch in range(chunks) for w in pieces[r * chunks + ch]]
+    for ws in pieces:
         act = pl.pallas_call(
-            functools.partial(expert_kernel, chunks),
+            functools.partial(expert_kernel, 1),
             out_shape=jax.ShapeDtypeStruct((4, 2, 2, 2 * MOST, wide), BF),
-            in_specs=[SM] + [ANY] * (8 + 5 * chunks),
+            in_specs=[SM] + [ANY] * 13,
             out_specs=VM,
             scratch_shapes=[
                 pltpu.VMEM((16 * MOST, 16 * width + 128), BF),
                 pltpu.VMEM((2, 8, 2, rows, 2 * wide), BF),
                 pltpu.SemaphoreType.DMA((8,)),
-                pltpu.SemaphoreType.DMA((5 * chunks, 8)),
+                pltpu.SemaphoreType.DMA((5, 8)),
             ],
-            compiler_params=pltpu.CompilerParams(vmem_limit_bytes=58 << 20),
+            compiler_params=pltpu.CompilerParams(vmem_limit_bytes=24 << 20),
             cost_estimate=pl.CostEstimate(
                 flops=16 * MOST * 16 * width * 8 * wide, bytes_accessed=12 << 20, transcendentals=16 * MOST * 2 * wide
             ),
@@ -201,7 +220,7 @@
         out_shape=jax.ShapeDtypeStruct((steps, n, 1024), BF),
         in_specs=[VM] * 3,
         out_specs=VM,
-        compiler_params=pltpu.CompilerParams(vmem_limit_bytes=32 << 20),
+        compiler_params=pltpu.CompilerParams(vmem_limit_bytes=24 << 20),
         name="combine",
     )(meta, *backs)
     return out.reshape(steps, n, 2, 2, 256)

time: 191 us -> 246 us (1.29)
  Pallas kernels: 25.5 us -> 79 us
  waiting for transfers between devices: 58.6 us -> 78.3 us
  starting transfers between devices: 66.8 us -> 55.4 us
  local copies, waits for them, and re-layouts: 17.5 us -> 13.6 us
  other arithmetic: 3.42 us -> 0.96 us
    pallas_call x2 -> x3, Pallas kernels: 20.4 us -> 73.9 us  [the longest x1 49.7 us: body(): pl.pallas_call(columns_kernel, out_shape=[jax.ShapeDtypeStruct((8, rows,...]
    ppermute x24, waiting for transfers between devices: 58.6 us -> 78.3 us  [ring(): return lax.ppermute(x, axis, [(i, (i + step) % size) for i in range(size)])]
    ppermute x24, starting transfers between devices: 50.8 us -> 40.1 us  [ring(): return lax.ppermute(x, axis, [(i, (i + step) % size) for i in range(size)])]
    select_n x2 -> x0, local copies, waits for them, and re-layouts: 4.95 us -> none  [body(): source = jnp.where(dp == 0, gate_train[0], up_train[0])]
    unnamed x26 -> x30, local copies, waits for them, and re-layouts: 3.99 us -> 8.85 us
    squeeze x2 -> x0, local copies, waits for them, and re-layouts: 2.75 us -> none  [the longest x1 1.38 us: body(): part = blocks[0, :, :depth]]
  transfers between devices with their start and end apart: 27 -> 27, of which waited for: 10 -> 8; matrix products, arithmetic and copies ran while one was open for 7% -> 1% of each run, Pallas kernels for 13% -> 32%
where the time goes in v3:
time: 246 us; the launch traced here: 245 us
  Pallas kernels  79 us (32%)
  waiting for transfers between devices  78.3 us (32%)
  starting transfers between devices  55.4 us (23%)
  blocking collectives  17.4 us (7%)
  local copies, waits for them, and re-layouts  13.6 us (6%)
    ppermute x24, waiting for transfers between devices, ring(): return lax.ppermute(x, axis, [(i, (i + step) % size) for i in range(size)])  78.3 us
    pallas_call x1, Pallas kernels, body(): pl.pallas_call(columns_kernel, out_shape=[jax.ShapeDtypeStruct((8, rows,...  49.7 us
    ppermute x24, starting transfers between devices, ring(): return lax.ppermute(x, axis, [(i, (i + step) % size) for i in range(size)])  40.1 us
    pallas_call x2, Pallas kernels, body(): pl.pallas_call(functools.partial(expert_kernel, 1), out_shape=jax.ShapeDt...  24.2 us
    all_to_all x1, blocking collectives, body(): lax.all_to_all(act.reshape(16, 2 * MOST, wide), ('y', 'c', 'xl'), split_a...  17.4 us
    all_to_all x2, starting transfers between devices, exchange(): return lax.all_to_all(x, 'z', split_axis=0, concat_axis=0, tiled=True)  10.3 us
    unnamed x30, local copies, waits for them, and re-layouts  8.85 us
    all_to_all x1, starting transfers between devices, body(): lax.all_to_all(act.reshape(16, 2 * MOST, wide), ('y', 'c', 'xl'), split_a...  4.94 us
  transfers between devices with their start and end apart: 27, of which 8 were waited for; matrix products, arithmetic and copies ran while one was open for 1% of the time, Pallas kernels for 32%

profile of v3, /device:TPU:1, one launch (start us, length us, event | category | flops | bytes accessed | tf_op | source)
XLA Modules:
  0.0 245.0 jit_solution(5760003160539311009)
XLA Ops:
  0.0 0.9 dynamic-slice_bitcast_fusion
  0.9 2.0 collective-permute-start
  2.9 2.0 collective-permute-done
  4.9 0.9 bitcast_select_fusion.1
  5.9 2.0 collective-permute-start.3
  7.8 4.0 %collective-permute-start.1 = (bf16[2,384,128]{2,1,0:T(8,128)(2,1)S(1)}, bf16[2,384,128]{2,1,0:T(8,128)(2,1)S(1)}, u32[]{:S(2)}, u32[]{:S(2)}) collective-permute-start(bf16[2,384,128]{2,1,0:T(8,128)(2,1)S(1)} %pad_maximum_fusion.refs_0_), channel_id=1, source_target_pairs={{0,14},{2,0},{4,2},{6,4},{8,6},{10,8},{12,10},{14,12},{1,15},{3,1}... | collective-permute-start | bytes 589832 | tf_op jit(solution)/shard_map/ppermute | solution.py:19
  11.9 3.3 %collective-permute-done.3.refs_7_ = bf16[2,384,128]{2,1,0:T(8,128)(2,1)S(1)} collective-permute-done((bf16[2,384,128]{2,1,0:T(8,128)(2,1)S(1)}, bf16[2,384,128]{2,1,0:T(8,128)(2,1)S(1)}, u32[]{:S(2)}, u32[]{:S(2)}) %collective-permute-start.3) | collective-permute-done | bytes 196640 | tf_op jit(solution)/shard_map/ppermute | solution.py:19
  15.2 2.7 %collective-permute-start.2 = (bf16[2,384,128]{2,1,0:T(8,128)(2,1)S(1)}, bf16[2,384,128]{2,1,0:T(8,128)(2,1)S(1)}, u32[]{:S(2)}, u32[]{:S(2)}) collective-permute-start(bf16[2,384,128]{2,1,0:T(8,128)(2,1)S(1)} %collective-permute-done.1.refs_1_), channel_id=1, source_target_pairs={{0,14},{2,0},{4,2},{6,4},{8,6},{10,8},{12,10},{14,12},{1,15},{3,1}... | collective-permute-start | bytes 589832 | tf_op jit(solution)/shard_map/ppermute | solution.py:19
  17.9 3.0 %collective-permute-done.4.refs_6_ = bf16[2,384,128]{2,1,0:T(8,128)(2,1)S(1)} collective-permute-done((bf16[2,384,128]{2,1,0:T(8,128)(2,1)S(1)}, bf16[2,384,128]{2,1,0:T(8,128)(2,1)S(1)}, u32[]{:S(2)}, u32[]{:S(2)}) %collective-permute-start.4) | collective-permute-done | bytes 196640 | tf_op jit(solution)/shard_map/ppermute | solution.py:19
  20.9 2.7 %collective-permute-start.6 = (bf16[2,384,128]{2,1,0:T(8,128)(2,1)S(1)}, bf16[2,384,128]{2,1,0:T(8,128)(2,1)S(1)}, u32[]{:S(2)}, u32[]{:S(2)}) collective-permute-start(bf16[2,384,128]{2,1,0:T(8,128)(2,1)S(1)} %collective-permute-done.2.refs_2_), channel_id=1, source_target_pairs={{0,14},{2,0},{4,2},{6,4},{8,6},{10,8},{12,10},{14,12},{1,15},{3,1}... | collective-permute-start | bytes 589832 | tf_op jit(solution)/shard_map/ppermute | solution.py:19
  23.6 0.6 stack.23.pos
  24.2 49.7 %columns.1 = (bf16[8,192,256]{2,1,0:T(8,128)(2,1)}, bf16[8,192,256]{2,1,0:T(8,128)(2,1)}) custom-call(s32[5]{0:T(128)} %stack.23.pos, bf16[1,192,4096]{2,1,0:T(8,128)(2,1)} %gate.1, bf16[1,192,4096]{2,1,0:T(8,128)(2,1)} %up.1), custom_call_target="tpu_custom_call" | custom-call | tf_op jit(solution)/shard_map/columns/pallas_call | solution.py:155
  73.9 5.0 %all-to-all-start = ((bf16[8,192,256]{2,1,0:T(8,128)(2,1)}), bf16[8,192,256]{2,1,0:T(8,128)(2,1)S(1)}, u32[]{:S(2)}, u32[]{:S(2)}) async-start(bf16[8,192,256]{2,1,0:T(8,128)(2,1)} %get-tuple-element.37), calls=%async_computation | async-start | bytes 1572864 | tf_op jit(solution)/shard_map/all_to_all | solution.py:165
  79.0 1.5 collective-permute-start.7
  80.5 1.3 collective-permute-start.8
  81.8 14.7 %collective-permute-done.7 = bf16[1,384,128]{2,1,0:T(8,128)(2,1)S(1)} collective-permute-done((bf16[1,384,128]{2,1,0:T(8,128)(2,1)S(1)}, bf16[1,384,128]{2,1,0:T(8,128)(2,1)S(1)}, u32[]{:S(2)}, u32[]{:S(2)}) %collective-permute-start.7) | collective-permute-done | bytes 98336 | tf_op jit(solution)/shard_map/ppermute | solution.py:19
  96.5 3.7 %dispatch.1 = (bf16[160,3200]{1,0:T(8,128)(2,1)S(1)}, bf16[160,3200]{1,0:T(8,128)(2,1)}, bf16[160,3200]{1,0:T(8,128)(2,1)}, bf16[160,3200]{1,0:T(8,128)(2,1)}) custom-call(s32[5]{0:T(128)S(1)} %copy-done.4, f32[4,4,128]{2,1,0:T(4,128)S(1)} %maximum_bitcast_fusion.meta, bf16[2,384,128]{2,1,0:T(8,128)(2,1)S(1)} %pad_maximum_fusion.refs_0_, ...), custom_call_target="tpu_custom_call" | custom-call | tf_op jit(solution)/shard_map/dispatch/pallas_call | solution.py:175
  100.2 4.8 %collective-permute-start.12 = (bf16[160,3200]{1,0:T(8,128)(2,1)S(1)}, bf16[160,3200]{1,0:T(8,128)(2,1)S(1)}, u32[]{:S(2)}, u32[]{:S(2)}) collective-permute-start(bf16[160,3200]{1,0:T(8,128)(2,1)S(1)} %get-tuple-element.30.refs_0_), channel_id=1, source_target_pairs={{0,16},{16,0},{1,17},{17,1},{2,18},{18,2},{3,19},{19,3},{4,20},{20... | collective-permute-start | bytes 3072008 | tf_op jit(solution)/shard_map/ppermute | solution.py:19
  105.0 1.0 copy-done.5
  106.0 1.2 collective-permute-done.12.refs_4_
  107.3 1.0 copy-done.8
  108.3 5.4 %all-to-all-start.1 = ((bf16[8,192,256]{2,1,0:T(8,128)(2,1)}), bf16[8,192,256]{2,1,0:T(8,128)(2,1)S(1)}, u32[]{:S(2)}, u32[]{:S(2)}) async-start(bf16[8,192,256]{2,1,0:T(8,128)(2,1)} %get-tuple-element.41), calls=%async_computation.1 | async-start | bytes 1572864 | tf_op jit(solution)/shard_map/all_to_all | solution.py:165
  113.6 1.3 collective-permute-start.9
  114.9 2.6 %collective-permute-start.10 = (bf16[160,3200]{1,0:T(8,128)(2,1)}, bf16[160,3200]{1,0:T(8,128)(2,1)}, u32[]{:S(2)}, u32[]{:S(2)}) collective-permute-start(bf16[160,3200]{1,0:T(8,128)(2,1)} %get-tuple-element.32), channel_id=1, source_target_pairs={{0,64},{32,96},{64,0},{96,32},{1,65},{33,97},{65,1},{97,33},{2,66}... | collective-permute-start | bytes 3072008 | tf_op jit(solution)/shard_map/ppermute | solution.py:19
  117.5 1.1 collective-permute-start.11
  118.6 2.5 %collective-permute-start.17 = (bf16[8,192,256]{2,1,0:T(8,128)(2,1)S(1)}, bf16[8,192,256]{2,1,0:T(8,128)(2,1)S(1)}, u32[]{:S(2)}, u32[]{:S(2)}) collective-permute-start(bf16[8,192,256]{2,1,0:T(8,128)(2,1)S(1)} %all-to-all-done.refs_8_), channel_id=1, source_target_pairs={{0,129},{1,0},{128,1},{129,128},{2,131},{3,2},{130,3},{131,130},{4... | collective-permute-start | bytes 2359304 | tf_op jit(solution)/shard_map/ppermute | solution.py:19
  121.1 15.3 %collective-permute-done.17.refs_10_ = bf16[8,192,256]{2,1,0:T(8,128)(2,1)S(1)} collective-permute-done((bf16[8,192,256]{2,1,0:T(8,128)(2,1)S(1)}, bf16[8,192,256]{2,1,0:T(8,128)(2,1)S(1)}, u32[]{:S(2)}, u32[]{:S(2)}) %collective-permute-start.17) | collective-permute-done | bytes 786464 | tf_op jit(solution)/shard_map/ppermute | solution.py:19
  136.5 3.6 %collective-permute-start.19 = (bf16[4,192,256]{2,1,0:T(8,128)(2,1)S(1)}, bf16[4,192,256]{2,1,0:T(8,128)(2,1)S(1)}, u32[]{:S(2)}, u32[]{:S(2)}) collective-permute-start(bf16[4,192,256]{2,1,0:T(8,128)(2,1)S(1)} %slice.25), channel_id=1, source_target_pairs={{0,129},{1,0},{128,1},{129,128},{2,131},{3,2},{130,3},{131,130},{4... | collective-permute-start | bytes 1179656 | tf_op jit(solution)/shard_map/ppermute | solution.py:19
  140.2 21.7 %collective-permute-done.10.refs_2_ = bf16[160,3200]{1,0:T(8,128)(2,1)} collective-permute-done((bf16[160,3200]{1,0:T(8,128)(2,1)}, bf16[160,3200]{1,0:T(8,128)(2,1)}, u32[]{:S(2)}, u32[]{:S(2)}) %collective-permute-start.10) | collective-permute-done | bytes 1024032 | tf_op jit(solution)/shard_map/ppermute | solution.py:19
  161.8 1.5 collective-permute-start.13
  163.4 0.5 collective-permute-start.15
  163.9 0.8 copy-done.11
  164.7 2.5 %collective-permute-start.21 = (bf16[8,192,256]{2,1,0:T(8,128)(2,1)S(1)}, bf16[8,192,256]{2,1,0:T(8,128)(2,1)S(1)}, u32[]{:S(2)}, u32[]{:S(2)}) collective-permute-start(bf16[8,192,256]{2,1,0:T(8,128)(2,1)S(1)} %all-to-all-done.1.refs_8_), channel_id=1, source_target_pairs={{0,129},{1,0},{128,1},{129,128},{2,131},{3,2},{130,3},{131,130},{4... | collective-permute-start | bytes 2359304 | tf_op jit(solution)/shard_map/ppermute | solution.py:19
  167.2 17.0 %collective-permute-done.21.refs_10_ = bf16[8,192,256]{2,1,0:T(8,128)(2,1)S(1)} collective-permute-done((bf16[8,192,256]{2,1,0:T(8,128)(2,1)S(1)}, bf16[8,192,256]{2,1,0:T(8,128)(2,1)S(1)}, u32[]{:S(2)}, u32[]{:S(2)}) %collective-permute-start.21) | collective-permute-done | bytes 786464 | tf_op jit(solution)/shard_map/ppermute | solution.py:19
  184.1 0.8 slice.27
  185.0 3.4 %collective-permute-start.23 = (bf16[4,192,256]{2,1,0:T(8,128)(2,1)}, bf16[4,192,256]{2,1,0:T(8,128)(2,1)}, u32[]{:S(2)}, u32[]{:S(2)}) collective-permute-start(bf16[4,192,256]{2,1,0:T(8,128)(2,1)} %slice.27), channel_id=1, source_target_pairs={{0,129},{1,0},{128,1},{129,128},{2,131},{3,2},{130,3},{131,130},{4... | collective-permute-start | bytes 1179656 | tf_op jit(solution)/shard_map/ppermute | solution.py:19
  188.4 0.8 slice.26
  189.4 1.2 copy-done.9
  190.6 13.1 %expert.2 = bf16[4,2,2,160,128]{4,3,2,1,0:T(8,128)(2,1)} custom-call(s32[5]{0:T(128)S(1)} %copy-done.4, bf16[160,3200]{1,0:T(8,128)(2,1)S(1)} %copy-done.6, bf16[160,3200]{1,0:T(8,128)(2,1)} %collective-permute-done.9.refs_1_, bf16[160,3200]{1,0:T(8,128)(2,1)} %collective-permute-done.10.refs_2_, bf16[160,3200]{1,0:T(8,128)(2,1)} %collective-permute-done.11.refs_3_, ...), custom_call_target="tpu_custom_call" | custom-call | flops 4026531840 | bytes 12582912 | tf_op jit(solution)/shard_map/expert/pallas_call | solution.py:199
  203.7 4.9 %all-to-all-start.2 = ((bf16[16,160,128]{2,1,0:T(8,128)(2,1)}), bf16[16,160,128]{2,1,0:T(8,128)(2,1)S(1)}, u32[]{:S(2)}, u32[]{:S(2)}) async-start(bf16[16,160,128]{2,1,0:T(8,128)(2,1)} %bitcast.11), calls=%async_computation.2 | async-start | bytes 1310720 | tf_op jit(solution)/shard_map/all_to_all | solution.py:216
  208.7 1.1 copy-done.1
  209.8 1.1 copy-done.3
  211.0 1.2 copy-done.7
  212.2 1.2 copy-done.10
  213.4 11.1 %expert.3 = bf16[4,2,2,160,128]{4,3,2,1,0:T(8,128)(2,1)S(1)} custom-call(s32[5]{0:T(128)S(1)} %copy-done.4, bf16[160,3200]{1,0:T(8,128)(2,1)S(1)} %copy-done.7, bf16[160,3200]{1,0:T(8,128)(2,1)} %collective-permute-done.9.refs_1_, bf16[160,3200]{1,0:T(8,128)(2,1)} %collective-permute-done.10.refs_2_, bf16[160,3200]{1,0:T(8,128)(2,1)} %collective-permute-done.11.refs_3_, ...), custom_call_target="tpu_custom_call" | custom-call | flops 4026531840 | bytes 12582912 | tf_op jit(solution)/shard_map/expert/pallas_call | solution.py:199
  224.5 17.4 %all_to_all.20 = bf16[16,160,128]{2,1,0:T(8,128)(2,1)S(1)} all-to-all(bf16[16,160,128]{2,1,0:T(8,128)(2,1)S(1)} %bitcast.21), channel_id=1, replica_groups=mesh['dp'=2,'y'=4,'c'=2,'z'=8,'xl'=2] {'y','c','xl'}, dimensions={0} | all-to-all | bytes 1310720 | tf_op jit(solution)/shard_map/all_to_all | solution.py:216
  242.0 1.4 combine.1
  243.4 1.6 reshape.23
  (56 shorter events, 0.5 us)
Async XLA Ops:
  0.9 4.0 %collective-permute-start = (bf16[2,192,128]{2,1,0:T(8,128)(2,1)S(1)}, bf16[2,192,128]{2,1,0:T(8,128)(2,1)S(1)}, u32[]{:S(2)}, u32[]{:S(2)}) collective-permute-start(bf16[2,192,128]{2,1,0:T(8,128)(2,1)S(1)} %dynamic-slice_bitcast_fusion), channel_id=1, source_target_pairs={{0,1},{1,0},{2,3},{3,2},{4,5},{5,4},{6,7},{7,6},{8,9},{9,8},{10,11... | collective-permute-start | bytes 294920 | tf_op jit(solution)/shard_map/ppermute | solution.py:19
  5.9 9.3 %collective-permute-start.3 = (bf16[2,384,128]{2,1,0:T(8,128)(2,1)S(1)}, bf16[2,384,128]{2,1,0:T(8,128)(2,1)S(1)}, u32[]{:S(2)}, u32[]{:S(2)}) collective-permute-start(bf16[2,384,128]{2,1,0:T(8,128)(2,1)S(1)} %pad_maximum_fusion.refs_0_), channel_id=1, source_target_pairs={{0,2},{2,4},{4,6},{6,8},{8,10},{10,12},{12,14},{14,0},{1,3},{3,5},... | collective-permute-start | bytes 589832 | tf_op jit(solution)/shard_map/ppermute | solution.py:19
  7.8 7.3 %collective-permute-start.1 = (bf16[2,384,128]{2,1,0:T(8,128)(2,1)S(1)}, bf16[2,384,128]{2,1,0:T(8,128)(2,1)S(1)}, u32[]{:S(2)}, u32[]{:S(2)}) collective-permute-start(bf16[2,384,128]{2,1,0:T(8,128)(2,1)S(1)} %pad_maximum_fusion.refs_0_), channel_id=1, source_target_pairs={{0,14},{2,0},{4,2},{6,4},{8,6},{10,8},{12,10},{14,12},{1,15},{3,1}... | collective-permute-start | bytes 589832 | tf_op jit(solution)/shard_map/ppermute | solution.py:19
  15.2 5.7 %collective-permute-start.4 = (bf16[2,384,128]{2,1,0:T(8,128)(2,1)S(1)}, bf16[2,384,128]{2,1,0:T(8,128)(2,1)S(1)}, u32[]{:S(2)}, u32[]{:S(2)}) collective-permute-start(bf16[2,384,128]{2,1,0:T(8,128)(2,1)S(1)} %collective-permute-done.3.refs_7_), channel_id=1, source_target_pairs={{0,2},{2,4},{4,6},{6,8},{8,10},{10,12},{12,14},{14,0},{1,3},{3,5},... | collective-permute-start | bytes 589832 | tf_op jit(solution)/shard_map/ppermute | solution.py:19
  15.2 5.7 %collective-permute-start.2 = (bf16[2,384,128]{2,1,0:T(8,128)(2,1)S(1)}, bf16[2,384,128]{2,1,0:T(8,128)(2,1)S(1)}, u32[]{:S(2)}, u32[]{:S(2)}) collective-permute-start(bf16[2,384,128]{2,1,0:T(8,128)(2,1)S(1)} %collective-permute-done.1.refs_1_), channel_id=1, source_target_pairs={{0,14},{2,0},{4,2},{6,4},{8,6},{10,8},{12,10},{14,12},{1,15},{3,1}... | collective-permute-start | bytes 589832 | tf_op jit(solution)/shard_map/ppermute | solution.py:19
  20.9 53.0 %collective-permute-start.5 = (bf16[2,384,128]{2,1,0:T(8,128)(2,1)S(1)}, bf16[2,384,128]{2,1,0:T(8,128)(2,1)S(1)}, u32[]{:S(2)}, u32[]{:S(2)}) collective-permute-start(bf16[2,384,128]{2,1,0:T(8,128)(2,1)S(1)} %collective-permute-done.4.refs_6_), channel_id=1, source_target_pairs={{0,2},{2,4},{4,6},{6,8},{8,10},{10,12},{12,14},{14,0},{1,3},{3,5},... | collective-permute-start | bytes 589832 | tf_op jit(solution)/shard_map/ppermute | solution.py:19
  20.9 53.0 %collective-permute-start.6 = (bf16[2,384,128]{2,1,0:T(8,128)(2,1)S(1)}, bf16[2,384,128]{2,1,0:T(8,128)(2,1)S(1)}, u32[]{:S(2)}, u32[]{:S(2)}) collective-permute-start(bf16[2,384,128]{2,1,0:T(8,128)(2,1)S(1)} %collective-permute-done.2.refs_2_), channel_id=1, source_target_pairs={{0,14},{2,0},{4,2},{6,4},{8,6},{10,8},{12,10},{14,12},{1,15},{3,1}... | collective-permute-start | bytes 589832 | tf_op jit(solution)/shard_map/ppermute | solution.py:19
  73.9 5.0 %copy-start.13 = (s32[4,128,2]{1,2,0:T(2,128)S(1)}, s32[4,128,2]{1,2,0:T(2,128)}, u32[]{:S(2)}) copy-start(s32[4,128,2]{1,2,0:T(2,128)} %param.6) | copy-start | bytes 12292
  73.9 7.9 %copy-start.14 = (f32[4,128,2]{1,2,0:T(2,128)S(1)}, f32[4,128,2]{1,2,0:T(2,128)}, u32[]{:S(2)}) copy-start(f32[4,128,2]{1,2,0:T(2,128)} %param.7) | copy-start | bytes 12292
  73.9 22.6 %copy-start.4 = (s32[5]{0:T(128)S(1)}, s32[5]{0:T(128)}, u32[]{:S(2)}) copy-start(s32[5]{0:T(128)} %stack.23.pos) | copy-start | bytes 64
  73.9 34.3 %all-to-all-start = ((bf16[8,192,256]{2,1,0:T(8,128)(2,1)}), bf16[8,192,256]{2,1,0:T(8,128)(2,1)S(1)}, u32[]{:S(2)}, u32[]{:S(2)}) async-start(bf16[8,192,256]{2,1,0:T(8,128)(2,1)} %get-tuple-element.37), calls=%async_computation | async-start | bytes 1572864 | tf_op jit(solution)/shard_map/all_to_all | solution.py:165
  79.0 17.5 %collective-permute-start.7 = (bf16[1,384,128]{2,1,0:T(8,128)(2,1)S(1)}, bf16[1,384,128]{2,1,0:T(8,128)(2,1)S(1)}, u32[]{:S(2)}, u32[]{:S(2)}) collective-permute-start(bf16[1,384,128]{2,1,0:T(8,128)(2,1)S(1)} %slice.18), channel_id=1, source_target_pairs={{0,2},{2,4},{4,6},{6,8},{8,10},{10,12},{12,14},{14,0},{1,3},{3,5},... | collective-permute-start | bytes 294920 | tf_op jit(solution)/shard_map/ppermute | solution.py:19
  80.5 16.0 %collective-permute-start.8 = (bf16[1,384,128]{2,1,0:T(8,128)(2,1)S(1)}, bf16[1,384,128]{2,1,0:T(8,128)(2,1)S(1)}, u32[]{:S(2)}, u32[]{:S(2)}) collective-permute-start(bf16[1,384,128]{2,1,0:T(8,128)(2,1)S(1)} %slice.19), channel_id=1, source_target_pairs={{0,14},{2,0},{4,2},{6,4},{8,6},{10,8},{12,10},{14,12},{1,15},{3,1}... | collective-permute-start | bytes 294920 | tf_op jit(solution)/shard_map/ppermute | solution.py:19
  100.2 7.1 %collective-permute-start.12 = (bf16[160,3200]{1,0:T(8,128)(2,1)S(1)}, bf16[160,3200]{1,0:T(8,128)(2,1)S(1)}, u32[]{:S(2)}, u32[]{:S(2)}) collective-permute-start(bf16[160,3200]{1,0:T(8,128)(2,1)S(1)} %get-tuple-element.30.refs_0_), channel_id=1, source_target_pairs={{0,16},{16,0},{1,17},{17,1},{2,18},{18,2},{3,19},{19,3},{4,20},{20... | collective-permute-start | bytes 3072008 | tf_op jit(solution)/shard_map/ppermute | solution.py:19
  105.0 1.0 copy-start.5
  107.3 1.0 copy-start.8
  108.3 56.4 %all-to-all-start.1 = ((bf16[8,192,256]{2,1,0:T(8,128)(2,1)}), bf16[8,192,256]{2,1,0:T(8,128)(2,1)S(1)}, u32[]{:S(2)}, u32[]{:S(2)}) async-start(bf16[8,192,256]{2,1,0:T(8,128)(2,1)} %get-tuple-element.41), calls=%async_computation.1 | async-start | bytes 1572864 | tf_op jit(solution)/shard_map/all_to_all | solution.py:165
  113.6 26.6 %collective-permute-start.9 = (bf16[160,3200]{1,0:T(8,128)(2,1)}, bf16[160,3200]{1,0:T(8,128)(2,1)}, u32[]{:S(2)}, u32[]{:S(2)}) collective-permute-start(bf16[160,3200]{1,0:T(8,128)(2,1)} %get-tuple-element.31), channel_id=1, source_target_pairs={{0,32},{32,64},{64,96},{96,0},{1,33},{33,65},{65,97},{97,1},{2,34}... | collective-permute-start | bytes 3072008 | tf_op jit(solution)/shard_map/ppermute | solution.py:19
  114.9 46.9 %collective-permute-start.10 = (bf16[160,3200]{1,0:T(8,128)(2,1)}, bf16[160,3200]{1,0:T(8,128)(2,1)}, u32[]{:S(2)}, u32[]{:S(2)}) collective-permute-start(bf16[160,3200]{1,0:T(8,128)(2,1)} %get-tuple-element.32), channel_id=1, source_target_pairs={{0,64},{32,96},{64,0},{96,32},{1,65},{33,97},{65,1},{97,33},{2,66}... | collective-permute-start | bytes 3072008 | tf_op jit(solution)/shard_map/ppermute | solution.py:19
  117.5 44.3 %collective-permute-start.11 = (bf16[160,3200]{1,0:T(8,128)(2,1)}, bf16[160,3200]{1,0:T(8,128)(2,1)}, u32[]{:S(2)}, u32[]{:S(2)}) collective-permute-start(bf16[160,3200]{1,0:T(8,128)(2,1)} %get-tuple-element.33), channel_id=1, source_target_pairs={{0,96},{32,0},{64,32},{96,64},{1,97},{33,1},{65,33},{97,65},{2,98}... | collective-permute-start | bytes 3072008 | tf_op jit(solution)/shard_map/ppermute | solution.py:19
  118.6 17.8 %collective-permute-start.17 = (bf16[8,192,256]{2,1,0:T(8,128)(2,1)S(1)}, bf16[8,192,256]{2,1,0:T(8,128)(2,1)S(1)}, u32[]{:S(2)}, u32[]{:S(2)}) collective-permute-start(bf16[8,192,256]{2,1,0:T(8,128)(2,1)S(1)} %all-to-all-done.refs_8_), channel_id=1, source_target_pairs={{0,129},{1,0},{128,1},{129,128},{2,131},{3,2},{130,3},{131,130},{4... | collective-permute-start | bytes 2359304 | tf_op jit(solution)/shard_map/ppermute | solution.py:19
  121.1 19.0 %collective-permute-start.16 = (bf16[8,192,256]{2,1,0:T(8,128)(2,1)S(1)}, bf16[8,192,256]{2,1,0:T(8,128)(2,1)S(1)}, u32[]{:S(2)}, u32[]{:S(2)}) collective-permute-start(bf16[8,192,256]{2,1,0:T(8,128)(2,1)S(1)} %all-to-all-done.refs_8_), channel_id=1, source_target_pairs={{0,1},{1,128},{128,129},{129,0},{2,3},{3,130},{130,131},{131,2},{4... | collective-permute-start | bytes 2359304 | tf_op jit(solution)/shard_map/ppermute | solution.py:19
  136.5 27.4 %collective-permute-start.19 = (bf16[4,192,256]{2,1,0:T(8,128)(2,1)S(1)}, bf16[4,192,256]{2,1,0:T(8,128)(2,1)S(1)}, u32[]{:S(2)}, u32[]{:S(2)}) collective-permute-start(bf16[4,192,256]{2,1,0:T(8,128)(2,1)S(1)} %slice.25), channel_id=1, source_target_pairs={{0,129},{1,0},{128,1},{129,128},{2,131},{3,2},{130,3},{131,130},{4... | collective-permute-start | bytes 1179656 | tf_op jit(solution)/shard_map/ppermute | solution.py:19
  140.1 23.8 %collective-permute-start.18 = (bf16[4,192,256]{2,1,0:T(8,128)(2,1)S(1)}, bf16[4,192,256]{2,1,0:T(8,128)(2,1)S(1)}, u32[]{:S(2)}, u32[]{:S(2)}) collective-permute-start(bf16[4,192,256]{2,1,0:T(8,128)(2,1)S(1)} %slice.24), channel_id=1, source_target_pairs={{0,1},{1,128},{128,129},{129,0},{2,3},{3,130},{130,131},{131,2},{4... | collective-permute-start | bytes 1179656 | tf_op jit(solution)/shard_map/ppermute | solution.py:19
  161.8 27.5 %collective-permute-start.13 = (bf16[160,3200]{1,0:T(8,128)(2,1)}, bf16[160,3200]{1,0:T(8,128)(2,1)}, u32[]{:S(2)}, u32[]{:S(2)}) collective-permute-start(bf16[160,3200]{1,0:T(8,128)(2,1)} %collective-permute-done.9.refs_1_), channel_id=1, source_target_pairs={{0,16},{16,0},{1,17},{17,1},{2,18},{18,2},{3,19},{19,3},{4,20},{20... | collective-permute-start | bytes 3072008 | tf_op jit(solution)/shard_map/ppermute | solution.py:19
  163.4 26.0 %collective-permute-start.14 = (bf16[160,3200]{1,0:T(8,128)(2,1)}, bf16[160,3200]{1,0:T(8,128)(2,1)}, u32[]{:S(2)}, u32[]{:S(2)}) collective-permute-start(bf16[160,3200]{1,0:T(8,128)(2,1)} %collective-permute-done.10.refs_2_), channel_id=1, source_target_pairs={{0,16},{16,0},{1,17},{17,1},{2,18},{18,2},{3,19},{19,3},{4,20},{20... | collective-permute-start | bytes 3072008 | tf_op jit(solution)/shard_map/ppermute | solution.py:19
  163.4 26.0 %collective-permute-start.15 = (bf16[160,3200]{1,0:T(8,128)(2,1)}, bf16[160,3200]{1,0:T(8,128)(2,1)}, u32[]{:S(2)}, u32[]{:S(2)}) collective-permute-start(bf16[160,3200]{1,0:T(8,128)(2,1)} %collective-permute-done.11.refs_3_), channel_id=1, source_target_pairs={{0,16},{16,0},{1,17},{17,1},{2,18},{18,2},{3,19},{19,3},{4,20},{20... | collective-permute-start | bytes 3072008 | tf_op jit(solution)/shard_map/ppermute | solution.py:19
  163.9 0.8 copy-start.11
  164.7 24.7 %copy-start.6 = (bf16[160,3200]{1,0:T(8,128)(2,1)S(1)}, bf16[160,3200]{1,0:T(8,128)(2,1)}, u32[]{:S(2)}) copy-start(bf16[160,3200]{1,0:T(8,128)(2,1)} %copy-done.5) | copy-start | bytes 3072004
  164.7 24.8 %copy-start.12 = (bf16[4,192,256]{2,1,0:T(8,128)(2,1)S(1)}, bf16[4,192,256]{2,1,0:T(8,128)(2,1)}, u32[]{:S(2)}) copy-start(bf16[4,192,256]{2,1,0:T(8,128)(2,1)} %copy-done.11) | copy-start | bytes 1179652
  164.7 19.5 %collective-permute-start.21 = (bf16[8,192,256]{2,1,0:T(8,128)(2,1)S(1)}, bf16[8,192,256]{2,1,0:T(8,128)(2,1)S(1)}, u32[]{:S(2)}, u32[]{:S(2)}) collective-permute-start(bf16[8,192,256]{2,1,0:T(8,128)(2,1)S(1)} %all-to-all-done.1.refs_8_), channel_id=1, source_target_pairs={{0,129},{1,0},{128,1},{129,128},{2,131},{3,2},{130,3},{131,130},{4... | collective-permute-start | bytes 2359304 | tf_op jit(solution)/shard_map/ppermute | solution.py:19
  167.2 21.2 %collective-permute-start.20 = (bf16[8,192,256]{2,1,0:T(8,128)(2,1)S(1)}, bf16[8,192,256]{2,1,0:T(8,128)(2,1)S(1)}, u32[]{:S(2)}, u32[]{:S(2)}) collective-permute-start(bf16[8,192,256]{2,1,0:T(8,128)(2,1)S(1)} %all-to-all-done.1.refs_8_), channel_id=1, source_target_pairs={{0,1},{1,128},{128,129},{129,0},{2,3},{3,130},{130,131},{131,2},{4... | collective-permute-start | bytes 2359304 | tf_op jit(solution)/shard_map/ppermute | solution.py:19
  184.1 4.2 %copy-start = (bf16[8,192,256]{2,1,0:T(8,128)(2,1)}, bf16[8,192,256]{2,1,0:T(8,128)(2,1)S(1)}, u32[]{:S(2)}) copy-start(bf16[8,192,256]{2,1,0:T(8,128)(2,1)S(1)} %collective-permute-done.21.refs_10_) | copy-start | bytes 2359300
  185.0 23.7 %collective-permute-start.23 = (bf16[4,192,256]{2,1,0:T(8,128)(2,1)}, bf16[4,192,256]{2,1,0:T(8,128)(2,1)}, u32[]{:S(2)}, u32[]{:S(2)}) collective-permute-start(bf16[4,192,256]{2,1,0:T(8,128)(2,1)} %slice.27), channel_id=1, source_target_pairs={{0,129},{1,0},{128,1},{129,128},{2,131},{3,2},{130,3},{131,130},{4... | collective-permute-start | bytes 1179656 | tf_op jit(solution)/shard_map/ppermute | solution.py:19
  188.4 1.0 copy-start.2
  189.4 19.3 %collective-permute-start.22 = (bf16[4,192,256]{2,1,0:T(8,128)(2,1)}, bf16[4,192,256]{2,1,0:T(8,128)(2,1)}, u32[]{:S(2)}, u32[]{:S(2)}) collective-permute-start(bf16[4,192,256]{2,1,0:T(8,128)(2,1)} %slice.26), channel_id=1, source_target_pairs={{0,1},{1,128},{128,129},{129,0},{2,3},{3,130},{130,131},{131,2},{4... | collective-permute-start | bytes 1179656 | tf_op jit(solution)/shard_map/ppermute | solution.py:19
  189.4 1.2 copy-start.9
  203.7 20.8 %all-to-all-start.2 = ((bf16[16,160,128]{2,1,0:T(8,128)(2,1)}), bf16[16,160,128]{2,1,0:T(8,128)(2,1)S(1)}, u32[]{:S(2)}, u32[]{:S(2)}) async-start(bf16[16,160,128]{2,1,0:T(8,128)(2,1)} %bitcast.11), calls=%async_computation.2 | async-start | bytes 1310720 | tf_op jit(solution)/shard_map/all_to_all | solution.py:216
  208.7 1.1 copy-start.1
  209.8 1.1 copy-start.3
  211.0 1.2 copy-start.7
  212.2 1.2 copy-start.10

commit v4 on v3

--- a/solution.py
+++ b/solution.py
@@ -1,5 +1,3 @@
-import functools
-
 import jax
 import jax.numpy as jnp
 from jax import lax
@@ -10,7 +8,6 @@
 MOST = 80
 X = ("dp", "xl")
 BF, F32 = jnp.bfloat16, jnp.float32
-ANY = pl.BlockSpec(memory_space=pl.ANY)
 VM = pl.BlockSpec(memory_space=pltpu.VMEM)
 SM = pl.BlockSpec(memory_space=pltpu.SMEM)
 
@@ -62,62 +59,36 @@
                 outs[d][s * MOST : (s + 1) * MOST, k * width : (k + 1) * width] = picked[d * MOST : (d + 1) * MOST]
 
 
-def columns_kernel(pos, gate, up, out_a, out_b, sem):
+def columns_kernel(pos, gate, up, out_a, out_b):
     for flag, src in ((0, gate), (1, up)):
 
         @pl.when(pos[3] == flag)
         def _(src=src):
-            copies = []
             for r, out in enumerate((out_a, out_b)):
                 for z in range(8):
                     for t in range(2):
-                        columns = pl.ds(z * 512 + t * 256 + r * 128, 128)
-                        copies.append(
-                            pltpu.make_async_copy(src.at[0, :, columns], out.at[z, :, pl.ds(t * 128, 128)], sem.at[len(copies)])
-                        )
-            for cp in copies:
-                cp.start()
-            for cp in copies:
-                cp.wait()
-
-
-def expert_kernel(chunks, pos, *refs):
-    xs, refs = refs[:8], refs[8:]
-    ws, refs = refs[: 5 * chunks], refs[5 * chunks :]
-    out, xbuf, wbuf, xsem, wsem = refs
-    y, c, xl, dp = pos[0], pos[1], pos[2], pos[3]
+                        first = z * 512 + t * 256 + r * 128
+                        out[z, :, t * 128 : (t + 1) * 128] = src[0, :, first : first + 128]
+
+
+def expert_kernel(pos, *refs):
+    xs, ws, out, wbuf = refs[:8], refs[8:13], refs[13], refs[14]
+    y, c, xl, dp, z = (pos[i] for i in range(5))
     rows = xs[0].shape[0]
-    depth = ws[0].shape[1]
-    width = 2 * 8 * depth * chunks
-    xcopies, wcopies = [], []
+    width = 16 * ws[0].shape[1]
+    for src, off, low in ((ws[0], 0, 0), (ws[1], 3, 0), (ws[2], 1, 0), (ws[3], 2, 0), (ws[4], 2, 4)):
+        j = lax.rem(dp * 2 + xl + off, 4)
+        for k in range(src.shape[0]):
+            wbuf[lax.div(j, 2), lax.rem(low + k + 8 - z, 8), lax.rem(j, 2)] = src[k]
     for g in range(8):
-        xcopies.append(pltpu.make_async_copy(xs[g], xbuf.at[pl.ds(g * rows, rows)], xsem.at[g]))
-    here = dp * 2 + xl
-    for ch in range(chunks):
-        own, left, right, far_a, far_b = ws[5 * ch : 5 * ch + 5]
-        span = pl.ds(ch * depth, depth)
-        for i, (src, off, zlo, zn) in enumerate(((own, 0, 0, 8), (left, 3, 0, 8), (right, 1, 0, 8), (far_a, 2, 0, 4), (far_b, 2, 4, 4))):
-            j = lax.rem(here + off, 4)
-            for k in range(zn):
-                dst = wbuf.at[lax.div(j, 2), lax.rem(zlo + k + 8 - pos[4], 8), lax.rem(j, 2), span]
-                wcopies.append(pltpu.make_async_copy(src.at[k], dst, wsem.at[ch * 5 + i, k]))
-    for cp in wcopies + xcopies:
-        cp.start()
-    for cp in wcopies:
-        cp.wait()
-    half = 4 * rows
-    for m in range(2):
-        for cp in xcopies[4 * m : 4 * m + 4]:
-            cp.wait()
-        part = slice(m * half, (m + 1) * half)
-        data = xbuf[part, :width]
-        rw = jnp.sum(xbuf[part, width:].astype(F32), axis=1, keepdims=True)
+        d, cc = g % 4, g // 4
+        data = xs[g][:, :width]
+        rw = jnp.sum(xs[g][:, width:].astype(F32), axis=1, keepdims=True)
         gate = jnp.dot(data, wbuf[0].reshape(width, 256), preferred_element_type=F32)
         up = jnp.dot(data, wbuf[1].reshape(width, 256), preferred_element_type=F32)
         act = (rw * (gate / (1.0 + jnp.exp(-gate)) * up)).astype(BF)
-        for d in range(4):
-            for t in range(2):
-                out[lax.rem(y + 4 - d, 4), c + m - 2 * c * m, t] = act[d * rows : (d + 1) * rows, t * 128 : (t + 1) * 128]
+        for t in range(2):
+            out[lax.rem(y + 4 - d, 4), c + cc - 2 * c * cc, t] = act[:, t * 128 : (t + 1) * 128]
 
 
 def combine_kernel(meta, recv_a, recv_b, out):
@@ -155,9 +126,9 @@
     blocks = pl.pallas_call(
         columns_kernel,
         out_shape=[jax.ShapeDtypeStruct((8, rows, 2 * wide), BF)] * 2,
-        in_specs=[SM, ANY, ANY],
-        out_specs=[ANY] * 2,
-        scratch_shapes=[pltpu.SemaphoreType.DMA((32,))],
+        in_specs=[SM, VM, VM],
+        out_specs=[VM] * 2,
+        compiler_params=pltpu.CompilerParams(vmem_limit_bytes=16 << 20),
         name="columns",
     )(pos, gate_train, up_train)
 
@@ -168,9 +139,9 @@
     for k in range(3):
         below.append(ring(below[-1], "z", 8, 1))
         above.append(ring(above[-1], "z", 8, -1))
-    own_a, below[3], above[3] = barrier((blocks[0], below[3], above[3]))
-    own_a = exchange(own_a)
-    opposite = jnp.concatenate([ring(below[3][:1], "z", 8, 1), ring(above[3][1:], "z", 8, -1)], axis=0)
+    last = barrier((blocks[0], ring(below[3][:1], "z", 8, 1), ring(above[3][1:], "z", 8, -1)))
+    own_a = exchange(last[0])
+    opposite = jnp.concatenate(last[1:], axis=0)
     feats = [pair] + above[1:] + [opposite] + below[:0:-1]
     sent = pl.pallas_call(
         dispatch_kernel,
@@ -197,16 +168,11 @@
     backs = []
     for ws in pieces:
         act = pl.pallas_call(
-            functools.partial(expert_kernel, 1),
+            expert_kernel,
             out_shape=jax.ShapeDtypeStruct((4, 2, 2, 2 * MOST, wide), BF),
-            in_specs=[SM] + [ANY] * 13,
+            in_specs=[SM] + [VM] * 13,
             out_specs=VM,
-            scratch_shapes=[
-                pltpu.VMEM((16 * MOST, 16 * width + 128), BF),
-                pltpu.VMEM((2, 8, 2, rows, 2 * wide), BF),
-                pltpu.SemaphoreType.DMA((8,)),
-                pltpu.SemaphoreType.DMA((5, 8)),
-            ],
+            scratch_shapes=[pltpu.VMEM((2, 8, 2, rows, 2 * wide), BF)],
             compiler_params=pltpu.CompilerParams(vmem_limit_bytes=24 << 20),
             cost_estimate=pl.CostEstimate(
                 flops=16 * MOST * 16 * width * 8 * wide, bytes_accessed=12 << 20, transcendentals=16 * MOST * 2 * wide

time: 246 us -> 184 us (0.75)
  Pallas kernels: 79 us -> 22.7 us
  waiting for transfers between devices: 78.3 us -> 66.3 us
  starting transfers between devices: 55.4 us -> 59.6 us
    pallas_call x1, Pallas kernels: 49.7 us -> 2.03 us  [body(): pl.pallas_call(columns_kernel, out_shape=[jax.ShapeDtypeStruct((8, rows,...]
    ppermute x24, waiting for transfers between devices: 78.3 us -> 66.2 us  [ring(): return lax.ppermute(x, axis, [(i, (i + step) % size) for i in range(size)])]
    pallas_call x2, Pallas kernels: 24.2 us -> 15.5 us  [body(): pl.pallas_call(expert_kernel, out_shape=jax.ShapeDtypeStruct((4, 2, 2, 2...]
    unnamed x30 -> x32, local copies, waits for them, and re-layouts: 8.85 us -> 11.7 us
    ppermute x24, starting transfers between devices: 40.1 us -> 42.9 us  [ring(): return lax.ppermute(x, axis, [(i, (i + step) % size) for i in range(size)])]
  transfers between devices with their start and end apart: 27 -> 27, of which waited for: 8 -> 10; matrix products, arithmetic and copies ran while one was open for 1% -> 1% of each run, Pallas kernels for 32% -> 12%
where the time goes in v4:
time: 184 us; the launch traced here: 183 us
  waiting for transfers between devices  66.3 us (36%)
  starting transfers between devices  59.6 us (32%)
  Pallas kernels  22.7 us (12%)
  blocking collectives  17.4 us (9%)
  local copies, waits for them, and re-layouts  15.9 us (9%)
    ppermute x24, waiting for transfers between devices, ring(): return lax.ppermute(x, axis, [(i, (i + step) % size) for i in range(size)])  66.2 us
    ppermute x24, starting transfers between devices, ring(): return lax.ppermute(x, axis, [(i, (i + step) % size) for i in range(size)])  42.9 us
    all_to_all x1, blocking collectives, body(): lax.all_to_all(act.reshape(16, 2 * MOST, wide), ('y', 'c', 'xl'), split_a...  17.4 us
    pallas_call x2, Pallas kernels, body(): pl.pallas_call(expert_kernel, out_shape=jax.ShapeDtypeStruct((4, 2, 2, 2...  15.5 us
    all_to_all x2, starting transfers between devices, exchange(): return lax.all_to_all(x, 'z', split_axis=0, concat_axis=0, tiled=True)  11.8 us
    unnamed x32, local copies, waits for them, and re-layouts  11.7 us
    all_to_all x1, starting transfers between devices, body(): lax.all_to_all(act.reshape(16, 2 * MOST, wide), ('y', 'c', 'xl'), split_a...  4.93 us
  transfers between devices with their start and end apart: 27, of which 10 were waited for; matrix products, arithmetic and copies ran while one was open for 1% of the time, Pallas kernels for 12%

profile of v4, /device:TPU:1, one launch (start us, length us, event | category | flops | bytes accessed | tf_op | source)
XLA Modules:
  0.0 183.1 jit_solution(2503656459709017030)
XLA Ops:
  0.0 0.9 dynamic-slice_bitcast_fusion
  0.9 2.0 %collective-permute-start = (bf16[2,192,128]{2,1,0:T(8,128)(2,1)S(1)}, bf16[2,192,128]{2,1,0:T(8,128)(2,1)S(1)}, u32[]{:S(2)}, u32[]{:S(2)}) collective-permute-start(bf16[2,192,128]{2,1,0:T(8,128)(2,1)S(1)} %dynamic-slice_bitcast_fusion), channel_id=1, source_target_pairs={{0,1},{1,0},{2,3},{3,2},{4,5},{5,4},{6,7},{7,6},{8,9},{9,8},{10,11... | collective-permute-start | bytes 294920 | tf_op jit(solution)/shard_map/ppermute | solution.py:16
  2.9 2.0 %collective-permute-done = bf16[2,192,128]{2,1,0:T(8,128)(2,1)S(1)} collective-permute-done((bf16[2,192,128]{2,1,0:T(8,128)(2,1)S(1)}, bf16[2,192,128]{2,1,0:T(8,128)(2,1)S(1)}, u32[]{:S(2)}, u32[]{:S(2)}) %collective-permute-start) | collective-permute-done | bytes 98336 | tf_op jit(solution)/shard_map/ppermute | solution.py:16
  4.9 0.9 bitcast_select_fusion.1
  5.9 2.0 %collective-permute-start.4 = (bf16[2,384,128]{2,1,0:T(8,128)(2,1)S(1)}, bf16[2,384,128]{2,1,0:T(8,128)(2,1)S(1)}, u32[]{:S(2)}, u32[]{:S(2)}) collective-permute-start(bf16[2,384,128]{2,1,0:T(8,128)(2,1)S(1)} %pad_maximum_fusion.refs_0_), channel_id=1, source_target_pairs={{0,2},{2,4},{4,6},{6,8},{8,10},{10,12},{12,14},{14,0},{1,3},{3,5},... | collective-permute-start | bytes 589832 | tf_op jit(solution)/shard_map/ppermute | solution.py:16
  7.8 4.0 %collective-permute-start.1 = (bf16[2,384,128]{2,1,0:T(8,128)(2,1)S(1)}, bf16[2,384,128]{2,1,0:T(8,128)(2,1)S(1)}, u32[]{:S(2)}, u32[]{:S(2)}) collective-permute-start(bf16[2,384,128]{2,1,0:T(8,128)(2,1)S(1)} %pad_maximum_fusion.refs_0_), channel_id=1, source_target_pairs={{0,14},{2,0},{4,2},{6,4},{8,6},{10,8},{12,10},{14,12},{1,15},{3,1}... | collective-permute-start | bytes 589832 | tf_op jit(solution)/shard_map/ppermute | solution.py:16
  11.9 3.3 %collective-permute-done.4.refs_7_ = bf16[2,384,128]{2,1,0:T(8,128)(2,1)S(1)} collective-permute-done((bf16[2,384,128]{2,1,0:T(8,128)(2,1)S(1)}, bf16[2,384,128]{2,1,0:T(8,128)(2,1)S(1)}, u32[]{:S(2)}, u32[]{:S(2)}) %collective-permute-start.4) | collective-permute-done | bytes 196640 | tf_op jit(solution)/shard_map/ppermute | solution.py:16
  15.2 2.7 %collective-permute-start.2 = (bf16[2,384,128]{2,1,0:T(8,128)(2,1)S(1)}, bf16[2,384,128]{2,1,0:T(8,128)(2,1)S(1)}, u32[]{:S(2)}, u32[]{:S(2)}) collective-permute-start(bf16[2,384,128]{2,1,0:T(8,128)(2,1)S(1)} %collective-permute-done.1.refs_1_), channel_id=1, source_target_pairs={{0,14},{2,0},{4,2},{6,4},{8,6},{10,8},{12,10},{14,12},{1,15},{3,1}... | collective-permute-start | bytes 589832 | tf_op jit(solution)/shard_map/ppermute | solution.py:16
  17.9 3.0 %collective-permute-done.5.refs_6_ = bf16[2,384,128]{2,1,0:T(8,128)(2,1)S(1)} collective-permute-done((bf16[2,384,128]{2,1,0:T(8,128)(2,1)S(1)}, bf16[2,384,128]{2,1,0:T(8,128)(2,1)S(1)}, u32[]{:S(2)}, u32[]{:S(2)}) %collective-permute-start.5) | collective-permute-done | bytes 196640 | tf_op jit(solution)/shard_map/ppermute | solution.py:16
  20.9 2.7 %collective-permute-start.3 = (bf16[2,384,128]{2,1,0:T(8,128)(2,1)S(1)}, bf16[2,384,128]{2,1,0:T(8,128)(2,1)S(1)}, u32[]{:S(2)}, u32[]{:S(2)}) collective-permute-start(bf16[2,384,128]{2,1,0:T(8,128)(2,1)S(1)} %collective-permute-done.2.refs_2_), channel_id=1, source_target_pairs={{0,14},{2,0},{4,2},{6,4},{8,6},{10,8},{12,10},{14,12},{1,15},{3,1}... | collective-permute-start | bytes 589832 | tf_op jit(solution)/shard_map/ppermute | solution.py:16
  23.6 3.0 %collective-permute-done.6.refs_5_ = bf16[2,384,128]{2,1,0:T(8,128)(2,1)S(1)} collective-permute-done((bf16[2,384,128]{2,1,0:T(8,128)(2,1)S(1)}, bf16[2,384,128]{2,1,0:T(8,128)(2,1)S(1)}, u32[]{:S(2)}, u32[]{:S(2)}) %collective-permute-start.6) | collective-permute-done | bytes 196640 | tf_op jit(solution)/shard_map/ppermute | solution.py:16
  26.8 2.7 %collective-permute-start.8 = (bf16[1,384,128]{2,1,0:T(8,128)(2,1)S(1)}, bf16[1,384,128]{2,1,0:T(8,128)(2,1)S(1)}, u32[]{:S(2)}, u32[]{:S(2)}) collective-permute-start(bf16[1,384,128]{2,1,0:T(8,128)(2,1)S(1)} %slice.25), channel_id=1, source_target_pairs={{0,14},{2,0},{4,2},{6,4},{8,6},{10,8},{12,10},{14,12},{1,15},{3,1}... | collective-permute-start | bytes 294920 | tf_op jit(solution)/shard_map/ppermute | solution.py:16
  29.6 1.4 copy-done
  31.0 1.4 copy-done.1
  32.4 2.0 %columns.1 = (bf16[8,192,256]{2,1,0:T(8,128)(2,1)}, bf16[8,192,256]{2,1,0:T(8,128)(2,1)}) custom-call(s32[5]{0:T(128)S(1)} %stack.23.pos, bf16[1,192,4096]{2,1,0:T(8,128)(2,1)S(1)} %copy-done, bf16[1,192,4096]{2,1,0:T(8,128)(2,1)S(1)} %copy-done.1), custom_call_target="tpu_custom_call" | custom-call | tf_op jit(solution)/shard_map/columns/pallas_call | solution.py:126
  34.4 5.0 %all-to-all-start = ((bf16[8,192,256]{2,1,0:T(8,128)(2,1)}), bf16[8,192,256]{2,1,0:T(8,128)(2,1)S(1)}, u32[]{:S(2)}, u32[]{:S(2)}) async-start(bf16[8,192,256]{2,1,0:T(8,128)(2,1)} %get-tuple-element.37), calls=%async_computation | async-start | bytes 1572864 | tf_op jit(solution)/shard_map/all_to_all | solution.py:136
  39.5 3.6 %dispatch.1 = (bf16[160,3200]{1,0:T(8,128)(2,1)S(1)}, bf16[160,3200]{1,0:T(8,128)(2,1)}, bf16[160,3200]{1,0:T(8,128)(2,1)}, bf16[160,3200]{1,0:T(8,128)(2,1)}) custom-call(s32[5]{0:T(128)S(1)} %stack.23.pos, f32[4,4,128]{2,1,0:T(4,128)S(1)} %maximum_bitcast_fusion.meta, bf16[2,384,128]{2,1,0:T(8,128)(2,1)S(1)} %pad_maximum_fusion.refs_0_, ...), custom_call_target="tpu_custom_call" | custom-call | tf_op jit(solution)/shard_map/dispatch/pallas_call | solution.py:146
  43.1 7.1 %collective-permute-start.12 = (bf16[160,3200]{1,0:T(8,128)(2,1)S(1)}, bf16[160,3200]{1,0:T(8,128)(2,1)S(1)}, u32[]{:S(2)}, u32[]{:S(2)}) collective-permute-start(bf16[160,3200]{1,0:T(8,128)(2,1)S(1)} %get-tuple-element.30.refs_0_), channel_id=1, source_target_pairs={{0,16},{16,0},{1,17},{17,1},{2,18},{18,2},{3,19},{19,3},{4,20},{20... | collective-permute-start | bytes 3072008 | tf_op jit(solution)/shard_map/ppermute | solution.py:16
  50.2 1.0 copy-done.6
  51.2 1.2 collective-permute-done.12.refs_4_
  52.5 1.0 copy-done.9
  53.6 6.8 %all-to-all-start.1 = ((bf16[8,192,256]{2,1,0:T(8,128)(2,1)}), bf16[8,192,256]{2,1,0:T(8,128)(2,1)S(1)}, u32[]{:S(2)}, u32[]{:S(2)}) async-start(bf16[8,192,256]{2,1,0:T(8,128)(2,1)} %get-tuple-element.41), calls=%async_computation.1 | async-start | bytes 1572864 | tf_op jit(solution)/shard_map/all_to_all | solution.py:136
  60.4 1.3 collective-permute-start.9
  61.7 2.6 %collective-permute-start.10 = (bf16[160,3200]{1,0:T(8,128)(2,1)}, bf16[160,3200]{1,0:T(8,128)(2,1)}, u32[]{:S(2)}, u32[]{:S(2)}) collective-permute-start(bf16[160,3200]{1,0:T(8,128)(2,1)} %get-tuple-element.32), channel_id=1, source_target_pairs={{0,64},{32,96},{64,0},{96,32},{1,65},{33,97},{65,1},{97,33},{2,66}... | collective-permute-start | bytes 3072008 | tf_op jit(solution)/shard_map/ppermute | solution.py:16
  64.3 1.1 collective-permute-start.11
  65.4 2.5 %collective-permute-start.17 = (bf16[8,192,256]{2,1,0:T(8,128)(2,1)S(1)}, bf16[8,192,256]{2,1,0:T(8,128)(2,1)S(1)}, u32[]{:S(2)}, u32[]{:S(2)}) collective-permute-start(bf16[8,192,256]{2,1,0:T(8,128)(2,1)S(1)} %all-to-all-done.refs_8_), channel_id=1, source_target_pairs={{0,129},{1,0},{128,1},{129,128},{2,131},{3,2},{130,3},{131,130},{4... | collective-permute-start | bytes 2359304 | tf_op jit(solution)/shard_map/ppermute | solution.py:16
  67.9 9.2 %collective-permute-done.17.refs_10_ = bf16[8,192,256]{2,1,0:T(8,128)(2,1)S(1)} collective-permute-done((bf16[8,192,256]{2,1,0:T(8,128)(2,1)S(1)}, bf16[8,192,256]{2,1,0:T(8,128)(2,1)S(1)}, u32[]{:S(2)}, u32[]{:S(2)}) %collective-permute-start.17) | collective-permute-done | bytes 786464 | tf_op jit(solution)/shard_map/ppermute | solution.py:16
  77.1 3.6 %collective-permute-start.19 = (bf16[4,192,256]{2,1,0:T(8,128)(2,1)S(1)}, bf16[4,192,256]{2,1,0:T(8,128)(2,1)S(1)}, u32[]{:S(2)}, u32[]{:S(2)}) collective-permute-start(bf16[4,192,256]{2,1,0:T(8,128)(2,1)S(1)} %slice.27), channel_id=1, source_target_pairs={{0,129},{1,0},{128,1},{129,128},{2,131},{3,2},{130,3},{131,130},{4... | collective-permute-start | bytes 1179656 | tf_op jit(solution)/shard_map/ppermute | solution.py:16
  80.8 21.6 %collective-permute-done.10.refs_2_ = bf16[160,3200]{1,0:T(8,128)(2,1)} collective-permute-done((bf16[160,3200]{1,0:T(8,128)(2,1)}, bf16[160,3200]{1,0:T(8,128)(2,1)}, u32[]{:S(2)}, u32[]{:S(2)}) %collective-permute-start.10) | collective-permute-done | bytes 1024032 | tf_op jit(solution)/shard_map/ppermute | solution.py:16
  102.4 5.7 %collective-permute-done.11.refs_3_ = bf16[160,3200]{1,0:T(8,128)(2,1)} collective-permute-done((bf16[160,3200]{1,0:T(8,128)(2,1)}, bf16[160,3200]{1,0:T(8,128)(2,1)}, u32[]{:S(2)}, u32[]{:S(2)}) %collective-permute-start.11) | collective-permute-done | bytes 1024032 | tf_op jit(solution)/shard_map/ppermute | solution.py:16
  108.1 2.0 %collective-permute-start.13 = (bf16[160,3200]{1,0:T(8,128)(2,1)}, bf16[160,3200]{1,0:T(8,128)(2,1)}, u32[]{:S(2)}, u32[]{:S(2)}) collective-permute-start(bf16[160,3200]{1,0:T(8,128)(2,1)} %collective-permute-done.9.refs_1_), channel_id=1, source_target_pairs={{0,16},{16,0},{1,17},{17,1},{2,18},{18,2},{3,19},{19,3},{4,20},{20... | collective-permute-start | bytes 3072008 | tf_op jit(solution)/shard_map/ppermute | solution.py:16
  110.7 0.8 copy-done.12
  111.4 2.5 %collective-permute-start.21 = (bf16[8,192,256]{2,1,0:T(8,128)(2,1)S(1)}, bf16[8,192,256]{2,1,0:T(8,128)(2,1)S(1)}, u32[]{:S(2)}, u32[]{:S(2)}) collective-permute-start(bf16[8,192,256]{2,1,0:T(8,128)(2,1)S(1)} %all-to-all-done.1.refs_8_), channel_id=1, source_target_pairs={{0,129},{1,0},{128,1},{129,128},{2,131},{3,2},{130,3},{131,130},{4... | collective-permute-start | bytes 2359304 | tf_op jit(solution)/shard_map/ppermute | solution.py:16
  113.9 17.0 %collective-permute-done.21.refs_10_ = bf16[8,192,256]{2,1,0:T(8,128)(2,1)S(1)} collective-permute-done((bf16[8,192,256]{2,1,0:T(8,128)(2,1)S(1)}, bf16[8,192,256]{2,1,0:T(8,128)(2,1)S(1)}, u32[]{:S(2)}, u32[]{:S(2)}) %collective-permute-start.21) | collective-permute-done | bytes 786464 | tf_op jit(solution)/shard_map/ppermute | solution.py:16
  130.9 0.8 slice.29
  131.7 3.4 %collective-permute-start.23 = (bf16[4,192,256]{2,1,0:T(8,128)(2,1)}, bf16[4,192,256]{2,1,0:T(8,128)(2,1)}, u32[]{:S(2)}, u32[]{:S(2)}) collective-permute-start(bf16[4,192,256]{2,1,0:T(8,128)(2,1)} %slice.29), channel_id=1, source_target_pairs={{0,129},{1,0},{128,1},{129,128},{2,131},{3,2},{130,3},{131,130},{4... | collective-permute-start | bytes 1179656 | tf_op jit(solution)/shard_map/ppermute | solution.py:16
  135.2 0.8 slice.28
  136.2 1.2 copy-done.10
  137.4 8.1 %expert.2 = bf16[4,2,2,160,128]{4,3,2,1,0:T(8,128)(2,1)} custom-call(s32[5]{0:T(128)S(1)} %stack.23.pos, bf16[160,3200]{1,0:T(8,128)(2,1)S(1)} %copy-done.7, bf16[160,3200]{1,0:T(8,128)(2,1)} %collective-permute-done.9.refs_1_, bf16[160,3200]{1,0:T(8,128)(2,1)} %collective-permute-done.10.refs_2_, bf16[160,3200]{1,0:T(8,128)(2,1)} %collective-permute-done.11.refs_3_, ...), custom_call_target="tpu_custom_call" | custom-call | flops 4026531840 | bytes 12582912 | tf_op jit(solution)/shard_map/expert/pallas_call | solution.py:170
  145.5 4.9 %all-to-all-start.2 = ((bf16[16,160,128]{2,1,0:T(8,128)(2,1)}), bf16[16,160,128]{2,1,0:T(8,128)(2,1)S(1)}, u32[]{:S(2)}, u32[]{:S(2)}) async-start(bf16[16,160,128]{2,1,0:T(8,128)(2,1)} %bitcast.11), calls=%async_computation.2 | async-start | bytes 1310720 | tf_op jit(solution)/shard_map/all_to_all | solution.py:182
  150.5 1.1 copy-done.3
  151.6 1.1 copy-done.5
  152.7 1.2 copy-done.8
  153.9 1.2 copy-done.11
  155.2 7.5 %expert.3 = bf16[4,2,2,160,128]{4,3,2,1,0:T(8,128)(2,1)S(1)} custom-call(s32[5]{0:T(128)S(1)} %stack.23.pos, bf16[160,3200]{1,0:T(8,128)(2,1)S(1)} %copy-done.8, bf16[160,3200]{1,0:T(8,128)(2,1)} %collective-permute-done.9.refs_1_, bf16[160,3200]{1,0:T(8,128)(2,1)} %collective-permute-done.10.refs_2_, bf16[160,3200]{1,0:T(8,128)(2,1)} %collective-permute-done.11.refs_3_, ...), custom_call_target="tpu_custom_call" | custom-call | flops 4026531840 | bytes 12582912 | tf_op jit(solution)/shard_map/expert/pallas_call | solution.py:170
  162.6 17.4 %all_to_all.20 = bf16[16,160,128]{2,1,0:T(8,128)(2,1)S(1)} all-to-all(bf16[16,160,128]{2,1,0:T(8,128)(2,1)S(1)} %bitcast.21), channel_id=1, replica_groups=mesh['dp'=2,'y'=4,'c'=2,'z'=8,'xl'=2] {'y','c','xl'}, dimensions={0} | all-to-all | bytes 1310720 | tf_op jit(solution)/shard_map/all_to_all | solution.py:182
  180.1 1.4 combine.1
  181.5 1.6 reshape.23
  (58 shorter events, 1.3 us)
Async XLA Ops:
  0.9 4.0 %collective-permute-start = (bf16[2,192,128]{2,1,0:T(8,128)(2,1)S(1)}, bf16[2,192,128]{2,1,0:T(8,128)(2,1)S(1)}, u32[]{:S(2)}, u32[]{:S(2)}) collective-permute-start(bf16[2,192,128]{2,1,0:T(8,128)(2,1)S(1)} %dynamic-slice_bitcast_fusion), channel_id=1, source_target_pairs={{0,1},{1,0},{2,3},{3,2},{4,5},{5,4},{6,7},{7,6},{8,9},{9,8},{10,11... | collective-permute-start | bytes 294920 | tf_op jit(solution)/shard_map/ppermute | solution.py:16
  5.9 9.3 %collective-permute-start.4 = (bf16[2,384,128]{2,1,0:T(8,128)(2,1)S(1)}, bf16[2,384,128]{2,1,0:T(8,128)(2,1)S(1)}, u32[]{:S(2)}, u32[]{:S(2)}) collective-permute-start(bf16[2,384,128]{2,1,0:T(8,128)(2,1)S(1)} %pad_maximum_fusion.refs_0_), channel_id=1, source_target_pairs={{0,2},{2,4},{4,6},{6,8},{8,10},{10,12},{12,14},{14,0},{1,3},{3,5},... | collective-permute-start | bytes 589832 | tf_op jit(solution)/shard_map/ppermute | solution.py:16
  7.8 7.3 %collective-permute-start.1 = (bf16[2,384,128]{2,1,0:T(8,128)(2,1)S(1)}, bf16[2,384,128]{2,1,0:T(8,128)(2,1)S(1)}, u32[]{:S(2)}, u32[]{:S(2)}) collective-permute-start(bf16[2,384,128]{2,1,0:T(8,128)(2,1)S(1)} %pad_maximum_fusion.refs_0_), channel_id=1, source_target_pairs={{0,14},{2,0},{4,2},{6,4},{8,6},{10,8},{12,10},{14,12},{1,15},{3,1}... | collective-permute-start | bytes 589832 | tf_op jit(solution)/shard_map/ppermute | solution.py:16
  15.2 5.7 %collective-permute-start.5 = (bf16[2,384,128]{2,1,0:T(8,128)(2,1)S(1)}, bf16[2,384,128]{2,1,0:T(8,128)(2,1)S(1)}, u32[]{:S(2)}, u32[]{:S(2)}) collective-permute-start(bf16[2,384,128]{2,1,0:T(8,128)(2,1)S(1)} %collective-permute-done.4.refs_7_), channel_id=1, source_target_pairs={{0,2},{2,4},{4,6},{6,8},{8,10},{10,12},{12,14},{14,0},{1,3},{3,5},... | collective-permute-start | bytes 589832 | tf_op jit(solution)/shard_map/ppermute | solution.py:16
  15.2 5.7 %collective-permute-start.2 = (bf16[2,384,128]{2,1,0:T(8,128)(2,1)S(1)}, bf16[2,384,128]{2,1,0:T(8,128)(2,1)S(1)}, u32[]{:S(2)}, u32[]{:S(2)}) collective-permute-start(bf16[2,384,128]{2,1,0:T(8,128)(2,1)S(1)} %collective-permute-done.1.refs_1_), channel_id=1, source_target_pairs={{0,14},{2,0},{4,2},{6,4},{8,6},{10,8},{12,10},{14,12},{1,15},{3,1}... | collective-permute-start | bytes 589832 | tf_op jit(solution)/shard_map/ppermute | solution.py:16
  20.9 5.7 %collective-permute-start.6 = (bf16[2,384,128]{2,1,0:T(8,128)(2,1)S(1)}, bf16[2,384,128]{2,1,0:T(8,128)(2,1)S(1)}, u32[]{:S(2)}, u32[]{:S(2)}) collective-permute-start(bf16[2,384,128]{2,1,0:T(8,128)(2,1)S(1)} %collective-permute-done.5.refs_6_), channel_id=1, source_target_pairs={{0,2},{2,4},{4,6},{6,8},{8,10},{10,12},{12,14},{14,0},{1,3},{3,5},... | collective-permute-start | bytes 589832 | tf_op jit(solution)/shard_map/ppermute | solution.py:16
  20.9 5.8 %collective-permute-start.3 = (bf16[2,384,128]{2,1,0:T(8,128)(2,1)S(1)}, bf16[2,384,128]{2,1,0:T(8,128)(2,1)S(1)}, u32[]{:S(2)}, u32[]{:S(2)}) collective-permute-start(bf16[2,384,128]{2,1,0:T(8,128)(2,1)S(1)} %collective-permute-done.2.refs_2_), channel_id=1, source_target_pairs={{0,14},{2,0},{4,2},{6,4},{8,6},{10,8},{12,10},{14,12},{1,15},{3,1}... | collective-permute-start | bytes 589832 | tf_op jit(solution)/shard_map/ppermute | solution.py:16
  26.6 7.8 %collective-permute-start.7 = (bf16[1,384,128]{2,1,0:T(8,128)(2,1)S(1)}, bf16[1,384,128]{2,1,0:T(8,128)(2,1)S(1)}, u32[]{:S(2)}, u32[]{:S(2)}) collective-permute-start(bf16[1,384,128]{2,1,0:T(8,128)(2,1)S(1)} %slice.24), channel_id=1, source_target_pairs={{0,2},{2,4},{4,6},{6,8},{8,10},{10,12},{12,14},{14,0},{1,3},{3,5},... | collective-permute-start | bytes 294920 | tf_op jit(solution)/shard_map/ppermute | solution.py:16
  26.8 7.7 %collective-permute-start.8 = (bf16[1,384,128]{2,1,0:T(8,128)(2,1)S(1)}, bf16[1,384,128]{2,1,0:T(8,128)(2,1)S(1)}, u32[]{:S(2)}, u32[]{:S(2)}) collective-permute-start(bf16[1,384,128]{2,1,0:T(8,128)(2,1)S(1)} %slice.25), channel_id=1, source_target_pairs={{0,14},{2,0},{4,2},{6,4},{8,6},{10,8},{12,10},{14,12},{1,15},{3,1}... | collective-permute-start | bytes 294920 | tf_op jit(solution)/shard_map/ppermute | solution.py:16
  29.6 1.4 copy-start
  31.0 1.4 copy-start.1
  34.4 5.0 %copy-start.14 = (s32[4,128,2]{1,2,0:T(2,128)S(1)}, s32[4,128,2]{1,2,0:T(2,128)}, u32[]{:S(2)}) copy-start(s32[4,128,2]{1,2,0:T(2,128)} %param.6) | copy-start | bytes 12292
  34.4 5.0 %copy-start.15 = (f32[4,128,2]{1,2,0:T(2,128)S(1)}, f32[4,128,2]{1,2,0:T(2,128)}, u32[]{:S(2)}) copy-start(f32[4,128,2]{1,2,0:T(2,128)} %param.7) | copy-start | bytes 12292
  34.4 19.1 %all-to-all-start = ((bf16[8,192,256]{2,1,0:T(8,128)(2,1)}), bf16[8,192,256]{2,1,0:T(8,128)(2,1)S(1)}, u32[]{:S(2)}, u32[]{:S(2)}) async-start(bf16[8,192,256]{2,1,0:T(8,128)(2,1)} %get-tuple-element.37), calls=%async_computation | async-start | bytes 1572864 | tf_op jit(solution)/shard_map/all_to_all | solution.py:136
  43.1 9.4 %collective-permute-start.12 = (bf16[160,3200]{1,0:T(8,128)(2,1)S(1)}, bf16[160,3200]{1,0:T(8,128)(2,1)S(1)}, u32[]{:S(2)}, u32[]{:S(2)}) collective-permute-start(bf16[160,3200]{1,0:T(8,128)(2,1)S(1)} %get-tuple-element.30.refs_0_), channel_id=1, source_target_pairs={{0,16},{16,0},{1,17},{17,1},{2,18},{18,2},{3,19},{19,3},{4,20},{20... | collective-permute-start | bytes 3072008 | tf_op jit(solution)/shard_map/ppermute | solution.py:16
  50.2 1.0 copy-start.6
  52.5 1.0 copy-start.9
  53.6 57.8 %all-to-all-start.1 = ((bf16[8,192,256]{2,1,0:T(8,128)(2,1)}), bf16[8,192,256]{2,1,0:T(8,128)(2,1)S(1)}, u32[]{:S(2)}, u32[]{:S(2)}) async-start(bf16[8,192,256]{2,1,0:T(8,128)(2,1)} %get-tuple-element.41), calls=%async_computation.1 | async-start | bytes 1572864 | tf_op jit(solution)/shard_map/all_to_all | solution.py:136
  60.4 20.5 %collective-permute-start.9 = (bf16[160,3200]{1,0:T(8,128)(2,1)}, bf16[160,3200]{1,0:T(8,128)(2,1)}, u32[]{:S(2)}, u32[]{:S(2)}) collective-permute-start(bf16[160,3200]{1,0:T(8,128)(2,1)} %get-tuple-element.31), channel_id=1, source_target_pairs={{0,32},{32,64},{64,96},{96,0},{1,33},{33,65},{65,97},{97,1},{2,34}... | collective-permute-start | bytes 3072008 | tf_op jit(solution)/shard_map/ppermute | solution.py:16
  61.7 40.8 %collective-permute-start.10 = (bf16[160,3200]{1,0:T(8,128)(2,1)}, bf16[160,3200]{1,0:T(8,128)(2,1)}, u32[]{:S(2)}, u32[]{:S(2)}) collective-permute-start(bf16[160,3200]{1,0:T(8,128)(2,1)} %get-tuple-element.32), channel_id=1, source_target_pairs={{0,64},{32,96},{64,0},{96,32},{1,65},{33,97},{65,1},{97,33},{2,66}... | collective-permute-start | bytes 3072008 | tf_op jit(solution)/shard_map/ppermute | solution.py:16
  64.3 43.8 %collective-permute-start.11 = (bf16[160,3200]{1,0:T(8,128)(2,1)}, bf16[160,3200]{1,0:T(8,128)(2,1)}, u32[]{:S(2)}, u32[]{:S(2)}) collective-permute-start(bf16[160,3200]{1,0:T(8,128)(2,1)} %get-tuple-element.33), channel_id=1, source_target_pairs={{0,96},{32,0},{64,32},{96,64},{1,97},{33,1},{65,33},{97,65},{2,98}... | collective-permute-start | bytes 3072008 | tf_op jit(solution)/shard_map/ppermute | solution.py:16
  65.4 11.7 %collective-permute-start.17 = (bf16[8,192,256]{2,1,0:T(8,128)(2,1)S(1)}, bf16[8,192,256]{2,1,0:T(8,128)(2,1)S(1)}, u32[]{:S(2)}, u32[]{:S(2)}) collective-permute-start(bf16[8,192,256]{2,1,0:T(8,128)(2,1)S(1)} %all-to-all-done.refs_8_), channel_id=1, source_target_pairs={{0,129},{1,0},{128,1},{129,128},{2,131},{3,2},{130,3},{131,130},{4... | collective-permute-start | bytes 2359304 | tf_op jit(solution)/shard_map/ppermute | solution.py:16
  67.9 12.9 %collective-permute-start.16 = (bf16[8,192,256]{2,1,0:T(8,128)(2,1)S(1)}, bf16[8,192,256]{2,1,0:T(8,128)(2,1)S(1)}, u32[]{:S(2)}, u32[]{:S(2)}) collective-permute-start(bf16[8,192,256]{2,1,0:T(8,128)(2,1)S(1)} %all-to-all-done.refs_8_), channel_id=1, source_target_pairs={{0,1},{1,128},{128,129},{129,0},{2,3},{3,130},{130,131},{131,2},{4... | collective-permute-start | bytes 2359304 | tf_op jit(solution)/shard_map/ppermute | solution.py:16
  77.1 33.5 %collective-permute-start.19 = (bf16[4,192,256]{2,1,0:T(8,128)(2,1)S(1)}, bf16[4,192,256]{2,1,0:T(8,128)(2,1)S(1)}, u32[]{:S(2)}, u32[]{:S(2)}) collective-permute-start(bf16[4,192,256]{2,1,0:T(8,128)(2,1)S(1)} %slice.27), channel_id=1, source_target_pairs={{0,129},{1,0},{128,1},{129,128},{2,131},{3,2},{130,3},{131,130},{4... | collective-permute-start | bytes 1179656 | tf_op jit(solution)/shard_map/ppermute | solution.py:16
  80.7 29.9 %collective-permute-start.18 = (bf16[4,192,256]{2,1,0:T(8,128)(2,1)S(1)}, bf16[4,192,256]{2,1,0:T(8,128)(2,1)S(1)}, u32[]{:S(2)}, u32[]{:S(2)}) collective-permute-start(bf16[4,192,256]{2,1,0:T(8,128)(2,1)S(1)} %slice.26), channel_id=1, source_target_pairs={{0,1},{1,128},{128,129},{129,0},{2,3},{3,130},{130,131},{131,2},{4... | collective-permute-start | bytes 1179656 | tf_op jit(solution)/shard_map/ppermute | solution.py:16
  108.1 28.1 %collective-permute-start.13 = (bf16[160,3200]{1,0:T(8,128)(2,1)}, bf16[160,3200]{1,0:T(8,128)(2,1)}, u32[]{:S(2)}, u32[]{:S(2)}) collective-permute-start(bf16[160,3200]{1,0:T(8,128)(2,1)} %collective-permute-done.9.refs_1_), channel_id=1, source_target_pairs={{0,16},{16,0},{1,17},{17,1},{2,18},{18,2},{3,19},{19,3},{4,20},{20... | collective-permute-start | bytes 3072008 | tf_op jit(solution)/shard_map/ppermute | solution.py:16
  110.1 26.0 %collective-permute-start.14 = (bf16[160,3200]{1,0:T(8,128)(2,1)}, bf16[160,3200]{1,0:T(8,128)(2,1)}, u32[]{:S(2)}, u32[]{:S(2)}) collective-permute-start(bf16[160,3200]{1,0:T(8,128)(2,1)} %collective-permute-done.10.refs_2_), channel_id=1, source_target_pairs={{0,16},{16,0},{1,17},{17,1},{2,18},{18,2},{3,19},{19,3},{4,20},{20... | collective-permute-start | bytes 3072008 | tf_op jit(solution)/shard_map/ppermute | solution.py:16
  110.1 26.0 %collective-permute-start.15 = (bf16[160,3200]{1,0:T(8,128)(2,1)}, bf16[160,3200]{1,0:T(8,128)(2,1)}, u32[]{:S(2)}, u32[]{:S(2)}) collective-permute-start(bf16[160,3200]{1,0:T(8,128)(2,1)} %collective-permute-done.11.refs_3_), channel_id=1, source_target_pairs={{0,16},{16,0},{1,17},{17,1},{2,18},{18,2},{3,19},{19,3},{4,20},{20... | collective-permute-start | bytes 3072008 | tf_op jit(solution)/shard_map/ppermute | solution.py:16
  110.7 0.8 copy-start.12
  111.4 24.8 %copy-start.7 = (bf16[160,3200]{1,0:T(8,128)(2,1)S(1)}, bf16[160,3200]{1,0:T(8,128)(2,1)}, u32[]{:S(2)}) copy-start(bf16[160,3200]{1,0:T(8,128)(2,1)} %copy-done.6) | copy-start | bytes 3072004
  111.4 24.8 %copy-start.13 = (bf16[4,192,256]{2,1,0:T(8,128)(2,1)S(1)}, bf16[4,192,256]{2,1,0:T(8,128)(2,1)}, u32[]{:S(2)}) copy-start(bf16[4,192,256]{2,1,0:T(8,128)(2,1)} %copy-done.12) | copy-start | bytes 1179652
  111.4 19.5 %collective-permute-start.21 = (bf16[8,192,256]{2,1,0:T(8,128)(2,1)S(1)}, bf16[8,192,256]{2,1,0:T(8,128)(2,1)S(1)}, u32[]{:S(2)}, u32[]{:S(2)}) collective-permute-start(bf16[8,192,256]{2,1,0:T(8,128)(2,1)S(1)} %all-to-all-done.1.refs_8_), channel_id=1, source_target_pairs={{0,129},{1,0},{128,1},{129,128},{2,131},{3,2},{130,3},{131,130},{4... | collective-permute-start | bytes 2359304 | tf_op jit(solution)/shard_map/ppermute | solution.py:16
  113.9 21.2 %collective-permute-start.20 = (bf16[8,192,256]{2,1,0:T(8,128)(2,1)S(1)}, bf16[8,192,256]{2,1,0:T(8,128)(2,1)S(1)}, u32[]{:S(2)}, u32[]{:S(2)}) collective-permute-start(bf16[8,192,256]{2,1,0:T(8,128)(2,1)S(1)} %all-to-all-done.1.refs_8_), channel_id=1, source_target_pairs={{0,1},{1,128},{128,129},{129,0},{2,3},{3,130},{130,131},{131,2},{4... | collective-permute-start | bytes 2359304 | tf_op jit(solution)/shard_map/ppermute | solution.py:16
  130.9 4.3 %copy-start.2 = (bf16[8,192,256]{2,1,0:T(8,128)(2,1)}, bf16[8,192,256]{2,1,0:T(8,128)(2,1)S(1)}, u32[]{:S(2)}) copy-start(bf16[8,192,256]{2,1,0:T(8,128)(2,1)S(1)} %collective-permute-done.21.refs_10_) | copy-start | bytes 2359300
  131.7 18.7 %collective-permute-start.23 = (bf16[4,192,256]{2,1,0:T(8,128)(2,1)}, bf16[4,192,256]{2,1,0:T(8,128)(2,1)}, u32[]{:S(2)}, u32[]{:S(2)}) collective-permute-start(bf16[4,192,256]{2,1,0:T(8,128)(2,1)} %slice.29), channel_id=1, source_target_pairs={{0,129},{1,0},{128,1},{129,128},{2,131},{3,2},{130,3},{131,130},{4... | collective-permute-start | bytes 1179656 | tf_op jit(solution)/shard_map/ppermute | solution.py:16
  135.2 1.0 copy-start.4
  136.2 14.3 %collective-permute-start.22 = (bf16[4,192,256]{2,1,0:T(8,128)(2,1)}, bf16[4,192,256]{2,1,0:T(8,128)(2,1)}, u32[]{:S(2)}, u32[]{:S(2)}) collective-permute-start(bf16[4,192,256]{2,1,0:T(8,128)(2,1)} %slice.28), channel_id=1, source_target_pairs={{0,1},{1,128},{128,129},{129,0},{2,3},{3,130},{130,131},{131,2},{4... | collective-permute-start | bytes 1179656 | tf_op jit(solution)/shard_map/ppermute | solution.py:16
  136.2 1.2 copy-start.10
  145.5 17.1 %all-to-all-start.2 = ((bf16[16,160,128]{2,1,0:T(8,128)(2,1)}), bf16[16,160,128]{2,1,0:T(8,128)(2,1)S(1)}, u32[]{:S(2)}, u32[]{:S(2)}) async-start(bf16[16,160,128]{2,1,0:T(8,128)(2,1)} %bitcast.11), calls=%async_computation.2 | async-start | bytes 1310720 | tf_op jit(solution)/shard_map/all_to_all | solution.py:182
  150.5 1.1 copy-start.3
  151.6 1.1 copy-start.5
  152.7 1.2 copy-start.8
  153.9 1.2 copy-start.11

commit v5 on v4

--- a/solution.py
+++ b/solution.py
@@ -8,6 +8,7 @@
 MOST = 80
 X = ("dp", "xl")
 BF, F32 = jnp.bfloat16, jnp.float32
+HBM = pl.BlockSpec(memory_space=pltpu.HBM)
 VM = pl.BlockSpec(memory_space=pltpu.VMEM)
 SM = pl.BlockSpec(memory_space=pltpu.SMEM)
 
@@ -59,16 +60,20 @@
                 outs[d][s * MOST : (s + 1) * MOST, k * width : (k + 1) * width] = picked[d * MOST : (d + 1) * MOST]
 
 
-def columns_kernel(pos, gate, up, out_a, out_b):
+def columns_kernel(pos, gate, up, out_a, out_b, held, sem):
     for flag, src in ((0, gate), (1, up)):
 
         @pl.when(pos[3] == flag)
         def _(src=src):
-            for r, out in enumerate((out_a, out_b)):
-                for z in range(8):
-                    for t in range(2):
-                        first = z * 512 + t * 256 + r * 128
-                        out[z, :, t * 128 : (t + 1) * 128] = src[0, :, first : first + 128]
+            copy = pltpu.make_async_copy(src.at[0], held, sem)
+            copy.start()
+            copy.wait()
+
+    for r, out in enumerate((out_a, out_b)):
+        for z in range(8):
+            for t in range(2):
+                first = z * 512 + t * 256 + r * 128
+                out[z, :, t * 128 : (t + 1) * 128] = held[:, first : first + 128]
 
 
 def expert_kernel(pos, *refs):
@@ -126,8 +131,9 @@
     blocks = pl.pallas_call(
         columns_kernel,
         out_shape=[jax.ShapeDtypeStruct((8, rows, 2 * wide), BF)] * 2,
-        in_specs=[SM, VM, VM],
+        in_specs=[SM, HBM, HBM],
         out_specs=[VM] * 2,
+        scratch_shapes=[pltpu.VMEM((rows, units), BF), pltpu.SemaphoreType.DMA(())],
         compiler_params=pltpu.CompilerParams(vmem_limit_bytes=16 << 20),
         name="columns",
     )(pos, gate_train, up_train)
@@ -135,14 +141,20 @@
     def exchange(x):
         return lax.all_to_all(x, "z", split_axis=0, concat_axis=0, tiled=True)
 
+    def spread(own):
+        left, right = ring(own, X, 4, 1), ring(own, X, 4, -1)
+        return [own, left, right, ring(left[:4], X, 4, 1), ring(right[4:], X, 4, -1)]
+
     below, above = [pair], [pair]
     for k in range(3):
+        if k == 2:
+            below[2], above[2], *blocks = barrier((below[2], above[2], *blocks))
         below.append(ring(below[-1], "z", 8, 1))
         above.append(ring(above[-1], "z", 8, -1))
     last = barrier((blocks[0], ring(below[3][:1], "z", 8, 1), ring(above[3][1:], "z", 8, -1)))
-    own_a = exchange(last[0])
     opposite = jnp.concatenate(last[1:], axis=0)
     feats = [pair] + above[1:] + [opposite] + below[:0:-1]
+    own_a = exchange(last[0])
     sent = pl.pallas_call(
         dispatch_kernel,
         out_shape=[jax.ShapeDtypeStruct((2 * MOST, 16 * width + 128), BF)] * 4,
@@ -151,20 +163,18 @@
         compiler_params=pltpu.CompilerParams(vmem_limit_bytes=24 << 20),
         name="dispatch",
     )(pos, meta, *feats)
-    held = [sent[0]] + [ring(sent[d], "y", 4, d) for d in (1, 2, 3)]
-    other = [ring(sent[0], "c", 2, 1)]
-    own_a, other[0] = barrier((own_a, other[0]))
-    own_b, own_a = barrier((blocks[1], own_a))
-    own_b = exchange(own_b)
-    pieces = []
-    for own in (own_a, own_b):
-        if pieces:
-            own, *pieces[0] = barrier((own, *pieces[0]))
-        left, right = ring(own, X, 4, 1), ring(own, X, 4, -1)
-        far_a, far_b = ring(left[:4], X, 4, 1), ring(right[4:], X, 4, -1)
-        pieces.append([own, left, right, far_a, far_b])
-    held[1:] = barrier(tuple(held[1:]))
-    other += [ring(h, "c", 2, 1) for h in held[1:]]
+    held = [sent[0], ring(sent[1], "y", 4, 1), None, ring(sent[3], "y", 4, 3)]
+    own_a, part_b, held[0], held[1], far_rows, held[3] = barrier((own_a, blocks[1], held[0], held[1], sent[2], held[3]))
+    own_b = exchange(part_b)
+    held[2] = ring(far_rows, "y", 4, 2)
+    ws_a = spread(own_a)
+    other = [ring(held[d], "c", 2, 1) if d != 2 else None for d in range(4)]
+    own_b, held[2], ws_a[3], ws_a[4], other[0], other[1], other[3] = barrier(
+        (own_b, held[2], ws_a[3], ws_a[4], other[0], other[1], other[3])
+    )
+    ws_b = spread(own_b)
+    other[2] = ring(held[2], "c", 2, 1)
+    pieces = [ws_a, ws_b]
     backs = []
     for ws in pieces:
         act = pl.pallas_call(
@@ -173,7 +183,7 @@
             in_specs=[SM] + [VM] * 13,
             out_specs=VM,
             scratch_shapes=[pltpu.VMEM((2, 8, 2, rows, 2 * wide), BF)],
-            compiler_params=pltpu.CompilerParams(vmem_limit_bytes=24 << 20),
+            compiler_params=pltpu.CompilerParams(vmem_limit_bytes=8 << 20),
             cost_estimate=pl.CostEstimate(
                 flops=16 * MOST * 16 * width * 8 * wide, bytes_accessed=12 << 20, transcendentals=16 * MOST * 2 * wide
             ),

time: 184 us -> 198 us (1.076)
  starting transfers between devices: 59.6 us -> 79.6 us
  waiting for transfers between devices: 66.3 us -> 50.5 us
  local copies, waits for them, and re-layouts: 15.9 us -> 27.6 us
  Pallas kernels: 22.7 us -> 20.1 us
    ppermute x24, starting transfers between devices: 42.9 us -> 62.7 us  [ring(): return lax.ppermute(x, axis, [(i, (i + step) % size) for i in range(size)])]
    ppermute x24, waiting for transfers between devices: 66.2 us -> 50.5 us  [ring(): return lax.ppermute(x, axis, [(i, (i + step) % size) for i in range(size)])]
    unnamed x32 -> x54, local copies, waits for them, and re-layouts: 11.7 us -> 23.3 us
  transfers between devices with their start and end apart: 27 -> 27, of which waited for: 10 -> 8; matrix products, arithmetic and copies ran while one was open for 1% -> 1% of each run, Pallas kernels for 12% -> 10%
where the time goes in v5:
time: 198 us; the launch traced here: 197 us
  starting transfers between devices  79.6 us (40%)
  waiting for transfers between devices  50.5 us (26%)
  local copies, waits for them, and re-layouts  27.6 us (14%)
  Pallas kernels  20.1 us (10%)
  blocking collectives  17.5 us (9%)
    ppermute x24, starting transfers between devices, ring(): return lax.ppermute(x, axis, [(i, (i + step) % size) for i in range(size)])  62.7 us
    ppermute x24, waiting for transfers between devices, ring(): return lax.ppermute(x, axis, [(i, (i + step) % size) for i in range(size)])  50.5 us
    unnamed x54, local copies, waits for them, and re-layouts  23.3 us
    all_to_all x1, blocking collectives, body(): lax.all_to_all(act.reshape(16, 2 * MOST, wide), ('y', 'c', 'xl'), split_a...  17.5 us
    pallas_call x2, Pallas kernels, body(): pl.pallas_call(expert_kernel, out_shape=jax.ShapeDtypeStruct((4, 2, 2, 2...  13.6 us
    all_to_all x2, starting transfers between devices, exchange(): return lax.all_to_all(x, 'z', split_axis=0, concat_axis=0, tiled=True)  12.2 us
    all_to_all x1, starting transfers between devices, body(): lax.all_to_all(act.reshape(16, 2 * MOST, wide), ('y', 'c', 'xl'), split_a...  4.81 us
  transfers between devices with their start and end apart: 27, of which 8 were waited for; matrix products, arithmetic and copies ran while one was open for 1% of the time, Pallas kernels for 10%

profile of v5, /device:TPU:1, one launch (start us, length us, event | category | flops | bytes accessed | tf_op | source)
XLA Modules:
  0.0 196.6 jit_solution(2665474622174744905)
XLA Ops:
  0.9 2.0 %collective-permute-start = (bf16[2,192,128]{2,1,0:T(8,128)(2,1)S(1)}, bf16[2,192,128]{2,1,0:T(8,128)(2,1)S(1)}, u32[]{:S(2)}, u32[]{:S(2)}) collective-permute-start(bf16[2,192,128]{2,1,0:T(8,128)(2,1)S(1)} %dynamic-slice_bitcast_fusion), channel_id=1, source_target_pairs={{0,1},{1,0},{2,3},{3,2},{4,5},{5,4},{6,7},{7,6},{8,9},{9,8},{10,11... | collective-permute-start | bytes 294920 | tf_op jit(solution)/shard_map/ppermute | solution.py:17
  2.9 2.0 %collective-permute-done = bf16[2,192,128]{2,1,0:T(8,128)(2,1)S(1)} collective-permute-done((bf16[2,192,128]{2,1,0:T(8,128)(2,1)S(1)}, bf16[2,192,128]{2,1,0:T(8,128)(2,1)S(1)}, u32[]{:S(2)}, u32[]{:S(2)}) %collective-permute-start) | collective-permute-done | bytes 98336 | tf_op jit(solution)/shard_map/ppermute | solution.py:17
  5.9 2.0 %collective-permute-start.1 = (bf16[2,384,128]{2,1,0:T(8,128)(2,1)S(1)}, bf16[2,384,128]{2,1,0:T(8,128)(2,1)S(1)}, u32[]{:S(2)}, u32[]{:S(2)}) collective-permute-start(bf16[2,384,128]{2,1,0:T(8,128)(2,1)S(1)} %pad_maximum_fusion.refs_0_), channel_id=1, source_target_pairs={{0,2},{2,4},{4,6},{6,8},{8,10},{10,12},{12,14},{14,0},{1,3},{3,5},... | collective-permute-start | bytes 589832 | tf_op jit(solution)/shard_map/ppermute | solution.py:17
  7.9 4.0 %collective-permute-start.3 = (bf16[2,384,128]{2,1,0:T(8,128)(2,1)S(1)}, bf16[2,384,128]{2,1,0:T(8,128)(2,1)S(1)}, u32[]{:S(2)}, u32[]{:S(2)}) collective-permute-start(bf16[2,384,128]{2,1,0:T(8,128)(2,1)S(1)} %pad_maximum_fusion.refs_0_), channel_id=1, source_target_pairs={{0,14},{2,0},{4,2},{6,4},{8,6},{10,8},{12,10},{14,12},{1,15},{3,1}... | collective-permute-start | bytes 589832 | tf_op jit(solution)/shard_map/ppermute | solution.py:17
  11.9 3.3 %collective-permute-done.1.refs_7_ = bf16[2,384,128]{2,1,0:T(8,128)(2,1)S(1)} collective-permute-done((bf16[2,384,128]{2,1,0:T(8,128)(2,1)S(1)}, bf16[2,384,128]{2,1,0:T(8,128)(2,1)S(1)}, u32[]{:S(2)}, u32[]{:S(2)}) %collective-permute-start.1) | collective-permute-done | bytes 196640 | tf_op jit(solution)/shard_map/ppermute | solution.py:17
  15.2 2.7 %collective-permute-start.4 = (bf16[2,384,128]{2,1,0:T(8,128)(2,1)S(1)}, bf16[2,384,128]{2,1,0:T(8,128)(2,1)S(1)}, u32[]{:S(2)}, u32[]{:S(2)}) collective-permute-start(bf16[2,384,128]{2,1,0:T(8,128)(2,1)S(1)} %collective-permute-done.3.refs_1_), channel_id=1, source_target_pairs={{0,14},{2,0},{4,2},{6,4},{8,6},{10,8},{12,10},{14,12},{1,15},{3,1}... | collective-permute-start | bytes 589832 | tf_op jit(solution)/shard_map/ppermute | solution.py:17
  17.9 1.4 copy-done
  19.4 1.4 copy-done.1
  20.8 2.1 %columns.1 = (bf16[8,192,256]{2,1,0:T(8,128)(2,1)}, bf16[8,192,256]{2,1,0:T(8,128)(2,1)}) custom-call(s32[5]{0:T(128)S(1)} %stack.23.pos, bf16[1,192,4096]{2,1,0:T(8,128)(2,1)S(1)} %copy-done, bf16[1,192,4096]{2,1,0:T(8,128)(2,1)S(1)} %copy-done.1), custom_call_target="tpu_custom_call" | custom-call | tf_op jit(solution)/shard_map/columns/pallas_call | solution.py:131
  23.0 2.7 %collective-permute-start.7 = (bf16[2,384,128]{2,1,0:T(8,128)(2,1)S(1)}, bf16[2,384,128]{2,1,0:T(8,128)(2,1)S(1)}, u32[]{:S(2)}, u32[]{:S(2)}) collective-permute-start(bf16[2,384,128]{2,1,0:T(8,128)(2,1)S(1)} %collective-permute-done.4.refs_2_), channel_id=1, source_target_pairs={{0,14},{2,0},{4,2},{6,4},{8,6},{10,8},{12,10},{14,12},{1,15},{3,1}... | collective-permute-start | bytes 589832 | tf_op jit(solution)/shard_map/ppermute | solution.py:17
  25.6 3.1 %collective-permute-done.5.refs_5_ = bf16[2,384,128]{2,1,0:T(8,128)(2,1)S(1)} collective-permute-done((bf16[2,384,128]{2,1,0:T(8,128)(2,1)S(1)}, bf16[2,384,128]{2,1,0:T(8,128)(2,1)S(1)}, u32[]{:S(2)}, u32[]{:S(2)}) %collective-permute-start.5) | collective-permute-done | bytes 196640 | tf_op jit(solution)/shard_map/ppermute | solution.py:17
  28.8 2.7 %collective-permute-start.8 = (bf16[1,384,128]{2,1,0:T(8,128)(2,1)S(1)}, bf16[1,384,128]{2,1,0:T(8,128)(2,1)S(1)}, u32[]{:S(2)}, u32[]{:S(2)}) collective-permute-start(bf16[1,384,128]{2,1,0:T(8,128)(2,1)S(1)} %slice.25), channel_id=1, source_target_pairs={{0,14},{2,0},{4,2},{6,4},{8,6},{10,8},{12,10},{14,12},{1,15},{3,1}... | collective-permute-start | bytes 294920 | tf_op jit(solution)/shard_map/ppermute | solution.py:17
  31.6 1.9 collective-permute-done.6
  33.5 5.8 %all-to-all-start = ((bf16[8,192,256]{2,1,0:T(8,128)(2,1)}), bf16[8,192,256]{2,1,0:T(8,128)(2,1)S(1)}, u32[]{:S(2)}, u32[]{:S(2)}) async-start(bf16[8,192,256]{2,1,0:T(8,128)(2,1)} %get-tuple-element.36), calls=%async_computation | async-start | bytes 1572864 | tf_op jit(solution)/shard_map/all_to_all | solution.py:142
  39.3 3.0 %dispatch.1 = (bf16[160,3200]{1,0:T(8,128)(2,1)S(1)}, bf16[160,3200]{1,0:T(8,128)(2,1)S(1)}, bf16[160,3200]{1,0:T(8,128)(2,1)}, bf16[160,3200]{1,0:T(8,128)(2,1)S(1)}) custom-call(s32[5]{0:T(128)S(1)} %stack.23.pos, f32[4,4,128]{2,1,0:T(4,128)S(1)} %maximum_bitcast_fusion.meta, bf16[2,384,128]{2,1,0:T(8,128)(2,1)S(1)} %pad_maximum_fusion.refs_0_, ...), custom_call_target="tpu_custom_call" | custom-call | tf_op jit(solution)/shard_map/dispatch/pallas_call | solution.py:158
  43.3 1.3 collective-permute-start.9
  44.6 1.4 collective-permute-start.10
  46.0 16.5 %collective-permute-done.9.refs_1_ = bf16[160,3200]{1,0:T(8,128)(2,1)S(1)} collective-permute-done((bf16[160,3200]{1,0:T(8,128)(2,1)S(1)}, bf16[160,3200]{1,0:T(8,128)(2,1)S(1)}, u32[]{:S(2)}, u32[]{:S(2)}) %collective-permute-start.9) | collective-permute-done | bytes 1024032 | tf_op jit(solution)/shard_map/ppermute | solution.py:17
  63.5 1.2 collective-permute-start.12
  64.7 1.7 collective-permute-start.11
  66.4 6.4 %all-to-all-start.1 = ((bf16[8,192,256]{2,1,0:T(8,128)(2,1)}), bf16[8,192,256]{2,1,0:T(8,128)(2,1)S(1)}, u32[]{:S(2)}, u32[]{:S(2)}) async-start(bf16[8,192,256]{2,1,0:T(8,128)(2,1)} %get-tuple-element.46), calls=%async_computation.1 | async-start | bytes 1572864 | tf_op jit(solution)/shard_map/all_to_all | solution.py:142
  72.7 1.5 collective-permute-start.14
  74.2 19.4 %collective-permute-start.16 = (bf16[160,3200]{1,0:T(8,128)(2,1)}, bf16[160,3200]{1,0:T(8,128)(2,1)S(1)}, u32[]{:S(2)}, u32[]{:S(2)}) collective-permute-start(bf16[160,3200]{1,0:T(8,128)(2,1)} %copy-done.6), channel_id=1, source_target_pairs={{0,16},{16,0},{1,17},{17,1},{2,18},{18,2},{3,19},{19,3},{4,20},{20... | collective-permute-start | bytes 3072008 | tf_op jit(solution)/shard_map/ppermute | solution.py:17
  94.3 2.7 %collective-permute-start.15 = (bf16[4,192,256]{2,1,0:T(8,128)(2,1)S(1)}, bf16[4,192,256]{2,1,0:T(8,128)(2,1)S(1)}, u32[]{:S(2)}, u32[]{:S(2)}) collective-permute-start(bf16[4,192,256]{2,1,0:T(8,128)(2,1)S(1)} %slice.27), channel_id=1, source_target_pairs={{0,129},{1,0},{128,1},{129,128},{2,131},{3,2},{130,3},{131,130},{4... | collective-permute-start | bytes 1179656 | tf_op jit(solution)/shard_map/ppermute | solution.py:17
  100.0 2.4 %collective-permute-done.13.refs_11_ = bf16[4,192,256]{2,1,0:T(8,128)(2,1)S(1)} collective-permute-done((bf16[4,192,256]{2,1,0:T(8,128)(2,1)S(1)}, bf16[4,192,256]{2,1,0:T(8,128)(2,1)S(1)}, u32[]{:S(2)}, u32[]{:S(2)}) %collective-permute-start.13) | collective-permute-done | bytes 393248 | tf_op jit(solution)/shard_map/ppermute | solution.py:17
  102.4 3.7 %collective-permute-done.15.refs_12_ = bf16[4,192,256]{2,1,0:T(8,128)(2,1)S(1)} collective-permute-done((bf16[4,192,256]{2,1,0:T(8,128)(2,1)S(1)}, bf16[4,192,256]{2,1,0:T(8,128)(2,1)S(1)}, u32[]{:S(2)}, u32[]{:S(2)}) %collective-permute-start.15) | collective-permute-done | bytes 393248 | tf_op jit(solution)/shard_map/ppermute | solution.py:17
  106.8 11.4 %collective-permute-start.19 = (bf16[160,3200]{1,0:T(8,128)(2,1)}, bf16[160,3200]{1,0:T(8,128)(2,1)S(1)}, u32[]{:S(2)}, u32[]{:S(2)}) collective-permute-start(bf16[160,3200]{1,0:T(8,128)(2,1)} %collective-permute-done.11.refs_2_), channel_id=1, source_target_pairs={{0,16},{16,0},{1,17},{17,1},{2,18},{18,2},{3,19},{19,3},{4,20},{20... | collective-permute-start | bytes 3072008 | tf_op jit(solution)/shard_map/ppermute | solution.py:17
  119.2 1.8 collective-permute-start.21
  120.9 17.6 %collective-permute-done.20.refs_9_ = bf16[8,192,256]{2,1,0:T(8,128)(2,1)S(1)} collective-permute-done((bf16[8,192,256]{2,1,0:T(8,128)(2,1)S(1)}, bf16[8,192,256]{2,1,0:T(8,128)(2,1)S(1)}, u32[]{:S(2)}, u32[]{:S(2)}) %collective-permute-start.20) | collective-permute-done | bytes 786464 | tf_op jit(solution)/shard_map/ppermute | solution.py:17
  140.7 2.4 %collective-permute-start.23 = (bf16[4,192,256]{2,1,0:T(8,128)(2,1)}, bf16[4,192,256]{2,1,0:T(8,128)(2,1)}, u32[]{:S(2)}, u32[]{:S(2)}) collective-permute-start(bf16[4,192,256]{2,1,0:T(8,128)(2,1)} %slice.29), channel_id=1, source_target_pairs={{0,129},{1,0},{128,1},{129,128},{2,131},{3,2},{130,3},{131,130},{4... | collective-permute-start | bytes 1179656 | tf_op jit(solution)/shard_map/ppermute | solution.py:17
  143.1 1.2 copy-done.10
  144.4 1.2 copy-done.13
  145.6 1.2 copy-done.16
  146.8 1.2 copy-done.19
  148.0 7.3 %expert.2 = bf16[4,2,2,160,128]{4,3,2,1,0:T(8,128)(2,1)} custom-call(s32[5]{0:T(128)S(1)} %stack.23.pos, bf16[160,3200]{1,0:T(8,128)(2,1)S(1)} %copy-done.7, bf16[160,3200]{1,0:T(8,128)(2,1)S(1)} %copy-done.10, bf16[160,3200]{1,0:T(8,128)(2,1)} %collective-permute-done.11.refs_2_, bf16[160,3200]{1,0:T(8,128)(2,1)} %collective-permute-done.10.refs_3_, ...), custom_call_target="tpu_custom_call" | custom-call | flops 4026531840 | bytes 12582912 | tf_op jit(solution)/shard_map/expert/pallas_call | solution.py:180
  155.3 4.8 %all-to-all-start.2 = ((bf16[16,160,128]{2,1,0:T(8,128)(2,1)}), bf16[16,160,128]{2,1,0:T(8,128)(2,1)S(1)}, u32[]{:S(2)}, u32[]{:S(2)}) async-start(bf16[16,160,128]{2,1,0:T(8,128)(2,1)} %bitcast.11), calls=%async_computation.2 | async-start | bytes 1310720 | tf_op jit(solution)/shard_map/all_to_all | solution.py:192
  160.2 1.1 copy-done.3
  161.3 1.1 copy-done.5
  162.4 1.2 copy-done.8
  163.6 1.2 copy-done.11
  164.9 1.2 copy-done.14
  166.1 1.2 copy-done.17
  167.3 1.2 copy-done.20
  168.5 1.2 copy-done.22
  169.7 6.3 %expert.3 = bf16[4,2,2,160,128]{4,3,2,1,0:T(8,128)(2,1)S(1)} custom-call(s32[5]{0:T(128)S(1)} %stack.23.pos, bf16[160,3200]{1,0:T(8,128)(2,1)S(1)} %copy-done.8, bf16[160,3200]{1,0:T(8,128)(2,1)S(1)} %copy-done.11, bf16[160,3200]{1,0:T(8,128)(2,1)} %collective-permute-done.11.refs_2_, bf16[160,3200]{1,0:T(8,128)(2,1)} %collective-permute-done.10.refs_3_, ...), custom_call_target="tpu_custom_call" | custom-call | flops 4026531840 | bytes 12582912 | tf_op jit(solution)/shard_map/expert/pallas_call | solution.py:180
  176.0 17.5 %all_to_all.20 = bf16[16,160,128]{2,1,0:T(8,128)(2,1)S(1)} all-to-all(bf16[16,160,128]{2,1,0:T(8,128)(2,1)S(1)} %bitcast.21), channel_id=1, replica_groups=mesh['dp'=2,'y'=4,'c'=2,'z'=8,'xl'=2] {'y','c','xl'}, dimensions={0} | all-to-all | bytes 1310720 | tf_op jit(solution)/shard_map/all_to_all | solution.py:192
  193.5 1.4 combine.1
  195.0 1.6 reshape.23
  (80 shorter events, 11.5 us)
Async XLA Ops:
  0.9 4.0 %collective-permute-start = (bf16[2,192,128]{2,1,0:T(8,128)(2,1)S(1)}, bf16[2,192,128]{2,1,0:T(8,128)(2,1)S(1)}, u32[]{:S(2)}, u32[]{:S(2)}) collective-permute-start(bf16[2,192,128]{2,1,0:T(8,128)(2,1)S(1)} %dynamic-slice_bitcast_fusion), channel_id=1, source_target_pairs={{0,1},{1,0},{2,3},{3,2},{4,5},{5,4},{6,7},{7,6},{8,9},{9,8},{10,11... | collective-permute-start | bytes 294920 | tf_op jit(solution)/shard_map/ppermute | solution.py:17
  5.9 9.3 %collective-permute-start.1 = (bf16[2,384,128]{2,1,0:T(8,128)(2,1)S(1)}, bf16[2,384,128]{2,1,0:T(8,128)(2,1)S(1)}, u32[]{:S(2)}, u32[]{:S(2)}) collective-permute-start(bf16[2,384,128]{2,1,0:T(8,128)(2,1)S(1)} %pad_maximum_fusion.refs_0_), channel_id=1, source_target_pairs={{0,2},{2,4},{4,6},{6,8},{8,10},{10,12},{12,14},{14,0},{1,3},{3,5},... | collective-permute-start | bytes 589832 | tf_op jit(solution)/shard_map/ppermute | solution.py:17
  7.9 7.3 %collective-permute-start.3 = (bf16[2,384,128]{2,1,0:T(8,128)(2,1)S(1)}, bf16[2,384,128]{2,1,0:T(8,128)(2,1)S(1)}, u32[]{:S(2)}, u32[]{:S(2)}) collective-permute-start(bf16[2,384,128]{2,1,0:T(8,128)(2,1)S(1)} %pad_maximum_fusion.refs_0_), channel_id=1, source_target_pairs={{0,14},{2,0},{4,2},{6,4},{8,6},{10,8},{12,10},{14,12},{1,15},{3,1}... | collective-permute-start | bytes 589832 | tf_op jit(solution)/shard_map/ppermute | solution.py:17
  15.2 7.7 %collective-permute-start.2 = (bf16[2,384,128]{2,1,0:T(8,128)(2,1)S(1)}, bf16[2,384,128]{2,1,0:T(8,128)(2,1)S(1)}, u32[]{:S(2)}, u32[]{:S(2)}) collective-permute-start(bf16[2,384,128]{2,1,0:T(8,128)(2,1)S(1)} %collective-permute-done.1.refs_7_), channel_id=1, source_target_pairs={{0,2},{2,4},{4,6},{6,8},{8,10},{10,12},{12,14},{14,0},{1,3},{3,5},... | collective-permute-start | bytes 589832 | tf_op jit(solution)/shard_map/ppermute | solution.py:17
  15.2 7.7 %collective-permute-start.4 = (bf16[2,384,128]{2,1,0:T(8,128)(2,1)S(1)}, bf16[2,384,128]{2,1,0:T(8,128)(2,1)S(1)}, u32[]{:S(2)}, u32[]{:S(2)}) collective-permute-start(bf16[2,384,128]{2,1,0:T(8,128)(2,1)S(1)} %collective-permute-done.3.refs_1_), channel_id=1, source_target_pairs={{0,14},{2,0},{4,2},{6,4},{8,6},{10,8},{12,10},{14,12},{1,15},{3,1}... | collective-permute-start | bytes 589832 | tf_op jit(solution)/shard_map/ppermute | solution.py:17
  17.9 1.4 copy-start
  19.4 1.4 copy-start.1
  22.8 16.4 %copy-start.25 = (s32[4,128,2]{1,2,0:T(2,128)S(1)}, s32[4,128,2]{1,2,0:T(2,128)}, u32[]{:S(2)}) copy-start(s32[4,128,2]{1,2,0:T(2,128)} %param.6) | copy-start | bytes 12292
  22.9 16.4 %copy-start.26 = (f32[4,128,2]{1,2,0:T(2,128)S(1)}, f32[4,128,2]{1,2,0:T(2,128)}, u32[]{:S(2)}) copy-start(f32[4,128,2]{1,2,0:T(2,128)} %param.7) | copy-start | bytes 12292
  22.9 5.8 %collective-permute-start.5 = (bf16[2,384,128]{2,1,0:T(8,128)(2,1)S(1)}, bf16[2,384,128]{2,1,0:T(8,128)(2,1)S(1)}, u32[]{:S(2)}, u32[]{:S(2)}) collective-permute-start(bf16[2,384,128]{2,1,0:T(8,128)(2,1)S(1)} %collective-permute-done.2.refs_6_), channel_id=1, source_target_pairs={{0,2},{2,4},{4,6},{6,8},{8,10},{10,12},{12,14},{14,0},{1,3},{3,5},... | collective-permute-start | bytes 589832 | tf_op jit(solution)/shard_map/ppermute | solution.py:17
  23.0 5.8 %collective-permute-start.7 = (bf16[2,384,128]{2,1,0:T(8,128)(2,1)S(1)}, bf16[2,384,128]{2,1,0:T(8,128)(2,1)S(1)}, u32[]{:S(2)}, u32[]{:S(2)}) collective-permute-start(bf16[2,384,128]{2,1,0:T(8,128)(2,1)S(1)} %collective-permute-done.4.refs_2_), channel_id=1, source_target_pairs={{0,14},{2,0},{4,2},{6,4},{8,6},{10,8},{12,10},{14,12},{1,15},{3,1}... | collective-permute-start | bytes 589832 | tf_op jit(solution)/shard_map/ppermute | solution.py:17
  28.7 4.8 %collective-permute-start.6 = (bf16[1,384,128]{2,1,0:T(8,128)(2,1)S(1)}, bf16[1,384,128]{2,1,0:T(8,128)(2,1)S(1)}, u32[]{:S(2)}, u32[]{:S(2)}) collective-permute-start(bf16[1,384,128]{2,1,0:T(8,128)(2,1)S(1)} %slice.24), channel_id=1, source_target_pairs={{0,2},{2,4},{4,6},{6,8},{8,10},{10,12},{12,14},{14,0},{1,3},{3,5},... | collective-permute-start | bytes 294920 | tf_op jit(solution)/shard_map/ppermute | solution.py:17
  28.8 4.6 %collective-permute-start.8 = (bf16[1,384,128]{2,1,0:T(8,128)(2,1)S(1)}, bf16[1,384,128]{2,1,0:T(8,128)(2,1)S(1)}, u32[]{:S(2)}, u32[]{:S(2)}) collective-permute-start(bf16[1,384,128]{2,1,0:T(8,128)(2,1)S(1)} %slice.25), channel_id=1, source_target_pairs={{0,14},{2,0},{4,2},{6,4},{8,6},{10,8},{12,10},{14,12},{1,15},{3,1}... | collective-permute-start | bytes 294920 | tf_op jit(solution)/shard_map/ppermute | solution.py:17
  33.5 30.0 %all-to-all-start = ((bf16[8,192,256]{2,1,0:T(8,128)(2,1)}), bf16[8,192,256]{2,1,0:T(8,128)(2,1)S(1)}, u32[]{:S(2)}, u32[]{:S(2)}) async-start(bf16[8,192,256]{2,1,0:T(8,128)(2,1)} %get-tuple-element.36), calls=%async_computation | async-start | bytes 1572864 | tf_op jit(solution)/shard_map/all_to_all | solution.py:142
  43.3 19.2 %collective-permute-start.9 = (bf16[160,3200]{1,0:T(8,128)(2,1)S(1)}, bf16[160,3200]{1,0:T(8,128)(2,1)S(1)}, u32[]{:S(2)}, u32[]{:S(2)}) collective-permute-start(bf16[160,3200]{1,0:T(8,128)(2,1)S(1)} %get-tuple-element.41), channel_id=1, source_target_pairs={{0,32},{32,64},{64,96},{96,0},{1,33},{33,65},{65,97},{97,1},{2,34}... | collective-permute-start | bytes 3072008 | tf_op jit(solution)/shard_map/ppermute | solution.py:17
  44.6 18.9 %collective-permute-start.10 = (bf16[160,3200]{1,0:T(8,128)(2,1)S(1)}, bf16[160,3200]{1,0:T(8,128)(2,1)}, u32[]{:S(2)}, u32[]{:S(2)}) collective-permute-start(bf16[160,3200]{1,0:T(8,128)(2,1)S(1)} %get-tuple-element.43), channel_id=1, source_target_pairs={{0,96},{32,0},{64,32},{96,64},{1,97},{33,1},{65,33},{97,65},{2,98}... | collective-permute-start | bytes 3072008 | tf_op jit(solution)/shard_map/ppermute | solution.py:17
  63.5 30.2 %collective-permute-start.12 = (bf16[8,192,256]{2,1,0:T(8,128)(2,1)S(1)}, bf16[8,192,256]{2,1,0:T(8,128)(2,1)S(1)}, u32[]{:S(2)}, u32[]{:S(2)}) collective-permute-start(bf16[8,192,256]{2,1,0:T(8,128)(2,1)S(1)} %all-to-all-done.refs_8_), channel_id=1, source_target_pairs={{0,1},{1,128},{128,129},{129,0},{2,3},{3,130},{130,131},{131,2},{4... | collective-permute-start | bytes 2359304 | tf_op jit(solution)/shard_map/ppermute | solution.py:17
  64.7 29.6 %collective-permute-start.11 = (bf16[160,3200]{1,0:T(8,128)(2,1)}, bf16[160,3200]{1,0:T(8,128)(2,1)}, u32[]{:S(2)}, u32[]{:S(2)}) collective-permute-start(bf16[160,3200]{1,0:T(8,128)(2,1)} %get-tuple-element.47), channel_id=1, source_target_pairs={{0,64},{32,96},{64,0},{96,32},{1,65},{33,97},{65,1},{97,33},{2,66}... | collective-permute-start | bytes 3072008 | tf_op jit(solution)/shard_map/ppermute | solution.py:17
  66.4 40.4 %all-to-all-start.1 = ((bf16[8,192,256]{2,1,0:T(8,128)(2,1)}), bf16[8,192,256]{2,1,0:T(8,128)(2,1)S(1)}, u32[]{:S(2)}, u32[]{:S(2)}) async-start(bf16[8,192,256]{2,1,0:T(8,128)(2,1)} %get-tuple-element.46), calls=%async_computation.1 | async-start | bytes 1572864 | tf_op jit(solution)/shard_map/all_to_all | solution.py:142
  72.7 21.4 %collective-permute-start.14 = (bf16[8,192,256]{2,1,0:T(8,128)(2,1)S(1)}, bf16[8,192,256]{2,1,0:T(8,128)(2,1)S(1)}, u32[]{:S(2)}, u32[]{:S(2)}) collective-permute-start(bf16[8,192,256]{2,1,0:T(8,128)(2,1)S(1)} %all-to-all-done.refs_8_), channel_id=1, source_target_pairs={{0,129},{1,0},{128,1},{129,128},{2,131},{3,2},{130,3},{131,130},{4... | collective-permute-start | bytes 2359304 | tf_op jit(solution)/shard_map/ppermute | solution.py:17
  74.2 22.9 %collective-permute-start.16 = (bf16[160,3200]{1,0:T(8,128)(2,1)}, bf16[160,3200]{1,0:T(8,128)(2,1)S(1)}, u32[]{:S(2)}, u32[]{:S(2)}) collective-permute-start(bf16[160,3200]{1,0:T(8,128)(2,1)} %copy-done.6), channel_id=1, source_target_pairs={{0,16},{16,0},{1,17},{17,1},{2,18},{18,2},{3,19},{19,3},{4,20},{20... | collective-permute-start | bytes 3072008 | tf_op jit(solution)/shard_map/ppermute | solution.py:17
  93.6 4.4 %collective-permute-start.17 = (bf16[160,3200]{1,0:T(8,128)(2,1)}, bf16[160,3200]{1,0:T(8,128)(2,1)S(1)}, u32[]{:S(2)}, u32[]{:S(2)}) collective-permute-start(bf16[160,3200]{1,0:T(8,128)(2,1)} %copy-done.9), channel_id=1, source_target_pairs={{0,16},{16,0},{1,17},{17,1},{2,18},{18,2},{3,19},{19,3},{4,20},{20... | collective-permute-start | bytes 3072008 | tf_op jit(solution)/shard_map/ppermute | solution.py:17
  93.6 5.4 %collective-permute-start.18 = (bf16[160,3200]{1,0:T(8,128)(2,1)}, bf16[160,3200]{1,0:T(8,128)(2,1)S(1)}, u32[]{:S(2)}, u32[]{:S(2)}) collective-permute-start(bf16[160,3200]{1,0:T(8,128)(2,1)} %collective-permute-done.10.refs_3_), channel_id=1, source_target_pairs={{0,16},{16,0},{1,17},{17,1},{2,18},{18,2},{3,19},{19,3},{4,20},{20... | collective-permute-start | bytes 3072008 | tf_op jit(solution)/shard_map/ppermute | solution.py:17
  94.2 8.2 %collective-permute-start.13 = (bf16[4,192,256]{2,1,0:T(8,128)(2,1)S(1)}, bf16[4,192,256]{2,1,0:T(8,128)(2,1)S(1)}, u32[]{:S(2)}, u32[]{:S(2)}) collective-permute-start(bf16[4,192,256]{2,1,0:T(8,128)(2,1)S(1)} %slice.26), channel_id=1, source_target_pairs={{0,1},{1,128},{128,129},{129,0},{2,3},{3,130},{130,131},{131,2},{4... | collective-permute-start | bytes 1179656 | tf_op jit(solution)/shard_map/ppermute | solution.py:17
  94.3 11.7 %collective-permute-start.15 = (bf16[4,192,256]{2,1,0:T(8,128)(2,1)S(1)}, bf16[4,192,256]{2,1,0:T(8,128)(2,1)S(1)}, u32[]{:S(2)}, u32[]{:S(2)}) collective-permute-start(bf16[4,192,256]{2,1,0:T(8,128)(2,1)S(1)} %slice.27), channel_id=1, source_target_pairs={{0,129},{1,0},{128,1},{129,128},{2,131},{3,2},{130,3},{131,130},{4... | collective-permute-start | bytes 1179656 | tf_op jit(solution)/shard_map/ppermute | solution.py:17
  106.8 36.3 %copy-start.7 = (bf16[160,3200]{1,0:T(8,128)(2,1)S(1)}, bf16[160,3200]{1,0:T(8,128)(2,1)}, u32[]{:S(2)}) copy-start(bf16[160,3200]{1,0:T(8,128)(2,1)} %copy-done.6) | copy-start | bytes 3072004
  106.8 36.3 %copy-start.24 = (bf16[4,192,256]{2,1,0:T(8,128)(2,1)S(1)}, bf16[4,192,256]{2,1,0:T(8,128)(2,1)}, u32[]{:S(2)}) copy-start(bf16[4,192,256]{2,1,0:T(8,128)(2,1)} %copy-done.23) | copy-start | bytes 1179652
  106.8 36.3 %collective-permute-start.19 = (bf16[160,3200]{1,0:T(8,128)(2,1)}, bf16[160,3200]{1,0:T(8,128)(2,1)S(1)}, u32[]{:S(2)}, u32[]{:S(2)}) collective-permute-start(bf16[160,3200]{1,0:T(8,128)(2,1)} %collective-permute-done.11.refs_2_), channel_id=1, source_target_pairs={{0,16},{16,0},{1,17},{17,1},{2,18},{18,2},{3,19},{19,3},{4,20},{20... | collective-permute-start | bytes 3072008 | tf_op jit(solution)/shard_map/ppermute | solution.py:17
  118.3 20.3 %collective-permute-start.20 = (bf16[8,192,256]{2,1,0:T(8,128)(2,1)S(1)}, bf16[8,192,256]{2,1,0:T(8,128)(2,1)S(1)}, u32[]{:S(2)}, u32[]{:S(2)}) collective-permute-start(bf16[8,192,256]{2,1,0:T(8,128)(2,1)S(1)} %all-to-all-done.1.refs_8_), channel_id=1, source_target_pairs={{0,1},{1,128},{128,129},{129,0},{2,3},{3,130},{130,131},{131,2},{4... | collective-permute-start | bytes 2359304 | tf_op jit(solution)/shard_map/ppermute | solution.py:17
  119.2 20.2 %collective-permute-start.21 = (bf16[8,192,256]{2,1,0:T(8,128)(2,1)S(1)}, bf16[8,192,256]{2,1,0:T(8,128)(2,1)S(1)}, u32[]{:S(2)}, u32[]{:S(2)}) collective-permute-start(bf16[8,192,256]{2,1,0:T(8,128)(2,1)S(1)} %all-to-all-done.1.refs_8_), channel_id=1, source_target_pairs={{0,129},{1,0},{128,1},{129,128},{2,131},{3,2},{130,3},{131,130},{4... | collective-permute-start | bytes 2359304 | tf_op jit(solution)/shard_map/ppermute | solution.py:17
  138.6 1.1 copy-start.2
  139.4 20.8 %collective-permute-start.22 = (bf16[4,192,256]{2,1,0:T(8,128)(2,1)}, bf16[4,192,256]{2,1,0:T(8,128)(2,1)}, u32[]{:S(2)}, u32[]{:S(2)}) collective-permute-start(bf16[4,192,256]{2,1,0:T(8,128)(2,1)} %slice.28), channel_id=1, source_target_pairs={{0,1},{1,128},{128,129},{129,0},{2,3},{3,130},{130,131},{131,2},{4... | collective-permute-start | bytes 1179656 | tf_op jit(solution)/shard_map/ppermute | solution.py:17
  139.6 1.0 copy-start.4
  140.7 19.5 %collective-permute-start.23 = (bf16[4,192,256]{2,1,0:T(8,128)(2,1)}, bf16[4,192,256]{2,1,0:T(8,128)(2,1)}, u32[]{:S(2)}, u32[]{:S(2)}) collective-permute-start(bf16[4,192,256]{2,1,0:T(8,128)(2,1)} %slice.29), channel_id=1, source_target_pairs={{0,129},{1,0},{128,1},{129,128},{2,131},{3,2},{130,3},{131,130},{4... | collective-permute-start | bytes 1179656 | tf_op jit(solution)/shard_map/ppermute | solution.py:17
  143.1 1.2 copy-start.10
  144.4 1.2 copy-start.13
  145.6 1.2 copy-start.16
  146.8 1.2 copy-start.19
  148.0 7.3 %copy-start.21 = (bf16[160,3200]{1,0:T(8,128)(2,1)}, bf16[160,3200]{1,0:T(8,128)(2,1)S(1)}, u32[]{:S(2)}) copy-start(bf16[160,3200]{1,0:T(8,128)(2,1)S(1)} %collective-permute-done.19.refs_6_) | copy-start | bytes 3072004
  155.3 20.7 %all-to-all-start.2 = ((bf16[16,160,128]{2,1,0:T(8,128)(2,1)}), bf16[16,160,128]{2,1,0:T(8,128)(2,1)S(1)}, u32[]{:S(2)}, u32[]{:S(2)}) async-start(bf16[16,160,128]{2,1,0:T(8,128)(2,1)} %bitcast.11), calls=%async_computation.2 | async-start | bytes 1310720 | tf_op jit(solution)/shard_map/all_to_all | solution.py:192
  160.2 1.1 copy-start.3
  161.3 1.1 copy-start.5
  162.4 1.2 copy-start.8
  163.6 1.2 copy-start.11
  164.9 1.2 copy-start.14
  166.1 1.2 copy-start.17
  167.3 1.2 copy-start.20
  168.5 1.2 copy-start.22
  (6 other events, 5.6 us)

commit v6 on v5

--- a/solution.py
+++ b/solution.py
@@ -8,7 +8,7 @@
 MOST = 80
 X = ("dp", "xl")
 BF, F32 = jnp.bfloat16, jnp.float32
-HBM = pl.BlockSpec(memory_space=pltpu.HBM)
+ANY = pl.BlockSpec(memory_space=pl.ANY)
 VM = pl.BlockSpec(memory_space=pltpu.VMEM)
 SM = pl.BlockSpec(memory_space=pltpu.SMEM)
 
@@ -77,20 +77,28 @@
 
 
 def expert_kernel(pos, *refs):
-    xs, ws, out, wbuf = refs[:8], refs[8:13], refs[13], refs[14]
+    xs, ws, (out, xbuf, wbuf, xsem, wsem) = refs[:8], refs[8:13], refs[13:]
     y, c, xl, dp, z = (pos[i] for i in range(5))
-    rows = xs[0].shape[0]
     width = 16 * ws[0].shape[1]
-    for src, off, low in ((ws[0], 0, 0), (ws[1], 3, 0), (ws[2], 1, 0), (ws[3], 2, 0), (ws[4], 2, 4)):
+    copies = []
+    for i, (src, off, low) in enumerate(((ws[0], 0, 0), (ws[1], 3, 0), (ws[2], 1, 0), (ws[3], 2, 0), (ws[4], 2, 4))):
         j = lax.rem(dp * 2 + xl + off, 4)
         for k in range(src.shape[0]):
-            wbuf[lax.div(j, 2), lax.rem(low + k + 8 - z, 8), lax.rem(j, 2)] = src[k]
+            place = wbuf.at[lax.div(j, 2), lax.rem(low + k + 8 - z, 8), lax.rem(j, 2)]
+            copies.append(pltpu.make_async_copy(src.at[k], place, wsem.at[i, k]))
+    for cp in copies:
+        cp.start()
+    rows = [pltpu.make_async_copy(xs[g], xbuf.at[g], xsem.at[g]) for g in range(8)]
+    for cp in rows:
+        cp.start()
+    for cp in copies:
+        cp.wait()
     for g in range(8):
         d, cc = g % 4, g // 4
-        data = xs[g][:, :width]
-        rw = jnp.sum(xs[g][:, width:].astype(F32), axis=1, keepdims=True)
-        gate = jnp.dot(data, wbuf[0].reshape(width, 256), preferred_element_type=F32)
-        up = jnp.dot(data, wbuf[1].reshape(width, 256), preferred_element_type=F32)
+        rows[g].wait()
+        rw = jnp.sum(xbuf[g, :, width:].astype(F32), axis=1, keepdims=True)
+        gate = jnp.dot(xbuf[g, :, :width], wbuf[0].reshape(width, 256), preferred_element_type=F32)
+        up = jnp.dot(xbuf[g, :, :width], wbuf[1].reshape(width, 256), preferred_element_type=F32)
         act = (rw * (gate / (1.0 + jnp.exp(-gate)) * up)).astype(BF)
         for t in range(2):
             out[lax.rem(y + 4 - d, 4), c + cc - 2 * c * cc, t] = act[:, t * 128 : (t + 1) * 128]
@@ -131,10 +139,10 @@
     blocks = pl.pallas_call(
         columns_kernel,
         out_shape=[jax.ShapeDtypeStruct((8, rows, 2 * wide), BF)] * 2,
-        in_specs=[SM, HBM, HBM],
+        in_specs=[SM, ANY, ANY],
         out_specs=[VM] * 2,
         scratch_shapes=[pltpu.VMEM((rows, units), BF), pltpu.SemaphoreType.DMA(())],
-        compiler_params=pltpu.CompilerParams(vmem_limit_bytes=16 << 20),
+        compiler_params=pltpu.CompilerParams(vmem_limit_bytes=58 << 20),
         name="columns",
     )(pos, gate_train, up_train)
 
@@ -164,26 +172,30 @@
         name="dispatch",
     )(pos, meta, *feats)
     held = [sent[0], ring(sent[1], "y", 4, 1), None, ring(sent[3], "y", 4, 3)]
-    own_a, part_b, held[0], held[1], far_rows, held[3] = barrier((own_a, blocks[1], held[0], held[1], sent[2], held[3]))
+    ws_a = spread(own_a)
+    part_b, ws_a[0], far_rows, held[1], held[3] = barrier((blocks[1], ws_a[0], sent[2], held[1], held[3]))
     own_b = exchange(part_b)
     held[2] = ring(far_rows, "y", 4, 2)
-    ws_a = spread(own_a)
-    other = [ring(held[d], "c", 2, 1) if d != 2 else None for d in range(4)]
-    own_b, held[2], ws_a[3], ws_a[4], other[0], other[1], other[3] = barrier(
-        (own_b, held[2], ws_a[3], ws_a[4], other[0], other[1], other[3])
+    own_b, held[2], ws_a[3], ws_a[4], held[0], held[1], held[3] = barrier(
+        (own_b, held[2], ws_a[3], ws_a[4], held[0], held[1], held[3])
     )
     ws_b = spread(own_b)
-    other[2] = ring(held[2], "c", 2, 1)
+    other = [ring(h, "c", 2, 1) for h in held]
     pieces = [ws_a, ws_b]
     backs = []
     for ws in pieces:
         act = pl.pallas_call(
             expert_kernel,
             out_shape=jax.ShapeDtypeStruct((4, 2, 2, 2 * MOST, wide), BF),
-            in_specs=[SM] + [VM] * 13,
+            in_specs=[SM] + [ANY] * 13,
             out_specs=VM,
-            scratch_shapes=[pltpu.VMEM((2, 8, 2, rows, 2 * wide), BF)],
-            compiler_params=pltpu.CompilerParams(vmem_limit_bytes=8 << 20),
+            scratch_shapes=[
+                pltpu.VMEM((8, 2 * MOST, 16 * width + 128), BF),
+                pltpu.VMEM((2, 8, 2, rows, 2 * wide), BF),
+                pltpu.SemaphoreType.DMA((8,)),
+                pltpu.SemaphoreType.DMA((5, 8)),
+            ],
+            compiler_params=pltpu.CompilerParams(vmem_limit_bytes=58 << 20),
             cost_estimate=pl.CostEstimate(
                 flops=16 * MOST * 16 * width * 8 * wide, bytes_accessed=12 << 20, transcendentals=16 * MOST * 2 * wide
             ),

time: 198 us -> 189 us (0.955)
  local copies, waits for them, and re-layouts: 27.6 us -> 7.35 us
  Pallas kernels: 20.1 us -> 29.7 us
  waiting for transfers between devices: 50.5 us -> 56.5 us
  starting transfers between devices: 79.6 us -> 76 us
    unnamed x54 -> x32, local copies, waits for them, and re-layouts: 23.3 us -> 4.12 us
    ppermute x24, starting transfers between devices: 62.7 us -> 43.8 us  [ring(): return lax.ppermute(x, axis, [(i, (i + step) % size) for i in range(size)])]
    all_to_all x1, starting transfers between devices: 4.81 us -> 20.1 us  [body(): lax.all_to_all(act.reshape(16, 2 * MOST, wide), ('y', 'c', 'xl'), split_a...]
    pallas_call x2, Pallas kernels: 13.6 us -> 22.7 us  [body(): pl.pallas_call(expert_kernel, out_shape=jax.ShapeDtypeStruct((4, 2, 2, 2...]
    ppermute x24, waiting for transfers between devices: 50.5 us -> 56.5 us  [ring(): return lax.ppermute(x, axis, [(i, (i + step) % size) for i in range(size)])]
  transfers between devices with their start and end apart: 27 -> 27, of which waited for: 8 -> 10; matrix products, arithmetic and copies ran while one was open for 1% -> 0% of each run, Pallas kernels for 10% -> 15%
where the time goes in v6:
time: 189 us
  starting transfers between devices  76 us (40%)
  waiting for transfers between devices  56.5 us (30%)
  Pallas kernels  29.7 us (16%)
  blocking collectives  17.6 us (9%)
  local copies, waits for them, and re-layouts  7.35 us (4%)
    ppermute x24, waiting for transfers between devices, ring(): return lax.ppermute(x, axis, [(i, (i + step) % size) for i in range(size)])  56.5 us
    ppermute x24, starting transfers between devices, ring(): return lax.ppermute(x, axis, [(i, (i + step) % size) for i in range(size)])  43.8 us
    pallas_call x2, Pallas kernels, body(): pl.pallas_call(expert_kernel, out_shape=jax.ShapeDtypeStruct((4, 2, 2, 2...  22.7 us
    all_to_all x1, starting transfers between devices, body(): lax.all_to_all(act.reshape(16, 2 * MOST, wide), ('y', 'c', 'xl'), split_a...  20.1 us
    all_to_all x1, blocking collectives, body(): lax.all_to_all(act.reshape(16, 2 * MOST, wide), ('y', 'c', 'xl'), split_a...  17.6 us
    all_to_all x2, starting transfers between devices, exchange(): return lax.all_to_all(x, 'z', split_axis=0, concat_axis=0, tiled=True)  12.2 us
    unnamed x32, local copies, waits for them, and re-layouts  4.12 us
  transfers between devices with their start and end apart: 27, of which 10 were waited for; matrix products, arithmetic and copies ran while one was open for 0% of the time, Pallas kernels for 15%

profile of v6, /device:TPU:1, one launch (start us, length us, event | category | flops | bytes accessed | tf_op | source)
XLA Modules:
  0.0 188.5 jit_solution(14318764794966279935)
XLA Ops:
  0.0 0.9 dynamic-slice_bitcast_fusion
  0.9 2.0 %collective-permute-start = (bf16[2,192,128]{2,1,0:T(8,128)(2,1)S(1)}, bf16[2,192,128]{2,1,0:T(8,128)(2,1)S(1)}, u32[]{:S(2)}, u32[]{:S(2)}) collective-permute-start(bf16[2,192,128]{2,1,0:T(8,128)(2,1)S(1)} %dynamic-slice_bitcast_fusion), channel_id=1, source_target_pairs={{0,1},{1,0},{2,3},{3,2},{4,5},{5,4},{6,7},{7,6},{8,9},{9,8},{10,11... | collective-permute-start | bytes 294920 | tf_op jit(solution)/shard_map/ppermute | solution.py:17
  2.9 2.0 %collective-permute-done = bf16[2,192,128]{2,1,0:T(8,128)(2,1)S(1)} collective-permute-done((bf16[2,192,128]{2,1,0:T(8,128)(2,1)S(1)}, bf16[2,192,128]{2,1,0:T(8,128)(2,1)S(1)}, u32[]{:S(2)}, u32[]{:S(2)}) %collective-permute-start) | collective-permute-done | bytes 98336 | tf_op jit(solution)/shard_map/ppermute | solution.py:17
  4.9 0.9 bitcast_select_fusion.1
  5.9 2.0 %collective-permute-start.1 = (bf16[2,384,128]{2,1,0:T(8,128)(2,1)S(1)}, bf16[2,384,128]{2,1,0:T(8,128)(2,1)S(1)}, u32[]{:S(2)}, u32[]{:S(2)}) collective-permute-start(bf16[2,384,128]{2,1,0:T(8,128)(2,1)S(1)} %pad_maximum_fusion.refs_0_), channel_id=1, source_target_pairs={{0,2},{2,4},{4,6},{6,8},{8,10},{10,12},{12,14},{14,0},{1,3},{3,5},... | collective-permute-start | bytes 589832 | tf_op jit(solution)/shard_map/ppermute | solution.py:17
  7.8 4.0 %collective-permute-start.3 = (bf16[2,384,128]{2,1,0:T(8,128)(2,1)S(1)}, bf16[2,384,128]{2,1,0:T(8,128)(2,1)S(1)}, u32[]{:S(2)}, u32[]{:S(2)}) collective-permute-start(bf16[2,384,128]{2,1,0:T(8,128)(2,1)S(1)} %pad_maximum_fusion.refs_0_), channel_id=1, source_target_pairs={{0,14},{2,0},{4,2},{6,4},{8,6},{10,8},{12,10},{14,12},{1,15},{3,1}... | collective-permute-start | bytes 589832 | tf_op jit(solution)/shard_map/ppermute | solution.py:17
  11.9 3.3 %collective-permute-done.1.refs_7_ = bf16[2,384,128]{2,1,0:T(8,128)(2,1)S(1)} collective-permute-done((bf16[2,384,128]{2,1,0:T(8,128)(2,1)S(1)}, bf16[2,384,128]{2,1,0:T(8,128)(2,1)S(1)}, u32[]{:S(2)}, u32[]{:S(2)}) %collective-permute-start.1) | collective-permute-done | bytes 196640 | tf_op jit(solution)/shard_map/ppermute | solution.py:17
  15.2 2.7 %collective-permute-start.4 = (bf16[2,384,128]{2,1,0:T(8,128)(2,1)S(1)}, bf16[2,384,128]{2,1,0:T(8,128)(2,1)S(1)}, u32[]{:S(2)}, u32[]{:S(2)}) collective-permute-start(bf16[2,384,128]{2,1,0:T(8,128)(2,1)S(1)} %collective-permute-done.3.refs_1_), channel_id=1, source_target_pairs={{0,14},{2,0},{4,2},{6,4},{8,6},{10,8},{12,10},{14,12},{1,15},{3,1}... | collective-permute-start | bytes 589832 | tf_op jit(solution)/shard_map/ppermute | solution.py:17
  17.9 0.6 stack.23.pos
  18.5 3.6 %columns.1 = (bf16[8,192,256]{2,1,0:T(8,128)(2,1)}, bf16[8,192,256]{2,1,0:T(8,128)(2,1)}) custom-call(s32[5]{0:T(128)} %stack.23.pos, bf16[1,192,4096]{2,1,0:T(8,128)(2,1)} %gate.1, bf16[1,192,4096]{2,1,0:T(8,128)(2,1)} %up.1), custom_call_target="tpu_custom_call" | custom-call | tf_op jit(solution)/shard_map/columns/pallas_call | solution.py:139
  22.1 0.1 collective-permute-start.5
  22.2 2.7 %collective-permute-start.7 = (bf16[2,384,128]{2,1,0:T(8,128)(2,1)S(1)}, bf16[2,384,128]{2,1,0:T(8,128)(2,1)S(1)}, u32[]{:S(2)}, u32[]{:S(2)}) collective-permute-start(bf16[2,384,128]{2,1,0:T(8,128)(2,1)S(1)} %collective-permute-done.4.refs_2_), channel_id=1, source_target_pairs={{0,14},{2,0},{4,2},{6,4},{8,6},{10,8},{12,10},{14,12},{1,15},{3,1}... | collective-permute-start | bytes 589832 | tf_op jit(solution)/shard_map/ppermute | solution.py:17
  24.9 3.1 %collective-permute-done.5.refs_5_ = bf16[2,384,128]{2,1,0:T(8,128)(2,1)S(1)} collective-permute-done((bf16[2,384,128]{2,1,0:T(8,128)(2,1)S(1)}, bf16[2,384,128]{2,1,0:T(8,128)(2,1)S(1)}, u32[]{:S(2)}, u32[]{:S(2)}) %collective-permute-start.5) | collective-permute-done | bytes 196640 | tf_op jit(solution)/shard_map/ppermute | solution.py:17
  28.1 2.7 %collective-permute-start.8 = (bf16[1,384,128]{2,1,0:T(8,128)(2,1)S(1)}, bf16[1,384,128]{2,1,0:T(8,128)(2,1)S(1)}, u32[]{:S(2)}, u32[]{:S(2)}) collective-permute-start(bf16[1,384,128]{2,1,0:T(8,128)(2,1)S(1)} %slice.25), channel_id=1, source_target_pairs={{0,14},{2,0},{4,2},{6,4},{8,6},{10,8},{12,10},{14,12},{1,15},{3,1}... | collective-permute-start | bytes 294920 | tf_op jit(solution)/shard_map/ppermute | solution.py:17
  30.8 1.9 %collective-permute-done.6 = bf16[1,384,128]{2,1,0:T(8,128)(2,1)S(1)} collective-permute-done((bf16[1,384,128]{2,1,0:T(8,128)(2,1)S(1)}, bf16[1,384,128]{2,1,0:T(8,128)(2,1)S(1)}, u32[]{:S(2)}, u32[]{:S(2)}) %collective-permute-start.6) | collective-permute-done | bytes 98336 | tf_op jit(solution)/shard_map/ppermute | solution.py:17
  32.7 5.8 %all-to-all-start = ((bf16[8,192,256]{2,1,0:T(8,128)(2,1)}), bf16[8,192,256]{2,1,0:T(8,128)(2,1)S(1)}, u32[]{:S(2)}, u32[]{:S(2)}) async-start(bf16[8,192,256]{2,1,0:T(8,128)(2,1)} %get-tuple-element.36), calls=%async_computation | async-start | bytes 1572864 | tf_op jit(solution)/shard_map/all_to_all | solution.py:150
  38.6 2.0 %dispatch.1 = (bf16[160,3200]{1,0:T(8,128)(2,1)S(1)}, bf16[160,3200]{1,0:T(8,128)(2,1)S(1)}, bf16[160,3200]{1,0:T(8,128)(2,1)S(1)}, bf16[160,3200]{1,0:T(8,128)(2,1)S(1)}) custom-call(s32[5]{0:T(128)S(1)} %copy-done, f32[4,4,128]{2,1,0:T(4,128)S(1)} %maximum_bitcast_fusion.meta, bf16[2,384,128]{2,1,0:T(8,128)(2,1)S(1)} %pad_maximum_fusion.refs_0_, ...), custom_call_target="tpu_custom_call" | custom-call | tf_op jit(solution)/shard_map/dispatch/pallas_call | solution.py:166
  40.7 1.0 copy-done.2
  41.6 1.3 collective-permute-start.9
  42.9 1.4 collective-permute-start.10
  44.4 16.6 %collective-permute-done.9.refs_1_ = bf16[160,3200]{1,0:T(8,128)(2,1)} collective-permute-done((bf16[160,3200]{1,0:T(8,128)(2,1)S(1)}, bf16[160,3200]{1,0:T(8,128)(2,1)}, u32[]{:S(2)}, u32[]{:S(2)}) %collective-permute-start.9) | collective-permute-done | bytes 1024032 | tf_op jit(solution)/shard_map/ppermute | solution.py:17
  61.0 6.4 %all-to-all-start.1 = ((bf16[8,192,256]{2,1,0:T(8,128)(2,1)}), bf16[8,192,256]{2,1,0:T(8,128)(2,1)}, u32[]{:S(2)}, u32[]{:S(2)}) async-start(bf16[8,192,256]{2,1,0:T(8,128)(2,1)} %get-tuple-element.42), calls=%async_computation.1 | async-start | bytes 1572864 | tf_op jit(solution)/shard_map/all_to_all | solution.py:150
  67.3 1.2 collective-permute-start.12
  68.5 1.5 collective-permute-start.14
  70.0 2.3 %collective-permute-start.11 = (bf16[160,3200]{1,0:T(8,128)(2,1)S(1)}, bf16[160,3200]{1,0:T(8,128)(2,1)S(1)}, u32[]{:S(2)}, u32[]{:S(2)}) collective-permute-start(bf16[160,3200]{1,0:T(8,128)(2,1)S(1)} %copy-done.3), channel_id=1, source_target_pairs={{0,64},{32,96},{64,0},{96,32},{1,65},{33,97},{65,1},{97,33},{2,66}... | collective-permute-start | bytes 3072008 | tf_op jit(solution)/shard_map/ppermute | solution.py:17
  72.3 7.6 %collective-permute-done.12.refs_9_ = bf16[8,192,256]{2,1,0:T(8,128)(2,1)S(1)} collective-permute-done((bf16[8,192,256]{2,1,0:T(8,128)(2,1)S(1)}, bf16[8,192,256]{2,1,0:T(8,128)(2,1)S(1)}, u32[]{:S(2)}, u32[]{:S(2)}) %collective-permute-start.12) | collective-permute-done | bytes 786464 | tf_op jit(solution)/shard_map/ppermute | solution.py:17
  79.9 0.2 collective-permute-start.13
  80.1 0.7 copy-done.5
  80.8 2.0 %collective-permute-start.15 = (bf16[4,192,256]{2,1,0:T(8,128)(2,1)S(1)}, bf16[4,192,256]{2,1,0:T(8,128)(2,1)}, u32[]{:S(2)}, u32[]{:S(2)}) collective-permute-start(bf16[4,192,256]{2,1,0:T(8,128)(2,1)S(1)} %slice.27), channel_id=1, source_target_pairs={{0,129},{1,0},{128,1},{129,128},{2,131},{3,2},{130,3},{131,130},{4... | collective-permute-start | bytes 1179656 | tf_op jit(solution)/shard_map/ppermute | solution.py:17
  82.8 4.6 %collective-permute-done.11.refs_2_ = bf16[160,3200]{1,0:T(8,128)(2,1)S(1)} collective-permute-done((bf16[160,3200]{1,0:T(8,128)(2,1)S(1)}, bf16[160,3200]{1,0:T(8,128)(2,1)S(1)}, u32[]{:S(2)}, u32[]{:S(2)}) %collective-permute-start.11) | collective-permute-done | bytes 1024032 | tf_op jit(solution)/shard_map/ppermute | solution.py:17
  87.4 4.9 %collective-permute-done.13.refs_11_ = bf16[4,192,256]{2,1,0:T(8,128)(2,1)S(1)} collective-permute-done((bf16[4,192,256]{2,1,0:T(8,128)(2,1)S(1)}, bf16[4,192,256]{2,1,0:T(8,128)(2,1)S(1)}, u32[]{:S(2)}, u32[]{:S(2)}) %collective-permute-start.13) | collective-permute-done | bytes 393248 | tf_op jit(solution)/shard_map/ppermute | solution.py:17
  92.3 0.7 copy-done.14
  93.1 13.6 %collective-permute-start.16 = (bf16[160,3200]{1,0:T(8,128)(2,1)S(1)}, bf16[160,3200]{1,0:T(8,128)(2,1)S(1)}, u32[]{:S(2)}, u32[]{:S(2)}) collective-permute-start(bf16[160,3200]{1,0:T(8,128)(2,1)S(1)} %get-tuple-element.47.refs_0_), channel_id=1, source_target_pairs={{0,16},{16,0},{1,17},{17,1},{2,18},{18,2},{3,19},{19,3},{4,20},{20... | collective-permute-start | bytes 3072008 | tf_op jit(solution)/shard_map/ppermute | solution.py:17
  106.7 0.1 collective-permute-start.17
  106.8 0.4 collective-permute-start.18
  107.2 0.1 collective-permute-start.19
  107.3 2.2 %collective-permute-done.20.refs_9_ = bf16[8,192,256]{2,1,0:T(8,128)(2,1)S(1)} collective-permute-done((bf16[8,192,256]{2,1,0:T(8,128)(2,1)}, bf16[8,192,256]{2,1,0:T(8,128)(2,1)S(1)}, u32[]{:S(2)}, u32[]{:S(2)}) %collective-permute-start.20) | collective-permute-done | bytes 786464 | tf_op jit(solution)/shard_map/ppermute | solution.py:17
  109.4 0.7 collective-permute-start.21
  110.2 10.3 %collective-permute-done.21.refs_10_ = bf16[8,192,256]{2,1,0:T(8,128)(2,1)S(1)} collective-permute-done((bf16[8,192,256]{2,1,0:T(8,128)(2,1)}, bf16[8,192,256]{2,1,0:T(8,128)(2,1)S(1)}, u32[]{:S(2)}, u32[]{:S(2)}) %collective-permute-start.21) | collective-permute-done | bytes 786464 | tf_op jit(solution)/shard_map/ppermute | solution.py:17
  120.5 2.8 %collective-permute-start.23 = (bf16[4,192,256]{2,1,0:T(8,128)(2,1)S(1)}, bf16[4,192,256]{2,1,0:T(8,128)(2,1)S(1)}, u32[]{:S(2)}, u32[]{:S(2)}) collective-permute-start(bf16[4,192,256]{2,1,0:T(8,128)(2,1)S(1)} %slice.29), channel_id=1, source_target_pairs={{0,129},{1,0},{128,1},{129,128},{2,131},{3,2},{130,3},{131,130},{4... | collective-permute-start | bytes 1179656 | tf_op jit(solution)/shard_map/ppermute | solution.py:17
  123.3 1.0 copy-done.13
  124.3 11.3 %expert.2 = bf16[4,2,2,160,128]{4,3,2,1,0:T(8,128)(2,1)} custom-call(s32[5]{0:T(128)} %stack.23.pos, bf16[160,3200]{1,0:T(8,128)(2,1)} %copy-done.1, bf16[160,3200]{1,0:T(8,128)(2,1)} %collective-permute-done.9.refs_1_, bf16[160,3200]{1,0:T(8,128)(2,1)} %copy-done.11, bf16[160,3200]{1,0:T(8,128)(2,1)} %collective-permute-done.10.refs_3_, ...), custom_call_target="tpu_custom_call" | custom-call | flops 4026531840 | bytes 12582912 | tf_op jit(solution)/shard_map/expert/pallas_call | solution.py:187
  135.6 20.1 %all-to-all-start.2 = ((bf16[16,160,128]{2,1,0:T(8,128)(2,1)}), bf16[16,160,128]{2,1,0:T(8,128)(2,1)S(1)}, u32[]{:S(2)}, u32[]{:S(2)}) async-start(bf16[16,160,128]{2,1,0:T(8,128)(2,1)} %bitcast.21), calls=%async_computation.2 | async-start | bytes 1310720 | tf_op jit(solution)/shard_map/all_to_all | solution.py:204
  155.8 0.7 copy-done.15
  156.5 11.3 %expert.3 = bf16[4,2,2,160,128]{4,3,2,1,0:T(8,128)(2,1)} custom-call(s32[5]{0:T(128)} %stack.23.pos, bf16[160,3200]{1,0:T(8,128)(2,1)} %copy-done.1, bf16[160,3200]{1,0:T(8,128)(2,1)} %collective-permute-done.9.refs_1_, bf16[160,3200]{1,0:T(8,128)(2,1)} %copy-done.11, bf16[160,3200]{1,0:T(8,128)(2,1)} %collective-permute-done.10.refs_3_, ...), custom_call_target="tpu_custom_call" | custom-call | flops 4026531840 | bytes 12582912 | tf_op jit(solution)/shard_map/expert/pallas_call | solution.py:187
  167.9 17.6 %all_to_all.20 = bf16[16,160,128]{2,1,0:T(8,128)(2,1)S(1)} all-to-all(bf16[16,160,128]{2,1,0:T(8,128)(2,1)} %bitcast.22), channel_id=1, replica_groups=mesh['dp'=2,'y'=4,'c'=2,'z'=8,'xl'=2] {'y','c','xl'}, dimensions={0} | all-to-all | bytes 1310720 | tf_op jit(solution)/shard_map/all_to_all | solution.py:204
  185.5 1.4 combine.1
  187.0 1.6 reshape.23
  (58 shorter events, 0.4 us)
Async XLA Ops:
  0.9 4.0 %collective-permute-start = (bf16[2,192,128]{2,1,0:T(8,128)(2,1)S(1)}, bf16[2,192,128]{2,1,0:T(8,128)(2,1)S(1)}, u32[]{:S(2)}, u32[]{:S(2)}) collective-permute-start(bf16[2,192,128]{2,1,0:T(8,128)(2,1)S(1)} %dynamic-slice_bitcast_fusion), channel_id=1, source_target_pairs={{0,1},{1,0},{2,3},{3,2},{4,5},{5,4},{6,7},{7,6},{8,9},{9,8},{10,11... | collective-permute-start | bytes 294920 | tf_op jit(solution)/shard_map/ppermute | solution.py:17
  5.9 9.3 %collective-permute-start.1 = (bf16[2,384,128]{2,1,0:T(8,128)(2,1)S(1)}, bf16[2,384,128]{2,1,0:T(8,128)(2,1)S(1)}, u32[]{:S(2)}, u32[]{:S(2)}) collective-permute-start(bf16[2,384,128]{2,1,0:T(8,128)(2,1)S(1)} %pad_maximum_fusion.refs_0_), channel_id=1, source_target_pairs={{0,2},{2,4},{4,6},{6,8},{8,10},{10,12},{12,14},{14,0},{1,3},{3,5},... | collective-permute-start | bytes 589832 | tf_op jit(solution)/shard_map/ppermute | solution.py:17
  7.8 7.3 %collective-permute-start.3 = (bf16[2,384,128]{2,1,0:T(8,128)(2,1)S(1)}, bf16[2,384,128]{2,1,0:T(8,128)(2,1)S(1)}, u32[]{:S(2)}, u32[]{:S(2)}) collective-permute-start(bf16[2,384,128]{2,1,0:T(8,128)(2,1)S(1)} %pad_maximum_fusion.refs_0_), channel_id=1, source_target_pairs={{0,14},{2,0},{4,2},{6,4},{8,6},{10,8},{12,10},{14,12},{1,15},{3,1}... | collective-permute-start | bytes 589832 | tf_op jit(solution)/shard_map/ppermute | solution.py:17
  15.2 6.9 %collective-permute-start.2 = (bf16[2,384,128]{2,1,0:T(8,128)(2,1)S(1)}, bf16[2,384,128]{2,1,0:T(8,128)(2,1)S(1)}, u32[]{:S(2)}, u32[]{:S(2)}) collective-permute-start(bf16[2,384,128]{2,1,0:T(8,128)(2,1)S(1)} %collective-permute-done.1.refs_7_), channel_id=1, source_target_pairs={{0,2},{2,4},{4,6},{6,8},{8,10},{10,12},{12,14},{14,0},{1,3},{3,5},... | collective-permute-start | bytes 589832 | tf_op jit(solution)/shard_map/ppermute | solution.py:17
  15.2 6.9 %collective-permute-start.4 = (bf16[2,384,128]{2,1,0:T(8,128)(2,1)S(1)}, bf16[2,384,128]{2,1,0:T(8,128)(2,1)S(1)}, u32[]{:S(2)}, u32[]{:S(2)}) collective-permute-start(bf16[2,384,128]{2,1,0:T(8,128)(2,1)S(1)} %collective-permute-done.3.refs_1_), channel_id=1, source_target_pairs={{0,14},{2,0},{4,2},{6,4},{8,6},{10,8},{12,10},{14,12},{1,15},{3,1}... | collective-permute-start | bytes 589832 | tf_op jit(solution)/shard_map/ppermute | solution.py:17
  22.1 16.4 %copy-start.9 = (s32[4,128,2]{1,2,0:T(2,128)S(1)}, s32[4,128,2]{1,2,0:T(2,128)}, u32[]{:S(2)}) copy-start(s32[4,128,2]{1,2,0:T(2,128)} %param.6) | copy-start | bytes 12292
  22.1 16.4 %copy-start.10 = (f32[4,128,2]{1,2,0:T(2,128)S(1)}, f32[4,128,2]{1,2,0:T(2,128)}, u32[]{:S(2)}) copy-start(f32[4,128,2]{1,2,0:T(2,128)} %param.7) | copy-start | bytes 12292
  22.1 16.5 %copy-start = (s32[5]{0:T(128)S(1)}, s32[5]{0:T(128)}, u32[]{:S(2)}) copy-start(s32[5]{0:T(128)} %stack.23.pos) | copy-start | bytes 64
  22.1 5.8 %collective-permute-start.5 = (bf16[2,384,128]{2,1,0:T(8,128)(2,1)S(1)}, bf16[2,384,128]{2,1,0:T(8,128)(2,1)S(1)}, u32[]{:S(2)}, u32[]{:S(2)}) collective-permute-start(bf16[2,384,128]{2,1,0:T(8,128)(2,1)S(1)} %collective-permute-done.2.refs_6_), channel_id=1, source_target_pairs={{0,2},{2,4},{4,6},{6,8},{8,10},{10,12},{12,14},{14,0},{1,3},{3,5},... | collective-permute-start | bytes 589832 | tf_op jit(solution)/shard_map/ppermute | solution.py:17
  22.2 5.8 %collective-permute-start.7 = (bf16[2,384,128]{2,1,0:T(8,128)(2,1)S(1)}, bf16[2,384,128]{2,1,0:T(8,128)(2,1)S(1)}, u32[]{:S(2)}, u32[]{:S(2)}) collective-permute-start(bf16[2,384,128]{2,1,0:T(8,128)(2,1)S(1)} %collective-permute-done.4.refs_2_), channel_id=1, source_target_pairs={{0,14},{2,0},{4,2},{6,4},{8,6},{10,8},{12,10},{14,12},{1,15},{3,1}... | collective-permute-start | bytes 589832 | tf_op jit(solution)/shard_map/ppermute | solution.py:17
  28.0 4.8 %collective-permute-start.6 = (bf16[1,384,128]{2,1,0:T(8,128)(2,1)S(1)}, bf16[1,384,128]{2,1,0:T(8,128)(2,1)S(1)}, u32[]{:S(2)}, u32[]{:S(2)}) collective-permute-start(bf16[1,384,128]{2,1,0:T(8,128)(2,1)S(1)} %slice.24), channel_id=1, source_target_pairs={{0,2},{2,4},{4,6},{6,8},{8,10},{10,12},{12,14},{14,0},{1,3},{3,5},... | collective-permute-start | bytes 294920 | tf_op jit(solution)/shard_map/ppermute | solution.py:17
  28.1 4.6 %collective-permute-start.8 = (bf16[1,384,128]{2,1,0:T(8,128)(2,1)S(1)}, bf16[1,384,128]{2,1,0:T(8,128)(2,1)S(1)}, u32[]{:S(2)}, u32[]{:S(2)}) collective-permute-start(bf16[1,384,128]{2,1,0:T(8,128)(2,1)S(1)} %slice.25), channel_id=1, source_target_pairs={{0,14},{2,0},{4,2},{6,4},{8,6},{10,8},{12,10},{14,12},{1,15},{3,1}... | collective-permute-start | bytes 294920 | tf_op jit(solution)/shard_map/ppermute | solution.py:17
  32.7 28.2 %all-to-all-start = ((bf16[8,192,256]{2,1,0:T(8,128)(2,1)}), bf16[8,192,256]{2,1,0:T(8,128)(2,1)S(1)}, u32[]{:S(2)}, u32[]{:S(2)}) async-start(bf16[8,192,256]{2,1,0:T(8,128)(2,1)} %get-tuple-element.36), calls=%async_computation | async-start | bytes 1572864 | tf_op jit(solution)/shard_map/all_to_all | solution.py:150
  40.6 1.0 copy-start.2
  41.6 51.5 %copy-start.1 = (bf16[160,3200]{1,0:T(8,128)(2,1)}, bf16[160,3200]{1,0:T(8,128)(2,1)S(1)}, u32[]{:S(2)}) copy-start(bf16[160,3200]{1,0:T(8,128)(2,1)S(1)} %get-tuple-element.47.refs_0_) | copy-start | bytes 3072004
  41.6 28.4 %copy-start.3 = (bf16[160,3200]{1,0:T(8,128)(2,1)S(1)}, bf16[160,3200]{1,0:T(8,128)(2,1)}, u32[]{:S(2)}) copy-start(bf16[160,3200]{1,0:T(8,128)(2,1)} %copy-done.2) | copy-start | bytes 3072004
  41.6 19.3 %collective-permute-start.9 = (bf16[160,3200]{1,0:T(8,128)(2,1)S(1)}, bf16[160,3200]{1,0:T(8,128)(2,1)}, u32[]{:S(2)}, u32[]{:S(2)}) collective-permute-start(bf16[160,3200]{1,0:T(8,128)(2,1)S(1)} %get-tuple-element.40), channel_id=1, source_target_pairs={{0,32},{32,64},{64,96},{96,0},{1,33},{33,65},{65,97},{97,1},{2,34}... | collective-permute-start | bytes 3072008 | tf_op jit(solution)/shard_map/ppermute | solution.py:17
  42.9 18.0 %collective-permute-start.10 = (bf16[160,3200]{1,0:T(8,128)(2,1)S(1)}, bf16[160,3200]{1,0:T(8,128)(2,1)}, u32[]{:S(2)}, u32[]{:S(2)}) collective-permute-start(bf16[160,3200]{1,0:T(8,128)(2,1)S(1)} %get-tuple-element.41), channel_id=1, source_target_pairs={{0,96},{32,0},{64,32},{96,64},{1,97},{33,1},{65,33},{97,65},{2,98}... | collective-permute-start | bytes 3072008 | tf_op jit(solution)/shard_map/ppermute | solution.py:17
  61.0 19.9 %copy-start.4 = (bf16[8,192,256]{2,1,0:T(8,128)(2,1)}, bf16[8,192,256]{2,1,0:T(8,128)(2,1)S(1)}, u32[]{:S(2)}) copy-start(bf16[8,192,256]{2,1,0:T(8,128)(2,1)S(1)} %all-to-all-done.refs_8_) | copy-start | bytes 2359300
  61.0 32.1 %all-to-all-start.1 = ((bf16[8,192,256]{2,1,0:T(8,128)(2,1)}), bf16[8,192,256]{2,1,0:T(8,128)(2,1)}, u32[]{:S(2)}, u32[]{:S(2)}) async-start(bf16[8,192,256]{2,1,0:T(8,128)(2,1)} %get-tuple-element.42), calls=%async_computation.1 | async-start | bytes 1572864 | tf_op jit(solution)/shard_map/all_to_all | solution.py:150
  67.3 12.6 %collective-permute-start.12 = (bf16[8,192,256]{2,1,0:T(8,128)(2,1)S(1)}, bf16[8,192,256]{2,1,0:T(8,128)(2,1)S(1)}, u32[]{:S(2)}, u32[]{:S(2)}) collective-permute-start(bf16[8,192,256]{2,1,0:T(8,128)(2,1)S(1)} %all-to-all-done.refs_8_), channel_id=1, source_target_pairs={{0,1},{1,128},{128,129},{129,0},{2,3},{3,130},{130,131},{131,2},{4... | collective-permute-start | bytes 2359304 | tf_op jit(solution)/shard_map/ppermute | solution.py:17
  68.5 12.2 %collective-permute-start.14 = (bf16[8,192,256]{2,1,0:T(8,128)(2,1)S(1)}, bf16[8,192,256]{2,1,0:T(8,128)(2,1)S(1)}, u32[]{:S(2)}, u32[]{:S(2)}) collective-permute-start(bf16[8,192,256]{2,1,0:T(8,128)(2,1)S(1)} %all-to-all-done.refs_8_), channel_id=1, source_target_pairs={{0,129},{1,0},{128,1},{129,128},{2,131},{3,2},{130,3},{131,130},{4... | collective-permute-start | bytes 2359304 | tf_op jit(solution)/shard_map/ppermute | solution.py:17
  70.0 17.4 %collective-permute-start.11 = (bf16[160,3200]{1,0:T(8,128)(2,1)S(1)}, bf16[160,3200]{1,0:T(8,128)(2,1)S(1)}, u32[]{:S(2)}, u32[]{:S(2)}) collective-permute-start(bf16[160,3200]{1,0:T(8,128)(2,1)S(1)} %copy-done.3), channel_id=1, source_target_pairs={{0,64},{32,96},{64,0},{96,32},{1,65},{33,97},{65,1},{97,33},{2,66}... | collective-permute-start | bytes 3072008 | tf_op jit(solution)/shard_map/ppermute | solution.py:17
  79.9 0.9 copy-start.5
  79.9 12.4 %collective-permute-start.13 = (bf16[4,192,256]{2,1,0:T(8,128)(2,1)S(1)}, bf16[4,192,256]{2,1,0:T(8,128)(2,1)S(1)}, u32[]{:S(2)}, u32[]{:S(2)}) collective-permute-start(bf16[4,192,256]{2,1,0:T(8,128)(2,1)S(1)} %slice.26), channel_id=1, source_target_pairs={{0,1},{1,128},{128,129},{129,0},{2,3},{3,130},{130,131},{131,2},{4... | collective-permute-start | bytes 1179656 | tf_op jit(solution)/shard_map/ppermute | solution.py:17
  80.8 11.5 %copy-start.6 = (bf16[8,192,256]{2,1,0:T(8,128)(2,1)}, bf16[8,192,256]{2,1,0:T(8,128)(2,1)S(1)}, u32[]{:S(2)}) copy-start(bf16[8,192,256]{2,1,0:T(8,128)(2,1)S(1)} %collective-permute-done.14.refs_10_) | copy-start | bytes 2359300
  80.8 12.2 %collective-permute-start.15 = (bf16[4,192,256]{2,1,0:T(8,128)(2,1)S(1)}, bf16[4,192,256]{2,1,0:T(8,128)(2,1)}, u32[]{:S(2)}, u32[]{:S(2)}) collective-permute-start(bf16[4,192,256]{2,1,0:T(8,128)(2,1)S(1)} %slice.27), channel_id=1, source_target_pairs={{0,129},{1,0},{128,1},{129,128},{2,131},{3,2},{130,3},{131,130},{4... | collective-permute-start | bytes 1179656 | tf_op jit(solution)/shard_map/ppermute | solution.py:17
  87.4 4.9 %copy-start.11 = (bf16[160,3200]{1,0:T(8,128)(2,1)}, bf16[160,3200]{1,0:T(8,128)(2,1)S(1)}, u32[]{:S(2)}) copy-start(bf16[160,3200]{1,0:T(8,128)(2,1)S(1)} %collective-permute-done.11.refs_2_) | copy-start | bytes 3072004
  92.3 0.7 copy-start.14
  93.1 16.4 %collective-permute-start.20 = (bf16[8,192,256]{2,1,0:T(8,128)(2,1)}, bf16[8,192,256]{2,1,0:T(8,128)(2,1)S(1)}, u32[]{:S(2)}, u32[]{:S(2)}) collective-permute-start(bf16[8,192,256]{2,1,0:T(8,128)(2,1)} %all-to-all-done.1.refs_8_), channel_id=1, source_target_pairs={{0,1},{1,128},{128,129},{129,0},{2,3},{3,130},{130,131},{131,2},{4... | collective-permute-start | bytes 2359304 | tf_op jit(solution)/shard_map/ppermute | solution.py:17
  93.1 27.4 %collective-permute-start.16 = (bf16[160,3200]{1,0:T(8,128)(2,1)S(1)}, bf16[160,3200]{1,0:T(8,128)(2,1)S(1)}, u32[]{:S(2)}, u32[]{:S(2)}) collective-permute-start(bf16[160,3200]{1,0:T(8,128)(2,1)S(1)} %get-tuple-element.47.refs_0_), channel_id=1, source_target_pairs={{0,16},{16,0},{1,17},{17,1},{2,18},{18,2},{3,19},{19,3},{4,20},{20... | collective-permute-start | bytes 3072008 | tf_op jit(solution)/shard_map/ppermute | solution.py:17
  106.7 16.6 %collective-permute-start.17 = (bf16[160,3200]{1,0:T(8,128)(2,1)}, bf16[160,3200]{1,0:T(8,128)(2,1)S(1)}, u32[]{:S(2)}, u32[]{:S(2)}) collective-permute-start(bf16[160,3200]{1,0:T(8,128)(2,1)} %collective-permute-done.9.refs_1_), channel_id=1, source_target_pairs={{0,16},{16,0},{1,17},{17,1},{2,18},{18,2},{3,19},{19,3},{4,20},{20... | collective-permute-start | bytes 3072008 | tf_op jit(solution)/shard_map/ppermute | solution.py:17
  106.8 16.5 %collective-permute-start.18 = (bf16[160,3200]{1,0:T(8,128)(2,1)}, bf16[160,3200]{1,0:T(8,128)(2,1)}, u32[]{:S(2)}, u32[]{:S(2)}) collective-permute-start(bf16[160,3200]{1,0:T(8,128)(2,1)} %copy-done.11), channel_id=1, source_target_pairs={{0,16},{16,0},{1,17},{17,1},{2,18},{18,2},{3,19},{19,3},{4,20},{20... | collective-permute-start | bytes 3072008 | tf_op jit(solution)/shard_map/ppermute | solution.py:17
  107.2 16.1 %collective-permute-start.19 = (bf16[160,3200]{1,0:T(8,128)(2,1)}, bf16[160,3200]{1,0:T(8,128)(2,1)}, u32[]{:S(2)}, u32[]{:S(2)}) collective-permute-start(bf16[160,3200]{1,0:T(8,128)(2,1)} %collective-permute-done.10.refs_3_), channel_id=1, source_target_pairs={{0,16},{16,0},{1,17},{17,1},{2,18},{18,2},{3,19},{19,3},{4,20},{20... | collective-permute-start | bytes 3072008 | tf_op jit(solution)/shard_map/ppermute | solution.py:17
  109.4 26.2 %copy-start.7 = (bf16[8,192,256]{2,1,0:T(8,128)(2,1)}, bf16[8,192,256]{2,1,0:T(8,128)(2,1)S(1)}, u32[]{:S(2)}) copy-start(bf16[8,192,256]{2,1,0:T(8,128)(2,1)S(1)} %collective-permute-done.20.refs_9_) | copy-start | bytes 2359300
  109.4 11.1 %collective-permute-start.21 = (bf16[8,192,256]{2,1,0:T(8,128)(2,1)}, bf16[8,192,256]{2,1,0:T(8,128)(2,1)S(1)}, u32[]{:S(2)}, u32[]{:S(2)}) collective-permute-start(bf16[8,192,256]{2,1,0:T(8,128)(2,1)} %all-to-all-done.1.refs_8_), channel_id=1, source_target_pairs={{0,129},{1,0},{128,1},{129,128},{2,131},{3,2},{130,3},{131,130},{4... | collective-permute-start | bytes 2359304 | tf_op jit(solution)/shard_map/ppermute | solution.py:17
  120.5 15.2 %copy-start.8 = (bf16[8,192,256]{2,1,0:T(8,128)(2,1)}, bf16[8,192,256]{2,1,0:T(8,128)(2,1)S(1)}, u32[]{:S(2)}) copy-start(bf16[8,192,256]{2,1,0:T(8,128)(2,1)S(1)} %collective-permute-done.21.refs_10_) | copy-start | bytes 2359300
  120.5 35.3 %collective-permute-start.22 = (bf16[4,192,256]{2,1,0:T(8,128)(2,1)S(1)}, bf16[4,192,256]{2,1,0:T(8,128)(2,1)}, u32[]{:S(2)}, u32[]{:S(2)}) collective-permute-start(bf16[4,192,256]{2,1,0:T(8,128)(2,1)S(1)} %slice.28), channel_id=1, source_target_pairs={{0,1},{1,128},{128,129},{129,0},{2,3},{3,130},{130,131},{131,2},{4... | collective-permute-start | bytes 1179656 | tf_op jit(solution)/shard_map/ppermute | solution.py:17
  120.5 2.8 %copy-start.12 = (bf16[160,3200]{1,0:T(8,128)(2,1)}, bf16[160,3200]{1,0:T(8,128)(2,1)S(1)}, u32[]{:S(2)}) copy-start(bf16[160,3200]{1,0:T(8,128)(2,1)S(1)} %collective-permute-done.16.refs_4_) | copy-start | bytes 3072004
  120.5 35.2 %collective-permute-start.23 = (bf16[4,192,256]{2,1,0:T(8,128)(2,1)S(1)}, bf16[4,192,256]{2,1,0:T(8,128)(2,1)S(1)}, u32[]{:S(2)}, u32[]{:S(2)}) collective-permute-start(bf16[4,192,256]{2,1,0:T(8,128)(2,1)S(1)} %slice.29), channel_id=1, source_target_pairs={{0,129},{1,0},{128,1},{129,128},{2,131},{3,2},{130,3},{131,130},{4... | collective-permute-start | bytes 1179656 | tf_op jit(solution)/shard_map/ppermute | solution.py:17
  123.3 1.0 copy-start.13
  135.6 32.2 %all-to-all-start.2 = ((bf16[16,160,128]{2,1,0:T(8,128)(2,1)}), bf16[16,160,128]{2,1,0:T(8,128)(2,1)S(1)}, u32[]{:S(2)}, u32[]{:S(2)}) async-start(bf16[16,160,128]{2,1,0:T(8,128)(2,1)} %bitcast.21), calls=%async_computation.2 | async-start | bytes 1310720 | tf_op jit(solution)/shard_map/all_to_all | solution.py:204
  155.8 0.8 copy-start.15

commit v7 on v6

--- a/solution.py
+++ b/solution.py
@@ -86,15 +86,17 @@
         for k in range(src.shape[0]):
             place = wbuf.at[lax.div(j, 2), lax.rem(low + k + 8 - z, 8), lax.rem(j, 2)]
             copies.append(pltpu.make_async_copy(src.at[k], place, wsem.at[i, k]))
+    rows = [pltpu.make_async_copy(xs[g], xbuf.at[g], xsem.at[g]) for g in range(8)]
     for cp in copies:
         cp.start()
-    rows = [pltpu.make_async_copy(xs[g], xbuf.at[g], xsem.at[g]) for g in range(8)]
-    for cp in rows:
-        cp.start()
+    rows[0].start()
     for cp in copies:
         cp.wait()
+    rows[1].start()
     for g in range(8):
         d, cc = g % 4, g // 4
+        if g < 6:
+            rows[g + 2].start()
         rows[g].wait()
         rw = jnp.sum(xbuf[g, :, width:].astype(F32), axis=1, keepdims=True)
         gate = jnp.dot(xbuf[g, :, :width], wbuf[0].reshape(width, 256), preferred_element_type=F32)
@@ -153,16 +155,18 @@
         left, right = ring(own, X, 4, 1), ring(own, X, 4, -1)
         return [own, left, right, ring(left[:4], X, 4, 1), ring(right[4:], X, 4, -1)]
 
+    own_a, pair = barrier((exchange(blocks[0]), pair))
+    ws_a = spread(own_a)
     below, above = [pair], [pair]
     for k in range(3):
-        if k == 2:
-            below[2], above[2], *blocks = barrier((below[2], above[2], *blocks))
         below.append(ring(below[-1], "z", 8, 1))
         above.append(ring(above[-1], "z", 8, -1))
-    last = barrier((blocks[0], ring(below[3][:1], "z", 8, 1), ring(above[3][1:], "z", 8, -1)))
+    *last, ws_a[1], ws_a[2] = barrier(
+        (blocks[1], ring(below[3][:1], "z", 8, 1), ring(above[3][1:], "z", 8, -1), ws_a[1], ws_a[2])
+    )
     opposite = jnp.concatenate(last[1:], axis=0)
     feats = [pair] + above[1:] + [opposite] + below[:0:-1]
-    own_a = exchange(last[0])
+    own_b = exchange(last[0])
     sent = pl.pallas_call(
         dispatch_kernel,
         out_shape=[jax.ShapeDtypeStruct((2 * MOST, 16 * width + 128), BF)] * 4,
@@ -172,15 +176,13 @@
         name="dispatch",
     )(pos, meta, *feats)
     held = [sent[0], ring(sent[1], "y", 4, 1), None, ring(sent[3], "y", 4, 3)]
-    ws_a = spread(own_a)
-    part_b, ws_a[0], far_rows, held[1], held[3] = barrier((blocks[1], ws_a[0], sent[2], held[1], held[3]))
-    own_b = exchange(part_b)
+    other = [ring(sent[0], "c", 2, 1)]
+    held[0], far_rows, held[1], held[3], other[0], ws_a[3], ws_a[4] = barrier(
+        (held[0], sent[2], held[1], held[3], other[0], ws_a[3], ws_a[4])
+    )
     held[2] = ring(far_rows, "y", 4, 2)
-    own_b, held[2], ws_a[3], ws_a[4], held[0], held[1], held[3] = barrier(
-        (own_b, held[2], ws_a[3], ws_a[4], held[0], held[1], held[3])
-    )
     ws_b = spread(own_b)
-    other = [ring(h, "c", 2, 1) for h in held]
+    other += [ring(h, "c", 2, 1) for h in held[1:]]
     pieces = [ws_a, ws_b]
     backs = []
     for ws in pieces:

time: 189 us -> 192 us (1.016)
  starting transfers between devices: 76 us -> 83.7 us
  local copies, waits for them, and re-layouts: 7.35 us -> 3.91 us
    ppermute x24, waiting for transfers between devices: 56.5 us -> 36.5 us  [ring(): return lax.ppermute(x, axis, [(i, (i + step) % size) for i in range(size)])]
    all_to_all x2, waiting for transfers between devices: 0.01 us -> 19.9 us  [exchange(): return lax.all_to_all(x, 'z', split_axis=0, concat_axis=0, tiled=True)]
    ppermute x24, starting transfers between devices: 43.8 us -> 62.9 us  [ring(): return lax.ppermute(x, axis, [(i, (i + step) % size) for i in range(size)])]
    all_to_all x1, starting transfers between devices: 20.1 us -> 7.28 us  [body(): lax.all_to_all(act.reshape(16, 2 * MOST, wide), ('y', 'c', 'xl'), split_a...]
    unnamed x32 -> x24, local copies, waits for them, and re-layouts: 4.12 us -> 0.78 us
  transfers between devices with their start and end apart: 27 -> 27, of which waited for: 10 -> 9; matrix products, arithmetic and copies ran while one was open for 0% -> 0% of each run, Pallas kernels for 15% -> 11%
where the time goes in v7:
time: 192 us; the launch traced here: 191 us
  starting transfers between devices  83.7 us (44%)
  waiting for transfers between devices  56.4 us (29%)
  Pallas kernels  29.1 us (15%)
  blocking collectives  17.6 us (9%)
  local copies, waits for them, and re-layouts  3.91 us (2%)
    ppermute x24, starting transfers between devices, ring(): return lax.ppermute(x, axis, [(i, (i + step) % size) for i in range(size)])  62.9 us
    ppermute x24, waiting for transfers between devices, ring(): return lax.ppermute(x, axis, [(i, (i + step) % size) for i in range(size)])  36.5 us
    pallas_call x2, Pallas kernels, body(): pl.pallas_call(expert_kernel, out_shape=jax.ShapeDtypeStruct((4, 2, 2, 2...  20.8 us
    all_to_all x2, waiting for transfers between devices, exchange(): return lax.all_to_all(x, 'z', split_axis=0, concat_axis=0, tiled=True)  19.9 us
    all_to_all x1, blocking collectives, body(): lax.all_to_all(act.reshape(16, 2 * MOST, wide), ('y', 'c', 'xl'), split_a...  17.6 us
    all_to_all x2, starting transfers between devices, exchange(): return lax.all_to_all(x, 'z', split_axis=0, concat_axis=0, tiled=True)  13.5 us
    all_to_all x1, starting transfers between devices, body(): lax.all_to_all(act.reshape(16, 2 * MOST, wide), ('y', 'c', 'xl'), split_a...  7.28 us
  transfers between devices with their start and end apart: 27, of which 9 were waited for; matrix products, arithmetic and copies ran while one was open for 0% of the time, Pallas kernels for 11%

profile of v7, /device:TPU:1, one launch (start us, length us, event | category | flops | bytes accessed | tf_op | source)
XLA Modules:
  0.0 191.1 jit_solution(14245532139751096570)
XLA Ops:
  0.0 0.7 stack.23.pos
  0.7 3.5 %columns.1 = (bf16[8,192,256]{2,1,0:T(8,128)(2,1)}, bf16[8,192,256]{2,1,0:T(8,128)(2,1)}) custom-call(s32[5]{0:T(128)} %stack.23.pos, bf16[1,192,4096]{2,1,0:T(8,128)(2,1)} %gate.1, bf16[1,192,4096]{2,1,0:T(8,128)(2,1)} %up.1), custom_call_target="tpu_custom_call" | custom-call | tf_op jit(solution)/shard_map/columns/pallas_call | solution.py:141
  4.1 0.0 copy-start.8
  4.2 0.0 copy-start.9
  4.2 0.0 copy-start.10
  4.2 9.2 %all-to-all-start = ((bf16[8,192,256]{2,1,0:T(8,128)(2,1)}), bf16[8,192,256]{2,1,0:T(8,128)(2,1)S(1)}, u32[]{:S(2)}, u32[]{:S(2)}) async-start(bf16[8,192,256]{2,1,0:T(8,128)(2,1)} %get-tuple-element.25), calls=%async_computation | async-start | bytes 1572864 | tf_op jit(solution)/shard_map/all_to_all | solution.py:152
  13.4 1.3 collective-permute-start
  14.7 2.3 %collective-permute-done = bf16[2,192,128]{2,1,0:T(8,128)(2,1)S(1)} collective-permute-done((bf16[2,192,128]{2,1,0:T(8,128)(2,1)S(1)}, bf16[2,192,128]{2,1,0:T(8,128)(2,1)S(1)}, u32[]{:S(2)}, u32[]{:S(2)}) %collective-permute-start) | collective-permute-done | bytes 98336 | tf_op jit(solution)/shard_map/ppermute | solution.py:17
  17.0 19.9 %all-to-all-done.refs_8_ = bf16[8,192,256]{2,1,0:T(8,128)(2,1)S(1)} async-done(((bf16[8,192,256]{2,1,0:T(8,128)(2,1)}), bf16[8,192,256]{2,1,0:T(8,128)(2,1)S(1)}, u32[]{:S(2)}, u32[]{:S(2)}) %all-to-all-start) | async-done | bytes 786464 | tf_op jit(solution)/shard_map/all_to_all | solution.py:152
  36.9 1.2 collective-permute-start.9
  38.1 1.5 collective-permute-start.10
  39.6 0.0 collective-permute-start.4
  39.6 2.7 %collective-permute-start.1 = (bf16[2,384,128]{2,1,0:T(8,128)(2,1)S(1)}, bf16[2,384,128]{2,1,0:T(8,128)(2,1)S(1)}, u32[]{:S(2)}, u32[]{:S(2)}) collective-permute-start(bf16[2,384,128]{2,1,0:T(8,128)(2,1)S(1)} %pad_maximum_fusion.refs_0_), channel_id=1, source_target_pairs={{0,14},{2,0},{4,2},{6,4},{8,6},{10,8},{12,10},{14,12},{1,15},{3,1}... | collective-permute-start | bytes 589832 | tf_op jit(solution)/shard_map/ppermute | solution.py:17
  42.3 3.9 %collective-permute-done.4.refs_7_ = bf16[2,384,128]{2,1,0:T(8,128)(2,1)S(1)} collective-permute-done((bf16[2,384,128]{2,1,0:T(8,128)(2,1)S(1)}, bf16[2,384,128]{2,1,0:T(8,128)(2,1)S(1)}, u32[]{:S(2)}, u32[]{:S(2)}) %collective-permute-start.4) | collective-permute-done | bytes 196640 | tf_op jit(solution)/shard_map/ppermute | solution.py:17
  46.2 0.0 collective-permute-start.5
  46.2 0.0 collective-permute-done.1.refs_1_
  46.2 2.7 %collective-permute-start.2 = (bf16[2,384,128]{2,1,0:T(8,128)(2,1)S(1)}, bf16[2,384,128]{2,1,0:T(8,128)(2,1)S(1)}, u32[]{:S(2)}, u32[]{:S(2)}) collective-permute-start(bf16[2,384,128]{2,1,0:T(8,128)(2,1)S(1)} %collective-permute-done.1.refs_1_), channel_id=1, source_target_pairs={{0,14},{2,0},{4,2},{6,4},{8,6},{10,8},{12,10},{14,12},{1,15},{3,1}... | collective-permute-start | bytes 589832 | tf_op jit(solution)/shard_map/ppermute | solution.py:17
  48.8 3.3 %collective-permute-done.5.refs_6_ = bf16[2,384,128]{2,1,0:T(8,128)(2,1)S(1)} collective-permute-done((bf16[2,384,128]{2,1,0:T(8,128)(2,1)S(1)}, bf16[2,384,128]{2,1,0:T(8,128)(2,1)S(1)}, u32[]{:S(2)}, u32[]{:S(2)}) %collective-permute-start.5) | collective-permute-done | bytes 196640 | tf_op jit(solution)/shard_map/ppermute | solution.py:17
  52.2 0.0 collective-permute-start.6
  52.2 2.7 %collective-permute-start.3 = (bf16[2,384,128]{2,1,0:T(8,128)(2,1)S(1)}, bf16[2,384,128]{2,1,0:T(8,128)(2,1)S(1)}, u32[]{:S(2)}, u32[]{:S(2)}) collective-permute-start(bf16[2,384,128]{2,1,0:T(8,128)(2,1)S(1)} %collective-permute-done.2.refs_2_), channel_id=1, source_target_pairs={{0,14},{2,0},{4,2},{6,4},{8,6},{10,8},{12,10},{14,12},{1,15},{3,1}... | collective-permute-start | bytes 589832 | tf_op jit(solution)/shard_map/ppermute | solution.py:17
  54.9 3.0 %collective-permute-done.6.refs_5_ = bf16[2,384,128]{2,1,0:T(8,128)(2,1)S(1)} collective-permute-done((bf16[2,384,128]{2,1,0:T(8,128)(2,1)S(1)}, bf16[2,384,128]{2,1,0:T(8,128)(2,1)S(1)}, u32[]{:S(2)}, u32[]{:S(2)}) %collective-permute-start.6) | collective-permute-done | bytes 196640 | tf_op jit(solution)/shard_map/ppermute | solution.py:17
  57.9 0.1 collective-permute-start.7
  58.0 2.7 %collective-permute-start.8 = (bf16[1,384,128]{2,1,0:T(8,128)(2,1)S(1)}, bf16[1,384,128]{2,1,0:T(8,128)(2,1)S(1)}, u32[]{:S(2)}, u32[]{:S(2)}) collective-permute-start(bf16[1,384,128]{2,1,0:T(8,128)(2,1)S(1)} %slice.25), channel_id=1, source_target_pairs={{0,14},{2,0},{4,2},{6,4},{8,6},{10,8},{12,10},{14,12},{1,15},{3,1}... | collective-permute-start | bytes 294920 | tf_op jit(solution)/shard_map/ppermute | solution.py:17
  60.8 1.9 collective-permute-done.7
  62.8 3.4 %dispatch.1 = (bf16[160,3200]{1,0:T(8,128)(2,1)S(1)}, bf16[160,3200]{1,0:T(8,128)(2,1)}, bf16[160,3200]{1,0:T(8,128)(2,1)S(1)}, bf16[160,3200]{1,0:T(8,128)(2,1)}) custom-call(s32[5]{0:T(128)S(1)} %copy-done, f32[4,4,128]{2,1,0:T(4,128)S(1)} %maximum_bitcast_fusion.meta, bf16[2,384,128]{2,1,0:T(8,128)(2,1)S(1)} %pad_maximum_fusion.refs_0_, ...), custom_call_target="tpu_custom_call" | custom-call | tf_op jit(solution)/shard_map/dispatch/pallas_call | solution.py:170
  66.1 1.3 collective-permute-start.11
  67.4 1.5 collective-permute-start.12
  68.9 5.6 %collective-permute-start.13 = (bf16[160,3200]{1,0:T(8,128)(2,1)S(1)}, bf16[160,3200]{1,0:T(8,128)(2,1)}, u32[]{:S(2)}, u32[]{:S(2)}) collective-permute-start(bf16[160,3200]{1,0:T(8,128)(2,1)S(1)} %get-tuple-element.35.refs_0_), channel_id=1, source_target_pairs={{0,16},{16,0},{1,17},{17,1},{2,18},{18,2},{3,19},{19,3},{4,20},{20... | collective-permute-start | bytes 3072008 | tf_op jit(solution)/shard_map/ppermute | solution.py:17
  74.5 0.1 collective-permute-start.14
  74.6 0.8 slice.27
  75.4 2.7 %collective-permute-start.15 = (bf16[4,192,256]{2,1,0:T(8,128)(2,1)}, bf16[4,192,256]{2,1,0:T(8,128)(2,1)}, u32[]{:S(2)}, u32[]{:S(2)}) collective-permute-start(bf16[4,192,256]{2,1,0:T(8,128)(2,1)} %slice.27), channel_id=1, source_target_pairs={{0,129},{1,0},{128,1},{129,128},{2,131},{3,2},{130,3},{131,130},{4... | collective-permute-start | bytes 1179656 | tf_op jit(solution)/shard_map/ppermute | solution.py:17
  78.1 4.3 %all-to-all-start.2 = ((bf16[8,192,256]{2,1,0:T(8,128)(2,1)}), bf16[8,192,256]{2,1,0:T(8,128)(2,1)S(1)}, u32[]{:S(2)}, u32[]{:S(2)}) async-start(bf16[8,192,256]{2,1,0:T(8,128)(2,1)} %get-tuple-element.44), calls=%async_computation.2 | async-start | bytes 1572864 | tf_op jit(solution)/shard_map/all_to_all | solution.py:152
  82.4 4.3 %collective-permute-done.14.refs_11_ = bf16[4,192,256]{2,1,0:T(8,128)(2,1)} collective-permute-done((bf16[4,192,256]{2,1,0:T(8,128)(2,1)S(1)}, bf16[4,192,256]{2,1,0:T(8,128)(2,1)}, u32[]{:S(2)}, u32[]{:S(2)}) %collective-permute-start.14) | collective-permute-done | bytes 393248 | tf_op jit(solution)/shard_map/ppermute | solution.py:17
  86.7 0.1 collective-permute-done.11.refs_1_
  86.8 2.3 %collective-permute-start.16 = (bf16[160,3200]{1,0:T(8,128)(2,1)S(1)}, bf16[160,3200]{1,0:T(8,128)(2,1)}, u32[]{:S(2)}, u32[]{:S(2)}) collective-permute-start(bf16[160,3200]{1,0:T(8,128)(2,1)S(1)} %get-tuple-element.37), channel_id=1, source_target_pairs={{0,64},{32,96},{64,0},{96,32},{1,65},{33,97},{65,1},{97,33},{2,66}... | collective-permute-start | bytes 3072008 | tf_op jit(solution)/shard_map/ppermute | solution.py:17
  89.1 16.6 %collective-permute-start.17 = (bf16[160,3200]{1,0:T(8,128)(2,1)}, bf16[160,3200]{1,0:T(8,128)(2,1)}, u32[]{:S(2)}, u32[]{:S(2)}) collective-permute-start(bf16[160,3200]{1,0:T(8,128)(2,1)} %collective-permute-done.11.refs_1_), channel_id=1, source_target_pairs={{0,16},{16,0},{1,17},{17,1},{2,18},{18,2},{3,19},{19,3},{4,20},{20... | collective-permute-start | bytes 3072008 | tf_op jit(solution)/shard_map/ppermute | solution.py:17
  105.7 12.6 %collective-permute-start.18 = (bf16[160,3200]{1,0:T(8,128)(2,1)}, bf16[160,3200]{1,0:T(8,128)(2,1)}, u32[]{:S(2)}, u32[]{:S(2)}) collective-permute-start(bf16[160,3200]{1,0:T(8,128)(2,1)} %collective-permute-done.16.refs_2_), channel_id=1, source_target_pairs={{0,16},{16,0},{1,17},{17,1},{2,18},{18,2},{3,19},{19,3},{4,20},{20... | collective-permute-start | bytes 3072008 | tf_op jit(solution)/shard_map/ppermute | solution.py:17
  118.3 2.7 %collective-permute-start.21 = (bf16[8,192,256]{2,1,0:T(8,128)(2,1)S(1)}, bf16[8,192,256]{2,1,0:T(8,128)(2,1)S(1)}, u32[]{:S(2)}, u32[]{:S(2)}) collective-permute-start(bf16[8,192,256]{2,1,0:T(8,128)(2,1)S(1)} %all-to-all-done.2.refs_8_), channel_id=1, source_target_pairs={{0,129},{1,0},{128,1},{129,128},{2,131},{3,2},{130,3},{131,130},{4... | collective-permute-start | bytes 2359304 | tf_op jit(solution)/shard_map/ppermute | solution.py:17
  121.0 17.6 %collective-permute-done.20.refs_9_ = bf16[8,192,256]{2,1,0:T(8,128)(2,1)S(1)} collective-permute-done((bf16[8,192,256]{2,1,0:T(8,128)(2,1)S(1)}, bf16[8,192,256]{2,1,0:T(8,128)(2,1)S(1)}, u32[]{:S(2)}, u32[]{:S(2)}) %collective-permute-start.20) | collective-permute-done | bytes 786464 | tf_op jit(solution)/shard_map/ppermute | solution.py:17
  138.6 0.1 collective-permute-start.22
  138.8 2.7 %collective-permute-start.23 = (bf16[4,192,256]{2,1,0:T(8,128)(2,1)S(1)}, bf16[4,192,256]{2,1,0:T(8,128)(2,1)}, u32[]{:S(2)}, u32[]{:S(2)}) collective-permute-start(bf16[4,192,256]{2,1,0:T(8,128)(2,1)S(1)} %slice.29), channel_id=1, source_target_pairs={{0,129},{1,0},{128,1},{129,128},{2,131},{3,2},{130,3},{131,130},{4... | collective-permute-start | bytes 1179656 | tf_op jit(solution)/shard_map/ppermute | solution.py:17
  141.5 10.4 %expert.2 = bf16[4,2,2,160,128]{4,3,2,1,0:T(8,128)(2,1)} custom-call(s32[5]{0:T(128)} %stack.23.pos, bf16[160,3200]{1,0:T(8,128)(2,1)} %copy-done.1, bf16[160,3200]{1,0:T(8,128)(2,1)} %collective-permute-done.11.refs_1_, bf16[160,3200]{1,0:T(8,128)(2,1)} %collective-permute-done.16.refs_2_, bf16[160,3200]{1,0:T(8,128)(2,1)} %collective-permute-done.12.refs_3_, ...), custom_call_target="tpu_custom_call" | custom-call | flops 4026531840 | bytes 12582912 | tf_op jit(solution)/shard_map/expert/pallas_call | solution.py:189
  152.0 7.3 %all-to-all-start.1 = ((bf16[16,160,128]{2,1,0:T(8,128)(2,1)}), bf16[16,160,128]{2,1,0:T(8,128)(2,1)S(1)}, u32[]{:S(2)}, u32[]{:S(2)}) async-start(bf16[16,160,128]{2,1,0:T(8,128)(2,1)} %bitcast.21), calls=%async_computation.1 | async-start | bytes 1310720 | tf_op jit(solution)/shard_map/all_to_all | solution.py:206
  159.3 0.7 copy-done.11
  160.0 10.4 %expert.3 = bf16[4,2,2,160,128]{4,3,2,1,0:T(8,128)(2,1)} custom-call(s32[5]{0:T(128)} %stack.23.pos, bf16[160,3200]{1,0:T(8,128)(2,1)} %copy-done.1, bf16[160,3200]{1,0:T(8,128)(2,1)} %collective-permute-done.11.refs_1_, bf16[160,3200]{1,0:T(8,128)(2,1)} %collective-permute-done.16.refs_2_, bf16[160,3200]{1,0:T(8,128)(2,1)} %collective-permute-done.12.refs_3_, ...), custom_call_target="tpu_custom_call" | custom-call | flops 4026531840 | bytes 12582912 | tf_op jit(solution)/shard_map/expert/pallas_call | solution.py:189
  170.4 17.6 %all_to_all.20 = bf16[16,160,128]{2,1,0:T(8,128)(2,1)S(1)} all-to-all(bf16[16,160,128]{2,1,0:T(8,128)(2,1)} %bitcast.22), channel_id=1, replica_groups=mesh['dp'=2,'y'=4,'c'=2,'z'=8,'xl'=2] {'y','c','xl'}, dimensions={0} | all-to-all | bytes 1310720 | tf_op jit(solution)/shard_map/all_to_all | solution.py:206
  188.0 1.5 combine.1
  189.5 1.6 reshape.23
  (50 shorter events, 0.3 us)
Async XLA Ops:
  4.1 9.2 %copy-start.8 = (bf16[4,128,192]{1,2,0:T(8,128)(2,1)S(1)}, bf16[4,128,192]{1,2,0:T(8,128)(2,1)}, u32[]{:S(2)}) copy-start(bf16[4,128,192]{1,2,0:T(8,128)(2,1)} %param.5) | copy-start | bytes 589828
  4.2 50.7 %copy-start.9 = (s32[4,128,2]{1,2,0:T(2,128)S(1)}, s32[4,128,2]{1,2,0:T(2,128)}, u32[]{:S(2)}) copy-start(s32[4,128,2]{1,2,0:T(2,128)} %param.6) | copy-start | bytes 12292
  4.2 56.6 %copy-start.10 = (f32[4,128,2]{1,2,0:T(2,128)S(1)}, f32[4,128,2]{1,2,0:T(2,128)}, u32[]{:S(2)}) copy-start(f32[4,128,2]{1,2,0:T(2,128)} %param.7) | copy-start | bytes 12292
  4.2 58.6 %copy-start = (s32[5]{0:T(128)S(1)}, s32[5]{0:T(128)}, u32[]{:S(2)}) copy-start(s32[5]{0:T(128)} %stack.23.pos) | copy-start | bytes 64
  4.2 32.7 %all-to-all-start = ((bf16[8,192,256]{2,1,0:T(8,128)(2,1)}), bf16[8,192,256]{2,1,0:T(8,128)(2,1)S(1)}, u32[]{:S(2)}, u32[]{:S(2)}) async-start(bf16[8,192,256]{2,1,0:T(8,128)(2,1)} %get-tuple-element.25), calls=%async_computation | async-start | bytes 1572864 | tf_op jit(solution)/shard_map/all_to_all | solution.py:152
  13.4 3.6 %collective-permute-start = (bf16[2,192,128]{2,1,0:T(8,128)(2,1)S(1)}, bf16[2,192,128]{2,1,0:T(8,128)(2,1)S(1)}, u32[]{:S(2)}, u32[]{:S(2)}) collective-permute-start(bf16[2,192,128]{2,1,0:T(8,128)(2,1)S(1)} %dynamic-slice_bitcast_fusion), channel_id=1, source_target_pairs={{0,1},{1,0},{2,3},{3,2},{4,5},{5,4},{6,7},{7,6},{8,9},{9,8},{10,11... | collective-permute-start | bytes 294920 | tf_op jit(solution)/shard_map/ppermute | solution.py:17
  36.9 37.6 %copy-start.2 = (bf16[8,192,256]{2,1,0:T(8,128)(2,1)}, bf16[8,192,256]{2,1,0:T(8,128)(2,1)S(1)}, u32[]{:S(2)}) copy-start(bf16[8,192,256]{2,1,0:T(8,128)(2,1)S(1)} %all-to-all-done.refs_8_) | copy-start | bytes 2359300
  36.9 25.8 %collective-permute-start.9 = (bf16[8,192,256]{2,1,0:T(8,128)(2,1)S(1)}, bf16[8,192,256]{2,1,0:T(8,128)(2,1)S(1)}, u32[]{:S(2)}, u32[]{:S(2)}) collective-permute-start(bf16[8,192,256]{2,1,0:T(8,128)(2,1)S(1)} %all-to-all-done.refs_8_), channel_id=1, source_target_pairs={{0,1},{1,128},{128,129},{129,0},{2,3},{3,130},{130,131},{131,2},{4... | collective-permute-start | bytes 2359304 | tf_op jit(solution)/shard_map/ppermute | solution.py:17
  38.1 24.6 %collective-permute-start.10 = (bf16[8,192,256]{2,1,0:T(8,128)(2,1)S(1)}, bf16[8,192,256]{2,1,0:T(8,128)(2,1)S(1)}, u32[]{:S(2)}, u32[]{:S(2)}) collective-permute-start(bf16[8,192,256]{2,1,0:T(8,128)(2,1)S(1)} %all-to-all-done.refs_8_), channel_id=1, source_target_pairs={{0,129},{1,0},{128,1},{129,128},{2,131},{3,2},{130,3},{131,130},{4... | collective-permute-start | bytes 2359304 | tf_op jit(solution)/shard_map/ppermute | solution.py:17
  39.6 6.6 %collective-permute-start.4 = (bf16[2,384,128]{2,1,0:T(8,128)(2,1)S(1)}, bf16[2,384,128]{2,1,0:T(8,128)(2,1)S(1)}, u32[]{:S(2)}, u32[]{:S(2)}) collective-permute-start(bf16[2,384,128]{2,1,0:T(8,128)(2,1)S(1)} %pad_maximum_fusion.refs_0_), channel_id=1, source_target_pairs={{0,2},{2,4},{4,6},{6,8},{8,10},{10,12},{12,14},{14,0},{1,3},{3,5},... | collective-permute-start | bytes 589832 | tf_op jit(solution)/shard_map/ppermute | solution.py:17
  39.6 6.6 %collective-permute-start.1 = (bf16[2,384,128]{2,1,0:T(8,128)(2,1)S(1)}, bf16[2,384,128]{2,1,0:T(8,128)(2,1)S(1)}, u32[]{:S(2)}, u32[]{:S(2)}) collective-permute-start(bf16[2,384,128]{2,1,0:T(8,128)(2,1)S(1)} %pad_maximum_fusion.refs_0_), channel_id=1, source_target_pairs={{0,14},{2,0},{4,2},{6,4},{8,6},{10,8},{12,10},{14,12},{1,15},{3,1}... | collective-permute-start | bytes 589832 | tf_op jit(solution)/shard_map/ppermute | solution.py:17
  46.2 6.0 %collective-permute-start.5 = (bf16[2,384,128]{2,1,0:T(8,128)(2,1)S(1)}, bf16[2,384,128]{2,1,0:T(8,128)(2,1)S(1)}, u32[]{:S(2)}, u32[]{:S(2)}) collective-permute-start(bf16[2,384,128]{2,1,0:T(8,128)(2,1)S(1)} %collective-permute-done.4.refs_7_), channel_id=1, source_target_pairs={{0,2},{2,4},{4,6},{6,8},{8,10},{10,12},{12,14},{14,0},{1,3},{3,5},... | collective-permute-start | bytes 589832 | tf_op jit(solution)/shard_map/ppermute | solution.py:17
  46.2 6.0 %collective-permute-start.2 = (bf16[2,384,128]{2,1,0:T(8,128)(2,1)S(1)}, bf16[2,384,128]{2,1,0:T(8,128)(2,1)S(1)}, u32[]{:S(2)}, u32[]{:S(2)}) collective-permute-start(bf16[2,384,128]{2,1,0:T(8,128)(2,1)S(1)} %collective-permute-done.1.refs_1_), channel_id=1, source_target_pairs={{0,14},{2,0},{4,2},{6,4},{8,6},{10,8},{12,10},{14,12},{1,15},{3,1}... | collective-permute-start | bytes 589832 | tf_op jit(solution)/shard_map/ppermute | solution.py:17
  52.2 5.7 %collective-permute-start.6 = (bf16[2,384,128]{2,1,0:T(8,128)(2,1)S(1)}, bf16[2,384,128]{2,1,0:T(8,128)(2,1)S(1)}, u32[]{:S(2)}, u32[]{:S(2)}) collective-permute-start(bf16[2,384,128]{2,1,0:T(8,128)(2,1)S(1)} %collective-permute-done.5.refs_6_), channel_id=1, source_target_pairs={{0,2},{2,4},{4,6},{6,8},{8,10},{10,12},{12,14},{14,0},{1,3},{3,5},... | collective-permute-start | bytes 589832 | tf_op jit(solution)/shard_map/ppermute | solution.py:17
  52.2 5.8 %collective-permute-start.3 = (bf16[2,384,128]{2,1,0:T(8,128)(2,1)S(1)}, bf16[2,384,128]{2,1,0:T(8,128)(2,1)S(1)}, u32[]{:S(2)}, u32[]{:S(2)}) collective-permute-start(bf16[2,384,128]{2,1,0:T(8,128)(2,1)S(1)} %collective-permute-done.2.refs_2_), channel_id=1, source_target_pairs={{0,14},{2,0},{4,2},{6,4},{8,6},{10,8},{12,10},{14,12},{1,15},{3,1}... | collective-permute-start | bytes 589832 | tf_op jit(solution)/shard_map/ppermute | solution.py:17
  57.9 4.8 %collective-permute-start.7 = (bf16[1,384,128]{2,1,0:T(8,128)(2,1)S(1)}, bf16[1,384,128]{2,1,0:T(8,128)(2,1)S(1)}, u32[]{:S(2)}, u32[]{:S(2)}) collective-permute-start(bf16[1,384,128]{2,1,0:T(8,128)(2,1)S(1)} %slice.24), channel_id=1, source_target_pairs={{0,2},{2,4},{4,6},{6,8},{8,10},{10,12},{12,14},{14,0},{1,3},{3,5},... | collective-permute-start | bytes 294920 | tf_op jit(solution)/shard_map/ppermute | solution.py:17
  58.0 4.6 %collective-permute-start.8 = (bf16[1,384,128]{2,1,0:T(8,128)(2,1)S(1)}, bf16[1,384,128]{2,1,0:T(8,128)(2,1)S(1)}, u32[]{:S(2)}, u32[]{:S(2)}) collective-permute-start(bf16[1,384,128]{2,1,0:T(8,128)(2,1)S(1)} %slice.25), channel_id=1, source_target_pairs={{0,14},{2,0},{4,2},{6,4},{8,6},{10,8},{12,10},{14,12},{1,15},{3,1}... | collective-permute-start | bytes 294920 | tf_op jit(solution)/shard_map/ppermute | solution.py:17
  62.7 12.7 %copy-start.4 = (bf16[8,192,256]{2,1,0:T(8,128)(2,1)}, bf16[8,192,256]{2,1,0:T(8,128)(2,1)S(1)}, u32[]{:S(2)}) copy-start(bf16[8,192,256]{2,1,0:T(8,128)(2,1)S(1)} %collective-permute-done.9.refs_9_) | copy-start | bytes 2359300
  62.7 12.7 %copy-start.5 = (bf16[8,192,256]{2,1,0:T(8,128)(2,1)}, bf16[8,192,256]{2,1,0:T(8,128)(2,1)S(1)}, u32[]{:S(2)}) copy-start(bf16[8,192,256]{2,1,0:T(8,128)(2,1)S(1)} %collective-permute-done.10.refs_10_) | copy-start | bytes 2359300
  66.1 11.9 %copy-start.1 = (bf16[160,3200]{1,0:T(8,128)(2,1)}, bf16[160,3200]{1,0:T(8,128)(2,1)S(1)}, u32[]{:S(2)}) copy-start(bf16[160,3200]{1,0:T(8,128)(2,1)S(1)} %get-tuple-element.35.refs_0_) | copy-start | bytes 3072004
  66.1 20.7 %collective-permute-start.11 = (bf16[160,3200]{1,0:T(8,128)(2,1)}, bf16[160,3200]{1,0:T(8,128)(2,1)}, u32[]{:S(2)}, u32[]{:S(2)}) collective-permute-start(bf16[160,3200]{1,0:T(8,128)(2,1)} %get-tuple-element.33), channel_id=1, source_target_pairs={{0,32},{32,64},{64,96},{96,0},{1,33},{33,65},{65,97},{97,1},{2,34}... | collective-permute-start | bytes 3072008 | tf_op jit(solution)/shard_map/ppermute | solution.py:17
  67.4 19.4 %collective-permute-start.12 = (bf16[160,3200]{1,0:T(8,128)(2,1)}, bf16[160,3200]{1,0:T(8,128)(2,1)}, u32[]{:S(2)}, u32[]{:S(2)}) collective-permute-start(bf16[160,3200]{1,0:T(8,128)(2,1)} %get-tuple-element.34), channel_id=1, source_target_pairs={{0,96},{32,0},{64,32},{96,64},{1,97},{33,1},{65,33},{97,65},{2,98}... | collective-permute-start | bytes 3072008 | tf_op jit(solution)/shard_map/ppermute | solution.py:17
  68.9 17.9 %collective-permute-start.13 = (bf16[160,3200]{1,0:T(8,128)(2,1)S(1)}, bf16[160,3200]{1,0:T(8,128)(2,1)}, u32[]{:S(2)}, u32[]{:S(2)}) collective-permute-start(bf16[160,3200]{1,0:T(8,128)(2,1)S(1)} %get-tuple-element.35.refs_0_), channel_id=1, source_target_pairs={{0,16},{16,0},{1,17},{17,1},{2,18},{18,2},{3,19},{19,3},{4,20},{20... | collective-permute-start | bytes 3072008 | tf_op jit(solution)/shard_map/ppermute | solution.py:17
  74.5 12.1 %collective-permute-start.14 = (bf16[4,192,256]{2,1,0:T(8,128)(2,1)S(1)}, bf16[4,192,256]{2,1,0:T(8,128)(2,1)}, u32[]{:S(2)}, u32[]{:S(2)}) collective-permute-start(bf16[4,192,256]{2,1,0:T(8,128)(2,1)S(1)} %slice.26), channel_id=1, source_target_pairs={{0,1},{1,128},{128,129},{129,0},{2,3},{3,130},{130,131},{131,2},{4... | collective-permute-start | bytes 1179656 | tf_op jit(solution)/shard_map/ppermute | solution.py:17
  75.4 11.3 %collective-permute-start.15 = (bf16[4,192,256]{2,1,0:T(8,128)(2,1)}, bf16[4,192,256]{2,1,0:T(8,128)(2,1)}, u32[]{:S(2)}, u32[]{:S(2)}) collective-permute-start(bf16[4,192,256]{2,1,0:T(8,128)(2,1)} %slice.27), channel_id=1, source_target_pairs={{0,129},{1,0},{128,1},{129,128},{2,131},{3,2},{130,3},{131,130},{4... | collective-permute-start | bytes 1179656 | tf_op jit(solution)/shard_map/ppermute | solution.py:17
  78.1 40.2 %all-to-all-start.2 = ((bf16[8,192,256]{2,1,0:T(8,128)(2,1)}), bf16[8,192,256]{2,1,0:T(8,128)(2,1)S(1)}, u32[]{:S(2)}, u32[]{:S(2)}) async-start(bf16[8,192,256]{2,1,0:T(8,128)(2,1)} %get-tuple-element.44), calls=%async_computation.2 | async-start | bytes 1572864 | tf_op jit(solution)/shard_map/all_to_all | solution.py:152
  86.8 18.9 %collective-permute-start.16 = (bf16[160,3200]{1,0:T(8,128)(2,1)S(1)}, bf16[160,3200]{1,0:T(8,128)(2,1)}, u32[]{:S(2)}, u32[]{:S(2)}) collective-permute-start(bf16[160,3200]{1,0:T(8,128)(2,1)S(1)} %get-tuple-element.37), channel_id=1, source_target_pairs={{0,64},{32,96},{64,0},{96,32},{1,65},{33,97},{65,1},{97,33},{2,66}... | collective-permute-start | bytes 3072008 | tf_op jit(solution)/shard_map/ppermute | solution.py:17
  89.1 52.4 %collective-permute-start.17 = (bf16[160,3200]{1,0:T(8,128)(2,1)}, bf16[160,3200]{1,0:T(8,128)(2,1)}, u32[]{:S(2)}, u32[]{:S(2)}) collective-permute-start(bf16[160,3200]{1,0:T(8,128)(2,1)} %collective-permute-done.11.refs_1_), channel_id=1, source_target_pairs={{0,16},{16,0},{1,17},{17,1},{2,18},{18,2},{3,19},{19,3},{4,20},{20... | collective-permute-start | bytes 3072008 | tf_op jit(solution)/shard_map/ppermute | solution.py:17
  105.7 35.9 %collective-permute-start.19 = (bf16[160,3200]{1,0:T(8,128)(2,1)}, bf16[160,3200]{1,0:T(8,128)(2,1)}, u32[]{:S(2)}, u32[]{:S(2)}) collective-permute-start(bf16[160,3200]{1,0:T(8,128)(2,1)} %collective-permute-done.12.refs_3_), channel_id=1, source_target_pairs={{0,16},{16,0},{1,17},{17,1},{2,18},{18,2},{3,19},{19,3},{4,20},{20... | collective-permute-start | bytes 3072008 | tf_op jit(solution)/shard_map/ppermute | solution.py:17
  105.7 35.8 %collective-permute-start.18 = (bf16[160,3200]{1,0:T(8,128)(2,1)}, bf16[160,3200]{1,0:T(8,128)(2,1)}, u32[]{:S(2)}, u32[]{:S(2)}) collective-permute-start(bf16[160,3200]{1,0:T(8,128)(2,1)} %collective-permute-done.16.refs_2_), channel_id=1, source_target_pairs={{0,16},{16,0},{1,17},{17,1},{2,18},{18,2},{3,19},{19,3},{4,20},{20... | collective-permute-start | bytes 3072008 | tf_op jit(solution)/shard_map/ppermute | solution.py:17
  118.3 33.7 %copy-start.3 = (bf16[8,192,256]{2,1,0:T(8,128)(2,1)}, bf16[8,192,256]{2,1,0:T(8,128)(2,1)S(1)}, u32[]{:S(2)}) copy-start(bf16[8,192,256]{2,1,0:T(8,128)(2,1)S(1)} %all-to-all-done.2.refs_8_) | copy-start | bytes 2359300
  118.3 20.3 %collective-permute-start.20 = (bf16[8,192,256]{2,1,0:T(8,128)(2,1)S(1)}, bf16[8,192,256]{2,1,0:T(8,128)(2,1)S(1)}, u32[]{:S(2)}, u32[]{:S(2)}) collective-permute-start(bf16[8,192,256]{2,1,0:T(8,128)(2,1)S(1)} %all-to-all-done.2.refs_8_), channel_id=1, source_target_pairs={{0,1},{1,128},{128,129},{129,0},{2,3},{3,130},{130,131},{131,2},{4... | collective-permute-start | bytes 2359304 | tf_op jit(solution)/shard_map/ppermute | solution.py:17
  118.3 20.4 %collective-permute-start.21 = (bf16[8,192,256]{2,1,0:T(8,128)(2,1)S(1)}, bf16[8,192,256]{2,1,0:T(8,128)(2,1)S(1)}, u32[]{:S(2)}, u32[]{:S(2)}) collective-permute-start(bf16[8,192,256]{2,1,0:T(8,128)(2,1)S(1)} %all-to-all-done.2.refs_8_), channel_id=1, source_target_pairs={{0,129},{1,0},{128,1},{129,128},{2,131},{3,2},{130,3},{131,130},{4... | collective-permute-start | bytes 2359304 | tf_op jit(solution)/shard_map/ppermute | solution.py:17
  138.6 13.3 %copy-start.6 = (bf16[8,192,256]{2,1,0:T(8,128)(2,1)}, bf16[8,192,256]{2,1,0:T(8,128)(2,1)S(1)}, u32[]{:S(2)}) copy-start(bf16[8,192,256]{2,1,0:T(8,128)(2,1)S(1)} %collective-permute-done.20.refs_9_) | copy-start | bytes 2359300
  138.6 20.6 %collective-permute-start.22 = (bf16[4,192,256]{2,1,0:T(8,128)(2,1)S(1)}, bf16[4,192,256]{2,1,0:T(8,128)(2,1)S(1)}, u32[]{:S(2)}, u32[]{:S(2)}) collective-permute-start(bf16[4,192,256]{2,1,0:T(8,128)(2,1)S(1)} %slice.28), channel_id=1, source_target_pairs={{0,1},{1,128},{128,129},{129,0},{2,3},{3,130},{130,131},{131,2},{4... | collective-permute-start | bytes 1179656 | tf_op jit(solution)/shard_map/ppermute | solution.py:17
  138.7 13.2 %copy-start.7 = (bf16[8,192,256]{2,1,0:T(8,128)(2,1)}, bf16[8,192,256]{2,1,0:T(8,128)(2,1)S(1)}, u32[]{:S(2)}) copy-start(bf16[8,192,256]{2,1,0:T(8,128)(2,1)S(1)} %collective-permute-done.21.refs_10_) | copy-start | bytes 2359300
  138.8 20.5 %collective-permute-start.23 = (bf16[4,192,256]{2,1,0:T(8,128)(2,1)S(1)}, bf16[4,192,256]{2,1,0:T(8,128)(2,1)}, u32[]{:S(2)}, u32[]{:S(2)}) collective-permute-start(bf16[4,192,256]{2,1,0:T(8,128)(2,1)S(1)} %slice.29), channel_id=1, source_target_pairs={{0,129},{1,0},{128,1},{129,128},{2,131},{3,2},{130,3},{131,130},{4... | collective-permute-start | bytes 1179656 | tf_op jit(solution)/shard_map/ppermute | solution.py:17
  152.0 18.4 %all-to-all-start.1 = ((bf16[16,160,128]{2,1,0:T(8,128)(2,1)}), bf16[16,160,128]{2,1,0:T(8,128)(2,1)S(1)}, u32[]{:S(2)}, u32[]{:S(2)}) async-start(bf16[16,160,128]{2,1,0:T(8,128)(2,1)} %bitcast.21), calls=%async_computation.1 | async-start | bytes 1310720 | tf_op jit(solution)/shard_map/all_to_all | solution.py:206
  159.2 0.7 copy-start.11

commit v8 on v7

--- a/solution.py
+++ b/solution.py
@@ -177,8 +177,8 @@
     )(pos, meta, *feats)
     held = [sent[0], ring(sent[1], "y", 4, 1), None, ring(sent[3], "y", 4, 3)]
     other = [ring(sent[0], "c", 2, 1)]
-    held[0], far_rows, held[1], held[3], other[0], ws_a[3], ws_a[4] = barrier(
-        (held[0], sent[2], held[1], held[3], other[0], ws_a[3], ws_a[4])
+    held[0], far_rows, held[1], held[3], other[0], ws_a[3], ws_a[4], own_b = barrier(
+        (held[0], sent[2], held[1], held[3], other[0], ws_a[3], ws_a[4], own_b)
     )
     held[2] = ring(far_rows, "y", 4, 2)
     ws_b = spread(own_b)

time: 192 us -> 194 us (1.010)
  starting transfers between devices: 83.7 us -> 64.1 us
  waiting for transfers between devices: 56.4 us -> 74.7 us
  local copies, waits for them, and re-layouts: 3.91 us -> 9.25 us
    ppermute x24, waiting for transfers between devices: 36.5 us -> 54.1 us  [ring(): return lax.ppermute(x, axis, [(i, (i + step) % size) for i in range(size)])]
    ppermute x24, starting transfers between devices: 62.9 us -> 45.9 us  [ring(): return lax.ppermute(x, axis, [(i, (i + step) % size) for i in range(size)])]
    unnamed x24 -> x44, local copies, waits for them, and re-layouts: 0.78 us -> 6.93 us
    all_to_all x1, starting transfers between devices: 7.28 us -> 4.75 us  [body(): lax.all_to_all(act.reshape(16, 2 * MOST, wide), ('y', 'c', 'xl'), split_a...]
  transfers between devices with their start and end apart: 27 -> 27, of which waited for: 9 -> 10; matrix products, arithmetic and copies ran while one was open for 0% -> 0% of each run, Pallas kernels for 11% -> 12%
where the time goes in v8:
time: 194 us; the launch traced here: 193 us
  waiting for transfers between devices  74.7 us (39%)
  starting transfers between devices  64.1 us (33%)
  Pallas kernels  27.8 us (14%)
  blocking collectives  17 us (9%)
  local copies, waits for them, and re-layouts  9.25 us (5%)
    ppermute x24, waiting for transfers between devices, ring(): return lax.ppermute(x, axis, [(i, (i + step) % size) for i in range(size)])  54.1 us
    ppermute x24, starting transfers between devices, ring(): return lax.ppermute(x, axis, [(i, (i + step) % size) for i in range(size)])  45.9 us
    pallas_call x2, Pallas kernels, body(): pl.pallas_call(expert_kernel, out_shape=jax.ShapeDtypeStruct((4, 2, 2, 2...  20.8 us
    all_to_all x2, waiting for transfers between devices, exchange(): return lax.all_to_all(x, 'z', split_axis=0, concat_axis=0, tiled=True)  19.9 us
    all_to_all x1, blocking collectives, body(): lax.all_to_all(act.reshape(16, 2 * MOST, wide), ('y', 'c', 'xl'), split_a...  17 us
    all_to_all x2, starting transfers between devices, exchange(): return lax.all_to_all(x, 'z', split_axis=0, concat_axis=0, tiled=True)  13.4 us
    unnamed x44, local copies, waits for them, and re-layouts  6.93 us
    all_to_all x1, starting transfers between devices, body(): lax.all_to_all(act.reshape(16, 2 * MOST, wide), ('y', 'c', 'xl'), split_a...  4.75 us
  transfers between devices with their start and end apart: 27, of which 10 were waited for; matrix products, arithmetic and copies ran while one was open for 0% of the time, Pallas kernels for 12%

profile of v8, /device:TPU:1, one launch (start us, length us, event | category | flops | bytes accessed | tf_op | source)
XLA Modules:
  0.0 193.3 jit_solution(2386322885181243681)
XLA Ops:
  0.0 0.6 stack.23.pos
  0.6 3.5 %columns.1 = (bf16[8,192,256]{2,1,0:T(8,128)(2,1)}, bf16[8,192,256]{2,1,0:T(8,128)(2,1)}) custom-call(s32[5]{0:T(128)} %stack.23.pos, bf16[1,192,4096]{2,1,0:T(8,128)(2,1)} %gate.1, bf16[1,192,4096]{2,1,0:T(8,128)(2,1)} %up.1), custom_call_target="tpu_custom_call" | custom-call | tf_op jit(solution)/shard_map/columns/pallas_call | solution.py:141
  4.2 9.2 %all-to-all-start = ((bf16[8,192,256]{2,1,0:T(8,128)(2,1)}), bf16[8,192,256]{2,1,0:T(8,128)(2,1)S(1)}, u32[]{:S(2)}, u32[]{:S(2)}) async-start(bf16[8,192,256]{2,1,0:T(8,128)(2,1)} %get-tuple-element.26), calls=%async_computation | async-start | bytes 1572864 | tf_op jit(solution)/shard_map/all_to_all | solution.py:152
  13.4 1.3 collective-permute-start
  14.7 2.3 %collective-permute-done = bf16[2,192,128]{2,1,0:T(8,128)(2,1)S(1)} collective-permute-done((bf16[2,192,128]{2,1,0:T(8,128)(2,1)S(1)}, bf16[2,192,128]{2,1,0:T(8,128)(2,1)S(1)}, u32[]{:S(2)}, u32[]{:S(2)}) %collective-permute-start) | collective-permute-done | bytes 98336 | tf_op jit(solution)/shard_map/ppermute | solution.py:17
  17.0 19.9 %all-to-all-done.refs_8_ = bf16[8,192,256]{2,1,0:T(8,128)(2,1)S(1)} async-done(((bf16[8,192,256]{2,1,0:T(8,128)(2,1)}), bf16[8,192,256]{2,1,0:T(8,128)(2,1)S(1)}, u32[]{:S(2)}, u32[]{:S(2)}) %all-to-all-start) | async-done | bytes 786464 | tf_op jit(solution)/shard_map/all_to_all | solution.py:152
  36.9 1.2 collective-permute-start.9
  38.1 1.5 collective-permute-start.10
  39.6 2.7 %collective-permute-start.1 = (bf16[2,384,128]{2,1,0:T(8,128)(2,1)S(1)}, bf16[2,384,128]{2,1,0:T(8,128)(2,1)S(1)}, u32[]{:S(2)}, u32[]{:S(2)}) collective-permute-start(bf16[2,384,128]{2,1,0:T(8,128)(2,1)S(1)} %pad_maximum_fusion.refs_0_), channel_id=1, source_target_pairs={{0,14},{2,0},{4,2},{6,4},{8,6},{10,8},{12,10},{14,12},{1,15},{3,1}... | collective-permute-start | bytes 589832 | tf_op jit(solution)/shard_map/ppermute | solution.py:17
  42.3 3.9 %collective-permute-done.4.refs_7_ = bf16[2,384,128]{2,1,0:T(8,128)(2,1)S(1)} collective-permute-done((bf16[2,384,128]{2,1,0:T(8,128)(2,1)S(1)}, bf16[2,384,128]{2,1,0:T(8,128)(2,1)S(1)}, u32[]{:S(2)}, u32[]{:S(2)}) %collective-permute-start.4) | collective-permute-done | bytes 196640 | tf_op jit(solution)/shard_map/ppermute | solution.py:17
  46.1 2.7 %collective-permute-start.2 = (bf16[2,384,128]{2,1,0:T(8,128)(2,1)S(1)}, bf16[2,384,128]{2,1,0:T(8,128)(2,1)S(1)}, u32[]{:S(2)}, u32[]{:S(2)}) collective-permute-start(bf16[2,384,128]{2,1,0:T(8,128)(2,1)S(1)} %collective-permute-done.1.refs_1_), channel_id=1, source_target_pairs={{0,14},{2,0},{4,2},{6,4},{8,6},{10,8},{12,10},{14,12},{1,15},{3,1}... | collective-permute-start | bytes 589832 | tf_op jit(solution)/shard_map/ppermute | solution.py:17
  48.8 3.3 %collective-permute-done.5.refs_6_ = bf16[2,384,128]{2,1,0:T(8,128)(2,1)S(1)} collective-permute-done((bf16[2,384,128]{2,1,0:T(8,128)(2,1)S(1)}, bf16[2,384,128]{2,1,0:T(8,128)(2,1)S(1)}, u32[]{:S(2)}, u32[]{:S(2)}) %collective-permute-start.5) | collective-permute-done | bytes 196640 | tf_op jit(solution)/shard_map/ppermute | solution.py:17
  52.2 2.7 %collective-permute-start.3 = (bf16[2,384,128]{2,1,0:T(8,128)(2,1)S(1)}, bf16[2,384,128]{2,1,0:T(8,128)(2,1)S(1)}, u32[]{:S(2)}, u32[]{:S(2)}) collective-permute-start(bf16[2,384,128]{2,1,0:T(8,128)(2,1)S(1)} %collective-permute-done.2.refs_2_), channel_id=1, source_target_pairs={{0,14},{2,0},{4,2},{6,4},{8,6},{10,8},{12,10},{14,12},{1,15},{3,1}... | collective-permute-start | bytes 589832 | tf_op jit(solution)/shard_map/ppermute | solution.py:17
  54.8 3.0 %collective-permute-done.6.refs_5_ = bf16[2,384,128]{2,1,0:T(8,128)(2,1)S(1)} collective-permute-done((bf16[2,384,128]{2,1,0:T(8,128)(2,1)S(1)}, bf16[2,384,128]{2,1,0:T(8,128)(2,1)S(1)}, u32[]{:S(2)}, u32[]{:S(2)}) %collective-permute-start.6) | collective-permute-done | bytes 196640 | tf_op jit(solution)/shard_map/ppermute | solution.py:17
  58.0 2.7 %collective-permute-start.8 = (bf16[1,384,128]{2,1,0:T(8,128)(2,1)S(1)}, bf16[1,384,128]{2,1,0:T(8,128)(2,1)S(1)}, u32[]{:S(2)}, u32[]{:S(2)}) collective-permute-start(bf16[1,384,128]{2,1,0:T(8,128)(2,1)S(1)} %slice.25), channel_id=1, source_target_pairs={{0,14},{2,0},{4,2},{6,4},{8,6},{10,8},{12,10},{14,12},{1,15},{3,1}... | collective-permute-start | bytes 294920 | tf_op jit(solution)/shard_map/ppermute | solution.py:17
  60.7 1.9 collective-permute-done.7
  62.7 0.9 copy-done.7
  63.6 4.2 %all-to-all-start.1 = ((bf16[8,192,256]{2,1,0:T(8,128)(2,1)}), bf16[8,192,256]{2,1,0:T(8,128)(2,1)}, u32[]{:S(2)}, u32[]{:S(2)}) async-start(bf16[8,192,256]{2,1,0:T(8,128)(2,1)} %get-tuple-element.36), calls=%async_computation.1 | async-start | bytes 1572864 | tf_op jit(solution)/shard_map/all_to_all | solution.py:152
  67.9 2.0 %dispatch.1 = (bf16[160,3200]{1,0:T(8,128)(2,1)S(1)}, bf16[160,3200]{1,0:T(8,128)(2,1)S(1)}, bf16[160,3200]{1,0:T(8,128)(2,1)S(1)}, bf16[160,3200]{1,0:T(8,128)(2,1)S(1)}) custom-call(s32[5]{0:T(128)S(1)} %copy-done, f32[4,4,128]{2,1,0:T(4,128)S(1)} %maximum_bitcast_fusion.meta, bf16[2,384,128]{2,1,0:T(8,128)(2,1)S(1)} %pad_maximum_fusion.refs_0_, ...), custom_call_target="tpu_custom_call" | custom-call | tf_op jit(solution)/shard_map/dispatch/pallas_call | solution.py:170
  70.0 1.0 copy-done.2
  71.0 1.3 collective-permute-start.11
  72.3 1.4 collective-permute-start.12
  73.7 6.0 %collective-permute-start.13 = (bf16[160,3200]{1,0:T(8,128)(2,1)S(1)}, bf16[160,3200]{1,0:T(8,128)(2,1)}, u32[]{:S(2)}, u32[]{:S(2)}) collective-permute-start(bf16[160,3200]{1,0:T(8,128)(2,1)S(1)} %get-tuple-element.37.refs_0_), channel_id=1, source_target_pairs={{0,16},{16,0},{1,17},{17,1},{2,18},{18,2},{3,19},{19,3},{4,20},{20... | collective-permute-start | bytes 3072008 | tf_op jit(solution)/shard_map/ppermute | solution.py:17
  79.7 0.5 collective-permute-start.14
  80.3 2.3 %collective-permute-start.15 = (bf16[4,192,256]{2,1,0:T(8,128)(2,1)S(1)}, bf16[4,192,256]{2,1,0:T(8,128)(2,1)S(1)}, u32[]{:S(2)}, u32[]{:S(2)}) collective-permute-start(bf16[4,192,256]{2,1,0:T(8,128)(2,1)S(1)} %slice.27), channel_id=1, source_target_pairs={{0,129},{1,0},{128,1},{129,128},{2,131},{3,2},{130,3},{131,130},{4... | collective-permute-start | bytes 1179656 | tf_op jit(solution)/shard_map/ppermute | solution.py:17
  82.6 9.2 %collective-permute-done.14.refs_11_ = bf16[4,192,256]{2,1,0:T(8,128)(2,1)S(1)} collective-permute-done((bf16[4,192,256]{2,1,0:T(8,128)(2,1)S(1)}, bf16[4,192,256]{2,1,0:T(8,128)(2,1)S(1)}, u32[]{:S(2)}, u32[]{:S(2)}) %collective-permute-start.14) | collective-permute-done | bytes 393248 | tf_op jit(solution)/shard_map/ppermute | solution.py:17
  91.8 0.8 copy-done.21
  92.6 0.3 copy-done.14
  93.0 1.0 copy-done.15
  93.9 1.9 collective-permute-start.16
  95.8 5.9 %collective-permute-start.17 = (bf16[160,3200]{1,0:T(8,128)(2,1)}, bf16[160,3200]{1,0:T(8,128)(2,1)S(1)}, u32[]{:S(2)}, u32[]{:S(2)}) collective-permute-start(bf16[160,3200]{1,0:T(8,128)(2,1)} %copy-done.14), channel_id=1, source_target_pairs={{0,16},{16,0},{1,17},{17,1},{2,18},{18,2},{3,19},{19,3},{4,20},{20... | collective-permute-start | bytes 3072008 | tf_op jit(solution)/shard_map/ppermute | solution.py:17
  101.7 12.6 %collective-permute-done.16.refs_2_ = bf16[160,3200]{1,0:T(8,128)(2,1)S(1)} collective-permute-done((bf16[160,3200]{1,0:T(8,128)(2,1)S(1)}, bf16[160,3200]{1,0:T(8,128)(2,1)S(1)}, u32[]{:S(2)}, u32[]{:S(2)}) %collective-permute-start.16) | collective-permute-done | bytes 1024032 | tf_op jit(solution)/shard_map/ppermute | solution.py:17
  114.3 6.2 %collective-permute-start.18 = (bf16[160,3200]{1,0:T(8,128)(2,1)S(1)}, bf16[160,3200]{1,0:T(8,128)(2,1)S(1)}, u32[]{:S(2)}, u32[]{:S(2)}) collective-permute-start(bf16[160,3200]{1,0:T(8,128)(2,1)S(1)} %collective-permute-done.16.refs_2_), channel_id=1, source_target_pairs={{0,16},{16,0},{1,17},{17,1},{2,18},{18,2},{3,19},{19,3},{4,20},{20... | collective-permute-start | bytes 3072008 | tf_op jit(solution)/shard_map/ppermute | solution.py:17
  120.6 0.2 collective-permute-start.20
  120.8 2.5 %collective-permute-start.21 = (bf16[8,192,256]{2,1,0:T(8,128)(2,1)}, bf16[8,192,256]{2,1,0:T(8,128)(2,1)S(1)}, u32[]{:S(2)}, u32[]{:S(2)}) collective-permute-start(bf16[8,192,256]{2,1,0:T(8,128)(2,1)} %all-to-all-done.1.refs_8_), channel_id=1, source_target_pairs={{0,129},{1,0},{128,1},{129,128},{2,131},{3,2},{130,3},{131,130},{4... | collective-permute-start | bytes 2359304 | tf_op jit(solution)/shard_map/ppermute | solution.py:17
  123.2 17.9 %collective-permute-done.20.refs_9_ = bf16[8,192,256]{2,1,0:T(8,128)(2,1)S(1)} collective-permute-done((bf16[8,192,256]{2,1,0:T(8,128)(2,1)}, bf16[8,192,256]{2,1,0:T(8,128)(2,1)S(1)}, u32[]{:S(2)}, u32[]{:S(2)}) %collective-permute-start.20) | collective-permute-done | bytes 786464 | tf_op jit(solution)/shard_map/ppermute | solution.py:17
  141.2 0.1 collective-permute-start.22
  141.3 2.7 %collective-permute-start.23 = (bf16[4,192,256]{2,1,0:T(8,128)(2,1)S(1)}, bf16[4,192,256]{2,1,0:T(8,128)(2,1)}, u32[]{:S(2)}, u32[]{:S(2)}) collective-permute-start(bf16[4,192,256]{2,1,0:T(8,128)(2,1)S(1)} %slice.29), channel_id=1, source_target_pairs={{0,129},{1,0},{128,1},{129,128},{2,131},{3,2},{130,3},{131,130},{4... | collective-permute-start | bytes 1179656 | tf_op jit(solution)/shard_map/ppermute | solution.py:17
  144.1 1.0 copy-done.17
  145.1 1.0 copy-done.18
  146.0 1.0 copy-done.19
  147.0 10.4 %expert.2 = bf16[4,2,2,160,128]{4,3,2,1,0:T(8,128)(2,1)} custom-call(s32[5]{0:T(128)} %stack.23.pos, bf16[160,3200]{1,0:T(8,128)(2,1)} %copy-done.1, bf16[160,3200]{1,0:T(8,128)(2,1)} %copy-done.14, bf16[160,3200]{1,0:T(8,128)(2,1)} %copy-done.16, bf16[160,3200]{1,0:T(8,128)(2,1)} %copy-done.15, bf16[160,3200]{1,0:T(8,128)(2,1)} %collective-permute-done.13.refs_4_, ...), custom_call_target="tpu_custom_call" | custom-call | flops 4026531840 | bytes 12582912 | tf_op jit(solution)/shard_map/expert/pallas_call | solution.py:189
  157.4 4.7 %all-to-all-start.2 = ((bf16[16,160,128]{2,1,0:T(8,128)(2,1)}), bf16[16,160,128]{2,1,0:T(8,128)(2,1)S(1)}, u32[]{:S(2)}, u32[]{:S(2)}) async-start(bf16[16,160,128]{2,1,0:T(8,128)(2,1)} %bitcast.21), calls=%async_computation.2 | async-start | bytes 1310720 | tf_op jit(solution)/shard_map/all_to_all | solution.py:206
  162.2 10.4 %expert.3 = bf16[4,2,2,160,128]{4,3,2,1,0:T(8,128)(2,1)} custom-call(s32[5]{0:T(128)} %stack.23.pos, bf16[160,3200]{1,0:T(8,128)(2,1)} %copy-done.1, bf16[160,3200]{1,0:T(8,128)(2,1)} %copy-done.14, bf16[160,3200]{1,0:T(8,128)(2,1)} %copy-done.16, bf16[160,3200]{1,0:T(8,128)(2,1)} %copy-done.15, bf16[160,3200]{1,0:T(8,128)(2,1)} %collective-permute-done.13.refs_4_, ...), custom_call_target="tpu_custom_call" | custom-call | flops 4026531840 | bytes 12582912 | tf_op jit(solution)/shard_map/expert/pallas_call | solution.py:189
  172.6 0.7 all-to-all-done.2
  173.3 17.0 %all_to_all.20 = bf16[16,160,128]{2,1,0:T(8,128)(2,1)S(1)} all-to-all(bf16[16,160,128]{2,1,0:T(8,128)(2,1)} %bitcast.22), channel_id=1, replica_groups=mesh['dp'=2,'y'=4,'c'=2,'z'=8,'xl'=2] {'y','c','xl'}, dimensions={0} | all-to-all | bytes 1310720 | tf_op jit(solution)/shard_map/all_to_all | solution.py:206
  190.3 1.4 combine.1
  191.7 1.6 reshape.23
  (70 shorter events, 0.4 us)
Async XLA Ops:
  4.1 9.2 %copy-start.11 = (bf16[4,128,192]{1,2,0:T(8,128)(2,1)S(1)}, bf16[4,128,192]{1,2,0:T(8,128)(2,1)}, u32[]{:S(2)}) copy-start(bf16[4,128,192]{1,2,0:T(8,128)(2,1)} %param.5) | copy-start | bytes 589828
  4.2 32.7 %all-to-all-start = ((bf16[8,192,256]{2,1,0:T(8,128)(2,1)}), bf16[8,192,256]{2,1,0:T(8,128)(2,1)S(1)}, u32[]{:S(2)}, u32[]{:S(2)}) async-start(bf16[8,192,256]{2,1,0:T(8,128)(2,1)} %get-tuple-element.26), calls=%async_computation | async-start | bytes 1572864 | tf_op jit(solution)/shard_map/all_to_all | solution.py:152
  13.3 54.5 %copy-start.12 = (s32[4,128,2]{1,2,0:T(2,128)S(1)}, s32[4,128,2]{1,2,0:T(2,128)}, u32[]{:S(2)}) copy-start(s32[4,128,2]{1,2,0:T(2,128)} %param.6) | copy-start | bytes 12292
  13.3 54.5 %copy-start.13 = (f32[4,128,2]{1,2,0:T(2,128)S(1)}, f32[4,128,2]{1,2,0:T(2,128)}, u32[]{:S(2)}) copy-start(f32[4,128,2]{1,2,0:T(2,128)} %param.7) | copy-start | bytes 12292
  13.4 3.6 %collective-permute-start = (bf16[2,192,128]{2,1,0:T(8,128)(2,1)S(1)}, bf16[2,192,128]{2,1,0:T(8,128)(2,1)S(1)}, u32[]{:S(2)}, u32[]{:S(2)}) collective-permute-start(bf16[2,192,128]{2,1,0:T(8,128)(2,1)S(1)} %dynamic-slice_bitcast_fusion), channel_id=1, source_target_pairs={{0,1},{1,0},{2,3},{3,2},{4,5},{5,4},{6,7},{7,6},{8,9},{9,8},{10,11... | collective-permute-start | bytes 294920 | tf_op jit(solution)/shard_map/ppermute | solution.py:17
  14.7 53.2 %copy-start = (s32[5]{0:T(128)S(1)}, s32[5]{0:T(128)}, u32[]{:S(2)}) copy-start(s32[5]{0:T(128)} %stack.23.pos) | copy-start | bytes 64
  36.9 33.1 %copy-start.4 = (bf16[8,192,256]{2,1,0:T(8,128)(2,1)}, bf16[8,192,256]{2,1,0:T(8,128)(2,1)S(1)}, u32[]{:S(2)}) copy-start(bf16[8,192,256]{2,1,0:T(8,128)(2,1)S(1)} %all-to-all-done.refs_8_) | copy-start | bytes 2359300
  36.9 25.8 %collective-permute-start.9 = (bf16[8,192,256]{2,1,0:T(8,128)(2,1)S(1)}, bf16[8,192,256]{2,1,0:T(8,128)(2,1)S(1)}, u32[]{:S(2)}, u32[]{:S(2)}) collective-permute-start(bf16[8,192,256]{2,1,0:T(8,128)(2,1)S(1)} %all-to-all-done.refs_8_), channel_id=1, source_target_pairs={{0,1},{1,128},{128,129},{129,0},{2,3},{3,130},{130,131},{131,2},{4... | collective-permute-start | bytes 2359304 | tf_op jit(solution)/shard_map/ppermute | solution.py:17
  38.1 24.6 %collective-permute-start.10 = (bf16[8,192,256]{2,1,0:T(8,128)(2,1)S(1)}, bf16[8,192,256]{2,1,0:T(8,128)(2,1)S(1)}, u32[]{:S(2)}, u32[]{:S(2)}) collective-permute-start(bf16[8,192,256]{2,1,0:T(8,128)(2,1)S(1)} %all-to-all-done.refs_8_), channel_id=1, source_target_pairs={{0,129},{1,0},{128,1},{129,128},{2,131},{3,2},{130,3},{131,130},{4... | collective-permute-start | bytes 2359304 | tf_op jit(solution)/shard_map/ppermute | solution.py:17
  39.6 6.6 %collective-permute-start.4 = (bf16[2,384,128]{2,1,0:T(8,128)(2,1)S(1)}, bf16[2,384,128]{2,1,0:T(8,128)(2,1)S(1)}, u32[]{:S(2)}, u32[]{:S(2)}) collective-permute-start(bf16[2,384,128]{2,1,0:T(8,128)(2,1)S(1)} %pad_maximum_fusion.refs_0_), channel_id=1, source_target_pairs={{0,2},{2,4},{4,6},{6,8},{8,10},{10,12},{12,14},{14,0},{1,3},{3,5},... | collective-permute-start | bytes 589832 | tf_op jit(solution)/shard_map/ppermute | solution.py:17
  39.6 6.6 %collective-permute-start.1 = (bf16[2,384,128]{2,1,0:T(8,128)(2,1)S(1)}, bf16[2,384,128]{2,1,0:T(8,128)(2,1)S(1)}, u32[]{:S(2)}, u32[]{:S(2)}) collective-permute-start(bf16[2,384,128]{2,1,0:T(8,128)(2,1)S(1)} %pad_maximum_fusion.refs_0_), channel_id=1, source_target_pairs={{0,14},{2,0},{4,2},{6,4},{8,6},{10,8},{12,10},{14,12},{1,15},{3,1}... | collective-permute-start | bytes 589832 | tf_op jit(solution)/shard_map/ppermute | solution.py:17
  46.1 6.0 %collective-permute-start.5 = (bf16[2,384,128]{2,1,0:T(8,128)(2,1)S(1)}, bf16[2,384,128]{2,1,0:T(8,128)(2,1)S(1)}, u32[]{:S(2)}, u32[]{:S(2)}) collective-permute-start(bf16[2,384,128]{2,1,0:T(8,128)(2,1)S(1)} %collective-permute-done.4.refs_7_), channel_id=1, source_target_pairs={{0,2},{2,4},{4,6},{6,8},{8,10},{10,12},{12,14},{14,0},{1,3},{3,5},... | collective-permute-start | bytes 589832 | tf_op jit(solution)/shard_map/ppermute | solution.py:17
  46.1 6.0 %collective-permute-start.2 = (bf16[2,384,128]{2,1,0:T(8,128)(2,1)S(1)}, bf16[2,384,128]{2,1,0:T(8,128)(2,1)S(1)}, u32[]{:S(2)}, u32[]{:S(2)}) collective-permute-start(bf16[2,384,128]{2,1,0:T(8,128)(2,1)S(1)} %collective-permute-done.1.refs_1_), channel_id=1, source_target_pairs={{0,14},{2,0},{4,2},{6,4},{8,6},{10,8},{12,10},{14,12},{1,15},{3,1}... | collective-permute-start | bytes 589832 | tf_op jit(solution)/shard_map/ppermute | solution.py:17
  52.2 5.7 %collective-permute-start.6 = (bf16[2,384,128]{2,1,0:T(8,128)(2,1)S(1)}, bf16[2,384,128]{2,1,0:T(8,128)(2,1)S(1)}, u32[]{:S(2)}, u32[]{:S(2)}) collective-permute-start(bf16[2,384,128]{2,1,0:T(8,128)(2,1)S(1)} %collective-permute-done.5.refs_6_), channel_id=1, source_target_pairs={{0,2},{2,4},{4,6},{6,8},{8,10},{10,12},{12,14},{14,0},{1,3},{3,5},... | collective-permute-start | bytes 589832 | tf_op jit(solution)/shard_map/ppermute | solution.py:17
  52.2 5.8 %collective-permute-start.3 = (bf16[2,384,128]{2,1,0:T(8,128)(2,1)S(1)}, bf16[2,384,128]{2,1,0:T(8,128)(2,1)S(1)}, u32[]{:S(2)}, u32[]{:S(2)}) collective-permute-start(bf16[2,384,128]{2,1,0:T(8,128)(2,1)S(1)} %collective-permute-done.2.refs_2_), channel_id=1, source_target_pairs={{0,14},{2,0},{4,2},{6,4},{8,6},{10,8},{12,10},{14,12},{1,15},{3,1}... | collective-permute-start | bytes 589832 | tf_op jit(solution)/shard_map/ppermute | solution.py:17
  57.9 4.8 %collective-permute-start.7 = (bf16[1,384,128]{2,1,0:T(8,128)(2,1)S(1)}, bf16[1,384,128]{2,1,0:T(8,128)(2,1)S(1)}, u32[]{:S(2)}, u32[]{:S(2)}) collective-permute-start(bf16[1,384,128]{2,1,0:T(8,128)(2,1)S(1)} %slice.24), channel_id=1, source_target_pairs={{0,2},{2,4},{4,6},{6,8},{8,10},{10,12},{12,14},{14,0},{1,3},{3,5},... | collective-permute-start | bytes 294920 | tf_op jit(solution)/shard_map/ppermute | solution.py:17
  58.0 4.6 %collective-permute-start.8 = (bf16[1,384,128]{2,1,0:T(8,128)(2,1)S(1)}, bf16[1,384,128]{2,1,0:T(8,128)(2,1)S(1)}, u32[]{:S(2)}, u32[]{:S(2)}) collective-permute-start(bf16[1,384,128]{2,1,0:T(8,128)(2,1)S(1)} %slice.25), channel_id=1, source_target_pairs={{0,14},{2,0},{4,2},{6,4},{8,6},{10,8},{12,10},{14,12},{1,15},{3,1}... | collective-permute-start | bytes 294920 | tf_op jit(solution)/shard_map/ppermute | solution.py:17
  62.7 5.2 %copy-start.5 = (bf16[8,192,256]{2,1,0:T(8,128)(2,1)}, bf16[8,192,256]{2,1,0:T(8,128)(2,1)S(1)}, u32[]{:S(2)}) copy-start(bf16[8,192,256]{2,1,0:T(8,128)(2,1)S(1)} %collective-permute-done.9.refs_9_) | copy-start | bytes 2359300
  62.7 0.9 copy-start.7
  63.6 30.3 %all-to-all-start.1 = ((bf16[8,192,256]{2,1,0:T(8,128)(2,1)}), bf16[8,192,256]{2,1,0:T(8,128)(2,1)}, u32[]{:S(2)}, u32[]{:S(2)}) async-start(bf16[8,192,256]{2,1,0:T(8,128)(2,1)} %get-tuple-element.36), calls=%async_computation.1 | async-start | bytes 1572864 | tf_op jit(solution)/shard_map/all_to_all | solution.py:152
  67.8 12.5 %copy-start.8 = (bf16[8,192,256]{2,1,0:T(8,128)(2,1)S(1)}, bf16[8,192,256]{2,1,0:T(8,128)(2,1)}, u32[]{:S(2)}) copy-start(bf16[8,192,256]{2,1,0:T(8,128)(2,1)} %copy-done.7) | copy-start | bytes 2359300
  67.9 11.8 %copy-start.6 = (bf16[8,192,256]{2,1,0:T(8,128)(2,1)S(1)}, bf16[8,192,256]{2,1,0:T(8,128)(2,1)}, u32[]{:S(2)}) copy-start(bf16[8,192,256]{2,1,0:T(8,128)(2,1)} %copy-done.5) | copy-start | bytes 2359300
  70.0 1.0 copy-start.2
  71.0 70.4 %copy-start.1 = (bf16[160,3200]{1,0:T(8,128)(2,1)}, bf16[160,3200]{1,0:T(8,128)(2,1)S(1)}, u32[]{:S(2)}) copy-start(bf16[160,3200]{1,0:T(8,128)(2,1)S(1)} %get-tuple-element.37.refs_0_) | copy-start | bytes 3072004
  71.0 22.9 %copy-start.3 = (bf16[160,3200]{1,0:T(8,128)(2,1)S(1)}, bf16[160,3200]{1,0:T(8,128)(2,1)}, u32[]{:S(2)}) copy-start(bf16[160,3200]{1,0:T(8,128)(2,1)} %copy-done.2) | copy-start | bytes 3072004
  71.0 20.8 %collective-permute-start.11 = (bf16[160,3200]{1,0:T(8,128)(2,1)S(1)}, bf16[160,3200]{1,0:T(8,128)(2,1)S(1)}, u32[]{:S(2)}, u32[]{:S(2)}) collective-permute-start(bf16[160,3200]{1,0:T(8,128)(2,1)S(1)} %get-tuple-element.34), channel_id=1, source_target_pairs={{0,32},{32,64},{64,96},{96,0},{1,33},{33,65},{65,97},{97,1},{2,34}... | collective-permute-start | bytes 3072008 | tf_op jit(solution)/shard_map/ppermute | solution.py:17
  72.3 19.5 %collective-permute-start.12 = (bf16[160,3200]{1,0:T(8,128)(2,1)S(1)}, bf16[160,3200]{1,0:T(8,128)(2,1)S(1)}, u32[]{:S(2)}, u32[]{:S(2)}) collective-permute-start(bf16[160,3200]{1,0:T(8,128)(2,1)S(1)} %get-tuple-element.35), channel_id=1, source_target_pairs={{0,96},{32,0},{64,32},{96,64},{1,97},{33,1},{65,33},{97,65},{2,98}... | collective-permute-start | bytes 3072008 | tf_op jit(solution)/shard_map/ppermute | solution.py:17
  73.7 20.2 %collective-permute-start.13 = (bf16[160,3200]{1,0:T(8,128)(2,1)S(1)}, bf16[160,3200]{1,0:T(8,128)(2,1)}, u32[]{:S(2)}, u32[]{:S(2)}) collective-permute-start(bf16[160,3200]{1,0:T(8,128)(2,1)S(1)} %get-tuple-element.37.refs_0_), channel_id=1, source_target_pairs={{0,16},{16,0},{1,17},{17,1},{2,18},{18,2},{3,19},{19,3},{4,20},{20... | collective-permute-start | bytes 3072008 | tf_op jit(solution)/shard_map/ppermute | solution.py:17
  79.7 12.0 %collective-permute-start.14 = (bf16[4,192,256]{2,1,0:T(8,128)(2,1)S(1)}, bf16[4,192,256]{2,1,0:T(8,128)(2,1)S(1)}, u32[]{:S(2)}, u32[]{:S(2)}) collective-permute-start(bf16[4,192,256]{2,1,0:T(8,128)(2,1)S(1)} %slice.26), channel_id=1, source_target_pairs={{0,1},{1,128},{128,129},{129,0},{2,3},{3,130},{130,131},{131,2},{4... | collective-permute-start | bytes 1179656 | tf_op jit(solution)/shard_map/ppermute | solution.py:17
  80.3 11.5 %collective-permute-start.15 = (bf16[4,192,256]{2,1,0:T(8,128)(2,1)S(1)}, bf16[4,192,256]{2,1,0:T(8,128)(2,1)S(1)}, u32[]{:S(2)}, u32[]{:S(2)}) collective-permute-start(bf16[4,192,256]{2,1,0:T(8,128)(2,1)S(1)} %slice.27), channel_id=1, source_target_pairs={{0,129},{1,0},{128,1},{129,128},{2,131},{3,2},{130,3},{131,130},{4... | collective-permute-start | bytes 1179656 | tf_op jit(solution)/shard_map/ppermute | solution.py:17
  91.8 54.2 %copy-start.20 = (bf16[4,192,256]{2,1,0:T(8,128)(2,1)}, bf16[4,192,256]{2,1,0:T(8,128)(2,1)S(1)}, u32[]{:S(2)}) copy-start(bf16[4,192,256]{2,1,0:T(8,128)(2,1)S(1)} %collective-permute-done.14.refs_11_) | copy-start | bytes 1179652
  91.8 1.2 copy-start.14
  93.0 1.0 copy-start.15
  93.9 20.4 %collective-permute-start.16 = (bf16[160,3200]{1,0:T(8,128)(2,1)S(1)}, bf16[160,3200]{1,0:T(8,128)(2,1)S(1)}, u32[]{:S(2)}, u32[]{:S(2)}) collective-permute-start(bf16[160,3200]{1,0:T(8,128)(2,1)S(1)} %copy-done.3), channel_id=1, source_target_pairs={{0,64},{32,96},{64,0},{96,32},{1,65},{33,97},{65,1},{97,33},{2,66}... | collective-permute-start | bytes 3072008 | tf_op jit(solution)/shard_map/ppermute | solution.py:17
  95.8 48.3 %collective-permute-start.17 = (bf16[160,3200]{1,0:T(8,128)(2,1)}, bf16[160,3200]{1,0:T(8,128)(2,1)S(1)}, u32[]{:S(2)}, u32[]{:S(2)}) collective-permute-start(bf16[160,3200]{1,0:T(8,128)(2,1)} %copy-done.14), channel_id=1, source_target_pairs={{0,16},{16,0},{1,17},{17,1},{2,18},{18,2},{3,19},{19,3},{4,20},{20... | collective-permute-start | bytes 3072008 | tf_op jit(solution)/shard_map/ppermute | solution.py:17
  101.7 43.3 %collective-permute-start.19 = (bf16[160,3200]{1,0:T(8,128)(2,1)}, bf16[160,3200]{1,0:T(8,128)(2,1)S(1)}, u32[]{:S(2)}, u32[]{:S(2)}) collective-permute-start(bf16[160,3200]{1,0:T(8,128)(2,1)} %copy-done.15), channel_id=1, source_target_pairs={{0,16},{16,0},{1,17},{17,1},{2,18},{18,2},{3,19},{19,3},{4,20},{20... | collective-permute-start | bytes 3072008 | tf_op jit(solution)/shard_map/ppermute | solution.py:17
  114.3 31.7 %copy-start.16 = (bf16[160,3200]{1,0:T(8,128)(2,1)}, bf16[160,3200]{1,0:T(8,128)(2,1)S(1)}, u32[]{:S(2)}) copy-start(bf16[160,3200]{1,0:T(8,128)(2,1)S(1)} %collective-permute-done.16.refs_2_) | copy-start | bytes 3072004
  114.3 31.7 %collective-permute-start.18 = (bf16[160,3200]{1,0:T(8,128)(2,1)S(1)}, bf16[160,3200]{1,0:T(8,128)(2,1)S(1)}, u32[]{:S(2)}, u32[]{:S(2)}) collective-permute-start(bf16[160,3200]{1,0:T(8,128)(2,1)S(1)} %collective-permute-done.16.refs_2_), channel_id=1, source_target_pairs={{0,16},{16,0},{1,17},{17,1},{2,18},{18,2},{3,19},{19,3},{4,20},{20... | collective-permute-start | bytes 3072008 | tf_op jit(solution)/shard_map/ppermute | solution.py:17
  120.6 20.6 %collective-permute-start.20 = (bf16[8,192,256]{2,1,0:T(8,128)(2,1)}, bf16[8,192,256]{2,1,0:T(8,128)(2,1)S(1)}, u32[]{:S(2)}, u32[]{:S(2)}) collective-permute-start(bf16[8,192,256]{2,1,0:T(8,128)(2,1)} %all-to-all-done.1.refs_8_), channel_id=1, source_target_pairs={{0,1},{1,128},{128,129},{129,0},{2,3},{3,130},{130,131},{131,2},{4... | collective-permute-start | bytes 2359304 | tf_op jit(solution)/shard_map/ppermute | solution.py:17
  120.8 20.5 %collective-permute-start.21 = (bf16[8,192,256]{2,1,0:T(8,128)(2,1)}, bf16[8,192,256]{2,1,0:T(8,128)(2,1)S(1)}, u32[]{:S(2)}, u32[]{:S(2)}) collective-permute-start(bf16[8,192,256]{2,1,0:T(8,128)(2,1)} %all-to-all-done.1.refs_8_), channel_id=1, source_target_pairs={{0,129},{1,0},{128,1},{129,128},{2,131},{3,2},{130,3},{131,130},{4... | collective-permute-start | bytes 2359304 | tf_op jit(solution)/shard_map/ppermute | solution.py:17
  141.2 16.2 %copy-start.9 = (bf16[8,192,256]{2,1,0:T(8,128)(2,1)}, bf16[8,192,256]{2,1,0:T(8,128)(2,1)S(1)}, u32[]{:S(2)}) copy-start(bf16[8,192,256]{2,1,0:T(8,128)(2,1)S(1)} %collective-permute-done.20.refs_9_) | copy-start | bytes 2359300
  141.2 21.0 %collective-permute-start.22 = (bf16[4,192,256]{2,1,0:T(8,128)(2,1)S(1)}, bf16[4,192,256]{2,1,0:T(8,128)(2,1)}, u32[]{:S(2)}, u32[]{:S(2)}) collective-permute-start(bf16[4,192,256]{2,1,0:T(8,128)(2,1)S(1)} %slice.28), channel_id=1, source_target_pairs={{0,1},{1,128},{128,129},{129,0},{2,3},{3,130},{130,131},{131,2},{4... | collective-permute-start | bytes 1179656 | tf_op jit(solution)/shard_map/ppermute | solution.py:17
  141.3 2.8 %copy-start.10 = (bf16[8,192,256]{2,1,0:T(8,128)(2,1)}, bf16[8,192,256]{2,1,0:T(8,128)(2,1)S(1)}, u32[]{:S(2)}) copy-start(bf16[8,192,256]{2,1,0:T(8,128)(2,1)S(1)} %collective-permute-done.21.refs_10_) | copy-start | bytes 2359300
  141.3 20.8 %collective-permute-start.23 = (bf16[4,192,256]{2,1,0:T(8,128)(2,1)S(1)}, bf16[4,192,256]{2,1,0:T(8,128)(2,1)}, u32[]{:S(2)}, u32[]{:S(2)}) collective-permute-start(bf16[4,192,256]{2,1,0:T(8,128)(2,1)S(1)} %slice.29), channel_id=1, source_target_pairs={{0,129},{1,0},{128,1},{129,128},{2,131},{3,2},{130,3},{131,130},{4... | collective-permute-start | bytes 1179656 | tf_op jit(solution)/shard_map/ppermute | solution.py:17
  144.1 1.0 copy-start.17
  145.1 1.0 copy-start.18
  146.0 1.0 copy-start.19
  157.4 15.9 %all-to-all-start.2 = ((bf16[16,160,128]{2,1,0:T(8,128)(2,1)}), bf16[16,160,128]{2,1,0:T(8,128)(2,1)S(1)}, u32[]{:S(2)}, u32[]{:S(2)}) async-start(bf16[16,160,128]{2,1,0:T(8,128)(2,1)} %bitcast.21), calls=%async_computation.2 | async-start | bytes 1310720 | tf_op jit(solution)/shard_map/all_to_all | solution.py:206
  (1 other events, 0.8 us)

commit v9 on v8

--- a/solution.py
+++ b/solution.py
@@ -151,22 +151,20 @@
     def exchange(x):
         return lax.all_to_all(x, "z", split_axis=0, concat_axis=0, tiled=True)
 
-    def spread(own):
-        left, right = ring(own, X, 4, 1), ring(own, X, 4, -1)
-        return [own, left, right, ring(left[:4], X, 4, 1), ring(right[4:], X, 4, -1)]
-
-    own_a, pair = barrier((exchange(blocks[0]), pair))
-    ws_a = spread(own_a)
+    def sides(own):
+        return ring(own, X, 4, 1), ring(own, X, 4, -1)
+
+    def far(left, right):
+        return ring(left[:4], X, 4, 1), ring(right[4:], X, 4, -1)
+
     below, above = [pair], [pair]
     for k in range(3):
         below.append(ring(below[-1], "z", 8, 1))
         above.append(ring(above[-1], "z", 8, -1))
-    *last, ws_a[1], ws_a[2] = barrier(
-        (blocks[1], ring(below[3][:1], "z", 8, 1), ring(above[3][1:], "z", 8, -1), ws_a[1], ws_a[2])
-    )
-    opposite = jnp.concatenate(last[1:], axis=0)
+    part_a, below[3], above[3] = barrier((blocks[0], below[3], above[3]))
+    own_a = exchange(part_a)
+    opposite = jnp.concatenate([ring(below[3][:1], "z", 8, 1), ring(above[3][1:], "z", 8, -1)], axis=0)
     feats = [pair] + above[1:] + [opposite] + below[:0:-1]
-    own_b = exchange(last[0])
     sent = pl.pallas_call(
         dispatch_kernel,
         out_shape=[jax.ShapeDtypeStruct((2 * MOST, 16 * width + 128), BF)] * 4,
@@ -175,18 +173,20 @@
         compiler_params=pltpu.CompilerParams(vmem_limit_bytes=24 << 20),
         name="dispatch",
     )(pos, meta, *feats)
-    held = [sent[0], ring(sent[1], "y", 4, 1), None, ring(sent[3], "y", 4, 3)]
-    other = [ring(sent[0], "c", 2, 1)]
-    held[0], far_rows, held[1], held[3], other[0], ws_a[3], ws_a[4], own_b = barrier(
-        (held[0], sent[2], held[1], held[3], other[0], ws_a[3], ws_a[4], own_b)
-    )
-    held[2] = ring(far_rows, "y", 4, 2)
-    ws_b = spread(own_b)
-    other += [ring(h, "c", 2, 1) for h in held[1:]]
-    pieces = [ws_a, ws_b]
-    backs = []
-    for ws in pieces:
-        act = pl.pallas_call(
+    near = ring(sent[1], "y", 4, 1), ring(sent[3], "y", 4, 3)
+    part_b, own_a = barrier((blocks[1], own_a))
+    own_b = exchange(part_b)
+    left_a, right_a = sides(own_a)
+    far_rows, *near = barrier((sent[2], *near))
+    held = [sent[0], near[0], ring(far_rows, "y", 4, 2), near[1]]
+    own_b, left_a, right_a, *held = barrier((own_b, left_a, right_a, *held))
+    far_a = far(left_a, right_a)
+    other = [ring(h, "c", 2, 1) for h in held]
+    own_b, *far_a = barrier((own_b, *far_a))
+    left_b, right_b = sides(own_b)
+
+    def expert(*ws):
+        return pl.pallas_call(
             expert_kernel,
             out_shape=jax.ShapeDtypeStruct((4, 2, 2, 2 * MOST, wide), BF),
             in_specs=[SM] + [ANY] * 13,
@@ -203,8 +203,15 @@
             ),
             name="expert",
         )(pos, *held, *other, *ws)
+
+    def give_back(act):
         back = lax.all_to_all(act.reshape(16, 2 * MOST, wide), ("y", "c", "xl"), split_axis=0, concat_axis=0, tiled=True)
-        backs.append(back.reshape(4, 2, 2, 2 * MOST, wide))
+        return back.reshape(4, 2, 2, 2 * MOST, wide)
+
+    act_a = expert(own_a, left_a, right_a, *far_a)
+    left_b, right_b, act_a = barrier((left_b, right_b, act_a))
+    back_a = give_back(act_a)
+    back_b = give_back(expert(own_b, left_b, right_b, *far(left_b, right_b)))
     out = pl.pallas_call(
         combine_kernel,
         out_shape=jax.ShapeDtypeStruct((steps, n, 1024), BF),
@@ -212,7 +219,7 @@
         out_specs=VM,
         compiler_params=pltpu.CompilerParams(vmem_limit_bytes=24 << 20),
         name="combine",
-    )(meta, *backs)
+    )(meta, back_a, back_b)
     return out.reshape(steps, n, 2, 2, 256)
 
 

time: 194 us -> 194 us (level)
  waiting for transfers between devices: 74.7 us -> 68.3 us
  starting transfers between devices: 64.1 us -> 67.5 us
    all_to_all x2, waiting for transfers between devices: 19.9 us -> 0.01 us  [exchange(): return lax.all_to_all(x, 'z', split_axis=0, concat_axis=0, tiled=True)]
    ppermute x24, waiting for transfers between devices: 54.1 us -> 67.7 us  [ring(): return lax.ppermute(x, axis, [(i, (i + step) % size) for i in range(size)])]
    unnamed x44 -> x30, local copies, waits for them, and re-layouts: 6.93 us -> 3.33 us
    all_to_all x1, starting transfers between devices: 4.75 us -> 8.08 us  [give_back(): lax.all_to_all(act.reshape(16, 2 * MOST, wide), ('y', 'c', 'xl'), split_a...]
    ppermute x24, starting transfers between devices: 45.9 us -> 48.1 us  [ring(): return lax.ppermute(x, axis, [(i, (i + step) % size) for i in range(size)])]
    all_to_all x2, starting transfers between devices: 13.4 us -> 11.4 us  [exchange(): return lax.all_to_all(x, 'z', split_axis=0, concat_axis=0, tiled=True)]
    slice x4, local copies, waits for them, and re-layouts: 0.11 us -> 2.09 us  [far(): return (ring(left[:4], X, 4, 1), ring(right[4:], X, 4, -1))]
  transfers between devices with their start and end apart: 27 -> 27, of which waited for: 10 -> 11; matrix products, arithmetic and copies ran while one was open for 0% -> 1% of each run, Pallas kernels for 12% -> 14%
where the time goes in v9:
time: 194 us; the launch traced here: 193 us
  waiting for transfers between devices  68.3 us (35%)
  starting transfers between devices  67.5 us (35%)
  Pallas kernels  29 us (15%)
  blocking collectives  18.6 us (10%)
  local copies, waits for them, and re-layouts  8.58 us (4%)
    ppermute x24, waiting for transfers between devices, ring(): return lax.ppermute(x, axis, [(i, (i + step) % size) for i in range(size)])  67.7 us
    ppermute x24, starting transfers between devices, ring(): return lax.ppermute(x, axis, [(i, (i + step) % size) for i in range(size)])  48.1 us
    pallas_call x2, Pallas kernels, expert(): pl.pallas_call(expert_kernel, out_shape=jax.ShapeDtypeStruct((4, 2, 2, 2...  20.7 us
    all_to_all x1, blocking collectives, give_back(): lax.all_to_all(act.reshape(16, 2 * MOST, wide), ('y', 'c', 'xl'), split_a...  18.6 us
    all_to_all x2, starting transfers between devices, exchange(): return lax.all_to_all(x, 'z', split_axis=0, concat_axis=0, tiled=True)  11.4 us
    all_to_all x1, starting transfers between devices, give_back(): lax.all_to_all(act.reshape(16, 2 * MOST, wide), ('y', 'c', 'xl'), split_a...  8.08 us
  transfers between devices with their start and end apart: 27, of which 11 were waited for; matrix products, arithmetic and copies ran while one was open for 1% of the time, Pallas kernels for 14%

profile of v9, /device:TPU:1, one launch (start us, length us, event | category | flops | bytes accessed | tf_op | source)
XLA Modules:
  0.0 193.3 jit_solution(108146798016989851)
XLA Ops:
  0.0 0.9 dynamic-slice_bitcast_fusion
  0.9 2.0 %collective-permute-start = (bf16[2,192,128]{2,1,0:T(8,128)(2,1)S(1)}, bf16[2,192,128]{2,1,0:T(8,128)(2,1)S(1)}, u32[]{:S(2)}, u32[]{:S(2)}) collective-permute-start(bf16[2,192,128]{2,1,0:T(8,128)(2,1)S(1)} %dynamic-slice_bitcast_fusion), channel_id=1, source_target_pairs={{0,1},{1,0},{2,3},{3,2},{4,5},{5,4},{6,7},{7,6},{8,9},{9,8},{10,11... | collective-permute-start | bytes 294920 | tf_op jit(solution)/shard_map/ppermute | solution.py:17
  2.9 2.0 %collective-permute-done = bf16[2,192,128]{2,1,0:T(8,128)(2,1)S(1)} collective-permute-done((bf16[2,192,128]{2,1,0:T(8,128)(2,1)S(1)}, bf16[2,192,128]{2,1,0:T(8,128)(2,1)S(1)}, u32[]{:S(2)}, u32[]{:S(2)}) %collective-permute-start) | collective-permute-done | bytes 98336 | tf_op jit(solution)/shard_map/ppermute | solution.py:17
  4.9 0.9 bitcast_select_fusion.1
  5.9 2.0 %collective-permute-start.1 = (bf16[2,384,128]{2,1,0:T(8,128)(2,1)S(1)}, bf16[2,384,128]{2,1,0:T(8,128)(2,1)S(1)}, u32[]{:S(2)}, u32[]{:S(2)}) collective-permute-start(bf16[2,384,128]{2,1,0:T(8,128)(2,1)S(1)} %pad_maximum_fusion.refs_0_), channel_id=1, source_target_pairs={{0,2},{2,4},{4,6},{6,8},{8,10},{10,12},{12,14},{14,0},{1,3},{3,5},... | collective-permute-start | bytes 589832 | tf_op jit(solution)/shard_map/ppermute | solution.py:17
  7.8 4.0 %collective-permute-start.4 = (bf16[2,384,128]{2,1,0:T(8,128)(2,1)S(1)}, bf16[2,384,128]{2,1,0:T(8,128)(2,1)S(1)}, u32[]{:S(2)}, u32[]{:S(2)}) collective-permute-start(bf16[2,384,128]{2,1,0:T(8,128)(2,1)S(1)} %pad_maximum_fusion.refs_0_), channel_id=1, source_target_pairs={{0,14},{2,0},{4,2},{6,4},{8,6},{10,8},{12,10},{14,12},{1,15},{3,1}... | collective-permute-start | bytes 589832 | tf_op jit(solution)/shard_map/ppermute | solution.py:17
  11.9 3.3 %collective-permute-done.1.refs_7_ = bf16[2,384,128]{2,1,0:T(8,128)(2,1)S(1)} collective-permute-done((bf16[2,384,128]{2,1,0:T(8,128)(2,1)S(1)}, bf16[2,384,128]{2,1,0:T(8,128)(2,1)S(1)}, u32[]{:S(2)}, u32[]{:S(2)}) %collective-permute-start.1) | collective-permute-done | bytes 196640 | tf_op jit(solution)/shard_map/ppermute | solution.py:17
  15.2 2.7 %collective-permute-start.5 = (bf16[2,384,128]{2,1,0:T(8,128)(2,1)S(1)}, bf16[2,384,128]{2,1,0:T(8,128)(2,1)S(1)}, u32[]{:S(2)}, u32[]{:S(2)}) collective-permute-start(bf16[2,384,128]{2,1,0:T(8,128)(2,1)S(1)} %collective-permute-done.4.refs_1_), channel_id=1, source_target_pairs={{0,14},{2,0},{4,2},{6,4},{8,6},{10,8},{12,10},{14,12},{1,15},{3,1}... | collective-permute-start | bytes 589832 | tf_op jit(solution)/shard_map/ppermute | solution.py:17
  17.9 3.0 %collective-permute-done.2.refs_6_ = bf16[2,384,128]{2,1,0:T(8,128)(2,1)S(1)} collective-permute-done((bf16[2,384,128]{2,1,0:T(8,128)(2,1)S(1)}, bf16[2,384,128]{2,1,0:T(8,128)(2,1)S(1)}, u32[]{:S(2)}, u32[]{:S(2)}) %collective-permute-start.2) | collective-permute-done | bytes 196640 | tf_op jit(solution)/shard_map/ppermute | solution.py:17
  20.9 2.7 %collective-permute-start.6 = (bf16[2,384,128]{2,1,0:T(8,128)(2,1)S(1)}, bf16[2,384,128]{2,1,0:T(8,128)(2,1)S(1)}, u32[]{:S(2)}, u32[]{:S(2)}) collective-permute-start(bf16[2,384,128]{2,1,0:T(8,128)(2,1)S(1)} %collective-permute-done.5.refs_2_), channel_id=1, source_target_pairs={{0,14},{2,0},{4,2},{6,4},{8,6},{10,8},{12,10},{14,12},{1,15},{3,1}... | collective-permute-start | bytes 589832 | tf_op jit(solution)/shard_map/ppermute | solution.py:17
  23.6 0.7 stack.23.pos
  24.3 3.5 %columns.1 = (bf16[8,192,256]{2,1,0:T(8,128)(2,1)}, bf16[8,192,256]{2,1,0:T(8,128)(2,1)}) custom-call(s32[5]{0:T(128)} %stack.23.pos, bf16[1,192,4096]{2,1,0:T(8,128)(2,1)} %gate.1, bf16[1,192,4096]{2,1,0:T(8,128)(2,1)} %up.1), custom_call_target="tpu_custom_call" | custom-call | tf_op jit(solution)/shard_map/columns/pallas_call | solution.py:141
  27.8 5.0 %all-to-all-start = ((bf16[8,192,256]{2,1,0:T(8,128)(2,1)}), bf16[8,192,256]{2,1,0:T(8,128)(2,1)S(1)}, u32[]{:S(2)}, u32[]{:S(2)}) async-start(bf16[8,192,256]{2,1,0:T(8,128)(2,1)} %get-tuple-element.34), calls=%async_computation | async-start | bytes 1572864 | tf_op jit(solution)/shard_map/all_to_all | solution.py:152
  32.8 2.8 %collective-permute-start.10 = (bf16[1,384,128]{2,1,0:T(8,128)(2,1)S(1)}, bf16[1,384,128]{2,1,0:T(8,128)(2,1)S(1)}, u32[]{:S(2)}, u32[]{:S(2)}) collective-permute-start(bf16[1,384,128]{2,1,0:T(8,128)(2,1)S(1)} %slice.19), channel_id=1, source_target_pairs={{0,14},{2,0},{4,2},{6,4},{8,6},{10,8},{12,10},{14,12},{1,15},{3,1}... | collective-permute-start | bytes 294920 | tf_op jit(solution)/shard_map/ppermute | solution.py:17
  35.7 12.5 %collective-permute-done.10 = bf16[1,384,128]{2,1,0:T(8,128)(2,1)S(1)} collective-permute-done((bf16[1,384,128]{2,1,0:T(8,128)(2,1)S(1)}, bf16[1,384,128]{2,1,0:T(8,128)(2,1)S(1)}, u32[]{:S(2)}, u32[]{:S(2)}) %collective-permute-start.10) | collective-permute-done | bytes 98336 | tf_op jit(solution)/shard_map/ppermute | solution.py:17
  48.2 2.2 %collective-permute-done.9 = bf16[1,384,128]{2,1,0:T(8,128)(2,1)S(1)} collective-permute-done((bf16[1,384,128]{2,1,0:T(8,128)(2,1)S(1)}, bf16[1,384,128]{2,1,0:T(8,128)(2,1)S(1)}, u32[]{:S(2)}, u32[]{:S(2)}) %collective-permute-start.9) | collective-permute-done | bytes 98336 | tf_op jit(solution)/shard_map/ppermute | solution.py:17
  50.4 3.3 %dispatch.1 = (bf16[160,3200]{1,0:T(8,128)(2,1)S(1)}, bf16[160,3200]{1,0:T(8,128)(2,1)}, bf16[160,3200]{1,0:T(8,128)(2,1)S(1)}, bf16[160,3200]{1,0:T(8,128)(2,1)}) custom-call(s32[5]{0:T(128)S(1)} %copy-done, f32[4,4,128]{2,1,0:T(4,128)S(1)} %maximum_bitcast_fusion.meta, bf16[2,384,128]{2,1,0:T(8,128)(2,1)S(1)} %pad_maximum_fusion.refs_0_, ...), custom_call_target="tpu_custom_call" | custom-call | tf_op jit(solution)/shard_map/dispatch/pallas_call | solution.py:168
  53.7 1.0 copy-done.2
  54.7 1.3 collective-permute-start.11
  56.0 1.4 collective-permute-start.12
  57.5 6.4 %all-to-all-start.1 = ((bf16[8,192,256]{2,1,0:T(8,128)(2,1)}), bf16[8,192,256]{2,1,0:T(8,128)(2,1)}, u32[]{:S(2)}, u32[]{:S(2)}) async-start(bf16[8,192,256]{2,1,0:T(8,128)(2,1)} %get-tuple-element.35), calls=%async_computation.1 | async-start | bytes 1572864 | tf_op jit(solution)/shard_map/all_to_all | solution.py:152
  63.9 11.8 %collective-permute-done.11.refs_1_ = bf16[160,3200]{1,0:T(8,128)(2,1)} collective-permute-done((bf16[160,3200]{1,0:T(8,128)(2,1)}, bf16[160,3200]{1,0:T(8,128)(2,1)}, u32[]{:S(2)}, u32[]{:S(2)}) %collective-permute-start.11) | collective-permute-done | bytes 1024032 | tf_op jit(solution)/shard_map/ppermute | solution.py:17
  75.6 2.3 %collective-permute-start.13 = (bf16[160,3200]{1,0:T(8,128)(2,1)S(1)}, bf16[160,3200]{1,0:T(8,128)(2,1)}, u32[]{:S(2)}, u32[]{:S(2)}) collective-permute-start(bf16[160,3200]{1,0:T(8,128)(2,1)S(1)} %copy-done.3), channel_id=1, source_target_pairs={{0,64},{32,96},{64,0},{96,32},{1,65},{33,97},{65,1},{97,33},{2,66}... | collective-permute-start | bytes 3072008 | tf_op jit(solution)/shard_map/ppermute | solution.py:17
  78.0 1.2 collective-permute-start.7
  79.2 1.5 collective-permute-start.8
  80.6 12.2 %collective-permute-done.13.refs_2_ = bf16[160,3200]{1,0:T(8,128)(2,1)} collective-permute-done((bf16[160,3200]{1,0:T(8,128)(2,1)S(1)}, bf16[160,3200]{1,0:T(8,128)(2,1)}, u32[]{:S(2)}, u32[]{:S(2)}) %collective-permute-start.13) | collective-permute-done | bytes 1024032 | tf_op jit(solution)/shard_map/ppermute | solution.py:17
  92.8 15.0 %collective-permute-start.18 = (bf16[160,3200]{1,0:T(8,128)(2,1)S(1)}, bf16[160,3200]{1,0:T(8,128)(2,1)S(1)}, u32[]{:S(2)}, u32[]{:S(2)}) collective-permute-start(bf16[160,3200]{1,0:T(8,128)(2,1)S(1)} %get-tuple-element.50.refs_0_), channel_id=1, source_target_pairs={{0,16},{16,0},{1,17},{17,1},{2,18},{18,2},{3,19},{19,3},{4,20},{20... | collective-permute-start | bytes 3072008 | tf_op jit(solution)/shard_map/ppermute | solution.py:17
  107.8 1.0 slice.20
  108.9 1.3 collective-permute-start.14
  110.7 0.3 collective-permute-start.21
  111.0 1.0 slice.21
  112.0 8.9 %collective-permute-done.14.refs_11_ = bf16[4,192,256]{2,1,0:T(8,128)(2,1)S(1)} collective-permute-done((bf16[4,192,256]{2,1,0:T(8,128)(2,1)S(1)}, bf16[4,192,256]{2,1,0:T(8,128)(2,1)S(1)}, u32[]{:S(2)}, u32[]{:S(2)}) %collective-permute-start.14) | collective-permute-done | bytes 393248 | tf_op jit(solution)/shard_map/ppermute | solution.py:17
  120.9 1.5 collective-permute-start.15
  122.4 8.4 %collective-permute-done.15.refs_12_ = bf16[4,192,256]{2,1,0:T(8,128)(2,1)S(1)} collective-permute-done((bf16[4,192,256]{2,1,0:T(8,128)(2,1)S(1)}, bf16[4,192,256]{2,1,0:T(8,128)(2,1)S(1)}, u32[]{:S(2)}, u32[]{:S(2)}) %collective-permute-start.15) | collective-permute-done | bytes 393248 | tf_op jit(solution)/shard_map/ppermute | solution.py:17
  130.8 2.7 %collective-permute-start.17 = (bf16[8,192,256]{2,1,0:T(8,128)(2,1)}, bf16[8,192,256]{2,1,0:T(8,128)(2,1)S(1)}, u32[]{:S(2)}, u32[]{:S(2)}) collective-permute-start(bf16[8,192,256]{2,1,0:T(8,128)(2,1)} %all-to-all-done.1.refs_8_), channel_id=1, source_target_pairs={{0,129},{1,0},{128,1},{129,128},{2,131},{3,2},{130,3},{131,130},{4... | collective-permute-start | bytes 2359304 | tf_op jit(solution)/shard_map/ppermute | solution.py:17
  133.6 0.9 copy-done.10
  134.5 0.4 copy-done.11
  134.9 1.0 copy-done.12
  135.9 10.3 %expert.2 = bf16[4,2,2,160,128]{4,3,2,1,0:T(8,128)(2,1)} custom-call(s32[5]{0:T(128)} %stack.23.pos, bf16[160,3200]{1,0:T(8,128)(2,1)} %copy-done.1, bf16[160,3200]{1,0:T(8,128)(2,1)} %collective-permute-done.11.refs_1_, bf16[160,3200]{1,0:T(8,128)(2,1)} %collective-permute-done.13.refs_2_, bf16[160,3200]{1,0:T(8,128)(2,1)} %collective-permute-done.12.refs_3_, ...), custom_call_target="tpu_custom_call" | custom-call | flops 4026531840 | bytes 12582912 | tf_op jit(solution)/shard_map/expert/pallas_call | solution.py:189
  146.2 3.4 %collective-permute-done.16.refs_9_ = bf16[8,192,256]{2,1,0:T(8,128)(2,1)S(1)} collective-permute-done((bf16[8,192,256]{2,1,0:T(8,128)(2,1)}, bf16[8,192,256]{2,1,0:T(8,128)(2,1)S(1)}, u32[]{:S(2)}, u32[]{:S(2)}) %collective-permute-start.16) | collective-permute-done | bytes 786464 | tf_op jit(solution)/shard_map/ppermute | solution.py:17
  149.6 0.9 collective-permute-start.22
  150.6 1.9 collective-permute-start.23
  152.5 8.1 %all-to-all-start.2 = ((bf16[16,160,128]{2,1,0:T(8,128)(2,1)}), bf16[16,160,128]{2,1,0:T(8,128)(2,1)S(1)}, u32[]{:S(2)}, u32[]{:S(2)}) async-start(bf16[16,160,128]{2,1,0:T(8,128)(2,1)} %bitcast.11), calls=%async_computation.2 | async-start | bytes 1310720 | tf_op jit(solution)/shard_map/all_to_all | solution.py:208
  160.6 10.4 %expert.3 = bf16[4,2,2,160,128]{4,3,2,1,0:T(8,128)(2,1)} custom-call(s32[5]{0:T(128)} %stack.23.pos, bf16[160,3200]{1,0:T(8,128)(2,1)} %copy-done.1, bf16[160,3200]{1,0:T(8,128)(2,1)} %collective-permute-done.11.refs_1_, bf16[160,3200]{1,0:T(8,128)(2,1)} %collective-permute-done.13.refs_2_, bf16[160,3200]{1,0:T(8,128)(2,1)} %collective-permute-done.12.refs_3_, ...), custom_call_target="tpu_custom_call" | custom-call | flops 4026531840 | bytes 12582912 | tf_op jit(solution)/shard_map/expert/pallas_call | solution.py:189
  171.0 0.6 all-to-all-done.2
  171.6 18.6 %all_to_all.20 = bf16[16,160,128]{2,1,0:T(8,128)(2,1)S(1)} all-to-all(bf16[16,160,128]{2,1,0:T(8,128)(2,1)} %bitcast.21), channel_id=1, replica_groups=mesh['dp'=2,'y'=4,'c'=2,'z'=8,'xl'=2] {'y','c','xl'}, dimensions={0} | all-to-all | bytes 1310720 | tf_op jit(solution)/shard_map/all_to_all | solution.py:208
  190.2 1.5 combine.1
  191.7 1.6 reshape.23
  (56 shorter events, 0.8 us)
Async XLA Ops:
  0.9 4.0 %collective-permute-start = (bf16[2,192,128]{2,1,0:T(8,128)(2,1)S(1)}, bf16[2,192,128]{2,1,0:T(8,128)(2,1)S(1)}, u32[]{:S(2)}, u32[]{:S(2)}) collective-permute-start(bf16[2,192,128]{2,1,0:T(8,128)(2,1)S(1)} %dynamic-slice_bitcast_fusion), channel_id=1, source_target_pairs={{0,1},{1,0},{2,3},{3,2},{4,5},{5,4},{6,7},{7,6},{8,9},{9,8},{10,11... | collective-permute-start | bytes 294920 | tf_op jit(solution)/shard_map/ppermute | solution.py:17
  5.9 9.3 %collective-permute-start.1 = (bf16[2,384,128]{2,1,0:T(8,128)(2,1)S(1)}, bf16[2,384,128]{2,1,0:T(8,128)(2,1)S(1)}, u32[]{:S(2)}, u32[]{:S(2)}) collective-permute-start(bf16[2,384,128]{2,1,0:T(8,128)(2,1)S(1)} %pad_maximum_fusion.refs_0_), channel_id=1, source_target_pairs={{0,2},{2,4},{4,6},{6,8},{8,10},{10,12},{12,14},{14,0},{1,3},{3,5},... | collective-permute-start | bytes 589832 | tf_op jit(solution)/shard_map/ppermute | solution.py:17
  7.8 7.3 %collective-permute-start.4 = (bf16[2,384,128]{2,1,0:T(8,128)(2,1)S(1)}, bf16[2,384,128]{2,1,0:T(8,128)(2,1)S(1)}, u32[]{:S(2)}, u32[]{:S(2)}) collective-permute-start(bf16[2,384,128]{2,1,0:T(8,128)(2,1)S(1)} %pad_maximum_fusion.refs_0_), channel_id=1, source_target_pairs={{0,14},{2,0},{4,2},{6,4},{8,6},{10,8},{12,10},{14,12},{1,15},{3,1}... | collective-permute-start | bytes 589832 | tf_op jit(solution)/shard_map/ppermute | solution.py:17
  15.2 5.7 %collective-permute-start.2 = (bf16[2,384,128]{2,1,0:T(8,128)(2,1)S(1)}, bf16[2,384,128]{2,1,0:T(8,128)(2,1)S(1)}, u32[]{:S(2)}, u32[]{:S(2)}) collective-permute-start(bf16[2,384,128]{2,1,0:T(8,128)(2,1)S(1)} %collective-permute-done.1.refs_7_), channel_id=1, source_target_pairs={{0,2},{2,4},{4,6},{6,8},{8,10},{10,12},{12,14},{14,0},{1,3},{3,5},... | collective-permute-start | bytes 589832 | tf_op jit(solution)/shard_map/ppermute | solution.py:17
  15.2 5.7 %collective-permute-start.5 = (bf16[2,384,128]{2,1,0:T(8,128)(2,1)S(1)}, bf16[2,384,128]{2,1,0:T(8,128)(2,1)S(1)}, u32[]{:S(2)}, u32[]{:S(2)}) collective-permute-start(bf16[2,384,128]{2,1,0:T(8,128)(2,1)S(1)} %collective-permute-done.4.refs_1_), channel_id=1, source_target_pairs={{0,14},{2,0},{4,2},{6,4},{8,6},{10,8},{12,10},{14,12},{1,15},{3,1}... | collective-permute-start | bytes 589832 | tf_op jit(solution)/shard_map/ppermute | solution.py:17
  20.9 6.9 %collective-permute-start.3 = (bf16[2,384,128]{2,1,0:T(8,128)(2,1)S(1)}, bf16[2,384,128]{2,1,0:T(8,128)(2,1)S(1)}, u32[]{:S(2)}, u32[]{:S(2)}) collective-permute-start(bf16[2,384,128]{2,1,0:T(8,128)(2,1)S(1)} %collective-permute-done.2.refs_6_), channel_id=1, source_target_pairs={{0,2},{2,4},{4,6},{6,8},{8,10},{10,12},{12,14},{14,0},{1,3},{3,5},... | collective-permute-start | bytes 589832 | tf_op jit(solution)/shard_map/ppermute | solution.py:17
  20.9 6.9 %collective-permute-start.6 = (bf16[2,384,128]{2,1,0:T(8,128)(2,1)S(1)}, bf16[2,384,128]{2,1,0:T(8,128)(2,1)S(1)}, u32[]{:S(2)}, u32[]{:S(2)}) collective-permute-start(bf16[2,384,128]{2,1,0:T(8,128)(2,1)S(1)} %collective-permute-done.5.refs_2_), channel_id=1, source_target_pairs={{0,14},{2,0},{4,2},{6,4},{8,6},{10,8},{12,10},{14,12},{1,15},{3,1}... | collective-permute-start | bytes 589832 | tf_op jit(solution)/shard_map/ppermute | solution.py:17
  27.7 5.0 %copy-start.7 = (s32[4,128,2]{1,2,0:T(2,128)S(1)}, s32[4,128,2]{1,2,0:T(2,128)}, u32[]{:S(2)}) copy-start(s32[4,128,2]{1,2,0:T(2,128)} %param.6) | copy-start | bytes 12292
  27.8 7.9 %copy-start.8 = (f32[4,128,2]{1,2,0:T(2,128)S(1)}, f32[4,128,2]{1,2,0:T(2,128)}, u32[]{:S(2)}) copy-start(f32[4,128,2]{1,2,0:T(2,128)} %param.7) | copy-start | bytes 12292
  27.8 22.6 %copy-start = (s32[5]{0:T(128)S(1)}, s32[5]{0:T(128)}, u32[]{:S(2)}) copy-start(s32[5]{0:T(128)} %stack.23.pos) | copy-start | bytes 64
  27.8 29.7 %all-to-all-start = ((bf16[8,192,256]{2,1,0:T(8,128)(2,1)}), bf16[8,192,256]{2,1,0:T(8,128)(2,1)S(1)}, u32[]{:S(2)}, u32[]{:S(2)}) async-start(bf16[8,192,256]{2,1,0:T(8,128)(2,1)} %get-tuple-element.34), calls=%async_computation | async-start | bytes 1572864 | tf_op jit(solution)/shard_map/all_to_all | solution.py:152
  32.8 15.4 %collective-permute-start.10 = (bf16[1,384,128]{2,1,0:T(8,128)(2,1)S(1)}, bf16[1,384,128]{2,1,0:T(8,128)(2,1)S(1)}, u32[]{:S(2)}, u32[]{:S(2)}) collective-permute-start(bf16[1,384,128]{2,1,0:T(8,128)(2,1)S(1)} %slice.19), channel_id=1, source_target_pairs={{0,14},{2,0},{4,2},{6,4},{8,6},{10,8},{12,10},{14,12},{1,15},{3,1}... | collective-permute-start | bytes 294920 | tf_op jit(solution)/shard_map/ppermute | solution.py:17
  35.6 14.8 %collective-permute-start.9 = (bf16[1,384,128]{2,1,0:T(8,128)(2,1)S(1)}, bf16[1,384,128]{2,1,0:T(8,128)(2,1)S(1)}, u32[]{:S(2)}, u32[]{:S(2)}) collective-permute-start(bf16[1,384,128]{2,1,0:T(8,128)(2,1)S(1)} %slice.18), channel_id=1, source_target_pairs={{0,2},{2,4},{4,6},{6,8},{8,10},{10,12},{12,14},{14,0},{1,3},{3,5},... | collective-permute-start | bytes 294920 | tf_op jit(solution)/shard_map/ppermute | solution.py:17
  53.7 1.0 copy-start.2
  54.7 57.3 %copy-start.1 = (bf16[160,3200]{1,0:T(8,128)(2,1)}, bf16[160,3200]{1,0:T(8,128)(2,1)S(1)}, u32[]{:S(2)}) copy-start(bf16[160,3200]{1,0:T(8,128)(2,1)S(1)} %get-tuple-element.50.refs_0_) | copy-start | bytes 3072004
  54.7 20.9 %copy-start.3 = (bf16[160,3200]{1,0:T(8,128)(2,1)S(1)}, bf16[160,3200]{1,0:T(8,128)(2,1)}, u32[]{:S(2)}) copy-start(bf16[160,3200]{1,0:T(8,128)(2,1)} %copy-done.2) | copy-start | bytes 3072004
  54.7 20.9 %collective-permute-start.11 = (bf16[160,3200]{1,0:T(8,128)(2,1)}, bf16[160,3200]{1,0:T(8,128)(2,1)}, u32[]{:S(2)}, u32[]{:S(2)}) collective-permute-start(bf16[160,3200]{1,0:T(8,128)(2,1)} %get-tuple-element.41), channel_id=1, source_target_pairs={{0,32},{32,64},{64,96},{96,0},{1,33},{33,65},{65,97},{97,1},{2,34}... | collective-permute-start | bytes 3072008 | tf_op jit(solution)/shard_map/ppermute | solution.py:17
  56.0 19.6 %collective-permute-start.12 = (bf16[160,3200]{1,0:T(8,128)(2,1)}, bf16[160,3200]{1,0:T(8,128)(2,1)}, u32[]{:S(2)}, u32[]{:S(2)}) collective-permute-start(bf16[160,3200]{1,0:T(8,128)(2,1)} %get-tuple-element.42), channel_id=1, source_target_pairs={{0,96},{32,0},{64,32},{96,64},{1,97},{33,1},{65,33},{97,65},{2,98}... | collective-permute-start | bytes 3072008 | tf_op jit(solution)/shard_map/ppermute | solution.py:17
  57.5 54.5 %copy-start.4 = (bf16[8,192,256]{2,1,0:T(8,128)(2,1)}, bf16[8,192,256]{2,1,0:T(8,128)(2,1)S(1)}, u32[]{:S(2)}) copy-start(bf16[8,192,256]{2,1,0:T(8,128)(2,1)S(1)} %all-to-all-done.refs_8_) | copy-start | bytes 2359300
  57.5 35.4 %all-to-all-start.1 = ((bf16[8,192,256]{2,1,0:T(8,128)(2,1)}), bf16[8,192,256]{2,1,0:T(8,128)(2,1)}, u32[]{:S(2)}, u32[]{:S(2)}) async-start(bf16[8,192,256]{2,1,0:T(8,128)(2,1)} %get-tuple-element.35), calls=%async_computation.1 | async-start | bytes 1572864 | tf_op jit(solution)/shard_map/all_to_all | solution.py:152
  75.6 17.2 %collective-permute-start.13 = (bf16[160,3200]{1,0:T(8,128)(2,1)S(1)}, bf16[160,3200]{1,0:T(8,128)(2,1)}, u32[]{:S(2)}, u32[]{:S(2)}) collective-permute-start(bf16[160,3200]{1,0:T(8,128)(2,1)S(1)} %copy-done.3), channel_id=1, source_target_pairs={{0,64},{32,96},{64,0},{96,32},{1,65},{33,97},{65,1},{97,33},{2,66}... | collective-permute-start | bytes 3072008 | tf_op jit(solution)/shard_map/ppermute | solution.py:17
  78.0 14.9 %collective-permute-start.7 = (bf16[8,192,256]{2,1,0:T(8,128)(2,1)S(1)}, bf16[8,192,256]{2,1,0:T(8,128)(2,1)}, u32[]{:S(2)}, u32[]{:S(2)}) collective-permute-start(bf16[8,192,256]{2,1,0:T(8,128)(2,1)S(1)} %all-to-all-done.refs_8_), channel_id=1, source_target_pairs={{0,1},{1,128},{128,129},{129,0},{2,3},{3,130},{130,131},{131,2},{4... | collective-permute-start | bytes 2359304 | tf_op jit(solution)/shard_map/ppermute | solution.py:17
  79.2 13.7 %collective-permute-start.8 = (bf16[8,192,256]{2,1,0:T(8,128)(2,1)S(1)}, bf16[8,192,256]{2,1,0:T(8,128)(2,1)}, u32[]{:S(2)}, u32[]{:S(2)}) collective-permute-start(bf16[8,192,256]{2,1,0:T(8,128)(2,1)S(1)} %all-to-all-done.refs_8_), channel_id=1, source_target_pairs={{0,129},{1,0},{128,1},{129,128},{2,131},{3,2},{130,3},{131,130},{4... | collective-permute-start | bytes 2359304 | tf_op jit(solution)/shard_map/ppermute | solution.py:17
  92.8 38.0 %collective-permute-start.18 = (bf16[160,3200]{1,0:T(8,128)(2,1)S(1)}, bf16[160,3200]{1,0:T(8,128)(2,1)S(1)}, u32[]{:S(2)}, u32[]{:S(2)}) collective-permute-start(bf16[160,3200]{1,0:T(8,128)(2,1)S(1)} %get-tuple-element.50.refs_0_), channel_id=1, source_target_pairs={{0,16},{16,0},{1,17},{17,1},{2,18},{18,2},{3,19},{19,3},{4,20},{20... | collective-permute-start | bytes 3072008 | tf_op jit(solution)/shard_map/ppermute | solution.py:17
  108.9 12.0 %collective-permute-start.14 = (bf16[4,192,256]{2,1,0:T(8,128)(2,1)S(1)}, bf16[4,192,256]{2,1,0:T(8,128)(2,1)S(1)}, u32[]{:S(2)}, u32[]{:S(2)}) collective-permute-start(bf16[4,192,256]{2,1,0:T(8,128)(2,1)S(1)} %slice.20), channel_id=1, source_target_pairs={{0,1},{1,128},{128,129},{129,0},{2,3},{3,130},{130,131},{131,2},{4... | collective-permute-start | bytes 1179656 | tf_op jit(solution)/shard_map/ppermute | solution.py:17
  110.2 23.4 %collective-permute-start.19 = (bf16[160,3200]{1,0:T(8,128)(2,1)}, bf16[160,3200]{1,0:T(8,128)(2,1)S(1)}, u32[]{:S(2)}, u32[]{:S(2)}) collective-permute-start(bf16[160,3200]{1,0:T(8,128)(2,1)} %collective-permute-done.11.refs_1_), channel_id=1, source_target_pairs={{0,16},{16,0},{1,17},{17,1},{2,18},{18,2},{3,19},{19,3},{4,20},{20... | collective-permute-start | bytes 3072008 | tf_op jit(solution)/shard_map/ppermute | solution.py:17
  110.4 23.1 %collective-permute-start.20 = (bf16[160,3200]{1,0:T(8,128)(2,1)}, bf16[160,3200]{1,0:T(8,128)(2,1)S(1)}, u32[]{:S(2)}, u32[]{:S(2)}) collective-permute-start(bf16[160,3200]{1,0:T(8,128)(2,1)} %collective-permute-done.13.refs_2_), channel_id=1, source_target_pairs={{0,16},{16,0},{1,17},{17,1},{2,18},{18,2},{3,19},{19,3},{4,20},{20... | collective-permute-start | bytes 3072008 | tf_op jit(solution)/shard_map/ppermute | solution.py:17
  110.7 22.9 %collective-permute-start.21 = (bf16[160,3200]{1,0:T(8,128)(2,1)}, bf16[160,3200]{1,0:T(8,128)(2,1)S(1)}, u32[]{:S(2)}, u32[]{:S(2)}) collective-permute-start(bf16[160,3200]{1,0:T(8,128)(2,1)} %collective-permute-done.12.refs_3_), channel_id=1, source_target_pairs={{0,16},{16,0},{1,17},{17,1},{2,18},{18,2},{3,19},{19,3},{4,20},{20... | collective-permute-start | bytes 3072008 | tf_op jit(solution)/shard_map/ppermute | solution.py:17
  120.9 12.6 %copy-start.13 = (bf16[4,192,256]{2,1,0:T(8,128)(2,1)}, bf16[4,192,256]{2,1,0:T(8,128)(2,1)S(1)}, u32[]{:S(2)}) copy-start(bf16[4,192,256]{2,1,0:T(8,128)(2,1)S(1)} %collective-permute-done.14.refs_11_) | copy-start | bytes 1179652
  120.9 9.9 %collective-permute-start.15 = (bf16[4,192,256]{2,1,0:T(8,128)(2,1)S(1)}, bf16[4,192,256]{2,1,0:T(8,128)(2,1)S(1)}, u32[]{:S(2)}, u32[]{:S(2)}) collective-permute-start(bf16[4,192,256]{2,1,0:T(8,128)(2,1)S(1)} %slice.21), channel_id=1, source_target_pairs={{0,129},{1,0},{128,1},{129,128},{2,131},{3,2},{130,3},{131,130},{4... | collective-permute-start | bytes 1179656 | tf_op jit(solution)/shard_map/ppermute | solution.py:17
  130.8 2.8 %copy-start.14 = (bf16[4,192,256]{2,1,0:T(8,128)(2,1)}, bf16[4,192,256]{2,1,0:T(8,128)(2,1)S(1)}, u32[]{:S(2)}) copy-start(bf16[4,192,256]{2,1,0:T(8,128)(2,1)S(1)} %collective-permute-done.15.refs_12_) | copy-start | bytes 1179652
  130.8 18.8 %collective-permute-start.16 = (bf16[8,192,256]{2,1,0:T(8,128)(2,1)}, bf16[8,192,256]{2,1,0:T(8,128)(2,1)S(1)}, u32[]{:S(2)}, u32[]{:S(2)}) collective-permute-start(bf16[8,192,256]{2,1,0:T(8,128)(2,1)} %all-to-all-done.1.refs_8_), channel_id=1, source_target_pairs={{0,1},{1,128},{128,129},{129,0},{2,3},{3,130},{130,131},{131,2},{4... | collective-permute-start | bytes 2359304 | tf_op jit(solution)/shard_map/ppermute | solution.py:17
  130.8 2.8 %copy-start.9 = (bf16[160,3200]{1,0:T(8,128)(2,1)}, bf16[160,3200]{1,0:T(8,128)(2,1)S(1)}, u32[]{:S(2)}) copy-start(bf16[160,3200]{1,0:T(8,128)(2,1)S(1)} %collective-permute-done.18.refs_4_) | copy-start | bytes 3072004
  130.8 18.8 %collective-permute-start.17 = (bf16[8,192,256]{2,1,0:T(8,128)(2,1)}, bf16[8,192,256]{2,1,0:T(8,128)(2,1)S(1)}, u32[]{:S(2)}, u32[]{:S(2)}) collective-permute-start(bf16[8,192,256]{2,1,0:T(8,128)(2,1)} %all-to-all-done.1.refs_8_), channel_id=1, source_target_pairs={{0,129},{1,0},{128,1},{129,128},{2,131},{3,2},{130,3},{131,130},{4... | collective-permute-start | bytes 2359304 | tf_op jit(solution)/shard_map/ppermute | solution.py:17
  133.5 1.0 copy-start.10
  133.6 1.3 copy-start.11
  134.9 1.0 copy-start.12
  149.6 11.0 %copy-start.5 = (bf16[8,192,256]{2,1,0:T(8,128)(2,1)}, bf16[8,192,256]{2,1,0:T(8,128)(2,1)S(1)}, u32[]{:S(2)}) copy-start(bf16[8,192,256]{2,1,0:T(8,128)(2,1)S(1)} %collective-permute-done.16.refs_9_) | copy-start | bytes 2359300
  149.6 11.0 %copy-start.6 = (bf16[8,192,256]{2,1,0:T(8,128)(2,1)}, bf16[8,192,256]{2,1,0:T(8,128)(2,1)S(1)}, u32[]{:S(2)}) copy-start(bf16[8,192,256]{2,1,0:T(8,128)(2,1)S(1)} %collective-permute-done.17.refs_10_) | copy-start | bytes 2359300
  149.6 10.9 %collective-permute-start.22 = (bf16[4,192,256]{2,1,0:T(8,128)(2,1)S(1)}, bf16[4,192,256]{2,1,0:T(8,128)(2,1)}, u32[]{:S(2)}, u32[]{:S(2)}) collective-permute-start(bf16[4,192,256]{2,1,0:T(8,128)(2,1)S(1)} %slice.22), channel_id=1, source_target_pairs={{0,1},{1,128},{128,129},{129,0},{2,3},{3,130},{130,131},{131,2},{4... | collective-permute-start | bytes 1179656 | tf_op jit(solution)/shard_map/ppermute | solution.py:17
  150.6 10.0 %collective-permute-start.23 = (bf16[4,192,256]{2,1,0:T(8,128)(2,1)S(1)}, bf16[4,192,256]{2,1,0:T(8,128)(2,1)}, u32[]{:S(2)}, u32[]{:S(2)}) collective-permute-start(bf16[4,192,256]{2,1,0:T(8,128)(2,1)S(1)} %slice.23), channel_id=1, source_target_pairs={{0,129},{1,0},{128,1},{129,128},{2,131},{3,2},{130,3},{131,130},{4... | collective-permute-start | bytes 1179656 | tf_op jit(solution)/shard_map/ppermute | solution.py:17
  152.5 19.1 %all-to-all-start.2 = ((bf16[16,160,128]{2,1,0:T(8,128)(2,1)}), bf16[16,160,128]{2,1,0:T(8,128)(2,1)S(1)}, u32[]{:S(2)}, u32[]{:S(2)}) async-start(bf16[16,160,128]{2,1,0:T(8,128)(2,1)} %bitcast.11), calls=%async_computation.2 | async-start | bytes 1310720 | tf_op jit(solution)/shard_map/all_to_all | solution.py:208

commit v10 on v9

--- a/solution.py
+++ b/solution.py
@@ -159,12 +159,13 @@
 
     below, above = [pair], [pair]
     for k in range(3):
+        if k == 2:
+            below[2], above[2], *blocks = barrier((below[2], above[2], *blocks))
         below.append(ring(below[-1], "z", 8, 1))
         above.append(ring(above[-1], "z", 8, -1))
-    part_a, below[3], above[3] = barrier((blocks[0], below[3], above[3]))
+    part_a, *last = barrier((blocks[0], ring(below[3][:1], "z", 8, 1), ring(above[3][1:], "z", 8, -1)))
     own_a = exchange(part_a)
-    opposite = jnp.concatenate([ring(below[3][:1], "z", 8, 1), ring(above[3][1:], "z", 8, -1)], axis=0)
-    feats = [pair] + above[1:] + [opposite] + below[:0:-1]
+    feats = [pair] + above[1:] + [jnp.concatenate(last, axis=0)] + below[:0:-1]
     sent = pl.pallas_call(
         dispatch_kernel,
         out_shape=[jax.ShapeDtypeStruct((2 * MOST, 16 * width + 128), BF)] * 4,
@@ -174,16 +175,20 @@
         name="dispatch",
     )(pos, meta, *feats)
     near = ring(sent[1], "y", 4, 1), ring(sent[3], "y", 4, 3)
+    other = [ring(sent[0], "c", 2, 1)]
     part_b, own_a = barrier((blocks[1], own_a))
     own_b = exchange(part_b)
     left_a, right_a = sides(own_a)
-    far_rows, *near = barrier((sent[2], *near))
-    held = [sent[0], near[0], ring(far_rows, "y", 4, 2), near[1]]
-    own_b, left_a, right_a, *held = barrier((own_b, left_a, right_a, *held))
+    far_rows, other[0], *near = barrier((sent[2], other[0], *near))
+    opposite = ring(far_rows, "y", 4, 2)
+    left_a, right_a, *near = barrier((left_a, right_a, *near))
     far_a = far(left_a, right_a)
-    other = [ring(h, "c", 2, 1) for h in held]
-    own_b, *far_a = barrier((own_b, *far_a))
+    other += [ring(h, "c", 2, 1) for h in near]
+    own_b, opposite, *rest = barrier((own_b, opposite, *far_a, *other))
+    far_a, other = rest[:2], rest[2:]
     left_b, right_b = sides(own_b)
+    held = [sent[0], near[0], opposite, near[1]]
+    other = [other[0], other[1], ring(opposite, "c", 2, 1), other[2]]
 
     def expert(*ws):
         return pl.pallas_call(

time: 194 us -> 162 us (0.84)
  waiting for transfers between devices: 68.3 us -> 34.9 us
  starting transfers between devices: 67.5 us -> 69.8 us
    ppermute x24, waiting for transfers between devices: 67.7 us -> 31.3 us  [ring(): return lax.ppermute(x, axis, [(i, (i + step) % size) for i in range(size)])]
    ppermute x24, starting transfers between devices: 48.1 us -> 54.4 us  [ring(): return lax.ppermute(x, axis, [(i, (i + step) % size) for i in range(size)])]
    all_to_all x2, waiting for transfers between devices: 0.01 us -> 3.57 us  [exchange(): return lax.all_to_all(x, 'z', split_axis=0, concat_axis=0, tiled=True)]
    all_to_all x1, starting transfers between devices: 8.08 us -> 5.42 us  [give_back(): lax.all_to_all(act.reshape(16, 2 * MOST, wide), ('y', 'c', 'xl'), split_a...]
  transfers between devices with their start and end apart: 27 -> 27, of which waited for: 11 -> 10; matrix products, arithmetic and copies ran while one was open for 1% -> 2% of each run, Pallas kernels for 14% -> 17%
where the time goes in v10:
time: 162 us; the launch traced here: 161 us
  starting transfers between devices  69.8 us (43%)
  waiting for transfers between devices  34.9 us (22%)
  Pallas kernels  29.1 us (18%)
  blocking collectives  18.5 us (11%)
  local copies, waits for them, and re-layouts  7.95 us (5%)
    ppermute x24, starting transfers between devices, ring(): return lax.ppermute(x, axis, [(i, (i + step) % size) for i in range(size)])  54.4 us
    ppermute x24, waiting for transfers between devices, ring(): return lax.ppermute(x, axis, [(i, (i + step) % size) for i in range(size)])  31.3 us
    pallas_call x2, Pallas kernels, expert(): pl.pallas_call(expert_kernel, out_shape=jax.ShapeDtypeStruct((4, 2, 2, 2...  20.7 us
    all_to_all x1, blocking collectives, give_back(): lax.all_to_all(act.reshape(16, 2 * MOST, wide), ('y', 'c', 'xl'), split_a...  18.5 us
    all_to_all x2, starting transfers between devices, exchange(): return lax.all_to_all(x, 'z', split_axis=0, concat_axis=0, tiled=True)  10 us
    all_to_all x1, starting transfers between devices, give_back(): lax.all_to_all(act.reshape(16, 2 * MOST, wide), ('y', 'c', 'xl'), split_a...  5.42 us
    pallas_call x1, Pallas kernels, body(): pl.pallas_call(columns_kernel, out_shape=[jax.ShapeDtypeStruct((8, rows,...  3.58 us
    all_to_all x2, waiting for transfers between devices, exchange(): return lax.all_to_all(x, 'z', split_axis=0, concat_axis=0, tiled=True)  3.57 us
  transfers between devices with their start and end apart: 27, of which 10 were waited for; matrix products, arithmetic and copies ran while one was open for 2% of the time, Pallas kernels for 17%

profile of v10, /device:TPU:1, one launch (start us, length us, event | category | flops | bytes accessed | tf_op | source)
XLA Modules:
  0.0 161.5 jit_solution(15963467196490860525)
XLA Ops:
  0.0 0.9 dynamic-slice_bitcast_fusion
  0.9 2.0 %collective-permute-start = (bf16[2,192,128]{2,1,0:T(8,128)(2,1)S(1)}, bf16[2,192,128]{2,1,0:T(8,128)(2,1)S(1)}, u32[]{:S(2)}, u32[]{:S(2)}) collective-permute-start(bf16[2,192,128]{2,1,0:T(8,128)(2,1)S(1)} %dynamic-slice_bitcast_fusion), channel_id=1, source_target_pairs={{0,1},{1,0},{2,3},{3,2},{4,5},{5,4},{6,7},{7,6},{8,9},{9,8},{10,11... | collective-permute-start | bytes 294920 | tf_op jit(solution)/shard_map/ppermute | solution.py:17
  2.9 2.0 %collective-permute-done = bf16[2,192,128]{2,1,0:T(8,128)(2,1)S(1)} collective-permute-done((bf16[2,192,128]{2,1,0:T(8,128)(2,1)S(1)}, bf16[2,192,128]{2,1,0:T(8,128)(2,1)S(1)}, u32[]{:S(2)}, u32[]{:S(2)}) %collective-permute-start) | collective-permute-done | bytes 98336 | tf_op jit(solution)/shard_map/ppermute | solution.py:17
  4.9 0.9 bitcast_select_fusion.1
  5.9 2.0 %collective-permute-start.1 = (bf16[2,384,128]{2,1,0:T(8,128)(2,1)S(1)}, bf16[2,384,128]{2,1,0:T(8,128)(2,1)S(1)}, u32[]{:S(2)}, u32[]{:S(2)}) collective-permute-start(bf16[2,384,128]{2,1,0:T(8,128)(2,1)S(1)} %pad_maximum_fusion.refs_0_), channel_id=1, source_target_pairs={{0,2},{2,4},{4,6},{6,8},{8,10},{10,12},{12,14},{14,0},{1,3},{3,5},... | collective-permute-start | bytes 589832 | tf_op jit(solution)/shard_map/ppermute | solution.py:17
  7.8 4.0 %collective-permute-start.3 = (bf16[2,384,128]{2,1,0:T(8,128)(2,1)S(1)}, bf16[2,384,128]{2,1,0:T(8,128)(2,1)S(1)}, u32[]{:S(2)}, u32[]{:S(2)}) collective-permute-start(bf16[2,384,128]{2,1,0:T(8,128)(2,1)S(1)} %pad_maximum_fusion.refs_0_), channel_id=1, source_target_pairs={{0,14},{2,0},{4,2},{6,4},{8,6},{10,8},{12,10},{14,12},{1,15},{3,1}... | collective-permute-start | bytes 589832 | tf_op jit(solution)/shard_map/ppermute | solution.py:17
  11.9 3.3 %collective-permute-done.1.refs_7_ = bf16[2,384,128]{2,1,0:T(8,128)(2,1)S(1)} collective-permute-done((bf16[2,384,128]{2,1,0:T(8,128)(2,1)S(1)}, bf16[2,384,128]{2,1,0:T(8,128)(2,1)S(1)}, u32[]{:S(2)}, u32[]{:S(2)}) %collective-permute-start.1) | collective-permute-done | bytes 196640 | tf_op jit(solution)/shard_map/ppermute | solution.py:17
  15.2 2.7 %collective-permute-start.4 = (bf16[2,384,128]{2,1,0:T(8,128)(2,1)S(1)}, bf16[2,384,128]{2,1,0:T(8,128)(2,1)S(1)}, u32[]{:S(2)}, u32[]{:S(2)}) collective-permute-start(bf16[2,384,128]{2,1,0:T(8,128)(2,1)S(1)} %collective-permute-done.3.refs_1_), channel_id=1, source_target_pairs={{0,14},{2,0},{4,2},{6,4},{8,6},{10,8},{12,10},{14,12},{1,15},{3,1}... | collective-permute-start | bytes 589832 | tf_op jit(solution)/shard_map/ppermute | solution.py:17
  17.9 0.6 stack.23.pos
  18.5 3.6 %columns.1 = (bf16[8,192,256]{2,1,0:T(8,128)(2,1)}, bf16[8,192,256]{2,1,0:T(8,128)(2,1)}) custom-call(s32[5]{0:T(128)} %stack.23.pos, bf16[1,192,4096]{2,1,0:T(8,128)(2,1)} %gate.1, bf16[1,192,4096]{2,1,0:T(8,128)(2,1)} %up.1), custom_call_target="tpu_custom_call" | custom-call | tf_op jit(solution)/shard_map/columns/pallas_call | solution.py:141
  22.2 2.7 %collective-permute-start.7 = (bf16[2,384,128]{2,1,0:T(8,128)(2,1)S(1)}, bf16[2,384,128]{2,1,0:T(8,128)(2,1)S(1)}, u32[]{:S(2)}, u32[]{:S(2)}) collective-permute-start(bf16[2,384,128]{2,1,0:T(8,128)(2,1)S(1)} %collective-permute-done.4.refs_2_), channel_id=1, source_target_pairs={{0,14},{2,0},{4,2},{6,4},{8,6},{10,8},{12,10},{14,12},{1,15},{3,1}... | collective-permute-start | bytes 589832 | tf_op jit(solution)/shard_map/ppermute | solution.py:17
  24.9 3.1 %collective-permute-done.5.refs_5_ = bf16[2,384,128]{2,1,0:T(8,128)(2,1)S(1)} collective-permute-done((bf16[2,384,128]{2,1,0:T(8,128)(2,1)S(1)}, bf16[2,384,128]{2,1,0:T(8,128)(2,1)S(1)}, u32[]{:S(2)}, u32[]{:S(2)}) %collective-permute-start.5) | collective-permute-done | bytes 196640 | tf_op jit(solution)/shard_map/ppermute | solution.py:17
  28.0 2.7 %collective-permute-start.8 = (bf16[1,384,128]{2,1,0:T(8,128)(2,1)S(1)}, bf16[1,384,128]{2,1,0:T(8,128)(2,1)S(1)}, u32[]{:S(2)}, u32[]{:S(2)}) collective-permute-start(bf16[1,384,128]{2,1,0:T(8,128)(2,1)S(1)} %slice.25), channel_id=1, source_target_pairs={{0,14},{2,0},{4,2},{6,4},{8,6},{10,8},{12,10},{14,12},{1,15},{3,1}... | collective-permute-start | bytes 294920 | tf_op jit(solution)/shard_map/ppermute | solution.py:17
  30.8 1.9 %collective-permute-done.6 = bf16[1,384,128]{2,1,0:T(8,128)(2,1)S(1)} collective-permute-done((bf16[1,384,128]{2,1,0:T(8,128)(2,1)S(1)}, bf16[1,384,128]{2,1,0:T(8,128)(2,1)S(1)}, u32[]{:S(2)}, u32[]{:S(2)}) %collective-permute-start.6) | collective-permute-done | bytes 98336 | tf_op jit(solution)/shard_map/ppermute | solution.py:17
  32.7 5.8 %all-to-all-start = ((bf16[8,192,256]{2,1,0:T(8,128)(2,1)}), bf16[8,192,256]{2,1,0:T(8,128)(2,1)S(1)}, u32[]{:S(2)}, u32[]{:S(2)}) async-start(bf16[8,192,256]{2,1,0:T(8,128)(2,1)} %get-tuple-element.44), calls=%async_computation | async-start | bytes 1572864 | tf_op jit(solution)/shard_map/all_to_all | solution.py:152
  38.6 3.4 %dispatch.1 = (bf16[160,3200]{1,0:T(8,128)(2,1)S(1)}, bf16[160,3200]{1,0:T(8,128)(2,1)}, bf16[160,3200]{1,0:T(8,128)(2,1)S(1)}, bf16[160,3200]{1,0:T(8,128)(2,1)}) custom-call(s32[5]{0:T(128)S(1)} %copy-done, f32[4,4,128]{2,1,0:T(4,128)S(1)} %maximum_bitcast_fusion.meta, bf16[2,384,128]{2,1,0:T(8,128)(2,1)S(1)} %pad_maximum_fusion.refs_0_, ...), custom_call_target="tpu_custom_call" | custom-call | tf_op jit(solution)/shard_map/dispatch/pallas_call | solution.py:169
  41.9 1.0 copy-done.2
  42.9 1.3 collective-permute-start.10
  44.2 1.4 collective-permute-start.11
  45.7 6.7 %collective-permute-start.9 = (bf16[160,3200]{1,0:T(8,128)(2,1)S(1)}, bf16[160,3200]{1,0:T(8,128)(2,1)}, u32[]{:S(2)}, u32[]{:S(2)}) collective-permute-start(bf16[160,3200]{1,0:T(8,128)(2,1)S(1)} %get-tuple-element.49.refs_0_), channel_id=1, source_target_pairs={{0,16},{16,0},{1,17},{17,1},{2,18},{18,2},{3,19},{19,3},{4,20},{20... | collective-permute-start | bytes 3072008 | tf_op jit(solution)/shard_map/ppermute | solution.py:17
  52.4 3.6 %all-to-all-done.refs_8_ = bf16[8,192,256]{2,1,0:T(8,128)(2,1)S(1)} async-done(((bf16[8,192,256]{2,1,0:T(8,128)(2,1)}), bf16[8,192,256]{2,1,0:T(8,128)(2,1)S(1)}, u32[]{:S(2)}, u32[]{:S(2)}) %all-to-all-start) | async-done | bytes 786464 | tf_op jit(solution)/shard_map/all_to_all | solution.py:152
  56.0 1.2 collective-permute-start.13
  57.2 1.5 collective-permute-start.14
  58.7 4.2 %all-to-all-start.1 = ((bf16[8,192,256]{2,1,0:T(8,128)(2,1)}), bf16[8,192,256]{2,1,0:T(8,128)(2,1)}, u32[]{:S(2)}, u32[]{:S(2)}) async-start(bf16[8,192,256]{2,1,0:T(8,128)(2,1)} %get-tuple-element.45), calls=%async_computation.1 | async-start | bytes 1572864 | tf_op jit(solution)/shard_map/all_to_all | solution.py:152
  62.9 3.0 %collective-permute-start.12 = (bf16[160,3200]{1,0:T(8,128)(2,1)S(1)}, bf16[160,3200]{1,0:T(8,128)(2,1)}, u32[]{:S(2)}, u32[]{:S(2)}) collective-permute-start(bf16[160,3200]{1,0:T(8,128)(2,1)S(1)} %copy-done.3), channel_id=1, source_target_pairs={{0,64},{32,96},{64,0},{96,32},{1,65},{33,97},{65,1},{97,33},{2,66}... | collective-permute-start | bytes 3072008 | tf_op jit(solution)/shard_map/ppermute | solution.py:17
  65.9 3.8 %collective-permute-done.13.refs_9_ = bf16[8,192,256]{2,1,0:T(8,128)(2,1)} collective-permute-done((bf16[8,192,256]{2,1,0:T(8,128)(2,1)S(1)}, bf16[8,192,256]{2,1,0:T(8,128)(2,1)}, u32[]{:S(2)}, u32[]{:S(2)}) %collective-permute-start.13) | collective-permute-done | bytes 786464 | tf_op jit(solution)/shard_map/ppermute | solution.py:17
  69.7 12.8 %collective-permute-start.17 = (bf16[160,3200]{1,0:T(8,128)(2,1)}, bf16[160,3200]{1,0:T(8,128)(2,1)}, u32[]{:S(2)}, u32[]{:S(2)}) collective-permute-start(bf16[160,3200]{1,0:T(8,128)(2,1)} %collective-permute-done.10.refs_1_), channel_id=1, source_target_pairs={{0,16},{16,0},{1,17},{17,1},{2,18},{18,2},{3,19},{19,3},{4,20},{20... | collective-permute-start | bytes 3072008 | tf_op jit(solution)/shard_map/ppermute | solution.py:17
  82.7 1.0 slice.20
  83.7 1.3 collective-permute-start.15
  85.0 1.0 slice.21
  86.0 1.5 collective-permute-start.16
  87.6 7.7 %collective-permute-done.15.refs_11_ = bf16[4,192,256]{2,1,0:T(8,128)(2,1)S(1)} collective-permute-done((bf16[4,192,256]{2,1,0:T(8,128)(2,1)S(1)}, bf16[4,192,256]{2,1,0:T(8,128)(2,1)S(1)}, u32[]{:S(2)}, u32[]{:S(2)}) %collective-permute-start.15) | collective-permute-done | bytes 393248 | tf_op jit(solution)/shard_map/ppermute | solution.py:17
  95.2 0.8 copy-done.10
  96.0 0.1 collective-permute-done.16.refs_12_
  96.2 1.7 %collective-permute-start.21 = (bf16[160,3200]{1,0:T(8,128)(2,1)}, bf16[160,3200]{1,0:T(8,128)(2,1)S(1)}, u32[]{:S(2)}, u32[]{:S(2)}) collective-permute-start(bf16[160,3200]{1,0:T(8,128)(2,1)} %collective-permute-done.12.refs_2_), channel_id=1, source_target_pairs={{0,16},{16,0},{1,17},{17,1},{2,18},{18,2},{3,19},{19,3},{4,20},{20... | collective-permute-start | bytes 3072008 | tf_op jit(solution)/shard_map/ppermute | solution.py:17
  97.8 1.2 collective-permute-start.19
  99.1 1.5 collective-permute-start.20
  100.5 1.0 copy-done.9
  101.5 10.3 %expert.2 = bf16[4,2,2,160,128]{4,3,2,1,0:T(8,128)(2,1)} custom-call(s32[5]{0:T(128)} %stack.23.pos, bf16[160,3200]{1,0:T(8,128)(2,1)} %copy-done.1, bf16[160,3200]{1,0:T(8,128)(2,1)} %collective-permute-done.10.refs_1_, bf16[160,3200]{1,0:T(8,128)(2,1)} %collective-permute-done.12.refs_2_, bf16[160,3200]{1,0:T(8,128)(2,1)} %collective-permute-done.11.refs_3_, ...), custom_call_target="tpu_custom_call" | custom-call | flops 4026531840 | bytes 12582912 | tf_op jit(solution)/shard_map/expert/pallas_call | solution.py:194
  111.8 6.5 %collective-permute-done.19.refs_9_ = bf16[8,192,256]{2,1,0:T(8,128)(2,1)S(1)} collective-permute-done((bf16[8,192,256]{2,1,0:T(8,128)(2,1)}, bf16[8,192,256]{2,1,0:T(8,128)(2,1)S(1)}, u32[]{:S(2)}, u32[]{:S(2)}) %collective-permute-start.19) | collective-permute-done | bytes 786464 | tf_op jit(solution)/shard_map/ppermute | solution.py:17
  118.4 0.7 collective-permute-start.22
  119.1 2.1 %collective-permute-start.23 = (bf16[4,192,256]{2,1,0:T(8,128)(2,1)S(1)}, bf16[4,192,256]{2,1,0:T(8,128)(2,1)}, u32[]{:S(2)}, u32[]{:S(2)}) collective-permute-start(bf16[4,192,256]{2,1,0:T(8,128)(2,1)S(1)} %slice.23), channel_id=1, source_target_pairs={{0,129},{1,0},{128,1},{129,128},{2,131},{3,2},{130,3},{131,130},{4... | collective-permute-start | bytes 1179656 | tf_op jit(solution)/shard_map/ppermute | solution.py:17
  121.2 5.4 %all-to-all-start.2 = ((bf16[16,160,128]{2,1,0:T(8,128)(2,1)}), bf16[16,160,128]{2,1,0:T(8,128)(2,1)S(1)}, u32[]{:S(2)}, u32[]{:S(2)}) async-start(bf16[16,160,128]{2,1,0:T(8,128)(2,1)} %bitcast.11), calls=%async_computation.2 | async-start | bytes 1310720 | tf_op jit(solution)/shard_map/all_to_all | solution.py:213
  126.7 2.9 %collective-permute-done.22.refs_11_ = bf16[4,192,256]{2,1,0:T(8,128)(2,1)} collective-permute-done((bf16[4,192,256]{2,1,0:T(8,128)(2,1)S(1)}, bf16[4,192,256]{2,1,0:T(8,128)(2,1)}, u32[]{:S(2)}, u32[]{:S(2)}) %collective-permute-start.22) | collective-permute-done | bytes 393248 | tf_op jit(solution)/shard_map/ppermute | solution.py:17
  129.6 10.4 %expert.3 = bf16[4,2,2,160,128]{4,3,2,1,0:T(8,128)(2,1)} custom-call(s32[5]{0:T(128)} %stack.23.pos, bf16[160,3200]{1,0:T(8,128)(2,1)} %copy-done.1, bf16[160,3200]{1,0:T(8,128)(2,1)} %collective-permute-done.10.refs_1_, bf16[160,3200]{1,0:T(8,128)(2,1)} %collective-permute-done.12.refs_2_, bf16[160,3200]{1,0:T(8,128)(2,1)} %collective-permute-done.11.refs_3_, ...), custom_call_target="tpu_custom_call" | custom-call | flops 4026531840 | bytes 12582912 | tf_op jit(solution)/shard_map/expert/pallas_call | solution.py:194
  139.9 18.5 %all_to_all.20 = bf16[16,160,128]{2,1,0:T(8,128)(2,1)S(1)} all-to-all(bf16[16,160,128]{2,1,0:T(8,128)(2,1)} %bitcast.21), channel_id=1, replica_groups=mesh['dp'=2,'y'=4,'c'=2,'z'=8,'xl'=2] {'y','c','xl'}, dimensions={0} | all-to-all | bytes 1310720 | tf_op jit(solution)/shard_map/all_to_all | solution.py:213
  158.4 1.5 combine.1
  159.9 1.6 reshape.23
  (48 shorter events, 0.5 us)
Async XLA Ops:
  0.9 4.0 %collective-permute-start = (bf16[2,192,128]{2,1,0:T(8,128)(2,1)S(1)}, bf16[2,192,128]{2,1,0:T(8,128)(2,1)S(1)}, u32[]{:S(2)}, u32[]{:S(2)}) collective-permute-start(bf16[2,192,128]{2,1,0:T(8,128)(2,1)S(1)} %dynamic-slice_bitcast_fusion), channel_id=1, source_target_pairs={{0,1},{1,0},{2,3},{3,2},{4,5},{5,4},{6,7},{7,6},{8,9},{9,8},{10,11... | collective-permute-start | bytes 294920 | tf_op jit(solution)/shard_map/ppermute | solution.py:17
  5.9 9.3 %collective-permute-start.1 = (bf16[2,384,128]{2,1,0:T(8,128)(2,1)S(1)}, bf16[2,384,128]{2,1,0:T(8,128)(2,1)S(1)}, u32[]{:S(2)}, u32[]{:S(2)}) collective-permute-start(bf16[2,384,128]{2,1,0:T(8,128)(2,1)S(1)} %pad_maximum_fusion.refs_0_), channel_id=1, source_target_pairs={{0,2},{2,4},{4,6},{6,8},{8,10},{10,12},{12,14},{14,0},{1,3},{3,5},... | collective-permute-start | bytes 589832 | tf_op jit(solution)/shard_map/ppermute | solution.py:17
  7.8 7.3 %collective-permute-start.3 = (bf16[2,384,128]{2,1,0:T(8,128)(2,1)S(1)}, bf16[2,384,128]{2,1,0:T(8,128)(2,1)S(1)}, u32[]{:S(2)}, u32[]{:S(2)}) collective-permute-start(bf16[2,384,128]{2,1,0:T(8,128)(2,1)S(1)} %pad_maximum_fusion.refs_0_), channel_id=1, source_target_pairs={{0,14},{2,0},{4,2},{6,4},{8,6},{10,8},{12,10},{14,12},{1,15},{3,1}... | collective-permute-start | bytes 589832 | tf_op jit(solution)/shard_map/ppermute | solution.py:17
  15.2 6.9 %collective-permute-start.2 = (bf16[2,384,128]{2,1,0:T(8,128)(2,1)S(1)}, bf16[2,384,128]{2,1,0:T(8,128)(2,1)S(1)}, u32[]{:S(2)}, u32[]{:S(2)}) collective-permute-start(bf16[2,384,128]{2,1,0:T(8,128)(2,1)S(1)} %collective-permute-done.1.refs_7_), channel_id=1, source_target_pairs={{0,2},{2,4},{4,6},{6,8},{8,10},{10,12},{12,14},{14,0},{1,3},{3,5},... | collective-permute-start | bytes 589832 | tf_op jit(solution)/shard_map/ppermute | solution.py:17
  15.2 6.9 %collective-permute-start.4 = (bf16[2,384,128]{2,1,0:T(8,128)(2,1)S(1)}, bf16[2,384,128]{2,1,0:T(8,128)(2,1)S(1)}, u32[]{:S(2)}, u32[]{:S(2)}) collective-permute-start(bf16[2,384,128]{2,1,0:T(8,128)(2,1)S(1)} %collective-permute-done.3.refs_1_), channel_id=1, source_target_pairs={{0,14},{2,0},{4,2},{6,4},{8,6},{10,8},{12,10},{14,12},{1,15},{3,1}... | collective-permute-start | bytes 589832 | tf_op jit(solution)/shard_map/ppermute | solution.py:17
  22.0 16.4 %copy-start.7 = (s32[4,128,2]{1,2,0:T(2,128)S(1)}, s32[4,128,2]{1,2,0:T(2,128)}, u32[]{:S(2)}) copy-start(s32[4,128,2]{1,2,0:T(2,128)} %param.6) | copy-start | bytes 12292
  22.1 16.4 %copy-start.8 = (f32[4,128,2]{1,2,0:T(2,128)S(1)}, f32[4,128,2]{1,2,0:T(2,128)}, u32[]{:S(2)}) copy-start(f32[4,128,2]{1,2,0:T(2,128)} %param.7) | copy-start | bytes 12292
  22.1 16.5 %copy-start = (s32[5]{0:T(128)S(1)}, s32[5]{0:T(128)}, u32[]{:S(2)}) copy-start(s32[5]{0:T(128)} %stack.23.pos) | copy-start | bytes 64
  22.1 5.8 %collective-permute-start.5 = (bf16[2,384,128]{2,1,0:T(8,128)(2,1)S(1)}, bf16[2,384,128]{2,1,0:T(8,128)(2,1)S(1)}, u32[]{:S(2)}, u32[]{:S(2)}) collective-permute-start(bf16[2,384,128]{2,1,0:T(8,128)(2,1)S(1)} %collective-permute-done.2.refs_6_), channel_id=1, source_target_pairs={{0,2},{2,4},{4,6},{6,8},{8,10},{10,12},{12,14},{14,0},{1,3},{3,5},... | collective-permute-start | bytes 589832 | tf_op jit(solution)/shard_map/ppermute | solution.py:17
  22.2 5.8 %collective-permute-start.7 = (bf16[2,384,128]{2,1,0:T(8,128)(2,1)S(1)}, bf16[2,384,128]{2,1,0:T(8,128)(2,1)S(1)}, u32[]{:S(2)}, u32[]{:S(2)}) collective-permute-start(bf16[2,384,128]{2,1,0:T(8,128)(2,1)S(1)} %collective-permute-done.4.refs_2_), channel_id=1, source_target_pairs={{0,14},{2,0},{4,2},{6,4},{8,6},{10,8},{12,10},{14,12},{1,15},{3,1}... | collective-permute-start | bytes 589832 | tf_op jit(solution)/shard_map/ppermute | solution.py:17
  27.9 4.8 %collective-permute-start.6 = (bf16[1,384,128]{2,1,0:T(8,128)(2,1)S(1)}, bf16[1,384,128]{2,1,0:T(8,128)(2,1)S(1)}, u32[]{:S(2)}, u32[]{:S(2)}) collective-permute-start(bf16[1,384,128]{2,1,0:T(8,128)(2,1)S(1)} %slice.24), channel_id=1, source_target_pairs={{0,2},{2,4},{4,6},{6,8},{8,10},{10,12},{12,14},{14,0},{1,3},{3,5},... | collective-permute-start | bytes 294920 | tf_op jit(solution)/shard_map/ppermute | solution.py:17
  28.0 4.6 %collective-permute-start.8 = (bf16[1,384,128]{2,1,0:T(8,128)(2,1)S(1)}, bf16[1,384,128]{2,1,0:T(8,128)(2,1)S(1)}, u32[]{:S(2)}, u32[]{:S(2)}) collective-permute-start(bf16[1,384,128]{2,1,0:T(8,128)(2,1)S(1)} %slice.25), channel_id=1, source_target_pairs={{0,14},{2,0},{4,2},{6,4},{8,6},{10,8},{12,10},{14,12},{1,15},{3,1}... | collective-permute-start | bytes 294920 | tf_op jit(solution)/shard_map/ppermute | solution.py:17
  32.7 23.3 %all-to-all-start = ((bf16[8,192,256]{2,1,0:T(8,128)(2,1)}), bf16[8,192,256]{2,1,0:T(8,128)(2,1)S(1)}, u32[]{:S(2)}, u32[]{:S(2)}) async-start(bf16[8,192,256]{2,1,0:T(8,128)(2,1)} %get-tuple-element.44), calls=%async_computation | async-start | bytes 1572864 | tf_op jit(solution)/shard_map/all_to_all | solution.py:152
  41.9 1.0 copy-start.2
  42.9 43.1 %copy-start.1 = (bf16[160,3200]{1,0:T(8,128)(2,1)}, bf16[160,3200]{1,0:T(8,128)(2,1)S(1)}, u32[]{:S(2)}) copy-start(bf16[160,3200]{1,0:T(8,128)(2,1)S(1)} %get-tuple-element.49.refs_0_) | copy-start | bytes 3072004
  42.9 20.0 %copy-start.3 = (bf16[160,3200]{1,0:T(8,128)(2,1)S(1)}, bf16[160,3200]{1,0:T(8,128)(2,1)}, u32[]{:S(2)}) copy-start(bf16[160,3200]{1,0:T(8,128)(2,1)} %copy-done.2) | copy-start | bytes 3072004
  42.9 19.9 %collective-permute-start.10 = (bf16[160,3200]{1,0:T(8,128)(2,1)}, bf16[160,3200]{1,0:T(8,128)(2,1)}, u32[]{:S(2)}, u32[]{:S(2)}) collective-permute-start(bf16[160,3200]{1,0:T(8,128)(2,1)} %get-tuple-element.50), channel_id=1, source_target_pairs={{0,32},{32,64},{64,96},{96,0},{1,33},{33,65},{65,97},{97,1},{2,34}... | collective-permute-start | bytes 3072008 | tf_op jit(solution)/shard_map/ppermute | solution.py:17
  44.2 18.7 %collective-permute-start.11 = (bf16[160,3200]{1,0:T(8,128)(2,1)}, bf16[160,3200]{1,0:T(8,128)(2,1)}, u32[]{:S(2)}, u32[]{:S(2)}) collective-permute-start(bf16[160,3200]{1,0:T(8,128)(2,1)} %get-tuple-element.51), channel_id=1, source_target_pairs={{0,96},{32,0},{64,32},{96,64},{1,97},{33,1},{65,33},{97,65},{2,98}... | collective-permute-start | bytes 3072008 | tf_op jit(solution)/shard_map/ppermute | solution.py:17
  45.7 17.2 %collective-permute-start.9 = (bf16[160,3200]{1,0:T(8,128)(2,1)S(1)}, bf16[160,3200]{1,0:T(8,128)(2,1)}, u32[]{:S(2)}, u32[]{:S(2)}) collective-permute-start(bf16[160,3200]{1,0:T(8,128)(2,1)S(1)} %get-tuple-element.49.refs_0_), channel_id=1, source_target_pairs={{0,16},{16,0},{1,17},{17,1},{2,18},{18,2},{3,19},{19,3},{4,20},{20... | collective-permute-start | bytes 3072008 | tf_op jit(solution)/shard_map/ppermute | solution.py:17
  56.0 30.0 %copy-start.4 = (bf16[8,192,256]{2,1,0:T(8,128)(2,1)}, bf16[8,192,256]{2,1,0:T(8,128)(2,1)S(1)}, u32[]{:S(2)}) copy-start(bf16[8,192,256]{2,1,0:T(8,128)(2,1)S(1)} %all-to-all-done.refs_8_) | copy-start | bytes 2359300
  56.0 13.7 %collective-permute-start.13 = (bf16[8,192,256]{2,1,0:T(8,128)(2,1)S(1)}, bf16[8,192,256]{2,1,0:T(8,128)(2,1)}, u32[]{:S(2)}, u32[]{:S(2)}) collective-permute-start(bf16[8,192,256]{2,1,0:T(8,128)(2,1)S(1)} %all-to-all-done.refs_8_), channel_id=1, source_target_pairs={{0,1},{1,128},{128,129},{129,0},{2,3},{3,130},{130,131},{131,2},{4... | collective-permute-start | bytes 2359304 | tf_op jit(solution)/shard_map/ppermute | solution.py:17
  57.2 12.5 %collective-permute-start.14 = (bf16[8,192,256]{2,1,0:T(8,128)(2,1)S(1)}, bf16[8,192,256]{2,1,0:T(8,128)(2,1)}, u32[]{:S(2)}, u32[]{:S(2)}) collective-permute-start(bf16[8,192,256]{2,1,0:T(8,128)(2,1)S(1)} %all-to-all-done.refs_8_), channel_id=1, source_target_pairs={{0,129},{1,0},{128,1},{129,128},{2,131},{3,2},{130,3},{131,130},{4... | collective-permute-start | bytes 2359304 | tf_op jit(solution)/shard_map/ppermute | solution.py:17
  58.7 37.5 %all-to-all-start.1 = ((bf16[8,192,256]{2,1,0:T(8,128)(2,1)}), bf16[8,192,256]{2,1,0:T(8,128)(2,1)}, u32[]{:S(2)}, u32[]{:S(2)}) async-start(bf16[8,192,256]{2,1,0:T(8,128)(2,1)} %get-tuple-element.45), calls=%async_computation.1 | async-start | bytes 1572864 | tf_op jit(solution)/shard_map/all_to_all | solution.py:152
  62.9 24.6 %collective-permute-start.12 = (bf16[160,3200]{1,0:T(8,128)(2,1)S(1)}, bf16[160,3200]{1,0:T(8,128)(2,1)}, u32[]{:S(2)}, u32[]{:S(2)}) collective-permute-start(bf16[160,3200]{1,0:T(8,128)(2,1)S(1)} %copy-done.3), channel_id=1, source_target_pairs={{0,64},{32,96},{64,0},{96,32},{1,65},{33,97},{65,1},{97,33},{2,66}... | collective-permute-start | bytes 3072008 | tf_op jit(solution)/shard_map/ppermute | solution.py:17
  69.7 26.4 %collective-permute-start.17 = (bf16[160,3200]{1,0:T(8,128)(2,1)}, bf16[160,3200]{1,0:T(8,128)(2,1)}, u32[]{:S(2)}, u32[]{:S(2)}) collective-permute-start(bf16[160,3200]{1,0:T(8,128)(2,1)} %collective-permute-done.10.refs_1_), channel_id=1, source_target_pairs={{0,16},{16,0},{1,17},{17,1},{2,18},{18,2},{3,19},{19,3},{4,20},{20... | collective-permute-start | bytes 3072008 | tf_op jit(solution)/shard_map/ppermute | solution.py:17
  82.6 13.6 %collective-permute-start.18 = (bf16[160,3200]{1,0:T(8,128)(2,1)}, bf16[160,3200]{1,0:T(8,128)(2,1)}, u32[]{:S(2)}, u32[]{:S(2)}) collective-permute-start(bf16[160,3200]{1,0:T(8,128)(2,1)} %collective-permute-done.11.refs_3_), channel_id=1, source_target_pairs={{0,16},{16,0},{1,17},{17,1},{2,18},{18,2},{3,19},{19,3},{4,20},{20... | collective-permute-start | bytes 3072008 | tf_op jit(solution)/shard_map/ppermute | solution.py:17
  83.7 11.6 %collective-permute-start.15 = (bf16[4,192,256]{2,1,0:T(8,128)(2,1)S(1)}, bf16[4,192,256]{2,1,0:T(8,128)(2,1)S(1)}, u32[]{:S(2)}, u32[]{:S(2)}) collective-permute-start(bf16[4,192,256]{2,1,0:T(8,128)(2,1)S(1)} %slice.20), channel_id=1, source_target_pairs={{0,1},{1,128},{128,129},{129,0},{2,3},{3,130},{130,131},{131,2},{4... | collective-permute-start | bytes 1179656 | tf_op jit(solution)/shard_map/ppermute | solution.py:17
  86.0 10.1 %collective-permute-start.16 = (bf16[4,192,256]{2,1,0:T(8,128)(2,1)S(1)}, bf16[4,192,256]{2,1,0:T(8,128)(2,1)}, u32[]{:S(2)}, u32[]{:S(2)}) collective-permute-start(bf16[4,192,256]{2,1,0:T(8,128)(2,1)S(1)} %slice.21), channel_id=1, source_target_pairs={{0,129},{1,0},{128,1},{129,128},{2,131},{3,2},{130,3},{131,130},{4... | collective-permute-start | bytes 1179656 | tf_op jit(solution)/shard_map/ppermute | solution.py:17
  95.2 0.8 copy-start.10
  96.2 4.4 %collective-permute-start.21 = (bf16[160,3200]{1,0:T(8,128)(2,1)}, bf16[160,3200]{1,0:T(8,128)(2,1)S(1)}, u32[]{:S(2)}, u32[]{:S(2)}) collective-permute-start(bf16[160,3200]{1,0:T(8,128)(2,1)} %collective-permute-done.12.refs_2_), channel_id=1, source_target_pairs={{0,16},{16,0},{1,17},{17,1},{2,18},{18,2},{3,19},{19,3},{4,20},{20... | collective-permute-start | bytes 3072008 | tf_op jit(solution)/shard_map/ppermute | solution.py:17
  97.8 20.5 %collective-permute-start.19 = (bf16[8,192,256]{2,1,0:T(8,128)(2,1)}, bf16[8,192,256]{2,1,0:T(8,128)(2,1)S(1)}, u32[]{:S(2)}, u32[]{:S(2)}) collective-permute-start(bf16[8,192,256]{2,1,0:T(8,128)(2,1)} %all-to-all-done.1.refs_8_), channel_id=1, source_target_pairs={{0,1},{1,128},{128,129},{129,0},{2,3},{3,130},{130,131},{131,2},{4... | collective-permute-start | bytes 2359304 | tf_op jit(solution)/shard_map/ppermute | solution.py:17
  99.1 19.3 %collective-permute-start.20 = (bf16[8,192,256]{2,1,0:T(8,128)(2,1)}, bf16[8,192,256]{2,1,0:T(8,128)(2,1)S(1)}, u32[]{:S(2)}, u32[]{:S(2)}) collective-permute-start(bf16[8,192,256]{2,1,0:T(8,128)(2,1)} %all-to-all-done.1.refs_8_), channel_id=1, source_target_pairs={{0,129},{1,0},{128,1},{129,128},{2,131},{3,2},{130,3},{131,130},{4... | collective-permute-start | bytes 2359304 | tf_op jit(solution)/shard_map/ppermute | solution.py:17
  100.5 1.0 copy-start.9
  118.3 11.2 %copy-start.5 = (bf16[8,192,256]{2,1,0:T(8,128)(2,1)}, bf16[8,192,256]{2,1,0:T(8,128)(2,1)S(1)}, u32[]{:S(2)}) copy-start(bf16[8,192,256]{2,1,0:T(8,128)(2,1)S(1)} %collective-permute-done.19.refs_9_) | copy-start | bytes 2359300
  118.4 11.2 %copy-start.6 = (bf16[8,192,256]{2,1,0:T(8,128)(2,1)}, bf16[8,192,256]{2,1,0:T(8,128)(2,1)S(1)}, u32[]{:S(2)}) copy-start(bf16[8,192,256]{2,1,0:T(8,128)(2,1)S(1)} %collective-permute-done.20.refs_10_) | copy-start | bytes 2359300
  118.4 11.2 %collective-permute-start.22 = (bf16[4,192,256]{2,1,0:T(8,128)(2,1)S(1)}, bf16[4,192,256]{2,1,0:T(8,128)(2,1)}, u32[]{:S(2)}, u32[]{:S(2)}) collective-permute-start(bf16[4,192,256]{2,1,0:T(8,128)(2,1)S(1)} %slice.22), channel_id=1, source_target_pairs={{0,1},{1,128},{128,129},{129,0},{2,3},{3,130},{130,131},{131,2},{4... | collective-permute-start | bytes 1179656 | tf_op jit(solution)/shard_map/ppermute | solution.py:17
  119.1 10.4 %collective-permute-start.23 = (bf16[4,192,256]{2,1,0:T(8,128)(2,1)S(1)}, bf16[4,192,256]{2,1,0:T(8,128)(2,1)}, u32[]{:S(2)}, u32[]{:S(2)}) collective-permute-start(bf16[4,192,256]{2,1,0:T(8,128)(2,1)S(1)} %slice.23), channel_id=1, source_target_pairs={{0,129},{1,0},{128,1},{129,128},{2,131},{3,2},{130,3},{131,130},{4... | collective-permute-start | bytes 1179656 | tf_op jit(solution)/shard_map/ppermute | solution.py:17
  121.2 18.7 %all-to-all-start.2 = ((bf16[16,160,128]{2,1,0:T(8,128)(2,1)}), bf16[16,160,128]{2,1,0:T(8,128)(2,1)S(1)}, u32[]{:S(2)}, u32[]{:S(2)}) async-start(bf16[16,160,128]{2,1,0:T(8,128)(2,1)} %bitcast.11), calls=%async_computation.2 | async-start | bytes 1310720 | tf_op jit(solution)/shard_map/all_to_all | solution.py:213

commit v11 on v10

--- a/solution.py
+++ b/solution.py
@@ -11,6 +11,10 @@
 ANY = pl.BlockSpec(memory_space=pl.ANY)
 VM = pl.BlockSpec(memory_space=pltpu.VMEM)
 SM = pl.BlockSpec(memory_space=pltpu.SMEM)
+
+
+def in_hbm(x):
+    return pltpu.with_memory_space_constraint(x, pltpu.HBM)
 
 
 def ring(x, axis, size, step):
@@ -140,13 +144,13 @@
     wide = units // 32
     blocks = pl.pallas_call(
         columns_kernel,
-        out_shape=[jax.ShapeDtypeStruct((8, rows, 2 * wide), BF)] * 2,
+        out_shape=[pltpu.VMEM((8, rows, 2 * wide), BF)] * 2,
         in_specs=[SM, ANY, ANY],
         out_specs=[VM] * 2,
         scratch_shapes=[pltpu.VMEM((rows, units), BF), pltpu.SemaphoreType.DMA(())],
-        compiler_params=pltpu.CompilerParams(vmem_limit_bytes=58 << 20),
+        compiler_params=pltpu.CompilerParams(vmem_limit_bytes=8 << 20),
         name="columns",
-    )(pos, gate_train, up_train)
+    )(pos, in_hbm(gate_train), in_hbm(up_train))
 
     def exchange(x):
         return lax.all_to_all(x, "z", split_axis=0, concat_axis=0, tiled=True)
@@ -168,10 +172,10 @@
     feats = [pair] + above[1:] + [jnp.concatenate(last, axis=0)] + below[:0:-1]
     sent = pl.pallas_call(
         dispatch_kernel,
-        out_shape=[jax.ShapeDtypeStruct((2 * MOST, 16 * width + 128), BF)] * 4,
+        out_shape=[pltpu.VMEM((2 * MOST, 16 * width + 128), BF)] * 4,
         in_specs=[SM] + [VM] * 9,
         out_specs=[VM] * 4,
-        compiler_params=pltpu.CompilerParams(vmem_limit_bytes=24 << 20),
+        compiler_params=pltpu.CompilerParams(vmem_limit_bytes=10 << 20),
         name="dispatch",
     )(pos, meta, *feats)
     near = ring(sent[1], "y", 4, 1), ring(sent[3], "y", 4, 3)
@@ -183,17 +187,16 @@
     opposite = ring(far_rows, "y", 4, 2)
     left_a, right_a, *near = barrier((left_a, right_a, *near))
     far_a = far(left_a, right_a)
-    other += [ring(h, "c", 2, 1) for h in near]
-    own_b, opposite, *rest = barrier((own_b, opposite, *far_a, *other))
-    far_a, other = rest[:2], rest[2:]
+    own_b, opposite, *rest = barrier((own_b, opposite, *near, *far_a))
+    near, far_a = rest[:2], rest[2:]
     left_b, right_b = sides(own_b)
     held = [sent[0], near[0], opposite, near[1]]
-    other = [other[0], other[1], ring(opposite, "c", 2, 1), other[2]]
+    other += [ring(h, "c", 2, 1) for h in held[1:]]
 
     def expert(*ws):
         return pl.pallas_call(
             expert_kernel,
-            out_shape=jax.ShapeDtypeStruct((4, 2, 2, 2 * MOST, wide), BF),
+            out_shape=pltpu.VMEM((4, 2, 2, 2 * MOST, wide), BF),
             in_specs=[SM] + [ANY] * 13,
             out_specs=VM,
             scratch_shapes=[
@@ -202,12 +205,12 @@
                 pltpu.SemaphoreType.DMA((8,)),
                 pltpu.SemaphoreType.DMA((5, 8)),
             ],
-            compiler_params=pltpu.CompilerParams(vmem_limit_bytes=58 << 20),
+            compiler_params=pltpu.CompilerParams(vmem_limit_bytes=18 << 20),
             cost_estimate=pl.CostEstimate(
                 flops=16 * MOST * 16 * width * 8 * wide, bytes_accessed=12 << 20, transcendentals=16 * MOST * 2 * wide
             ),
             name="expert",
-        )(pos, *held, *other, *ws)
+        )(pos, *map(in_hbm, (*held, *other)), *ws)
 
     def give_back(act):
         back = lax.all_to_all(act.reshape(16, 2 * MOST, wide), ("y", "c", "xl"), split_axis=0, concat_axis=0, tiled=True)
@@ -222,7 +225,7 @@
         out_shape=jax.ShapeDtypeStruct((steps, n, 1024), BF),
         in_specs=[VM] * 3,
         out_specs=VM,
-        compiler_params=pltpu.CompilerParams(vmem_limit_bytes=24 << 20),
+        compiler_params=pltpu.CompilerParams(vmem_limit_bytes=10 << 20),
         name="combine",
     )(meta, back_a, back_b)
     return out.reshape(steps, n, 2, 2, 256)

time: 162 us -> 171 us (1.056)
  Pallas kernels: 29.1 us -> 34.1 us
  local copies, waits for them, and re-layouts: 7.95 us -> 11.9 us
  blocking collectives: 18.5 us -> 20.6 us
    pallas_call x4, Pallas kernels: 27.6 us -> 32.6 us  [the longest x2 25.6 us: expert(): pl.pallas_call(expert_kernel, out_shape=pltpu.VMEM((4, 2, 2, 2 * MOST, wi...]
    unnamed x22 -> x30, local copies, waits for them, and re-layouts: 2.76 us -> 7.62 us
    ppermute x24, starting transfers between devices: 54.4 us -> 51.6 us  [ring(): return lax.ppermute(x, axis, [(i, (i + step) % size) for i in range(size)])]
    all_to_all x1, blocking collectives: 18.5 us -> 20.6 us  [give_back(): lax.all_to_all(act.reshape(16, 2 * MOST, wide), ('y', 'c', 'xl'), split_a...]
    all_to_all x1, starting transfers between devices: 5.42 us -> 7.19 us  [give_back(): lax.all_to_all(act.reshape(16, 2 * MOST, wide), ('y', 'c', 'xl'), split_a...]
  transfers between devices with their start and end apart: 27 -> 27, of which waited for: 10 -> 14; matrix products, arithmetic and copies ran while one was open for 2% -> 1% of each run, Pallas kernels for 17% -> 19%
where the time goes in v11:
time: 171 us; the launch traced here: 170 us
  starting transfers between devices  68.4 us (40%)
  Pallas kernels  34.1 us (20%)
  waiting for transfers between devices  33.8 us (20%)
  blocking collectives  20.6 us (12%)
  local copies, waits for them, and re-layouts  11.9 us (7%)
    ppermute x24, starting transfers between devices, ring(): return lax.ppermute(x, axis, [(i, (i + step) % size) for i in range(size)])  51.6 us
    ppermute x24, waiting for transfers between devices, ring(): return lax.ppermute(x, axis, [(i, (i + step) % size) for i in range(size)])  30.7 us
    pallas_call x2, Pallas kernels, expert(): pl.pallas_call(expert_kernel, out_shape=pltpu.VMEM((4, 2, 2, 2 * MOST, wi...  25.6 us
    all_to_all x1, blocking collectives, give_back(): lax.all_to_all(act.reshape(16, 2 * MOST, wide), ('y', 'c', 'xl'), split_a...  20.6 us
    all_to_all x2, starting transfers between devices, exchange(): return lax.all_to_all(x, 'z', split_axis=0, concat_axis=0, tiled=True)  9.61 us
    unnamed x30, local copies, waits for them, and re-layouts  7.62 us
    all_to_all x1, starting transfers between devices, give_back(): lax.all_to_all(act.reshape(16, 2 * MOST, wide), ('y', 'c', 'xl'), split_a...  7.19 us
    pallas_call x1, Pallas kernels, body(): pl.pallas_call(dispatch_kernel, out_shape=[pltpu.VMEM((2 * MOST, 16 * wid...  3.67 us
  transfers between devices with their start and end apart: 27, of which 14 were waited for; matrix products, arithmetic and copies ran while one was open for 1% of the time, Pallas kernels for 19%

profile of v11, /device:TPU:1, one launch (start us, length us, event | category | flops | bytes accessed | tf_op | source)
XLA Modules:
  0.0 170.0 jit_solution(8594079724159025628)
XLA Ops:
  0.0 0.9 dynamic-slice_bitcast_fusion
  0.9 2.0 %collective-permute-start = (bf16[2,192,128]{2,1,0:T(8,128)(2,1)S(1)}, bf16[2,192,128]{2,1,0:T(8,128)(2,1)S(1)}, u32[]{:S(2)}, u32[]{:S(2)}) collective-permute-start(bf16[2,192,128]{2,1,0:T(8,128)(2,1)S(1)} %dynamic-slice_bitcast_fusion), channel_id=1, source_target_pairs={{0,1},{1,0},{2,3},{3,2},{4,5},{5,4},{6,7},{7,6},{8,9},{9,8},{10,11... | collective-permute-start | bytes 294920 | tf_op jit(solution)/shard_map/ppermute | solution.py:21
  2.9 2.0 %collective-permute-done = bf16[2,192,128]{2,1,0:T(8,128)(2,1)S(1)} collective-permute-done((bf16[2,192,128]{2,1,0:T(8,128)(2,1)S(1)}, bf16[2,192,128]{2,1,0:T(8,128)(2,1)S(1)}, u32[]{:S(2)}, u32[]{:S(2)}) %collective-permute-start) | collective-permute-done | bytes 98336 | tf_op jit(solution)/shard_map/ppermute | solution.py:21
  4.9 0.9 bitcast_select_fusion.1
  5.9 2.0 %collective-permute-start.1 = (bf16[2,384,128]{2,1,0:T(8,128)(2,1)S(1)}, bf16[2,384,128]{2,1,0:T(8,128)(2,1)S(1)}, u32[]{:S(2)}, u32[]{:S(2)}) collective-permute-start(bf16[2,384,128]{2,1,0:T(8,128)(2,1)S(1)} %pad_maximum_fusion.refs_0_), channel_id=1, source_target_pairs={{0,2},{2,4},{4,6},{6,8},{8,10},{10,12},{12,14},{14,0},{1,3},{3,5},... | collective-permute-start | bytes 589832 | tf_op jit(solution)/shard_map/ppermute | solution.py:21
  7.9 4.0 %collective-permute-start.3 = (bf16[2,384,128]{2,1,0:T(8,128)(2,1)S(1)}, bf16[2,384,128]{2,1,0:T(8,128)(2,1)S(1)}, u32[]{:S(2)}, u32[]{:S(2)}) collective-permute-start(bf16[2,384,128]{2,1,0:T(8,128)(2,1)S(1)} %pad_maximum_fusion.refs_0_), channel_id=1, source_target_pairs={{0,14},{2,0},{4,2},{6,4},{8,6},{10,8},{12,10},{14,12},{1,15},{3,1}... | collective-permute-start | bytes 589832 | tf_op jit(solution)/shard_map/ppermute | solution.py:21
  11.9 3.3 %collective-permute-done.1.refs_7_ = bf16[2,384,128]{2,1,0:T(8,128)(2,1)S(1)} collective-permute-done((bf16[2,384,128]{2,1,0:T(8,128)(2,1)S(1)}, bf16[2,384,128]{2,1,0:T(8,128)(2,1)S(1)}, u32[]{:S(2)}, u32[]{:S(2)}) %collective-permute-start.1) | collective-permute-done | bytes 196640 | tf_op jit(solution)/shard_map/ppermute | solution.py:21
  15.2 2.7 %collective-permute-start.4 = (bf16[2,384,128]{2,1,0:T(8,128)(2,1)S(1)}, bf16[2,384,128]{2,1,0:T(8,128)(2,1)S(1)}, u32[]{:S(2)}, u32[]{:S(2)}) collective-permute-start(bf16[2,384,128]{2,1,0:T(8,128)(2,1)S(1)} %collective-permute-done.3.refs_1_), channel_id=1, source_target_pairs={{0,14},{2,0},{4,2},{6,4},{8,6},{10,8},{12,10},{14,12},{1,15},{3,1}... | collective-permute-start | bytes 589832 | tf_op jit(solution)/shard_map/ppermute | solution.py:21
  17.9 3.4 %columns.1 = (bf16[8,192,256]{2,1,0:T(8,128)(2,1)}, bf16[8,192,256]{2,1,0:T(8,128)(2,1)}) custom-call(s32[5]{0:T(128)S(1)} %stack.23.pos, bf16[1,192,4096]{2,1,0:T(8,128)(2,1)} %gate.1, bf16[1,192,4096]{2,1,0:T(8,128)(2,1)} %up.1), custom_call_target="tpu_custom_call" | custom-call | tf_op jit(solution)/shard_map/columns/pallas_call | solution.py:145
  21.5 2.7 %collective-permute-start.7 = (bf16[2,384,128]{2,1,0:T(8,128)(2,1)S(1)}, bf16[2,384,128]{2,1,0:T(8,128)(2,1)S(1)}, u32[]{:S(2)}, u32[]{:S(2)}) collective-permute-start(bf16[2,384,128]{2,1,0:T(8,128)(2,1)S(1)} %collective-permute-done.4.refs_2_), channel_id=1, source_target_pairs={{0,14},{2,0},{4,2},{6,4},{8,6},{10,8},{12,10},{14,12},{1,15},{3,1}... | collective-permute-start | bytes 589832 | tf_op jit(solution)/shard_map/ppermute | solution.py:21
  24.1 3.1 %collective-permute-done.5.refs_5_ = bf16[2,384,128]{2,1,0:T(8,128)(2,1)S(1)} collective-permute-done((bf16[2,384,128]{2,1,0:T(8,128)(2,1)S(1)}, bf16[2,384,128]{2,1,0:T(8,128)(2,1)S(1)}, u32[]{:S(2)}, u32[]{:S(2)}) %collective-permute-start.5) | collective-permute-done | bytes 196640 | tf_op jit(solution)/shard_map/ppermute | solution.py:21
  27.3 2.7 %collective-permute-start.8 = (bf16[1,384,128]{2,1,0:T(8,128)(2,1)S(1)}, bf16[1,384,128]{2,1,0:T(8,128)(2,1)S(1)}, u32[]{:S(2)}, u32[]{:S(2)}) collective-permute-start(bf16[1,384,128]{2,1,0:T(8,128)(2,1)S(1)} %slice.25), channel_id=1, source_target_pairs={{0,14},{2,0},{4,2},{6,4},{8,6},{10,8},{12,10},{14,12},{1,15},{3,1}... | collective-permute-start | bytes 294920 | tf_op jit(solution)/shard_map/ppermute | solution.py:21
  30.0 1.9 %collective-permute-done.6 = bf16[1,384,128]{2,1,0:T(8,128)(2,1)S(1)} collective-permute-done((bf16[1,384,128]{2,1,0:T(8,128)(2,1)S(1)}, bf16[1,384,128]{2,1,0:T(8,128)(2,1)S(1)}, u32[]{:S(2)}, u32[]{:S(2)}) %collective-permute-start.6) | collective-permute-done | bytes 98336 | tf_op jit(solution)/shard_map/ppermute | solution.py:21
  32.0 5.9 %all-to-all-start = ((bf16[8,192,256]{2,1,0:T(8,128)(2,1)}), bf16[8,192,256]{2,1,0:T(8,128)(2,1)S(1)}, u32[]{:S(2)}, u32[]{:S(2)}) async-start(bf16[8,192,256]{2,1,0:T(8,128)(2,1)} %get-tuple-element.43), calls=%async_computation | async-start | bytes 1572864 | tf_op jit(solution)/shard_map/all_to_all | solution.py:156
  37.9 3.7 %dispatch.1 = (bf16[160,3200]{1,0:T(8,128)(2,1)}, bf16[160,3200]{1,0:T(8,128)(2,1)}, bf16[160,3200]{1,0:T(8,128)(2,1)S(1)}, bf16[160,3200]{1,0:T(8,128)(2,1)}) custom-call(s32[5]{0:T(128)S(1)} %stack.23.pos, f32[4,4,128]{2,1,0:T(4,128)S(1)} %maximum_bitcast_fusion.meta, bf16[2,384,128]{2,1,0:T(8,128)(2,1)S(1)} %pad_maximum_fusion.refs_0_, ...), custom_call_target="tpu_custom_call" | custom-call | tf_op jit(solution)/shard_map/dispatch/pallas_call | solution.py:173
  41.5 1.0 copy-done.4
  42.5 1.3 collective-permute-start.10
  43.8 1.5 collective-permute-start.11
  45.3 6.8 %collective-permute-start.9 = (bf16[160,3200]{1,0:T(8,128)(2,1)}, bf16[160,3200]{1,0:T(8,128)(2,1)}, u32[]{:S(2)}, u32[]{:S(2)}) collective-permute-start(bf16[160,3200]{1,0:T(8,128)(2,1)} %get-tuple-element.48.refs_0_), channel_id=1, source_target_pairs={{0,16},{16,0},{1,17},{17,1},{2,18},{18,2},{3,19},{19,3},{4,20},{20... | collective-permute-start | bytes 3072008 | tf_op jit(solution)/shard_map/ppermute | solution.py:21
  52.1 3.2 %all-to-all-done.refs_8_ = bf16[8,192,256]{2,1,0:T(8,128)(2,1)S(1)} async-done(((bf16[8,192,256]{2,1,0:T(8,128)(2,1)}), bf16[8,192,256]{2,1,0:T(8,128)(2,1)S(1)}, u32[]{:S(2)}, u32[]{:S(2)}) %all-to-all-start) | async-done | bytes 786464 | tf_op jit(solution)/shard_map/all_to_all | solution.py:156
  55.2 3.8 %all-to-all-start.1 = ((bf16[8,192,256]{2,1,0:T(8,128)(2,1)}), bf16[8,192,256]{2,1,0:T(8,128)(2,1)S(1)}, u32[]{:S(2)}, u32[]{:S(2)}) async-start(bf16[8,192,256]{2,1,0:T(8,128)(2,1)} %get-tuple-element.44), calls=%async_computation.1 | async-start | bytes 1572864 | tf_op jit(solution)/shard_map/all_to_all | solution.py:156
  59.0 1.2 collective-permute-start.13
  60.2 1.5 collective-permute-start.14
  62.0 2.6 %collective-permute-start.12 = (bf16[160,3200]{1,0:T(8,128)(2,1)}, bf16[160,3200]{1,0:T(8,128)(2,1)S(1)}, u32[]{:S(2)}, u32[]{:S(2)}) collective-permute-start(bf16[160,3200]{1,0:T(8,128)(2,1)} %copy-done.4), channel_id=1, source_target_pairs={{0,64},{32,96},{64,0},{96,32},{1,65},{33,97},{65,1},{97,33},{2,66}... | collective-permute-start | bytes 3072008 | tf_op jit(solution)/shard_map/ppermute | solution.py:21
  64.6 8.1 %collective-permute-done.13.refs_9_ = bf16[8,192,256]{2,1,0:T(8,128)(2,1)S(1)} collective-permute-done((bf16[8,192,256]{2,1,0:T(8,128)(2,1)S(1)}, bf16[8,192,256]{2,1,0:T(8,128)(2,1)S(1)}, u32[]{:S(2)}, u32[]{:S(2)}) %collective-permute-start.13) | collective-permute-done | bytes 786464 | tf_op jit(solution)/shard_map/ppermute | solution.py:21
  72.7 1.0 collective-permute-start.15
  73.7 1.9 %collective-permute-start.16 = (bf16[4,192,256]{2,1,0:T(8,128)(2,1)S(1)}, bf16[4,192,256]{2,1,0:T(8,128)(2,1)S(1)}, u32[]{:S(2)}, u32[]{:S(2)}) collective-permute-start(bf16[4,192,256]{2,1,0:T(8,128)(2,1)S(1)} %slice.21), channel_id=1, source_target_pairs={{0,129},{1,0},{128,1},{129,128},{2,131},{3,2},{130,3},{131,130},{4... | collective-permute-start | bytes 1179656 | tf_op jit(solution)/shard_map/ppermute | solution.py:21
  75.6 5.2 %collective-permute-done.12.refs_2_ = bf16[160,3200]{1,0:T(8,128)(2,1)S(1)} collective-permute-done((bf16[160,3200]{1,0:T(8,128)(2,1)}, bf16[160,3200]{1,0:T(8,128)(2,1)S(1)}, u32[]{:S(2)}, u32[]{:S(2)}) %collective-permute-start.12) | collective-permute-done | bytes 1024032 | tf_op jit(solution)/shard_map/ppermute | solution.py:21
  80.8 3.1 %collective-permute-done.15.refs_11_ = bf16[4,192,256]{2,1,0:T(8,128)(2,1)S(1)} collective-permute-done((bf16[4,192,256]{2,1,0:T(8,128)(2,1)S(1)}, bf16[4,192,256]{2,1,0:T(8,128)(2,1)S(1)}, u32[]{:S(2)}, u32[]{:S(2)}) %collective-permute-start.15) | collective-permute-done | bytes 393248 | tf_op jit(solution)/shard_map/ppermute | solution.py:21
  84.8 11.8 %collective-permute-start.19 = (bf16[160,3200]{1,0:T(8,128)(2,1)}, bf16[160,3200]{1,0:T(8,128)(2,1)S(1)}, u32[]{:S(2)}, u32[]{:S(2)}) collective-permute-start(bf16[160,3200]{1,0:T(8,128)(2,1)} %collective-permute-done.10.refs_1_), channel_id=1, source_target_pairs={{0,16},{16,0},{1,17},{17,1},{2,18},{18,2},{3,19},{19,3},{4,20},{20... | collective-permute-start | bytes 3072008 | tf_op jit(solution)/shard_map/ppermute | solution.py:21
  97.1 1.2 collective-permute-start.17
  98.3 1.5 collective-permute-start.18
  100.5 1.5 collective-permute-done.21.refs_7_
  102.0 1.0 copy-done.14
  103.0 1.0 copy-done.6
  103.9 13.2 %expert.2 = bf16[4,2,2,160,128]{4,3,2,1,0:T(8,128)(2,1)} custom-call(s32[5]{0:T(128)S(1)} %stack.23.pos, bf16[160,3200]{1,0:T(8,128)(2,1)} %get-tuple-element.48.refs_0_, bf16[160,3200]{1,0:T(8,128)(2,1)} %collective-permute-done.10.refs_1_, bf16[160,3200]{1,0:T(8,128)(2,1)} %copy-done.11, bf16[160,3200]{1,0:T(8,128)(2,1)} %collective-permute-done.11.refs_3_, ...), custom_call_target="tpu_custom_call" | custom-call | flops 4026531840 | bytes 12582912 | tf_op jit(solution)/shard_map/expert/pallas_call | solution.py:197
  117.5 0.8 slice.22
  118.3 1.0 copy-done
  119.3 0.9 collective-permute-start.22
  120.2 0.8 slice.23
  121.0 1.7 %collective-permute-start.23 = (bf16[4,192,256]{2,1,0:T(8,128)(2,1)}, bf16[4,192,256]{2,1,0:T(8,128)(2,1)S(1)}, u32[]{:S(2)}, u32[]{:S(2)}) collective-permute-start(bf16[4,192,256]{2,1,0:T(8,128)(2,1)} %slice.23), channel_id=1, source_target_pairs={{0,129},{1,0},{128,1},{129,128},{2,131},{3,2},{130,3},{131,130},{4... | collective-permute-start | bytes 1179656 | tf_op jit(solution)/shard_map/ppermute | solution.py:21
  122.8 7.2 %all-to-all-start.2 = ((bf16[16,160,128]{2,1,0:T(8,128)(2,1)}), bf16[16,160,128]{2,1,0:T(8,128)(2,1)S(1)}, u32[]{:S(2)}, u32[]{:S(2)}) async-start(bf16[16,160,128]{2,1,0:T(8,128)(2,1)} %bitcast.11), calls=%async_computation.2 | async-start | bytes 1310720 | tf_op jit(solution)/shard_map/all_to_all | solution.py:216
  131.8 1.1 copy-done.3
  133.0 1.0 copy-done.8
  134.0 12.4 %expert.3 = bf16[4,2,2,160,128]{4,3,2,1,0:T(8,128)(2,1)S(1)} custom-call(s32[5]{0:T(128)S(1)} %stack.23.pos, bf16[160,3200]{1,0:T(8,128)(2,1)} %get-tuple-element.48.refs_0_, bf16[160,3200]{1,0:T(8,128)(2,1)} %collective-permute-done.10.refs_1_, bf16[160,3200]{1,0:T(8,128)(2,1)} %copy-done.11, bf16[160,3200]{1,0:T(8,128)(2,1)} %collective-permute-done.11.refs_3_, ...), custom_call_target="tpu_custom_call" | custom-call | flops 4026531840 | bytes 12582912 | tf_op jit(solution)/shard_map/expert/pallas_call | solution.py:197
  146.3 20.6 %all_to_all.20 = bf16[16,160,128]{2,1,0:T(8,128)(2,1)S(1)} all-to-all(bf16[16,160,128]{2,1,0:T(8,128)(2,1)S(1)} %bitcast.21), channel_id=1, replica_groups=mesh['dp'=2,'y'=4,'c'=2,'z'=8,'xl'=2] {'y','c','xl'}, dimensions={0} | all-to-all | bytes 1310720 | tf_op jit(solution)/shard_map/all_to_all | solution.py:216
  167.0 1.4 combine.1
  168.4 1.6 reshape.23
  (56 shorter events, 4.9 us)
Async XLA Ops:
  0.9 4.0 %collective-permute-start = (bf16[2,192,128]{2,1,0:T(8,128)(2,1)S(1)}, bf16[2,192,128]{2,1,0:T(8,128)(2,1)S(1)}, u32[]{:S(2)}, u32[]{:S(2)}) collective-permute-start(bf16[2,192,128]{2,1,0:T(8,128)(2,1)S(1)} %dynamic-slice_bitcast_fusion), channel_id=1, source_target_pairs={{0,1},{1,0},{2,3},{3,2},{4,5},{5,4},{6,7},{7,6},{8,9},{9,8},{10,11... | collective-permute-start | bytes 294920 | tf_op jit(solution)/shard_map/ppermute | solution.py:21
  5.9 9.3 %collective-permute-start.1 = (bf16[2,384,128]{2,1,0:T(8,128)(2,1)S(1)}, bf16[2,384,128]{2,1,0:T(8,128)(2,1)S(1)}, u32[]{:S(2)}, u32[]{:S(2)}) collective-permute-start(bf16[2,384,128]{2,1,0:T(8,128)(2,1)S(1)} %pad_maximum_fusion.refs_0_), channel_id=1, source_target_pairs={{0,2},{2,4},{4,6},{6,8},{8,10},{10,12},{12,14},{14,0},{1,3},{3,5},... | collective-permute-start | bytes 589832 | tf_op jit(solution)/shard_map/ppermute | solution.py:21
  7.9 7.3 %collective-permute-start.3 = (bf16[2,384,128]{2,1,0:T(8,128)(2,1)S(1)}, bf16[2,384,128]{2,1,0:T(8,128)(2,1)S(1)}, u32[]{:S(2)}, u32[]{:S(2)}) collective-permute-start(bf16[2,384,128]{2,1,0:T(8,128)(2,1)S(1)} %pad_maximum_fusion.refs_0_), channel_id=1, source_target_pairs={{0,14},{2,0},{4,2},{6,4},{8,6},{10,8},{12,10},{14,12},{1,15},{3,1}... | collective-permute-start | bytes 589832 | tf_op jit(solution)/shard_map/ppermute | solution.py:21
  15.2 6.2 %collective-permute-start.2 = (bf16[2,384,128]{2,1,0:T(8,128)(2,1)S(1)}, bf16[2,384,128]{2,1,0:T(8,128)(2,1)S(1)}, u32[]{:S(2)}, u32[]{:S(2)}) collective-permute-start(bf16[2,384,128]{2,1,0:T(8,128)(2,1)S(1)} %collective-permute-done.1.refs_7_), channel_id=1, source_target_pairs={{0,2},{2,4},{4,6},{6,8},{8,10},{10,12},{12,14},{14,0},{1,3},{3,5},... | collective-permute-start | bytes 589832 | tf_op jit(solution)/shard_map/ppermute | solution.py:21
  15.2 6.2 %collective-permute-start.4 = (bf16[2,384,128]{2,1,0:T(8,128)(2,1)S(1)}, bf16[2,384,128]{2,1,0:T(8,128)(2,1)S(1)}, u32[]{:S(2)}, u32[]{:S(2)}) collective-permute-start(bf16[2,384,128]{2,1,0:T(8,128)(2,1)S(1)} %collective-permute-done.3.refs_1_), channel_id=1, source_target_pairs={{0,14},{2,0},{4,2},{6,4},{8,6},{10,8},{12,10},{14,12},{1,15},{3,1}... | collective-permute-start | bytes 589832 | tf_op jit(solution)/shard_map/ppermute | solution.py:21
  21.3 16.5 %copy-start.9 = (s32[4,128,2]{1,2,0:T(2,128)S(1)}, s32[4,128,2]{1,2,0:T(2,128)}, u32[]{:S(2)}) copy-start(s32[4,128,2]{1,2,0:T(2,128)} %param.6) | copy-start | bytes 12292
  21.3 16.5 %copy-start.10 = (f32[4,128,2]{1,2,0:T(2,128)S(1)}, f32[4,128,2]{1,2,0:T(2,128)}, u32[]{:S(2)}) copy-start(f32[4,128,2]{1,2,0:T(2,128)} %param.7) | copy-start | bytes 12292
  21.4 5.8 %collective-permute-start.5 = (bf16[2,384,128]{2,1,0:T(8,128)(2,1)S(1)}, bf16[2,384,128]{2,1,0:T(8,128)(2,1)S(1)}, u32[]{:S(2)}, u32[]{:S(2)}) collective-permute-start(bf16[2,384,128]{2,1,0:T(8,128)(2,1)S(1)} %collective-permute-done.2.refs_6_), channel_id=1, source_target_pairs={{0,2},{2,4},{4,6},{6,8},{8,10},{10,12},{12,14},{14,0},{1,3},{3,5},... | collective-permute-start | bytes 589832 | tf_op jit(solution)/shard_map/ppermute | solution.py:21
  21.5 5.8 %collective-permute-start.7 = (bf16[2,384,128]{2,1,0:T(8,128)(2,1)S(1)}, bf16[2,384,128]{2,1,0:T(8,128)(2,1)S(1)}, u32[]{:S(2)}, u32[]{:S(2)}) collective-permute-start(bf16[2,384,128]{2,1,0:T(8,128)(2,1)S(1)} %collective-permute-done.4.refs_2_), channel_id=1, source_target_pairs={{0,14},{2,0},{4,2},{6,4},{8,6},{10,8},{12,10},{14,12},{1,15},{3,1}... | collective-permute-start | bytes 589832 | tf_op jit(solution)/shard_map/ppermute | solution.py:21
  27.2 4.8 %collective-permute-start.6 = (bf16[1,384,128]{2,1,0:T(8,128)(2,1)S(1)}, bf16[1,384,128]{2,1,0:T(8,128)(2,1)S(1)}, u32[]{:S(2)}, u32[]{:S(2)}) collective-permute-start(bf16[1,384,128]{2,1,0:T(8,128)(2,1)S(1)} %slice.24), channel_id=1, source_target_pairs={{0,2},{2,4},{4,6},{6,8},{8,10},{10,12},{12,14},{14,0},{1,3},{3,5},... | collective-permute-start | bytes 294920 | tf_op jit(solution)/shard_map/ppermute | solution.py:21
  27.3 4.6 %collective-permute-start.8 = (bf16[1,384,128]{2,1,0:T(8,128)(2,1)S(1)}, bf16[1,384,128]{2,1,0:T(8,128)(2,1)S(1)}, u32[]{:S(2)}, u32[]{:S(2)}) collective-permute-start(bf16[1,384,128]{2,1,0:T(8,128)(2,1)S(1)} %slice.25), channel_id=1, source_target_pairs={{0,14},{2,0},{4,2},{6,4},{8,6},{10,8},{12,10},{14,12},{1,15},{3,1}... | collective-permute-start | bytes 294920 | tf_op jit(solution)/shard_map/ppermute | solution.py:21
  32.0 23.3 %all-to-all-start = ((bf16[8,192,256]{2,1,0:T(8,128)(2,1)}), bf16[8,192,256]{2,1,0:T(8,128)(2,1)S(1)}, u32[]{:S(2)}, u32[]{:S(2)}) async-start(bf16[8,192,256]{2,1,0:T(8,128)(2,1)} %get-tuple-element.43), calls=%async_computation | async-start | bytes 1572864 | tf_op jit(solution)/shard_map/all_to_all | solution.py:156
  41.5 1.0 copy-start.4
  42.5 19.5 %collective-permute-start.10 = (bf16[160,3200]{1,0:T(8,128)(2,1)}, bf16[160,3200]{1,0:T(8,128)(2,1)}, u32[]{:S(2)}, u32[]{:S(2)}) collective-permute-start(bf16[160,3200]{1,0:T(8,128)(2,1)} %get-tuple-element.49), channel_id=1, source_target_pairs={{0,32},{32,64},{64,96},{96,0},{1,33},{33,65},{65,97},{97,1},{2,34}... | collective-permute-start | bytes 3072008 | tf_op jit(solution)/shard_map/ppermute | solution.py:21
  43.8 18.2 %collective-permute-start.11 = (bf16[160,3200]{1,0:T(8,128)(2,1)}, bf16[160,3200]{1,0:T(8,128)(2,1)}, u32[]{:S(2)}, u32[]{:S(2)}) collective-permute-start(bf16[160,3200]{1,0:T(8,128)(2,1)} %get-tuple-element.50), channel_id=1, source_target_pairs={{0,96},{32,0},{64,32},{96,64},{1,97},{33,1},{65,33},{97,65},{2,98}... | collective-permute-start | bytes 3072008 | tf_op jit(solution)/shard_map/ppermute | solution.py:21
  45.3 16.8 %collective-permute-start.9 = (bf16[160,3200]{1,0:T(8,128)(2,1)}, bf16[160,3200]{1,0:T(8,128)(2,1)}, u32[]{:S(2)}, u32[]{:S(2)}) collective-permute-start(bf16[160,3200]{1,0:T(8,128)(2,1)} %get-tuple-element.48.refs_0_), channel_id=1, source_target_pairs={{0,16},{16,0},{1,17},{17,1},{2,18},{18,2},{3,19},{19,3},{4,20},{20... | collective-permute-start | bytes 3072008 | tf_op jit(solution)/shard_map/ppermute | solution.py:21
  55.2 29.5 %all-to-all-start.1 = ((bf16[8,192,256]{2,1,0:T(8,128)(2,1)}), bf16[8,192,256]{2,1,0:T(8,128)(2,1)S(1)}, u32[]{:S(2)}, u32[]{:S(2)}) async-start(bf16[8,192,256]{2,1,0:T(8,128)(2,1)} %get-tuple-element.44), calls=%async_computation.1 | async-start | bytes 1572864 | tf_op jit(solution)/shard_map/all_to_all | solution.py:156
  59.0 13.7 %collective-permute-start.13 = (bf16[8,192,256]{2,1,0:T(8,128)(2,1)S(1)}, bf16[8,192,256]{2,1,0:T(8,128)(2,1)S(1)}, u32[]{:S(2)}, u32[]{:S(2)}) collective-permute-start(bf16[8,192,256]{2,1,0:T(8,128)(2,1)S(1)} %all-to-all-done.refs_8_), channel_id=1, source_target_pairs={{0,1},{1,128},{128,129},{129,0},{2,3},{3,130},{130,131},{131,2},{4... | collective-permute-start | bytes 2359304 | tf_op jit(solution)/shard_map/ppermute | solution.py:21
  60.2 12.5 %collective-permute-start.14 = (bf16[8,192,256]{2,1,0:T(8,128)(2,1)S(1)}, bf16[8,192,256]{2,1,0:T(8,128)(2,1)S(1)}, u32[]{:S(2)}, u32[]{:S(2)}) collective-permute-start(bf16[8,192,256]{2,1,0:T(8,128)(2,1)S(1)} %all-to-all-done.refs_8_), channel_id=1, source_target_pairs={{0,129},{1,0},{128,1},{129,128},{2,131},{3,2},{130,3},{131,130},{4... | collective-permute-start | bytes 2359304 | tf_op jit(solution)/shard_map/ppermute | solution.py:21
  62.0 18.8 %collective-permute-start.12 = (bf16[160,3200]{1,0:T(8,128)(2,1)}, bf16[160,3200]{1,0:T(8,128)(2,1)S(1)}, u32[]{:S(2)}, u32[]{:S(2)}) collective-permute-start(bf16[160,3200]{1,0:T(8,128)(2,1)} %copy-done.4), channel_id=1, source_target_pairs={{0,64},{32,96},{64,0},{96,32},{1,65},{33,97},{65,1},{97,33},{2,66}... | collective-permute-start | bytes 3072008 | tf_op jit(solution)/shard_map/ppermute | solution.py:21
  72.7 11.3 %collective-permute-start.15 = (bf16[4,192,256]{2,1,0:T(8,128)(2,1)S(1)}, bf16[4,192,256]{2,1,0:T(8,128)(2,1)S(1)}, u32[]{:S(2)}, u32[]{:S(2)}) collective-permute-start(bf16[4,192,256]{2,1,0:T(8,128)(2,1)S(1)} %slice.20), channel_id=1, source_target_pairs={{0,1},{1,128},{128,129},{129,0},{2,3},{3,130},{130,131},{131,2},{4... | collective-permute-start | bytes 1179656 | tf_op jit(solution)/shard_map/ppermute | solution.py:21
  73.7 10.3 %collective-permute-start.16 = (bf16[4,192,256]{2,1,0:T(8,128)(2,1)S(1)}, bf16[4,192,256]{2,1,0:T(8,128)(2,1)S(1)}, u32[]{:S(2)}, u32[]{:S(2)}) collective-permute-start(bf16[4,192,256]{2,1,0:T(8,128)(2,1)S(1)} %slice.21), channel_id=1, source_target_pairs={{0,129},{1,0},{128,1},{129,128},{2,131},{3,2},{130,3},{131,130},{4... | collective-permute-start | bytes 1179656 | tf_op jit(solution)/shard_map/ppermute | solution.py:21
  80.8 3.1 %copy-start.11 = (bf16[160,3200]{1,0:T(8,128)(2,1)}, bf16[160,3200]{1,0:T(8,128)(2,1)S(1)}, u32[]{:S(2)}) copy-start(bf16[160,3200]{1,0:T(8,128)(2,1)S(1)} %collective-permute-done.12.refs_2_) | copy-start | bytes 3072004
  84.0 0.8 copy-start.5
  84.8 15.0 %collective-permute-start.19 = (bf16[160,3200]{1,0:T(8,128)(2,1)}, bf16[160,3200]{1,0:T(8,128)(2,1)S(1)}, u32[]{:S(2)}, u32[]{:S(2)}) collective-permute-start(bf16[160,3200]{1,0:T(8,128)(2,1)} %collective-permute-done.10.refs_1_), channel_id=1, source_target_pairs={{0,16},{16,0},{1,17},{17,1},{2,18},{18,2},{3,19},{19,3},{4,20},{20... | collective-permute-start | bytes 3072008 | tf_op jit(solution)/shard_map/ppermute | solution.py:21
  96.6 3.9 %collective-permute-start.20 = (bf16[160,3200]{1,0:T(8,128)(2,1)}, bf16[160,3200]{1,0:T(8,128)(2,1)S(1)}, u32[]{:S(2)}, u32[]{:S(2)}) collective-permute-start(bf16[160,3200]{1,0:T(8,128)(2,1)} %copy-done.11), channel_id=1, source_target_pairs={{0,16},{16,0},{1,17},{17,1},{2,18},{18,2},{3,19},{19,3},{4,20},{20... | collective-permute-start | bytes 3072008 | tf_op jit(solution)/shard_map/ppermute | solution.py:21
  96.6 5.4 %collective-permute-start.21 = (bf16[160,3200]{1,0:T(8,128)(2,1)}, bf16[160,3200]{1,0:T(8,128)(2,1)S(1)}, u32[]{:S(2)}, u32[]{:S(2)}) collective-permute-start(bf16[160,3200]{1,0:T(8,128)(2,1)} %collective-permute-done.11.refs_3_), channel_id=1, source_target_pairs={{0,16},{16,0},{1,17},{17,1},{2,18},{18,2},{3,19},{19,3},{4,20},{20... | collective-permute-start | bytes 3072008 | tf_op jit(solution)/shard_map/ppermute | solution.py:21
  97.1 20.4 %collective-permute-start.17 = (bf16[8,192,256]{2,1,0:T(8,128)(2,1)S(1)}, bf16[8,192,256]{2,1,0:T(8,128)(2,1)S(1)}, u32[]{:S(2)}, u32[]{:S(2)}) collective-permute-start(bf16[8,192,256]{2,1,0:T(8,128)(2,1)S(1)} %all-to-all-done.1.refs_8_), channel_id=1, source_target_pairs={{0,1},{1,128},{128,129},{129,0},{2,3},{3,130},{130,131},{131,2},{4... | collective-permute-start | bytes 2359304 | tf_op jit(solution)/shard_map/ppermute | solution.py:21
  98.3 19.2 %collective-permute-start.18 = (bf16[8,192,256]{2,1,0:T(8,128)(2,1)S(1)}, bf16[8,192,256]{2,1,0:T(8,128)(2,1)S(1)}, u32[]{:S(2)}, u32[]{:S(2)}) collective-permute-start(bf16[8,192,256]{2,1,0:T(8,128)(2,1)S(1)} %all-to-all-done.1.refs_8_), channel_id=1, source_target_pairs={{0,129},{1,0},{128,1},{129,128},{2,131},{3,2},{130,3},{131,130},{4... | collective-permute-start | bytes 2359304 | tf_op jit(solution)/shard_map/ppermute | solution.py:21
  99.8 2.2 %copy-start.12 = (bf16[160,3200]{1,0:T(8,128)(2,1)}, bf16[160,3200]{1,0:T(8,128)(2,1)S(1)}, u32[]{:S(2)}) copy-start(bf16[160,3200]{1,0:T(8,128)(2,1)S(1)} %collective-permute-done.19.refs_5_) | copy-start | bytes 3072004
  100.5 1.5 copy-start.13
  102.0 1.0 copy-start.14
  103.0 1.0 copy-start.6
  117.5 2.7 %copy-start.2 = (bf16[8,192,256]{2,1,0:T(8,128)(2,1)}, bf16[8,192,256]{2,1,0:T(8,128)(2,1)S(1)}, u32[]{:S(2)}) copy-start(bf16[8,192,256]{2,1,0:T(8,128)(2,1)S(1)} %collective-permute-done.18.refs_10_) | copy-start | bytes 2359300
  118.3 1.0 copy-start
  119.3 11.3 %collective-permute-start.22 = (bf16[4,192,256]{2,1,0:T(8,128)(2,1)}, bf16[4,192,256]{2,1,0:T(8,128)(2,1)S(1)}, u32[]{:S(2)}, u32[]{:S(2)}) collective-permute-start(bf16[4,192,256]{2,1,0:T(8,128)(2,1)} %slice.22), channel_id=1, source_target_pairs={{0,1},{1,128},{128,129},{129,0},{2,3},{3,130},{130,131},{131,2},{4... | collective-permute-start | bytes 1179656 | tf_op jit(solution)/shard_map/ppermute | solution.py:21
  120.2 11.6 %copy-start.1 = (bf16[8,192,256]{2,1,0:T(8,128)(2,1)S(1)}, bf16[8,192,256]{2,1,0:T(8,128)(2,1)}, u32[]{:S(2)}) copy-start(bf16[8,192,256]{2,1,0:T(8,128)(2,1)} %copy-done) | copy-start | bytes 2359300
  121.0 10.1 %collective-permute-start.23 = (bf16[4,192,256]{2,1,0:T(8,128)(2,1)}, bf16[4,192,256]{2,1,0:T(8,128)(2,1)S(1)}, u32[]{:S(2)}, u32[]{:S(2)}) collective-permute-start(bf16[4,192,256]{2,1,0:T(8,128)(2,1)} %slice.23), channel_id=1, source_target_pairs={{0,129},{1,0},{128,1},{129,128},{2,131},{3,2},{130,3},{131,130},{4... | collective-permute-start | bytes 1179656 | tf_op jit(solution)/shard_map/ppermute | solution.py:21
  122.8 23.6 %all-to-all-start.2 = ((bf16[16,160,128]{2,1,0:T(8,128)(2,1)}), bf16[16,160,128]{2,1,0:T(8,128)(2,1)S(1)}, u32[]{:S(2)}, u32[]{:S(2)}) async-start(bf16[16,160,128]{2,1,0:T(8,128)(2,1)} %bitcast.11), calls=%async_computation.2 | async-start | bytes 1310720 | tf_op jit(solution)/shard_map/all_to_all | solution.py:216
  131.1 0.8 copy-start.7
  131.8 1.1 copy-start.3
  133.0 1.0 copy-start.8

commit v12 on v11

--- a/solution.py
+++ b/solution.py
@@ -81,26 +81,18 @@
 
 
 def expert_kernel(pos, *refs):
-    xs, ws, (out, xbuf, wbuf, xsem, wsem) = refs[:8], refs[8:13], refs[13:]
+    xs, ws, (out, xbuf, wbuf, xsem) = refs[:8], refs[8:13], refs[13:]
     y, c, xl, dp, z = (pos[i] for i in range(5))
     width = 16 * ws[0].shape[1]
-    copies = []
-    for i, (src, off, low) in enumerate(((ws[0], 0, 0), (ws[1], 3, 0), (ws[2], 1, 0), (ws[3], 2, 0), (ws[4], 2, 4))):
+    rows = [pltpu.make_async_copy(xs[g], xbuf.at[g], xsem.at[g]) for g in range(8)]
+    for cp in rows:
+        cp.start()
+    for src, off, low in ((ws[0], 0, 0), (ws[1], 3, 0), (ws[2], 1, 0), (ws[3], 2, 0), (ws[4], 2, 4)):
         j = lax.rem(dp * 2 + xl + off, 4)
         for k in range(src.shape[0]):
-            place = wbuf.at[lax.div(j, 2), lax.rem(low + k + 8 - z, 8), lax.rem(j, 2)]
-            copies.append(pltpu.make_async_copy(src.at[k], place, wsem.at[i, k]))
-    rows = [pltpu.make_async_copy(xs[g], xbuf.at[g], xsem.at[g]) for g in range(8)]
-    for cp in copies:
-        cp.start()
-    rows[0].start()
-    for cp in copies:
-        cp.wait()
-    rows[1].start()
+            wbuf[lax.div(j, 2), lax.rem(low + k + 8 - z, 8), lax.rem(j, 2)] = src[k]
     for g in range(8):
         d, cc = g % 4, g // 4
-        if g < 6:
-            rows[g + 2].start()
         rows[g].wait()
         rw = jnp.sum(xbuf[g, :, width:].astype(F32), axis=1, keepdims=True)
         gate = jnp.dot(xbuf[g, :, :width], wbuf[0].reshape(width, 256), preferred_element_type=F32)
@@ -197,13 +189,12 @@
         return pl.pallas_call(
             expert_kernel,
             out_shape=pltpu.VMEM((4, 2, 2, 2 * MOST, wide), BF),
-            in_specs=[SM] + [ANY] * 13,
+            in_specs=[SM] + [ANY] * 8 + [VM] * 5,
             out_specs=VM,
             scratch_shapes=[
                 pltpu.VMEM((8, 2 * MOST, 16 * width + 128), BF),
                 pltpu.VMEM((2, 8, 2, rows, 2 * wide), BF),
                 pltpu.SemaphoreType.DMA((8,)),
-                pltpu.SemaphoreType.DMA((5, 8)),
             ],
             compiler_params=pltpu.CompilerParams(vmem_limit_bytes=18 << 20),
             cost_estimate=pl.CostEstimate(

time: 171 us -> 166 us (0.971)
  Pallas kernels: 34.1 us -> 24.4 us
  waiting for transfers between devices: 33.8 us -> 38.3 us
    pallas_call x2, Pallas kernels: 25.6 us -> 15.9 us  [expert(): pl.pallas_call(expert_kernel, out_shape=pltpu.VMEM((4, 2, 2, 2 * MOST, wi...]
    ppermute x24, waiting for transfers between devices: 30.7 us -> 35 us  [ring(): return lax.ppermute(x, axis, [(i, (i + step) % size) for i in range(size)])]
  transfers between devices with their start and end apart: 27 -> 27, of which waited for: 14 -> 14; matrix products, arithmetic and copies ran while one was open for 1% -> 1% of each run, Pallas kernels for 19% -> 14%
where the time goes in v12:
time: 166 us; the launch traced here: 165 us
  starting transfers between devices  68.4 us (41%)
  waiting for transfers between devices  38.3 us (23%)
  Pallas kernels  24.4 us (15%)
  blocking collectives  20.9 us (13%)
  local copies, waits for them, and re-layouts  11.9 us (7%)
    ppermute x24, starting transfers between devices, ring(): return lax.ppermute(x, axis, [(i, (i + step) % size) for i in range(size)])  51.6 us
    ppermute x24, waiting for transfers between devices, ring(): return lax.ppermute(x, axis, [(i, (i + step) % size) for i in range(size)])  35 us
    all_to_all x1, blocking collectives, give_back(): lax.all_to_all(act.reshape(16, 2 * MOST, wide), ('y', 'c', 'xl'), split_a...  20.9 us
    pallas_call x2, Pallas kernels, expert(): pl.pallas_call(expert_kernel, out_shape=pltpu.VMEM((4, 2, 2, 2 * MOST, wi...  15.9 us
    all_to_all x2, starting transfers between devices, exchange(): return lax.all_to_all(x, 'z', split_axis=0, concat_axis=0, tiled=True)  9.61 us
    unnamed x30, local copies, waits for them, and re-layouts  7.62 us
    all_to_all x1, starting transfers between devices, give_back(): lax.all_to_all(act.reshape(16, 2 * MOST, wide), ('y', 'c', 'xl'), split_a...  7.19 us
    pallas_call x1, Pallas kernels, body(): pl.pallas_call(dispatch_kernel, out_shape=[pltpu.VMEM((2 * MOST, 16 * wid...  3.67 us
  transfers between devices with their start and end apart: 27, of which 14 were waited for; matrix products, arithmetic and copies ran while one was open for 1% of the time, Pallas kernels for 14%

profile of v12, /device:TPU:1, one launch (start us, length us, event | category | flops | bytes accessed | tf_op | source)
XLA Modules:
  0.0 165.0 jit_solution(11003104716198867090)
XLA Ops:
  0.0 0.9 dynamic-slice_bitcast_fusion
  0.9 2.0 %collective-permute-start = (bf16[2,192,128]{2,1,0:T(8,128)(2,1)S(1)}, bf16[2,192,128]{2,1,0:T(8,128)(2,1)S(1)}, u32[]{:S(2)}, u32[]{:S(2)}) collective-permute-start(bf16[2,192,128]{2,1,0:T(8,128)(2,1)S(1)} %dynamic-slice_bitcast_fusion), channel_id=1, source_target_pairs={{0,1},{1,0},{2,3},{3,2},{4,5},{5,4},{6,7},{7,6},{8,9},{9,8},{10,11... | collective-permute-start | bytes 294920 | tf_op jit(solution)/shard_map/ppermute | solution.py:21
  2.9 2.0 %collective-permute-done = bf16[2,192,128]{2,1,0:T(8,128)(2,1)S(1)} collective-permute-done((bf16[2,192,128]{2,1,0:T(8,128)(2,1)S(1)}, bf16[2,192,128]{2,1,0:T(8,128)(2,1)S(1)}, u32[]{:S(2)}, u32[]{:S(2)}) %collective-permute-start) | collective-permute-done | bytes 98336 | tf_op jit(solution)/shard_map/ppermute | solution.py:21
  4.9 0.9 bitcast_select_fusion.1
  5.9 2.0 %collective-permute-start.1 = (bf16[2,384,128]{2,1,0:T(8,128)(2,1)S(1)}, bf16[2,384,128]{2,1,0:T(8,128)(2,1)S(1)}, u32[]{:S(2)}, u32[]{:S(2)}) collective-permute-start(bf16[2,384,128]{2,1,0:T(8,128)(2,1)S(1)} %pad_maximum_fusion.refs_0_), channel_id=1, source_target_pairs={{0,2},{2,4},{4,6},{6,8},{8,10},{10,12},{12,14},{14,0},{1,3},{3,5},... | collective-permute-start | bytes 589832 | tf_op jit(solution)/shard_map/ppermute | solution.py:21
  7.9 4.0 %collective-permute-start.3 = (bf16[2,384,128]{2,1,0:T(8,128)(2,1)S(1)}, bf16[2,384,128]{2,1,0:T(8,128)(2,1)S(1)}, u32[]{:S(2)}, u32[]{:S(2)}) collective-permute-start(bf16[2,384,128]{2,1,0:T(8,128)(2,1)S(1)} %pad_maximum_fusion.refs_0_), channel_id=1, source_target_pairs={{0,14},{2,0},{4,2},{6,4},{8,6},{10,8},{12,10},{14,12},{1,15},{3,1}... | collective-permute-start | bytes 589832 | tf_op jit(solution)/shard_map/ppermute | solution.py:21
  11.9 3.3 %collective-permute-done.1.refs_7_ = bf16[2,384,128]{2,1,0:T(8,128)(2,1)S(1)} collective-permute-done((bf16[2,384,128]{2,1,0:T(8,128)(2,1)S(1)}, bf16[2,384,128]{2,1,0:T(8,128)(2,1)S(1)}, u32[]{:S(2)}, u32[]{:S(2)}) %collective-permute-start.1) | collective-permute-done | bytes 196640 | tf_op jit(solution)/shard_map/ppermute | solution.py:21
  15.2 2.7 %collective-permute-start.4 = (bf16[2,384,128]{2,1,0:T(8,128)(2,1)S(1)}, bf16[2,384,128]{2,1,0:T(8,128)(2,1)S(1)}, u32[]{:S(2)}, u32[]{:S(2)}) collective-permute-start(bf16[2,384,128]{2,1,0:T(8,128)(2,1)S(1)} %collective-permute-done.3.refs_1_), channel_id=1, source_target_pairs={{0,14},{2,0},{4,2},{6,4},{8,6},{10,8},{12,10},{14,12},{1,15},{3,1}... | collective-permute-start | bytes 589832 | tf_op jit(solution)/shard_map/ppermute | solution.py:21
  17.9 3.4 %columns.1 = (bf16[8,192,256]{2,1,0:T(8,128)(2,1)}, bf16[8,192,256]{2,1,0:T(8,128)(2,1)}) custom-call(s32[5]{0:T(128)S(1)} %stack.23.pos, bf16[1,192,4096]{2,1,0:T(8,128)(2,1)} %gate.1, bf16[1,192,4096]{2,1,0:T(8,128)(2,1)} %up.1), custom_call_target="tpu_custom_call" | custom-call | tf_op jit(solution)/shard_map/columns/pallas_call | solution.py:137
  21.5 2.7 %collective-permute-start.7 = (bf16[2,384,128]{2,1,0:T(8,128)(2,1)S(1)}, bf16[2,384,128]{2,1,0:T(8,128)(2,1)S(1)}, u32[]{:S(2)}, u32[]{:S(2)}) collective-permute-start(bf16[2,384,128]{2,1,0:T(8,128)(2,1)S(1)} %collective-permute-done.4.refs_2_), channel_id=1, source_target_pairs={{0,14},{2,0},{4,2},{6,4},{8,6},{10,8},{12,10},{14,12},{1,15},{3,1}... | collective-permute-start | bytes 589832 | tf_op jit(solution)/shard_map/ppermute | solution.py:21
  24.1 3.1 %collective-permute-done.5.refs_5_ = bf16[2,384,128]{2,1,0:T(8,128)(2,1)S(1)} collective-permute-done((bf16[2,384,128]{2,1,0:T(8,128)(2,1)S(1)}, bf16[2,384,128]{2,1,0:T(8,128)(2,1)S(1)}, u32[]{:S(2)}, u32[]{:S(2)}) %collective-permute-start.5) | collective-permute-done | bytes 196640 | tf_op jit(solution)/shard_map/ppermute | solution.py:21
  27.3 2.7 %collective-permute-start.8 = (bf16[1,384,128]{2,1,0:T(8,128)(2,1)S(1)}, bf16[1,384,128]{2,1,0:T(8,128)(2,1)S(1)}, u32[]{:S(2)}, u32[]{:S(2)}) collective-permute-start(bf16[1,384,128]{2,1,0:T(8,128)(2,1)S(1)} %slice.25), channel_id=1, source_target_pairs={{0,14},{2,0},{4,2},{6,4},{8,6},{10,8},{12,10},{14,12},{1,15},{3,1}... | collective-permute-start | bytes 294920 | tf_op jit(solution)/shard_map/ppermute | solution.py:21
  30.0 1.9 %collective-permute-done.6 = bf16[1,384,128]{2,1,0:T(8,128)(2,1)S(1)} collective-permute-done((bf16[1,384,128]{2,1,0:T(8,128)(2,1)S(1)}, bf16[1,384,128]{2,1,0:T(8,128)(2,1)S(1)}, u32[]{:S(2)}, u32[]{:S(2)}) %collective-permute-start.6) | collective-permute-done | bytes 98336 | tf_op jit(solution)/shard_map/ppermute | solution.py:21
  32.0 5.9 %all-to-all-start = ((bf16[8,192,256]{2,1,0:T(8,128)(2,1)}), bf16[8,192,256]{2,1,0:T(8,128)(2,1)S(1)}, u32[]{:S(2)}, u32[]{:S(2)}) async-start(bf16[8,192,256]{2,1,0:T(8,128)(2,1)} %get-tuple-element.43), calls=%async_computation | async-start | bytes 1572864 | tf_op jit(solution)/shard_map/all_to_all | solution.py:148
  37.9 3.7 %dispatch.1 = (bf16[160,3200]{1,0:T(8,128)(2,1)}, bf16[160,3200]{1,0:T(8,128)(2,1)}, bf16[160,3200]{1,0:T(8,128)(2,1)S(1)}, bf16[160,3200]{1,0:T(8,128)(2,1)}) custom-call(s32[5]{0:T(128)S(1)} %stack.23.pos, f32[4,4,128]{2,1,0:T(4,128)S(1)} %maximum_bitcast_fusion.meta, bf16[2,384,128]{2,1,0:T(8,128)(2,1)S(1)} %pad_maximum_fusion.refs_0_, ...), custom_call_target="tpu_custom_call" | custom-call | tf_op jit(solution)/shard_map/dispatch/pallas_call | solution.py:165
  41.5 1.0 copy-done.4
  42.5 1.3 collective-permute-start.10
  43.8 1.5 collective-permute-start.11
  45.3 6.8 %collective-permute-start.9 = (bf16[160,3200]{1,0:T(8,128)(2,1)}, bf16[160,3200]{1,0:T(8,128)(2,1)}, u32[]{:S(2)}, u32[]{:S(2)}) collective-permute-start(bf16[160,3200]{1,0:T(8,128)(2,1)} %get-tuple-element.48.refs_0_), channel_id=1, source_target_pairs={{0,16},{16,0},{1,17},{17,1},{2,18},{18,2},{3,19},{19,3},{4,20},{20... | collective-permute-start | bytes 3072008 | tf_op jit(solution)/shard_map/ppermute | solution.py:21
  52.1 3.2 %all-to-all-done.refs_8_ = bf16[8,192,256]{2,1,0:T(8,128)(2,1)S(1)} async-done(((bf16[8,192,256]{2,1,0:T(8,128)(2,1)}), bf16[8,192,256]{2,1,0:T(8,128)(2,1)S(1)}, u32[]{:S(2)}, u32[]{:S(2)}) %all-to-all-start) | async-done | bytes 786464 | tf_op jit(solution)/shard_map/all_to_all | solution.py:148
  55.2 3.8 %all-to-all-start.1 = ((bf16[8,192,256]{2,1,0:T(8,128)(2,1)}), bf16[8,192,256]{2,1,0:T(8,128)(2,1)S(1)}, u32[]{:S(2)}, u32[]{:S(2)}) async-start(bf16[8,192,256]{2,1,0:T(8,128)(2,1)} %get-tuple-element.44), calls=%async_computation.1 | async-start | bytes 1572864 | tf_op jit(solution)/shard_map/all_to_all | solution.py:148
  59.0 1.2 collective-permute-start.13
  60.2 1.5 collective-permute-start.14
  62.0 2.6 %collective-permute-start.12 = (bf16[160,3200]{1,0:T(8,128)(2,1)}, bf16[160,3200]{1,0:T(8,128)(2,1)S(1)}, u32[]{:S(2)}, u32[]{:S(2)}) collective-permute-start(bf16[160,3200]{1,0:T(8,128)(2,1)} %copy-done.4), channel_id=1, source_target_pairs={{0,64},{32,96},{64,0},{96,32},{1,65},{33,97},{65,1},{97,33},{2,66}... | collective-permute-start | bytes 3072008 | tf_op jit(solution)/shard_map/ppermute | solution.py:21
  64.6 8.1 %collective-permute-done.13.refs_9_ = bf16[8,192,256]{2,1,0:T(8,128)(2,1)S(1)} collective-permute-done((bf16[8,192,256]{2,1,0:T(8,128)(2,1)S(1)}, bf16[8,192,256]{2,1,0:T(8,128)(2,1)S(1)}, u32[]{:S(2)}, u32[]{:S(2)}) %collective-permute-start.13) | collective-permute-done | bytes 786464 | tf_op jit(solution)/shard_map/ppermute | solution.py:21
  72.7 1.0 collective-permute-start.15
  73.7 1.9 %collective-permute-start.16 = (bf16[4,192,256]{2,1,0:T(8,128)(2,1)S(1)}, bf16[4,192,256]{2,1,0:T(8,128)(2,1)S(1)}, u32[]{:S(2)}, u32[]{:S(2)}) collective-permute-start(bf16[4,192,256]{2,1,0:T(8,128)(2,1)S(1)} %slice.21), channel_id=1, source_target_pairs={{0,129},{1,0},{128,1},{129,128},{2,131},{3,2},{130,3},{131,130},{4... | collective-permute-start | bytes 1179656 | tf_op jit(solution)/shard_map/ppermute | solution.py:21
  75.6 5.2 %collective-permute-done.12.refs_2_ = bf16[160,3200]{1,0:T(8,128)(2,1)S(1)} collective-permute-done((bf16[160,3200]{1,0:T(8,128)(2,1)}, bf16[160,3200]{1,0:T(8,128)(2,1)S(1)}, u32[]{:S(2)}, u32[]{:S(2)}) %collective-permute-start.12) | collective-permute-done | bytes 1024032 | tf_op jit(solution)/shard_map/ppermute | solution.py:21
  80.8 3.1 %collective-permute-done.15.refs_11_ = bf16[4,192,256]{2,1,0:T(8,128)(2,1)S(1)} collective-permute-done((bf16[4,192,256]{2,1,0:T(8,128)(2,1)S(1)}, bf16[4,192,256]{2,1,0:T(8,128)(2,1)S(1)}, u32[]{:S(2)}, u32[]{:S(2)}) %collective-permute-start.15) | collective-permute-done | bytes 393248 | tf_op jit(solution)/shard_map/ppermute | solution.py:21
  84.8 11.8 %collective-permute-start.19 = (bf16[160,3200]{1,0:T(8,128)(2,1)}, bf16[160,3200]{1,0:T(8,128)(2,1)S(1)}, u32[]{:S(2)}, u32[]{:S(2)}) collective-permute-start(bf16[160,3200]{1,0:T(8,128)(2,1)} %collective-permute-done.10.refs_1_), channel_id=1, source_target_pairs={{0,16},{16,0},{1,17},{17,1},{2,18},{18,2},{3,19},{19,3},{4,20},{20... | collective-permute-start | bytes 3072008 | tf_op jit(solution)/shard_map/ppermute | solution.py:21
  97.1 1.2 collective-permute-start.17
  98.3 1.5 collective-permute-start.18
  100.5 1.5 collective-permute-done.21.refs_7_
  102.0 1.0 copy-done.14
  103.0 1.0 copy-done.6
  103.9 8.4 %expert.2 = bf16[4,2,2,160,128]{4,3,2,1,0:T(8,128)(2,1)} custom-call(s32[5]{0:T(128)S(1)} %stack.23.pos, bf16[160,3200]{1,0:T(8,128)(2,1)} %get-tuple-element.48.refs_0_, bf16[160,3200]{1,0:T(8,128)(2,1)} %collective-permute-done.10.refs_1_, bf16[160,3200]{1,0:T(8,128)(2,1)} %copy-done.11, bf16[160,3200]{1,0:T(8,128)(2,1)} %collective-permute-done.11.refs_3_, ...), custom_call_target="tpu_custom_call" | custom-call | flops 4026531840 | bytes 12582912 | tf_op jit(solution)/shard_map/expert/pallas_call | solution.py:189
  112.3 5.1 %collective-permute-done.17.refs_9_ = bf16[8,192,256]{2,1,0:T(8,128)(2,1)S(1)} collective-permute-done((bf16[8,192,256]{2,1,0:T(8,128)(2,1)S(1)}, bf16[8,192,256]{2,1,0:T(8,128)(2,1)S(1)}, u32[]{:S(2)}, u32[]{:S(2)}) %collective-permute-start.17) | collective-permute-done | bytes 786464 | tf_op jit(solution)/shard_map/ppermute | solution.py:21
  117.5 0.8 slice.22
  118.3 1.0 copy-done
  119.9 0.8 slice.23
  120.7 2.0 %collective-permute-start.23 = (bf16[4,192,256]{2,1,0:T(8,128)(2,1)}, bf16[4,192,256]{2,1,0:T(8,128)(2,1)S(1)}, u32[]{:S(2)}, u32[]{:S(2)}) collective-permute-start(bf16[4,192,256]{2,1,0:T(8,128)(2,1)} %slice.23), channel_id=1, source_target_pairs={{0,129},{1,0},{128,1},{129,128},{2,131},{3,2},{130,3},{131,130},{4... | collective-permute-start | bytes 1179656 | tf_op jit(solution)/shard_map/ppermute | solution.py:21
  122.8 7.2 %all-to-all-start.2 = ((bf16[16,160,128]{2,1,0:T(8,128)(2,1)}), bf16[16,160,128]{2,1,0:T(8,128)(2,1)S(1)}, u32[]{:S(2)}, u32[]{:S(2)}) async-start(bf16[16,160,128]{2,1,0:T(8,128)(2,1)} %bitcast.11), calls=%async_computation.2 | async-start | bytes 1310720 | tf_op jit(solution)/shard_map/all_to_all | solution.py:207
  131.3 1.1 copy-done.3
  132.4 1.0 copy-done.8
  133.4 7.5 %expert.3 = bf16[4,2,2,160,128]{4,3,2,1,0:T(8,128)(2,1)S(1)} custom-call(s32[5]{0:T(128)S(1)} %stack.23.pos, bf16[160,3200]{1,0:T(8,128)(2,1)} %get-tuple-element.48.refs_0_, bf16[160,3200]{1,0:T(8,128)(2,1)} %collective-permute-done.10.refs_1_, bf16[160,3200]{1,0:T(8,128)(2,1)} %copy-done.11, bf16[160,3200]{1,0:T(8,128)(2,1)} %collective-permute-done.11.refs_3_, ...), custom_call_target="tpu_custom_call" | custom-call | flops 4026531840 | bytes 12582912 | tf_op jit(solution)/shard_map/expert/pallas_call | solution.py:189
  141.1 20.9 %all_to_all.20 = bf16[16,160,128]{2,1,0:T(8,128)(2,1)S(1)} all-to-all(bf16[16,160,128]{2,1,0:T(8,128)(2,1)S(1)} %bitcast.21), channel_id=1, replica_groups=mesh['dp'=2,'y'=4,'c'=2,'z'=8,'xl'=2] {'y','c','xl'}, dimensions={0} | all-to-all | bytes 1310720 | tf_op jit(solution)/shard_map/all_to_all | solution.py:207
  162.0 1.4 combine.1
  163.5 1.6 reshape.23
  (56 shorter events, 4.9 us)
Async XLA Ops:
  0.9 4.0 %collective-permute-start = (bf16[2,192,128]{2,1,0:T(8,128)(2,1)S(1)}, bf16[2,192,128]{2,1,0:T(8,128)(2,1)S(1)}, u32[]{:S(2)}, u32[]{:S(2)}) collective-permute-start(bf16[2,192,128]{2,1,0:T(8,128)(2,1)S(1)} %dynamic-slice_bitcast_fusion), channel_id=1, source_target_pairs={{0,1},{1,0},{2,3},{3,2},{4,5},{5,4},{6,7},{7,6},{8,9},{9,8},{10,11... | collective-permute-start | bytes 294920 | tf_op jit(solution)/shard_map/ppermute | solution.py:21
  5.9 9.3 %collective-permute-start.1 = (bf16[2,384,128]{2,1,0:T(8,128)(2,1)S(1)}, bf16[2,384,128]{2,1,0:T(8,128)(2,1)S(1)}, u32[]{:S(2)}, u32[]{:S(2)}) collective-permute-start(bf16[2,384,128]{2,1,0:T(8,128)(2,1)S(1)} %pad_maximum_fusion.refs_0_), channel_id=1, source_target_pairs={{0,2},{2,4},{4,6},{6,8},{8,10},{10,12},{12,14},{14,0},{1,3},{3,5},... | collective-permute-start | bytes 589832 | tf_op jit(solution)/shard_map/ppermute | solution.py:21
  7.9 7.3 %collective-permute-start.3 = (bf16[2,384,128]{2,1,0:T(8,128)(2,1)S(1)}, bf16[2,384,128]{2,1,0:T(8,128)(2,1)S(1)}, u32[]{:S(2)}, u32[]{:S(2)}) collective-permute-start(bf16[2,384,128]{2,1,0:T(8,128)(2,1)S(1)} %pad_maximum_fusion.refs_0_), channel_id=1, source_target_pairs={{0,14},{2,0},{4,2},{6,4},{8,6},{10,8},{12,10},{14,12},{1,15},{3,1}... | collective-permute-start | bytes 589832 | tf_op jit(solution)/shard_map/ppermute | solution.py:21
  15.2 6.2 %collective-permute-start.2 = (bf16[2,384,128]{2,1,0:T(8,128)(2,1)S(1)}, bf16[2,384,128]{2,1,0:T(8,128)(2,1)S(1)}, u32[]{:S(2)}, u32[]{:S(2)}) collective-permute-start(bf16[2,384,128]{2,1,0:T(8,128)(2,1)S(1)} %collective-permute-done.1.refs_7_), channel_id=1, source_target_pairs={{0,2},{2,4},{4,6},{6,8},{8,10},{10,12},{12,14},{14,0},{1,3},{3,5},... | collective-permute-start | bytes 589832 | tf_op jit(solution)/shard_map/ppermute | solution.py:21
  15.2 6.2 %collective-permute-start.4 = (bf16[2,384,128]{2,1,0:T(8,128)(2,1)S(1)}, bf16[2,384,128]{2,1,0:T(8,128)(2,1)S(1)}, u32[]{:S(2)}, u32[]{:S(2)}) collective-permute-start(bf16[2,384,128]{2,1,0:T(8,128)(2,1)S(1)} %collective-permute-done.3.refs_1_), channel_id=1, source_target_pairs={{0,14},{2,0},{4,2},{6,4},{8,6},{10,8},{12,10},{14,12},{1,15},{3,1}... | collective-permute-start | bytes 589832 | tf_op jit(solution)/shard_map/ppermute | solution.py:21
  21.3 16.5 %copy-start.9 = (s32[4,128,2]{1,2,0:T(2,128)S(1)}, s32[4,128,2]{1,2,0:T(2,128)}, u32[]{:S(2)}) copy-start(s32[4,128,2]{1,2,0:T(2,128)} %param.6) | copy-start | bytes 12292
  21.3 16.5 %copy-start.10 = (f32[4,128,2]{1,2,0:T(2,128)S(1)}, f32[4,128,2]{1,2,0:T(2,128)}, u32[]{:S(2)}) copy-start(f32[4,128,2]{1,2,0:T(2,128)} %param.7) | copy-start | bytes 12292
  21.4 5.8 %collective-permute-start.5 = (bf16[2,384,128]{2,1,0:T(8,128)(2,1)S(1)}, bf16[2,384,128]{2,1,0:T(8,128)(2,1)S(1)}, u32[]{:S(2)}, u32[]{:S(2)}) collective-permute-start(bf16[2,384,128]{2,1,0:T(8,128)(2,1)S(1)} %collective-permute-done.2.refs_6_), channel_id=1, source_target_pairs={{0,2},{2,4},{4,6},{6,8},{8,10},{10,12},{12,14},{14,0},{1,3},{3,5},... | collective-permute-start | bytes 589832 | tf_op jit(solution)/shard_map/ppermute | solution.py:21
  21.5 5.8 %collective-permute-start.7 = (bf16[2,384,128]{2,1,0:T(8,128)(2,1)S(1)}, bf16[2,384,128]{2,1,0:T(8,128)(2,1)S(1)}, u32[]{:S(2)}, u32[]{:S(2)}) collective-permute-start(bf16[2,384,128]{2,1,0:T(8,128)(2,1)S(1)} %collective-permute-done.4.refs_2_), channel_id=1, source_target_pairs={{0,14},{2,0},{4,2},{6,4},{8,6},{10,8},{12,10},{14,12},{1,15},{3,1}... | collective-permute-start | bytes 589832 | tf_op jit(solution)/shard_map/ppermute | solution.py:21
  27.2 4.8 %collective-permute-start.6 = (bf16[1,384,128]{2,1,0:T(8,128)(2,1)S(1)}, bf16[1,384,128]{2,1,0:T(8,128)(2,1)S(1)}, u32[]{:S(2)}, u32[]{:S(2)}) collective-permute-start(bf16[1,384,128]{2,1,0:T(8,128)(2,1)S(1)} %slice.24), channel_id=1, source_target_pairs={{0,2},{2,4},{4,6},{6,8},{8,10},{10,12},{12,14},{14,0},{1,3},{3,5},... | collective-permute-start | bytes 294920 | tf_op jit(solution)/shard_map/ppermute | solution.py:21
  27.3 4.6 %collective-permute-start.8 = (bf16[1,384,128]{2,1,0:T(8,128)(2,1)S(1)}, bf16[1,384,128]{2,1,0:T(8,128)(2,1)S(1)}, u32[]{:S(2)}, u32[]{:S(2)}) collective-permute-start(bf16[1,384,128]{2,1,0:T(8,128)(2,1)S(1)} %slice.25), channel_id=1, source_target_pairs={{0,14},{2,0},{4,2},{6,4},{8,6},{10,8},{12,10},{14,12},{1,15},{3,1}... | collective-permute-start | bytes 294920 | tf_op jit(solution)/shard_map/ppermute | solution.py:21
  32.0 23.3 %all-to-all-start = ((bf16[8,192,256]{2,1,0:T(8,128)(2,1)}), bf16[8,192,256]{2,1,0:T(8,128)(2,1)S(1)}, u32[]{:S(2)}, u32[]{:S(2)}) async-start(bf16[8,192,256]{2,1,0:T(8,128)(2,1)} %get-tuple-element.43), calls=%async_computation | async-start | bytes 1572864 | tf_op jit(solution)/shard_map/all_to_all | solution.py:148
  41.5 1.0 copy-start.4
  42.5 19.5 %collective-permute-start.10 = (bf16[160,3200]{1,0:T(8,128)(2,1)}, bf16[160,3200]{1,0:T(8,128)(2,1)}, u32[]{:S(2)}, u32[]{:S(2)}) collective-permute-start(bf16[160,3200]{1,0:T(8,128)(2,1)} %get-tuple-element.49), channel_id=1, source_target_pairs={{0,32},{32,64},{64,96},{96,0},{1,33},{33,65},{65,97},{97,1},{2,34}... | collective-permute-start | bytes 3072008 | tf_op jit(solution)/shard_map/ppermute | solution.py:21
  43.8 18.2 %collective-permute-start.11 = (bf16[160,3200]{1,0:T(8,128)(2,1)}, bf16[160,3200]{1,0:T(8,128)(2,1)}, u32[]{:S(2)}, u32[]{:S(2)}) collective-permute-start(bf16[160,3200]{1,0:T(8,128)(2,1)} %get-tuple-element.50), channel_id=1, source_target_pairs={{0,96},{32,0},{64,32},{96,64},{1,97},{33,1},{65,33},{97,65},{2,98}... | collective-permute-start | bytes 3072008 | tf_op jit(solution)/shard_map/ppermute | solution.py:21
  45.3 16.8 %collective-permute-start.9 = (bf16[160,3200]{1,0:T(8,128)(2,1)}, bf16[160,3200]{1,0:T(8,128)(2,1)}, u32[]{:S(2)}, u32[]{:S(2)}) collective-permute-start(bf16[160,3200]{1,0:T(8,128)(2,1)} %get-tuple-element.48.refs_0_), channel_id=1, source_target_pairs={{0,16},{16,0},{1,17},{17,1},{2,18},{18,2},{3,19},{19,3},{4,20},{20... | collective-permute-start | bytes 3072008 | tf_op jit(solution)/shard_map/ppermute | solution.py:21
  55.2 29.5 %all-to-all-start.1 = ((bf16[8,192,256]{2,1,0:T(8,128)(2,1)}), bf16[8,192,256]{2,1,0:T(8,128)(2,1)S(1)}, u32[]{:S(2)}, u32[]{:S(2)}) async-start(bf16[8,192,256]{2,1,0:T(8,128)(2,1)} %get-tuple-element.44), calls=%async_computation.1 | async-start | bytes 1572864 | tf_op jit(solution)/shard_map/all_to_all | solution.py:148
  59.0 13.7 %collective-permute-start.13 = (bf16[8,192,256]{2,1,0:T(8,128)(2,1)S(1)}, bf16[8,192,256]{2,1,0:T(8,128)(2,1)S(1)}, u32[]{:S(2)}, u32[]{:S(2)}) collective-permute-start(bf16[8,192,256]{2,1,0:T(8,128)(2,1)S(1)} %all-to-all-done.refs_8_), channel_id=1, source_target_pairs={{0,1},{1,128},{128,129},{129,0},{2,3},{3,130},{130,131},{131,2},{4... | collective-permute-start | bytes 2359304 | tf_op jit(solution)/shard_map/ppermute | solution.py:21
  60.2 12.5 %collective-permute-start.14 = (bf16[8,192,256]{2,1,0:T(8,128)(2,1)S(1)}, bf16[8,192,256]{2,1,0:T(8,128)(2,1)S(1)}, u32[]{:S(2)}, u32[]{:S(2)}) collective-permute-start(bf16[8,192,256]{2,1,0:T(8,128)(2,1)S(1)} %all-to-all-done.refs_8_), channel_id=1, source_target_pairs={{0,129},{1,0},{128,1},{129,128},{2,131},{3,2},{130,3},{131,130},{4... | collective-permute-start | bytes 2359304 | tf_op jit(solution)/shard_map/ppermute | solution.py:21
  62.0 18.8 %collective-permute-start.12 = (bf16[160,3200]{1,0:T(8,128)(2,1)}, bf16[160,3200]{1,0:T(8,128)(2,1)S(1)}, u32[]{:S(2)}, u32[]{:S(2)}) collective-permute-start(bf16[160,3200]{1,0:T(8,128)(2,1)} %copy-done.4), channel_id=1, source_target_pairs={{0,64},{32,96},{64,0},{96,32},{1,65},{33,97},{65,1},{97,33},{2,66}... | collective-permute-start | bytes 3072008 | tf_op jit(solution)/shard_map/ppermute | solution.py:21
  72.7 11.3 %collective-permute-start.15 = (bf16[4,192,256]{2,1,0:T(8,128)(2,1)S(1)}, bf16[4,192,256]{2,1,0:T(8,128)(2,1)S(1)}, u32[]{:S(2)}, u32[]{:S(2)}) collective-permute-start(bf16[4,192,256]{2,1,0:T(8,128)(2,1)S(1)} %slice.20), channel_id=1, source_target_pairs={{0,1},{1,128},{128,129},{129,0},{2,3},{3,130},{130,131},{131,2},{4... | collective-permute-start | bytes 1179656 | tf_op jit(solution)/shard_map/ppermute | solution.py:21
  73.7 10.3 %collective-permute-start.16 = (bf16[4,192,256]{2,1,0:T(8,128)(2,1)S(1)}, bf16[4,192,256]{2,1,0:T(8,128)(2,1)S(1)}, u32[]{:S(2)}, u32[]{:S(2)}) collective-permute-start(bf16[4,192,256]{2,1,0:T(8,128)(2,1)S(1)} %slice.21), channel_id=1, source_target_pairs={{0,129},{1,0},{128,1},{129,128},{2,131},{3,2},{130,3},{131,130},{4... | collective-permute-start | bytes 1179656 | tf_op jit(solution)/shard_map/ppermute | solution.py:21
  80.8 3.1 %copy-start.11 = (bf16[160,3200]{1,0:T(8,128)(2,1)}, bf16[160,3200]{1,0:T(8,128)(2,1)S(1)}, u32[]{:S(2)}) copy-start(bf16[160,3200]{1,0:T(8,128)(2,1)S(1)} %collective-permute-done.12.refs_2_) | copy-start | bytes 3072004
  84.0 0.8 copy-start.5
  84.8 15.0 %collective-permute-start.19 = (bf16[160,3200]{1,0:T(8,128)(2,1)}, bf16[160,3200]{1,0:T(8,128)(2,1)S(1)}, u32[]{:S(2)}, u32[]{:S(2)}) collective-permute-start(bf16[160,3200]{1,0:T(8,128)(2,1)} %collective-permute-done.10.refs_1_), channel_id=1, source_target_pairs={{0,16},{16,0},{1,17},{17,1},{2,18},{18,2},{3,19},{19,3},{4,20},{20... | collective-permute-start | bytes 3072008 | tf_op jit(solution)/shard_map/ppermute | solution.py:21
  96.6 3.9 %collective-permute-start.20 = (bf16[160,3200]{1,0:T(8,128)(2,1)}, bf16[160,3200]{1,0:T(8,128)(2,1)S(1)}, u32[]{:S(2)}, u32[]{:S(2)}) collective-permute-start(bf16[160,3200]{1,0:T(8,128)(2,1)} %copy-done.11), channel_id=1, source_target_pairs={{0,16},{16,0},{1,17},{17,1},{2,18},{18,2},{3,19},{19,3},{4,20},{20... | collective-permute-start | bytes 3072008 | tf_op jit(solution)/shard_map/ppermute | solution.py:21
  96.6 5.4 %collective-permute-start.21 = (bf16[160,3200]{1,0:T(8,128)(2,1)}, bf16[160,3200]{1,0:T(8,128)(2,1)S(1)}, u32[]{:S(2)}, u32[]{:S(2)}) collective-permute-start(bf16[160,3200]{1,0:T(8,128)(2,1)} %collective-permute-done.11.refs_3_), channel_id=1, source_target_pairs={{0,16},{16,0},{1,17},{17,1},{2,18},{18,2},{3,19},{19,3},{4,20},{20... | collective-permute-start | bytes 3072008 | tf_op jit(solution)/shard_map/ppermute | solution.py:21
  97.1 20.4 %collective-permute-start.17 = (bf16[8,192,256]{2,1,0:T(8,128)(2,1)S(1)}, bf16[8,192,256]{2,1,0:T(8,128)(2,1)S(1)}, u32[]{:S(2)}, u32[]{:S(2)}) collective-permute-start(bf16[8,192,256]{2,1,0:T(8,128)(2,1)S(1)} %all-to-all-done.1.refs_8_), channel_id=1, source_target_pairs={{0,1},{1,128},{128,129},{129,0},{2,3},{3,130},{130,131},{131,2},{4... | collective-permute-start | bytes 2359304 | tf_op jit(solution)/shard_map/ppermute | solution.py:21
  98.3 19.2 %collective-permute-start.18 = (bf16[8,192,256]{2,1,0:T(8,128)(2,1)S(1)}, bf16[8,192,256]{2,1,0:T(8,128)(2,1)S(1)}, u32[]{:S(2)}, u32[]{:S(2)}) collective-permute-start(bf16[8,192,256]{2,1,0:T(8,128)(2,1)S(1)} %all-to-all-done.1.refs_8_), channel_id=1, source_target_pairs={{0,129},{1,0},{128,1},{129,128},{2,131},{3,2},{130,3},{131,130},{4... | collective-permute-start | bytes 2359304 | tf_op jit(solution)/shard_map/ppermute | solution.py:21
  99.8 2.2 %copy-start.12 = (bf16[160,3200]{1,0:T(8,128)(2,1)}, bf16[160,3200]{1,0:T(8,128)(2,1)S(1)}, u32[]{:S(2)}) copy-start(bf16[160,3200]{1,0:T(8,128)(2,1)S(1)} %collective-permute-done.19.refs_5_) | copy-start | bytes 3072004
  100.5 1.5 copy-start.13
  102.0 1.0 copy-start.14
  103.0 1.0 copy-start.6
  117.5 2.4 %copy-start.2 = (bf16[8,192,256]{2,1,0:T(8,128)(2,1)}, bf16[8,192,256]{2,1,0:T(8,128)(2,1)S(1)}, u32[]{:S(2)}) copy-start(bf16[8,192,256]{2,1,0:T(8,128)(2,1)S(1)} %collective-permute-done.18.refs_10_) | copy-start | bytes 2359300
  118.3 1.0 copy-start
  119.3 11.3 %collective-permute-start.22 = (bf16[4,192,256]{2,1,0:T(8,128)(2,1)}, bf16[4,192,256]{2,1,0:T(8,128)(2,1)S(1)}, u32[]{:S(2)}, u32[]{:S(2)}) collective-permute-start(bf16[4,192,256]{2,1,0:T(8,128)(2,1)} %slice.22), channel_id=1, source_target_pairs={{0,1},{1,128},{128,129},{129,0},{2,3},{3,130},{130,131},{131,2},{4... | collective-permute-start | bytes 1179656 | tf_op jit(solution)/shard_map/ppermute | solution.py:21
  119.9 11.4 %copy-start.1 = (bf16[8,192,256]{2,1,0:T(8,128)(2,1)S(1)}, bf16[8,192,256]{2,1,0:T(8,128)(2,1)}, u32[]{:S(2)}) copy-start(bf16[8,192,256]{2,1,0:T(8,128)(2,1)} %copy-done) | copy-start | bytes 2359300
  120.7 9.8 %collective-permute-start.23 = (bf16[4,192,256]{2,1,0:T(8,128)(2,1)}, bf16[4,192,256]{2,1,0:T(8,128)(2,1)S(1)}, u32[]{:S(2)}, u32[]{:S(2)}) collective-permute-start(bf16[4,192,256]{2,1,0:T(8,128)(2,1)} %slice.23), channel_id=1, source_target_pairs={{0,129},{1,0},{128,1},{129,128},{2,131},{3,2},{130,3},{131,130},{4... | collective-permute-start | bytes 1179656 | tf_op jit(solution)/shard_map/ppermute | solution.py:21
  122.8 18.3 %all-to-all-start.2 = ((bf16[16,160,128]{2,1,0:T(8,128)(2,1)}), bf16[16,160,128]{2,1,0:T(8,128)(2,1)S(1)}, u32[]{:S(2)}, u32[]{:S(2)}) async-start(bf16[16,160,128]{2,1,0:T(8,128)(2,1)} %bitcast.11), calls=%async_computation.2 | async-start | bytes 1310720 | tf_op jit(solution)/shard_map/all_to_all | solution.py:207
  130.6 0.8 copy-start.7
  131.3 1.1 copy-start.3
  132.4 1.0 copy-start.8

commit v13 on v10

--- a/solution.py
+++ b/solution.py
@@ -77,29 +77,36 @@
 
 
 def expert_kernel(pos, *refs):
-    xs, ws, (out, xbuf, wbuf, xsem, wsem) = refs[:8], refs[8:13], refs[13:]
+    xs, ws, (out, xbuf, wbuf, gates, xsem, wsem) = refs[:8], refs[8:13], refs[13:]
     y, c, xl, dp, z = (pos[i] for i in range(5))
     width = 16 * ws[0].shape[1]
-    copies = []
-    for i, (src, off, low) in enumerate(((ws[0], 0, 0), (ws[1], 3, 0), (ws[2], 1, 0), (ws[3], 2, 0), (ws[4], 2, 4))):
-        j = lax.rem(dp * 2 + xl + off, 4)
-        for k in range(src.shape[0]):
-            place = wbuf.at[lax.div(j, 2), lax.rem(low + k + 8 - z, 8), lax.rem(j, 2)]
-            copies.append(pltpu.make_async_copy(src.at[k], place, wsem.at[i, k]))
+    for here in range(4):
+
+        @pl.when(dp * 2 + xl == here)
+        def _(here=here):
+            for slot in range(4):
+                for src, low in {0: [(ws[0], 0)], 3: [(ws[1], 0)], 1: [(ws[2], 0)], 2: [(ws[3], 0), (ws[4], 4)]}[(slot - here) % 4]:
+                    for k in range(src.shape[0]):
+                        place = wbuf.at[slot // 2, lax.rem(low + k + 8 - z, 8), slot % 2]
+                        pltpu.make_async_copy(src.at[k], place, wsem.at[slot, low + k]).start()
+
+    def wait(half):
+        for slot in (2 * half, 2 * half + 1):
+            for k in range(8):
+                pltpu.make_async_copy(ws[0].at[k], wbuf.at[half, k, slot % 2], wsem.at[slot, k]).wait()
+
     rows = [pltpu.make_async_copy(xs[g], xbuf.at[g], xsem.at[g]) for g in range(8)]
-    for cp in copies:
+    for cp in rows:
         cp.start()
-    rows[0].start()
-    for cp in copies:
-        cp.wait()
-    rows[1].start()
+    wait(0)
+    for g in range(8):
+        rows[g].wait()
+        gates[g] = jnp.dot(xbuf[g, :, :width], wbuf[0].reshape(width, 256), preferred_element_type=F32)
+    wait(1)
     for g in range(8):
         d, cc = g % 4, g // 4
-        if g < 6:
-            rows[g + 2].start()
-        rows[g].wait()
         rw = jnp.sum(xbuf[g, :, width:].astype(F32), axis=1, keepdims=True)
-        gate = jnp.dot(xbuf[g, :, :width], wbuf[0].reshape(width, 256), preferred_element_type=F32)
+        gate = gates[g]
         up = jnp.dot(xbuf[g, :, :width], wbuf[1].reshape(width, 256), preferred_element_type=F32)
         act = (rw * (gate / (1.0 + jnp.exp(-gate)) * up)).astype(BF)
         for t in range(2):
@@ -179,16 +186,15 @@
     part_b, own_a = barrier((blocks[1], own_a))
     own_b = exchange(part_b)
     left_a, right_a = sides(own_a)
-    far_rows, other[0], *near = barrier((sent[2], other[0], *near))
+    left_a, right_a, far_rows, other[0], *near = barrier((left_a, right_a, sent[2], other[0], *near))
+    far_a = far(left_a, right_a)
     opposite = ring(far_rows, "y", 4, 2)
-    left_a, right_a, *near = barrier((left_a, right_a, *near))
-    far_a = far(left_a, right_a)
-    other += [ring(h, "c", 2, 1) for h in near]
-    own_b, opposite, *rest = barrier((own_b, opposite, *far_a, *other))
-    far_a, other = rest[:2], rest[2:]
+    own_b, opposite, *rest = barrier((own_b, opposite, *far_a, *near))
+    far_a, near = rest[:2], rest[2:]
     left_b, right_b = sides(own_b)
     held = [sent[0], near[0], opposite, near[1]]
-    other = [other[0], other[1], ring(opposite, "c", 2, 1), other[2]]
+    left_b, right_b, *rest = barrier((left_b, right_b, *held[1:]))
+    other += [ring(h, "c", 2, 1) for h in rest]
 
     def expert(*ws):
         return pl.pallas_call(
@@ -199,8 +205,9 @@
             scratch_shapes=[
                 pltpu.VMEM((8, 2 * MOST, 16 * width + 128), BF),
                 pltpu.VMEM((2, 8, 2, rows, 2 * wide), BF),
+                pltpu.VMEM((8, 2 * MOST, 256), F32),
                 pltpu.SemaphoreType.DMA((8,)),
-                pltpu.SemaphoreType.DMA((5, 8)),
+                pltpu.SemaphoreType.DMA((4, 8)),
             ],
             compiler_params=pltpu.CompilerParams(vmem_limit_bytes=58 << 20),
             cost_estimate=pl.CostEstimate(
@@ -214,7 +221,6 @@
         return back.reshape(4, 2, 2, 2 * MOST, wide)
 
     act_a = expert(own_a, left_a, right_a, *far_a)
-    left_b, right_b, act_a = barrier((left_b, right_b, act_a))
     back_a = give_back(act_a)
     back_b = give_back(expert(own_b, left_b, right_b, *far(left_b, right_b)))
     out = pl.pallas_call(

time: 162 us -> 177 us (1.093)
  waiting for transfers between devices: 34.9 us -> 59.2 us
  starting transfers between devices: 69.8 us -> 58.2 us
  Pallas kernels: 29.1 us -> 31.7 us
    ppermute x24, waiting for transfers between devices: 31.3 us -> 55.1 us  [ring(): return lax.ppermute(x, axis, [(i, (i + step) % size) for i in range(size)])]
    ppermute x24, starting transfers between devices: 54.4 us -> 43.1 us  [ring(): return lax.ppermute(x, axis, [(i, (i + step) % size) for i in range(size)])]
    pallas_call x2, Pallas kernels: 20.7 us -> 23.4 us  [expert(): pl.pallas_call(expert_kernel, out_shape=jax.ShapeDtypeStruct((4, 2, 2, 2...]
  transfers between devices with their start and end apart: 27 -> 27, of which waited for: 10 -> 12; matrix products, arithmetic and copies ran while one was open for 2% -> 2% of each run, Pallas kernels for 17% -> 17%
where the time goes in v13:
time: 177 us; the launch traced here: 176 us
  waiting for transfers between devices  59.2 us (33%)
  starting transfers between devices  58.2 us (33%)
  Pallas kernels  31.7 us (18%)
  blocking collectives  17.6 us (10%)
  local copies, waits for them, and re-layouts  7.88 us (4%)
    ppermute x24, waiting for transfers between devices, ring(): return lax.ppermute(x, axis, [(i, (i + step) % size) for i in range(size)])  55.1 us
    ppermute x24, starting transfers between devices, ring(): return lax.ppermute(x, axis, [(i, (i + step) % size) for i in range(size)])  43.1 us
    pallas_call x2, Pallas kernels, expert(): pl.pallas_call(expert_kernel, out_shape=jax.ShapeDtypeStruct((4, 2, 2, 2...  23.4 us
    all_to_all x1, blocking collectives, give_back(): lax.all_to_all(act.reshape(16, 2 * MOST, wide), ('y', 'c', 'xl'), split_a...  17.6 us
    all_to_all x2, starting transfers between devices, exchange(): return lax.all_to_all(x, 'z', split_axis=0, concat_axis=0, tiled=True)  10 us
    all_to_all x1, starting transfers between devices, give_back(): lax.all_to_all(act.reshape(16, 2 * MOST, wide), ('y', 'c', 'xl'), split_a...  5.03 us
    all_to_all x2, waiting for transfers between devices, exchange(): return lax.all_to_all(x, 'z', split_axis=0, concat_axis=0, tiled=True)  4.1 us
  transfers between devices with their start and end apart: 27, of which 12 were waited for; matrix products, arithmetic and copies ran while one was open for 2% of the time, Pallas kernels for 17%

profile of v13, /device:TPU:1, one launch (start us, length us, event | category | flops | bytes accessed | tf_op | source)
XLA Modules:
  0.0 175.7 jit_solution(8456230461531964682)
XLA Ops:
  0.0 0.9 dynamic-slice_bitcast_fusion
  0.9 2.0 %collective-permute-start = (bf16[2,192,128]{2,1,0:T(8,128)(2,1)S(1)}, bf16[2,192,128]{2,1,0:T(8,128)(2,1)S(1)}, u32[]{:S(2)}, u32[]{:S(2)}) collective-permute-start(bf16[2,192,128]{2,1,0:T(8,128)(2,1)S(1)} %dynamic-slice_bitcast_fusion), channel_id=1, source_target_pairs={{0,1},{1,0},{2,3},{3,2},{4,5},{5,4},{6,7},{7,6},{8,9},{9,8},{10,11... | collective-permute-start | bytes 294920 | tf_op jit(solution)/shard_map/ppermute | solution.py:17
  2.9 2.0 %collective-permute-done = bf16[2,192,128]{2,1,0:T(8,128)(2,1)S(1)} collective-permute-done((bf16[2,192,128]{2,1,0:T(8,128)(2,1)S(1)}, bf16[2,192,128]{2,1,0:T(8,128)(2,1)S(1)}, u32[]{:S(2)}, u32[]{:S(2)}) %collective-permute-start) | collective-permute-done | bytes 98336 | tf_op jit(solution)/shard_map/ppermute | solution.py:17
  4.9 0.9 bitcast_select_fusion.1
  5.9 2.0 %collective-permute-start.2 = (bf16[2,384,128]{2,1,0:T(8,128)(2,1)S(1)}, bf16[2,384,128]{2,1,0:T(8,128)(2,1)S(1)}, u32[]{:S(2)}, u32[]{:S(2)}) collective-permute-start(bf16[2,384,128]{2,1,0:T(8,128)(2,1)S(1)} %pad_maximum_fusion.refs_0_), channel_id=1, source_target_pairs={{0,2},{2,4},{4,6},{6,8},{8,10},{10,12},{12,14},{14,0},{1,3},{3,5},... | collective-permute-start | bytes 589832 | tf_op jit(solution)/shard_map/ppermute | solution.py:17
  7.8 4.0 %collective-permute-start.1 = (bf16[2,384,128]{2,1,0:T(8,128)(2,1)S(1)}, bf16[2,384,128]{2,1,0:T(8,128)(2,1)S(1)}, u32[]{:S(2)}, u32[]{:S(2)}) collective-permute-start(bf16[2,384,128]{2,1,0:T(8,128)(2,1)S(1)} %pad_maximum_fusion.refs_0_), channel_id=1, source_target_pairs={{0,14},{2,0},{4,2},{6,4},{8,6},{10,8},{12,10},{14,12},{1,15},{3,1}... | collective-permute-start | bytes 589832 | tf_op jit(solution)/shard_map/ppermute | solution.py:17
  11.9 3.3 %collective-permute-done.2.refs_7_ = bf16[2,384,128]{2,1,0:T(8,128)(2,1)S(1)} collective-permute-done((bf16[2,384,128]{2,1,0:T(8,128)(2,1)S(1)}, bf16[2,384,128]{2,1,0:T(8,128)(2,1)S(1)}, u32[]{:S(2)}, u32[]{:S(2)}) %collective-permute-start.2) | collective-permute-done | bytes 196640 | tf_op jit(solution)/shard_map/ppermute | solution.py:17
  15.2 2.7 %collective-permute-start.4 = (bf16[2,384,128]{2,1,0:T(8,128)(2,1)S(1)}, bf16[2,384,128]{2,1,0:T(8,128)(2,1)S(1)}, u32[]{:S(2)}, u32[]{:S(2)}) collective-permute-start(bf16[2,384,128]{2,1,0:T(8,128)(2,1)S(1)} %collective-permute-done.1.refs_1_), channel_id=1, source_target_pairs={{0,14},{2,0},{4,2},{6,4},{8,6},{10,8},{12,10},{14,12},{1,15},{3,1}... | collective-permute-start | bytes 589832 | tf_op jit(solution)/shard_map/ppermute | solution.py:17
  17.9 0.7 stack.23.pos
  18.5 3.5 %columns.1 = (bf16[8,192,256]{2,1,0:T(8,128)(2,1)}, bf16[8,192,256]{2,1,0:T(8,128)(2,1)}) custom-call(s32[5]{0:T(128)} %stack.23.pos, bf16[1,192,4096]{2,1,0:T(8,128)(2,1)} %gate.1, bf16[1,192,4096]{2,1,0:T(8,128)(2,1)} %up.1), custom_call_target="tpu_custom_call" | custom-call | tf_op jit(solution)/shard_map/columns/pallas_call | solution.py:148
  22.2 2.7 %collective-permute-start.5 = (bf16[2,384,128]{2,1,0:T(8,128)(2,1)S(1)}, bf16[2,384,128]{2,1,0:T(8,128)(2,1)S(1)}, u32[]{:S(2)}, u32[]{:S(2)}) collective-permute-start(bf16[2,384,128]{2,1,0:T(8,128)(2,1)S(1)} %collective-permute-done.4.refs_2_), channel_id=1, source_target_pairs={{0,14},{2,0},{4,2},{6,4},{8,6},{10,8},{12,10},{14,12},{1,15},{3,1}... | collective-permute-start | bytes 589832 | tf_op jit(solution)/shard_map/ppermute | solution.py:17
  24.8 3.1 %collective-permute-done.6.refs_5_ = bf16[2,384,128]{2,1,0:T(8,128)(2,1)S(1)} collective-permute-done((bf16[2,384,128]{2,1,0:T(8,128)(2,1)S(1)}, bf16[2,384,128]{2,1,0:T(8,128)(2,1)S(1)}, u32[]{:S(2)}, u32[]{:S(2)}) %collective-permute-start.6) | collective-permute-done | bytes 196640 | tf_op jit(solution)/shard_map/ppermute | solution.py:17
  28.0 2.7 %collective-permute-start.8 = (bf16[1,384,128]{2,1,0:T(8,128)(2,1)S(1)}, bf16[1,384,128]{2,1,0:T(8,128)(2,1)S(1)}, u32[]{:S(2)}, u32[]{:S(2)}) collective-permute-start(bf16[1,384,128]{2,1,0:T(8,128)(2,1)S(1)} %slice.25), channel_id=1, source_target_pairs={{0,14},{2,0},{4,2},{6,4},{8,6},{10,8},{12,10},{14,12},{1,15},{3,1}... | collective-permute-start | bytes 294920 | tf_op jit(solution)/shard_map/ppermute | solution.py:17
  30.7 1.9 %collective-permute-done.7 = bf16[1,384,128]{2,1,0:T(8,128)(2,1)S(1)} collective-permute-done((bf16[1,384,128]{2,1,0:T(8,128)(2,1)S(1)}, bf16[1,384,128]{2,1,0:T(8,128)(2,1)S(1)}, u32[]{:S(2)}, u32[]{:S(2)}) %collective-permute-start.7) | collective-permute-done | bytes 98336 | tf_op jit(solution)/shard_map/ppermute | solution.py:17
  32.6 5.8 %all-to-all-start = ((bf16[8,192,256]{2,1,0:T(8,128)(2,1)}), bf16[8,192,256]{2,1,0:T(8,128)(2,1)S(1)}, u32[]{:S(2)}, u32[]{:S(2)}) async-start(bf16[8,192,256]{2,1,0:T(8,128)(2,1)} %get-tuple-element.46), calls=%async_computation | async-start | bytes 1572864 | tf_op jit(solution)/shard_map/all_to_all | solution.py:159
  38.5 3.4 %dispatch.1 = (bf16[160,3200]{1,0:T(8,128)(2,1)S(1)}, bf16[160,3200]{1,0:T(8,128)(2,1)}, bf16[160,3200]{1,0:T(8,128)(2,1)S(1)}, bf16[160,3200]{1,0:T(8,128)(2,1)}) custom-call(s32[5]{0:T(128)S(1)} %copy-done, f32[4,4,128]{2,1,0:T(4,128)S(1)} %maximum_bitcast_fusion.meta, bf16[2,384,128]{2,1,0:T(8,128)(2,1)S(1)} %pad_maximum_fusion.refs_0_, ...), custom_call_target="tpu_custom_call" | custom-call | tf_op jit(solution)/shard_map/dispatch/pallas_call | solution.py:176
  41.9 1.0 copy-done.2
  42.9 6.2 %collective-permute-start.11 = (bf16[160,3200]{1,0:T(8,128)(2,1)S(1)}, bf16[160,3200]{1,0:T(8,128)(2,1)}, u32[]{:S(2)}, u32[]{:S(2)}) collective-permute-start(bf16[160,3200]{1,0:T(8,128)(2,1)S(1)} %get-tuple-element.44.refs_0_), channel_id=1, source_target_pairs={{0,16},{16,0},{1,17},{17,1},{2,18},{18,2},{3,19},{19,3},{4,20},{20... | collective-permute-start | bytes 3072008 | tf_op jit(solution)/shard_map/ppermute | solution.py:17
  49.1 1.3 collective-permute-start.12
  50.4 1.4 collective-permute-start.13
  51.8 4.1 %all-to-all-done.refs_8_ = bf16[8,192,256]{2,1,0:T(8,128)(2,1)S(1)} async-done(((bf16[8,192,256]{2,1,0:T(8,128)(2,1)}), bf16[8,192,256]{2,1,0:T(8,128)(2,1)S(1)}, u32[]{:S(2)}, u32[]{:S(2)}) %all-to-all-start) | async-done | bytes 786464 | tf_op jit(solution)/shard_map/all_to_all | solution.py:159
  55.9 1.2 collective-permute-start.9
  57.1 1.5 collective-permute-start.10
  58.6 4.2 %all-to-all-start.1 = ((bf16[8,192,256]{2,1,0:T(8,128)(2,1)}), bf16[8,192,256]{2,1,0:T(8,128)(2,1)}, u32[]{:S(2)}, u32[]{:S(2)}) async-start(bf16[8,192,256]{2,1,0:T(8,128)(2,1)} %get-tuple-element.47), calls=%async_computation.1 | async-start | bytes 1572864 | tf_op jit(solution)/shard_map/all_to_all | solution.py:159
  62.8 12.2 %collective-permute-done.12.refs_1_ = bf16[160,3200]{1,0:T(8,128)(2,1)} collective-permute-done((bf16[160,3200]{1,0:T(8,128)(2,1)}, bf16[160,3200]{1,0:T(8,128)(2,1)}, u32[]{:S(2)}, u32[]{:S(2)}) %collective-permute-start.12) | collective-permute-done | bytes 1024032 | tf_op jit(solution)/shard_map/ppermute | solution.py:17
  75.0 2.3 %collective-permute-start.14 = (bf16[160,3200]{1,0:T(8,128)(2,1)S(1)}, bf16[160,3200]{1,0:T(8,128)(2,1)}, u32[]{:S(2)}, u32[]{:S(2)}) collective-permute-start(bf16[160,3200]{1,0:T(8,128)(2,1)S(1)} %copy-done.3), channel_id=1, source_target_pairs={{0,64},{32,96},{64,0},{96,32},{1,65},{33,97},{65,1},{97,33},{2,66}... | collective-permute-start | bytes 3072008 | tf_op jit(solution)/shard_map/ppermute | solution.py:17
  77.4 1.0 slice.20
  78.4 1.3 collective-permute-start.15
  79.7 1.0 slice.21
  80.7 1.5 collective-permute-start.16
  82.3 5.1 %collective-permute-done.15.refs_11_ = bf16[4,192,256]{2,1,0:T(8,128)(2,1)S(1)} collective-permute-done((bf16[4,192,256]{2,1,0:T(8,128)(2,1)S(1)}, bf16[4,192,256]{2,1,0:T(8,128)(2,1)S(1)}, u32[]{:S(2)}, u32[]{:S(2)}) %collective-permute-start.15) | collective-permute-done | bytes 393248 | tf_op jit(solution)/shard_map/ppermute | solution.py:17
  87.4 0.7 copy-done.11
  88.2 10.6 %collective-permute-done.14.refs_2_ = bf16[160,3200]{1,0:T(8,128)(2,1)} collective-permute-done((bf16[160,3200]{1,0:T(8,128)(2,1)S(1)}, bf16[160,3200]{1,0:T(8,128)(2,1)}, u32[]{:S(2)}, u32[]{:S(2)}) %collective-permute-start.14) | collective-permute-done | bytes 1024032 | tf_op jit(solution)/shard_map/ppermute | solution.py:17
  98.8 1.2 collective-permute-start.17
  100.0 1.5 collective-permute-start.18
  101.5 14.8 %collective-permute-done.17.refs_9_ = bf16[8,192,256]{2,1,0:T(8,128)(2,1)S(1)} collective-permute-done((bf16[8,192,256]{2,1,0:T(8,128)(2,1)}, bf16[8,192,256]{2,1,0:T(8,128)(2,1)S(1)}, u32[]{:S(2)}, u32[]{:S(2)}) %collective-permute-start.17) | collective-permute-done | bytes 786464 | tf_op jit(solution)/shard_map/ppermute | solution.py:17
  116.2 4.0 %collective-permute-start.19 = (bf16[160,3200]{1,0:T(8,128)(2,1)}, bf16[160,3200]{1,0:T(8,128)(2,1)S(1)}, u32[]{:S(2)}, u32[]{:S(2)}) collective-permute-start(bf16[160,3200]{1,0:T(8,128)(2,1)} %collective-permute-done.12.refs_1_), channel_id=1, source_target_pairs={{0,16},{16,0},{1,17},{17,1},{2,18},{18,2},{3,19},{19,3},{4,20},{20... | collective-permute-start | bytes 3072008 | tf_op jit(solution)/shard_map/ppermute | solution.py:17
  120.3 0.4 collective-permute-start.21
  120.8 1.5 collective-permute-start.22
  122.3 1.4 collective-permute-start.23
  123.7 2.0 %collective-permute-done.20.refs_6_ = bf16[160,3200]{1,0:T(8,128)(2,1)S(1)} collective-permute-done((bf16[160,3200]{1,0:T(8,128)(2,1)}, bf16[160,3200]{1,0:T(8,128)(2,1)S(1)}, u32[]{:S(2)}, u32[]{:S(2)}) %collective-permute-start.20) | collective-permute-done | bytes 1024032 | tf_op jit(solution)/shard_map/ppermute | solution.py:17
  125.8 0.9 copy-done.10
  126.6 11.7 %expert.2 = bf16[4,2,2,160,128]{4,3,2,1,0:T(8,128)(2,1)} custom-call(s32[5]{0:T(128)} %stack.23.pos, bf16[160,3200]{1,0:T(8,128)(2,1)} %copy-done.1, bf16[160,3200]{1,0:T(8,128)(2,1)} %collective-permute-done.12.refs_1_, bf16[160,3200]{1,0:T(8,128)(2,1)} %collective-permute-done.14.refs_2_, bf16[160,3200]{1,0:T(8,128)(2,1)} %collective-permute-done.13.refs_3_, ...), custom_call_target="tpu_custom_call" | custom-call | flops 4026531840 | bytes 12582912 | tf_op jit(solution)/shard_map/expert/pallas_call | solution.py:200
  138.3 5.0 %all-to-all-start.2 = ((bf16[16,160,128]{2,1,0:T(8,128)(2,1)}), bf16[16,160,128]{2,1,0:T(8,128)(2,1)S(1)}, u32[]{:S(2)}, u32[]{:S(2)}) async-start(bf16[16,160,128]{2,1,0:T(8,128)(2,1)} %bitcast.21), calls=%async_computation.2 | async-start | bytes 1310720 | tf_op jit(solution)/shard_map/all_to_all | solution.py:220
  143.4 11.7 %expert.3 = bf16[4,2,2,160,128]{4,3,2,1,0:T(8,128)(2,1)} custom-call(s32[5]{0:T(128)} %stack.23.pos, bf16[160,3200]{1,0:T(8,128)(2,1)} %copy-done.1, bf16[160,3200]{1,0:T(8,128)(2,1)} %collective-permute-done.12.refs_1_, bf16[160,3200]{1,0:T(8,128)(2,1)} %collective-permute-done.14.refs_2_, bf16[160,3200]{1,0:T(8,128)(2,1)} %collective-permute-done.13.refs_3_, ...), custom_call_target="tpu_custom_call" | custom-call | flops 4026531840 | bytes 12582912 | tf_op jit(solution)/shard_map/expert/pallas_call | solution.py:200
  155.1 17.6 %all_to_all.20 = bf16[16,160,128]{2,1,0:T(8,128)(2,1)S(1)} all-to-all(bf16[16,160,128]{2,1,0:T(8,128)(2,1)} %bitcast.22), channel_id=1, replica_groups=mesh['dp'=2,'y'=4,'c'=2,'z'=8,'xl'=2] {'y','c','xl'}, dimensions={0} | all-to-all | bytes 1310720 | tf_op jit(solution)/shard_map/all_to_all | solution.py:220
  172.7 1.4 combine.1
  174.2 1.6 reshape.23
  (50 shorter events, 0.7 us)
Async XLA Ops:
  0.9 4.0 %collective-permute-start = (bf16[2,192,128]{2,1,0:T(8,128)(2,1)S(1)}, bf16[2,192,128]{2,1,0:T(8,128)(2,1)S(1)}, u32[]{:S(2)}, u32[]{:S(2)}) collective-permute-start(bf16[2,192,128]{2,1,0:T(8,128)(2,1)S(1)} %dynamic-slice_bitcast_fusion), channel_id=1, source_target_pairs={{0,1},{1,0},{2,3},{3,2},{4,5},{5,4},{6,7},{7,6},{8,9},{9,8},{10,11... | collective-permute-start | bytes 294920 | tf_op jit(solution)/shard_map/ppermute | solution.py:17
  5.9 9.3 %collective-permute-start.2 = (bf16[2,384,128]{2,1,0:T(8,128)(2,1)S(1)}, bf16[2,384,128]{2,1,0:T(8,128)(2,1)S(1)}, u32[]{:S(2)}, u32[]{:S(2)}) collective-permute-start(bf16[2,384,128]{2,1,0:T(8,128)(2,1)S(1)} %pad_maximum_fusion.refs_0_), channel_id=1, source_target_pairs={{0,2},{2,4},{4,6},{6,8},{8,10},{10,12},{12,14},{14,0},{1,3},{3,5},... | collective-permute-start | bytes 589832 | tf_op jit(solution)/shard_map/ppermute | solution.py:17
  7.8 7.3 %collective-permute-start.1 = (bf16[2,384,128]{2,1,0:T(8,128)(2,1)S(1)}, bf16[2,384,128]{2,1,0:T(8,128)(2,1)S(1)}, u32[]{:S(2)}, u32[]{:S(2)}) collective-permute-start(bf16[2,384,128]{2,1,0:T(8,128)(2,1)S(1)} %pad_maximum_fusion.refs_0_), channel_id=1, source_target_pairs={{0,14},{2,0},{4,2},{6,4},{8,6},{10,8},{12,10},{14,12},{1,15},{3,1}... | collective-permute-start | bytes 589832 | tf_op jit(solution)/shard_map/ppermute | solution.py:17
  15.2 6.9 %collective-permute-start.3 = (bf16[2,384,128]{2,1,0:T(8,128)(2,1)S(1)}, bf16[2,384,128]{2,1,0:T(8,128)(2,1)S(1)}, u32[]{:S(2)}, u32[]{:S(2)}) collective-permute-start(bf16[2,384,128]{2,1,0:T(8,128)(2,1)S(1)} %collective-permute-done.2.refs_7_), channel_id=1, source_target_pairs={{0,2},{2,4},{4,6},{6,8},{8,10},{10,12},{12,14},{14,0},{1,3},{3,5},... | collective-permute-start | bytes 589832 | tf_op jit(solution)/shard_map/ppermute | solution.py:17
  15.2 6.9 %collective-permute-start.4 = (bf16[2,384,128]{2,1,0:T(8,128)(2,1)S(1)}, bf16[2,384,128]{2,1,0:T(8,128)(2,1)S(1)}, u32[]{:S(2)}, u32[]{:S(2)}) collective-permute-start(bf16[2,384,128]{2,1,0:T(8,128)(2,1)S(1)} %collective-permute-done.1.refs_1_), channel_id=1, source_target_pairs={{0,14},{2,0},{4,2},{6,4},{8,6},{10,8},{12,10},{14,12},{1,15},{3,1}... | collective-permute-start | bytes 589832 | tf_op jit(solution)/shard_map/ppermute | solution.py:17
  22.0 16.4 %copy-start.7 = (s32[4,128,2]{1,2,0:T(2,128)S(1)}, s32[4,128,2]{1,2,0:T(2,128)}, u32[]{:S(2)}) copy-start(s32[4,128,2]{1,2,0:T(2,128)} %param.6) | copy-start | bytes 12292
  22.0 16.4 %copy-start.8 = (f32[4,128,2]{1,2,0:T(2,128)S(1)}, f32[4,128,2]{1,2,0:T(2,128)}, u32[]{:S(2)}) copy-start(f32[4,128,2]{1,2,0:T(2,128)} %param.7) | copy-start | bytes 12292
  22.0 16.5 %copy-start = (s32[5]{0:T(128)S(1)}, s32[5]{0:T(128)}, u32[]{:S(2)}) copy-start(s32[5]{0:T(128)} %stack.23.pos) | copy-start | bytes 64
  22.1 5.8 %collective-permute-start.6 = (bf16[2,384,128]{2,1,0:T(8,128)(2,1)S(1)}, bf16[2,384,128]{2,1,0:T(8,128)(2,1)S(1)}, u32[]{:S(2)}, u32[]{:S(2)}) collective-permute-start(bf16[2,384,128]{2,1,0:T(8,128)(2,1)S(1)} %collective-permute-done.3.refs_6_), channel_id=1, source_target_pairs={{0,2},{2,4},{4,6},{6,8},{8,10},{10,12},{12,14},{14,0},{1,3},{3,5},... | collective-permute-start | bytes 589832 | tf_op jit(solution)/shard_map/ppermute | solution.py:17
  22.2 5.8 %collective-permute-start.5 = (bf16[2,384,128]{2,1,0:T(8,128)(2,1)S(1)}, bf16[2,384,128]{2,1,0:T(8,128)(2,1)S(1)}, u32[]{:S(2)}, u32[]{:S(2)}) collective-permute-start(bf16[2,384,128]{2,1,0:T(8,128)(2,1)S(1)} %collective-permute-done.4.refs_2_), channel_id=1, source_target_pairs={{0,14},{2,0},{4,2},{6,4},{8,6},{10,8},{12,10},{14,12},{1,15},{3,1}... | collective-permute-start | bytes 589832 | tf_op jit(solution)/shard_map/ppermute | solution.py:17
  27.9 4.8 %collective-permute-start.7 = (bf16[1,384,128]{2,1,0:T(8,128)(2,1)S(1)}, bf16[1,384,128]{2,1,0:T(8,128)(2,1)S(1)}, u32[]{:S(2)}, u32[]{:S(2)}) collective-permute-start(bf16[1,384,128]{2,1,0:T(8,128)(2,1)S(1)} %slice.24), channel_id=1, source_target_pairs={{0,2},{2,4},{4,6},{6,8},{8,10},{10,12},{12,14},{14,0},{1,3},{3,5},... | collective-permute-start | bytes 294920 | tf_op jit(solution)/shard_map/ppermute | solution.py:17
  28.0 4.6 %collective-permute-start.8 = (bf16[1,384,128]{2,1,0:T(8,128)(2,1)S(1)}, bf16[1,384,128]{2,1,0:T(8,128)(2,1)S(1)}, u32[]{:S(2)}, u32[]{:S(2)}) collective-permute-start(bf16[1,384,128]{2,1,0:T(8,128)(2,1)S(1)} %slice.25), channel_id=1, source_target_pairs={{0,14},{2,0},{4,2},{6,4},{8,6},{10,8},{12,10},{14,12},{1,15},{3,1}... | collective-permute-start | bytes 294920 | tf_op jit(solution)/shard_map/ppermute | solution.py:17
  32.6 23.3 %all-to-all-start = ((bf16[8,192,256]{2,1,0:T(8,128)(2,1)}), bf16[8,192,256]{2,1,0:T(8,128)(2,1)S(1)}, u32[]{:S(2)}, u32[]{:S(2)}) async-start(bf16[8,192,256]{2,1,0:T(8,128)(2,1)} %get-tuple-element.46), calls=%async_computation | async-start | bytes 1572864 | tf_op jit(solution)/shard_map/all_to_all | solution.py:159
  41.9 1.0 copy-start.2
  42.9 37.8 %copy-start.1 = (bf16[160,3200]{1,0:T(8,128)(2,1)}, bf16[160,3200]{1,0:T(8,128)(2,1)S(1)}, u32[]{:S(2)}) copy-start(bf16[160,3200]{1,0:T(8,128)(2,1)S(1)} %get-tuple-element.44.refs_0_) | copy-start | bytes 3072004
  42.9 32.1 %copy-start.3 = (bf16[160,3200]{1,0:T(8,128)(2,1)S(1)}, bf16[160,3200]{1,0:T(8,128)(2,1)}, u32[]{:S(2)}) copy-start(bf16[160,3200]{1,0:T(8,128)(2,1)} %copy-done.2) | copy-start | bytes 3072004
  42.9 19.9 %collective-permute-start.11 = (bf16[160,3200]{1,0:T(8,128)(2,1)S(1)}, bf16[160,3200]{1,0:T(8,128)(2,1)}, u32[]{:S(2)}, u32[]{:S(2)}) collective-permute-start(bf16[160,3200]{1,0:T(8,128)(2,1)S(1)} %get-tuple-element.44.refs_0_), channel_id=1, source_target_pairs={{0,16},{16,0},{1,17},{17,1},{2,18},{18,2},{3,19},{19,3},{4,20},{20... | collective-permute-start | bytes 3072008 | tf_op jit(solution)/shard_map/ppermute | solution.py:17
  49.1 25.9 %collective-permute-start.12 = (bf16[160,3200]{1,0:T(8,128)(2,1)}, bf16[160,3200]{1,0:T(8,128)(2,1)}, u32[]{:S(2)}, u32[]{:S(2)}) collective-permute-start(bf16[160,3200]{1,0:T(8,128)(2,1)} %get-tuple-element.50), channel_id=1, source_target_pairs={{0,32},{32,64},{64,96},{96,0},{1,33},{33,65},{65,97},{97,1},{2,34}... | collective-permute-start | bytes 3072008 | tf_op jit(solution)/shard_map/ppermute | solution.py:17
  50.4 24.6 %collective-permute-start.13 = (bf16[160,3200]{1,0:T(8,128)(2,1)}, bf16[160,3200]{1,0:T(8,128)(2,1)}, u32[]{:S(2)}, u32[]{:S(2)}) collective-permute-start(bf16[160,3200]{1,0:T(8,128)(2,1)} %get-tuple-element.51), channel_id=1, source_target_pairs={{0,96},{32,0},{64,32},{96,64},{1,97},{33,1},{65,33},{97,65},{2,98}... | collective-permute-start | bytes 3072008 | tf_op jit(solution)/shard_map/ppermute | solution.py:17
  55.9 24.8 %copy-start.4 = (bf16[8,192,256]{2,1,0:T(8,128)(2,1)}, bf16[8,192,256]{2,1,0:T(8,128)(2,1)S(1)}, u32[]{:S(2)}) copy-start(bf16[8,192,256]{2,1,0:T(8,128)(2,1)S(1)} %all-to-all-done.refs_8_) | copy-start | bytes 2359300
  55.9 19.1 %collective-permute-start.9 = (bf16[8,192,256]{2,1,0:T(8,128)(2,1)S(1)}, bf16[8,192,256]{2,1,0:T(8,128)(2,1)}, u32[]{:S(2)}, u32[]{:S(2)}) collective-permute-start(bf16[8,192,256]{2,1,0:T(8,128)(2,1)S(1)} %all-to-all-done.refs_8_), channel_id=1, source_target_pairs={{0,1},{1,128},{128,129},{129,0},{2,3},{3,130},{130,131},{131,2},{4... | collective-permute-start | bytes 2359304 | tf_op jit(solution)/shard_map/ppermute | solution.py:17
  57.1 17.9 %collective-permute-start.10 = (bf16[8,192,256]{2,1,0:T(8,128)(2,1)S(1)}, bf16[8,192,256]{2,1,0:T(8,128)(2,1)}, u32[]{:S(2)}, u32[]{:S(2)}) collective-permute-start(bf16[8,192,256]{2,1,0:T(8,128)(2,1)S(1)} %all-to-all-done.refs_8_), channel_id=1, source_target_pairs={{0,129},{1,0},{128,1},{129,128},{2,131},{3,2},{130,3},{131,130},{4... | collective-permute-start | bytes 2359304 | tf_op jit(solution)/shard_map/ppermute | solution.py:17
  58.6 29.6 %all-to-all-start.1 = ((bf16[8,192,256]{2,1,0:T(8,128)(2,1)}), bf16[8,192,256]{2,1,0:T(8,128)(2,1)}, u32[]{:S(2)}, u32[]{:S(2)}) async-start(bf16[8,192,256]{2,1,0:T(8,128)(2,1)} %get-tuple-element.47), calls=%async_computation.1 | async-start | bytes 1572864 | tf_op jit(solution)/shard_map/all_to_all | solution.py:159
  75.0 23.7 %collective-permute-start.14 = (bf16[160,3200]{1,0:T(8,128)(2,1)S(1)}, bf16[160,3200]{1,0:T(8,128)(2,1)}, u32[]{:S(2)}, u32[]{:S(2)}) collective-permute-start(bf16[160,3200]{1,0:T(8,128)(2,1)S(1)} %copy-done.3), channel_id=1, source_target_pairs={{0,64},{32,96},{64,0},{96,32},{1,65},{33,97},{65,1},{97,33},{2,66}... | collective-permute-start | bytes 3072008 | tf_op jit(solution)/shard_map/ppermute | solution.py:17
  78.4 9.0 %collective-permute-start.15 = (bf16[4,192,256]{2,1,0:T(8,128)(2,1)S(1)}, bf16[4,192,256]{2,1,0:T(8,128)(2,1)S(1)}, u32[]{:S(2)}, u32[]{:S(2)}) collective-permute-start(bf16[4,192,256]{2,1,0:T(8,128)(2,1)S(1)} %slice.20), channel_id=1, source_target_pairs={{0,1},{1,128},{128,129},{129,0},{2,3},{3,130},{130,131},{131,2},{4... | collective-permute-start | bytes 1179656 | tf_op jit(solution)/shard_map/ppermute | solution.py:17
  80.7 7.5 %collective-permute-start.16 = (bf16[4,192,256]{2,1,0:T(8,128)(2,1)S(1)}, bf16[4,192,256]{2,1,0:T(8,128)(2,1)}, u32[]{:S(2)}, u32[]{:S(2)}) collective-permute-start(bf16[4,192,256]{2,1,0:T(8,128)(2,1)S(1)} %slice.21), channel_id=1, source_target_pairs={{0,129},{1,0},{128,1},{129,128},{2,131},{3,2},{130,3},{131,130},{4... | collective-permute-start | bytes 1179656 | tf_op jit(solution)/shard_map/ppermute | solution.py:17
  87.4 0.7 copy-start.11
  98.8 17.4 %collective-permute-start.17 = (bf16[8,192,256]{2,1,0:T(8,128)(2,1)}, bf16[8,192,256]{2,1,0:T(8,128)(2,1)S(1)}, u32[]{:S(2)}, u32[]{:S(2)}) collective-permute-start(bf16[8,192,256]{2,1,0:T(8,128)(2,1)} %all-to-all-done.1.refs_8_), channel_id=1, source_target_pairs={{0,1},{1,128},{128,129},{129,0},{2,3},{3,130},{130,131},{131,2},{4... | collective-permute-start | bytes 2359304 | tf_op jit(solution)/shard_map/ppermute | solution.py:17
  100.0 16.2 %collective-permute-start.18 = (bf16[8,192,256]{2,1,0:T(8,128)(2,1)}, bf16[8,192,256]{2,1,0:T(8,128)(2,1)S(1)}, u32[]{:S(2)}, u32[]{:S(2)}) collective-permute-start(bf16[8,192,256]{2,1,0:T(8,128)(2,1)} %all-to-all-done.1.refs_8_), channel_id=1, source_target_pairs={{0,129},{1,0},{128,1},{129,128},{2,131},{3,2},{130,3},{131,130},{4... | collective-permute-start | bytes 2359304 | tf_op jit(solution)/shard_map/ppermute | solution.py:17
  116.2 22.1 %copy-start.5 = (bf16[8,192,256]{2,1,0:T(8,128)(2,1)}, bf16[8,192,256]{2,1,0:T(8,128)(2,1)S(1)}, u32[]{:S(2)}) copy-start(bf16[8,192,256]{2,1,0:T(8,128)(2,1)S(1)} %collective-permute-done.17.refs_9_) | copy-start | bytes 2359300
  116.2 22.1 %copy-start.6 = (bf16[8,192,256]{2,1,0:T(8,128)(2,1)}, bf16[8,192,256]{2,1,0:T(8,128)(2,1)S(1)}, u32[]{:S(2)}) copy-start(bf16[8,192,256]{2,1,0:T(8,128)(2,1)S(1)} %collective-permute-done.18.refs_10_) | copy-start | bytes 2359300
  116.2 7.4 %collective-permute-start.19 = (bf16[160,3200]{1,0:T(8,128)(2,1)}, bf16[160,3200]{1,0:T(8,128)(2,1)S(1)}, u32[]{:S(2)}, u32[]{:S(2)}) collective-permute-start(bf16[160,3200]{1,0:T(8,128)(2,1)} %collective-permute-done.12.refs_1_), channel_id=1, source_target_pairs={{0,16},{16,0},{1,17},{17,1},{2,18},{18,2},{3,19},{19,3},{4,20},{20... | collective-permute-start | bytes 3072008 | tf_op jit(solution)/shard_map/ppermute | solution.py:17
  120.2 5.4 %collective-permute-start.20 = (bf16[160,3200]{1,0:T(8,128)(2,1)}, bf16[160,3200]{1,0:T(8,128)(2,1)S(1)}, u32[]{:S(2)}, u32[]{:S(2)}) collective-permute-start(bf16[160,3200]{1,0:T(8,128)(2,1)} %collective-permute-done.14.refs_2_), channel_id=1, source_target_pairs={{0,16},{16,0},{1,17},{17,1},{2,18},{18,2},{3,19},{19,3},{4,20},{20... | collective-permute-start | bytes 3072008 | tf_op jit(solution)/shard_map/ppermute | solution.py:17
  120.3 5.4 %collective-permute-start.21 = (bf16[160,3200]{1,0:T(8,128)(2,1)}, bf16[160,3200]{1,0:T(8,128)(2,1)}, u32[]{:S(2)}, u32[]{:S(2)}) collective-permute-start(bf16[160,3200]{1,0:T(8,128)(2,1)} %collective-permute-done.13.refs_3_), channel_id=1, source_target_pairs={{0,16},{16,0},{1,17},{17,1},{2,18},{18,2},{3,19},{19,3},{4,20},{20... | collective-permute-start | bytes 3072008 | tf_op jit(solution)/shard_map/ppermute | solution.py:17
  120.8 22.6 %collective-permute-start.22 = (bf16[4,192,256]{2,1,0:T(8,128)(2,1)S(1)}, bf16[4,192,256]{2,1,0:T(8,128)(2,1)}, u32[]{:S(2)}, u32[]{:S(2)}) collective-permute-start(bf16[4,192,256]{2,1,0:T(8,128)(2,1)S(1)} %slice.22), channel_id=1, source_target_pairs={{0,1},{1,128},{128,129},{129,0},{2,3},{3,130},{130,131},{131,2},{4... | collective-permute-start | bytes 1179656 | tf_op jit(solution)/shard_map/ppermute | solution.py:17
  122.3 21.1 %collective-permute-start.23 = (bf16[4,192,256]{2,1,0:T(8,128)(2,1)S(1)}, bf16[4,192,256]{2,1,0:T(8,128)(2,1)}, u32[]{:S(2)}, u32[]{:S(2)}) collective-permute-start(bf16[4,192,256]{2,1,0:T(8,128)(2,1)S(1)} %slice.23), channel_id=1, source_target_pairs={{0,129},{1,0},{128,1},{129,128},{2,131},{3,2},{130,3},{131,130},{4... | collective-permute-start | bytes 1179656 | tf_op jit(solution)/shard_map/ppermute | solution.py:17
  123.7 2.1 %copy-start.9 = (bf16[160,3200]{1,0:T(8,128)(2,1)}, bf16[160,3200]{1,0:T(8,128)(2,1)S(1)}, u32[]{:S(2)}) copy-start(bf16[160,3200]{1,0:T(8,128)(2,1)S(1)} %collective-permute-done.19.refs_5_) | copy-start | bytes 3072004
  125.6 1.0 copy-start.10
  138.3 16.7 %all-to-all-start.2 = ((bf16[16,160,128]{2,1,0:T(8,128)(2,1)}), bf16[16,160,128]{2,1,0:T(8,128)(2,1)S(1)}, u32[]{:S(2)}, u32[]{:S(2)}) async-start(bf16[16,160,128]{2,1,0:T(8,128)(2,1)} %bitcast.21), calls=%async_computation.2 | async-start | bytes 1310720 | tf_op jit(solution)/shard_map/all_to_all | solution.py:220

commit v14 on v10

--- a/solution.py
+++ b/solution.py
@@ -157,15 +157,20 @@
     def far(left, right):
         return ring(left[:4], X, 4, 1), ring(right[4:], X, 4, -1)
 
-    below, above = [pair], [pair]
-    for k in range(3):
-        if k == 2:
-            below[2], above[2], *blocks = barrier((below[2], above[2], *blocks))
-        below.append(ring(below[-1], "z", 8, 1))
-        above.append(ring(above[-1], "z", 8, -1))
-    part_a, *last = barrier((blocks[0], ring(below[3][:1], "z", 8, 1), ring(above[3][1:], "z", 8, -1)))
+    below = [pair, ring(pair, "z", 8, 1), ring(pair, "z", 8, 2)]
+    above = [pair, ring(pair, "z", 8, -1), ring(pair, "z", 8, -2)]
+    below[1], above[1], below[2], above[2], *blocks = barrier((below[1], above[1], below[2], above[2], *blocks))
+    part_a, *last = barrier(
+        (
+            blocks[0],
+            ring(above[2], "z", 8, -1),
+            ring(below[2][:1], "z", 8, 2),
+            ring(above[2][1:], "z", 8, -2),
+            ring(below[2], "z", 8, 1),
+        )
+    )
     own_a = exchange(part_a)
-    feats = [pair] + above[1:] + [jnp.concatenate(last, axis=0)] + below[:0:-1]
+    feats = [*above, last[0], jnp.concatenate(last[1:3], axis=0), last[3], *below[:0:-1]]
     sent = pl.pallas_call(
         dispatch_kernel,
         out_shape=[jax.ShapeDtypeStruct((2 * MOST, 16 * width + 128), BF)] * 4,

time: 162 us -> 164 us (1.012)
  waiting for transfers between devices: 34.9 us -> 40.6 us
  starting transfers between devices: 69.8 us -> 64.2 us
  blocking collectives: 18.5 us -> 20.6 us
    ppermute x24, starting transfers between devices: 54.4 us -> 47.8 us  [ring(): return lax.ppermute(x, axis, [(i, (i + step) % size) for i in range(size)])]
    all_to_all x2, waiting for transfers between devices: 3.57 us -> 7.49 us  [exchange(): return lax.all_to_all(x, 'z', split_axis=0, concat_axis=0, tiled=True)]
    all_to_all x1, starting transfers between devices: 5.42 us -> 8.33 us  [give_back(): lax.all_to_all(act.reshape(16, 2 * MOST, wide), ('y', 'c', 'xl'), split_a...]
    all_to_all x1, blocking collectives: 18.5 us -> 20.6 us  [give_back(): lax.all_to_all(act.reshape(16, 2 * MOST, wide), ('y', 'c', 'xl'), split_a...]
    all_to_all x2, starting transfers between devices: 10 us -> 7.98 us  [exchange(): return lax.all_to_all(x, 'z', split_axis=0, concat_axis=0, tiled=True)]
  transfers between devices with their start and end apart: 27 -> 27, of which waited for: 10 -> 12; matrix products, arithmetic and copies ran while one was open for 2% -> 2% of each run, Pallas kernels for 17% -> 17%
where the time goes in v14:
time: 164 us
  starting transfers between devices  64.2 us (39%)
  waiting for transfers between devices  40.6 us (25%)
  Pallas kernels  29.1 us (18%)
  blocking collectives  20.6 us (13%)
  local copies, waits for them, and re-layouts  7.95 us (5%)
    ppermute x24, starting transfers between devices, ring(): return lax.ppermute(x, axis, [(i, (i + step) % size) for i in range(size)])  47.8 us
    ppermute x24, waiting for transfers between devices, ring(): return lax.ppermute(x, axis, [(i, (i + step) % size) for i in range(size)])  32.4 us
    pallas_call x2, Pallas kernels, expert(): pl.pallas_call(expert_kernel, out_shape=jax.ShapeDtypeStruct((4, 2, 2, 2...  20.7 us
    all_to_all x1, blocking collectives, give_back(): lax.all_to_all(act.reshape(16, 2 * MOST, wide), ('y', 'c', 'xl'), split_a...  20.6 us
    all_to_all x1, starting transfers between devices, give_back(): lax.all_to_all(act.reshape(16, 2 * MOST, wide), ('y', 'c', 'xl'), split_a...  8.33 us
    all_to_all x2, starting transfers between devices, exchange(): return lax.all_to_all(x, 'z', split_axis=0, concat_axis=0, tiled=True)  7.98 us
    all_to_all x2, waiting for transfers between devices, exchange(): return lax.all_to_all(x, 'z', split_axis=0, concat_axis=0, tiled=True)  7.49 us
    pallas_call x1, Pallas kernels, body(): pl.pallas_call(columns_kernel, out_shape=[jax.ShapeDtypeStruct((8, rows,...  3.58 us
  transfers between devices with their start and end apart: 27, of which 12 were waited for; matrix products, arithmetic and copies ran while one was open for 2% of the time, Pallas kernels for 17%

profile of v14, /device:TPU:1, one launch (start us, length us, event | category | flops | bytes accessed | tf_op | source)
XLA Modules:
  0.0 163.6 jit_solution(10972599626735701013)
XLA Ops:
  0.0 0.9 dynamic-slice_bitcast_fusion
  0.9 2.0 %collective-permute-start = (bf16[2,192,128]{2,1,0:T(8,128)(2,1)S(1)}, bf16[2,192,128]{2,1,0:T(8,128)(2,1)S(1)}, u32[]{:S(2)}, u32[]{:S(2)}) collective-permute-start(bf16[2,192,128]{2,1,0:T(8,128)(2,1)S(1)} %dynamic-slice_bitcast_fusion), channel_id=1, source_target_pairs={{0,1},{1,0},{2,3},{3,2},{4,5},{5,4},{6,7},{7,6},{8,9},{9,8},{10,11... | collective-permute-start | bytes 294920 | tf_op jit(solution)/shard_map/ppermute | solution.py:17
  2.9 2.0 %collective-permute-done = bf16[2,192,128]{2,1,0:T(8,128)(2,1)S(1)} collective-permute-done((bf16[2,192,128]{2,1,0:T(8,128)(2,1)S(1)}, bf16[2,192,128]{2,1,0:T(8,128)(2,1)S(1)}, u32[]{:S(2)}, u32[]{:S(2)}) %collective-permute-start) | collective-permute-done | bytes 98336 | tf_op jit(solution)/shard_map/ppermute | solution.py:17
  4.9 0.9 bitcast_select_fusion.1
  5.9 2.0 %collective-permute-start.1 = (bf16[2,384,128]{2,1,0:T(8,128)(2,1)S(1)}, bf16[2,384,128]{2,1,0:T(8,128)(2,1)S(1)}, u32[]{:S(2)}, u32[]{:S(2)}) collective-permute-start(bf16[2,384,128]{2,1,0:T(8,128)(2,1)S(1)} %pad_maximum_fusion.refs_0_), channel_id=1, source_target_pairs={{0,2},{2,4},{4,6},{6,8},{8,10},{10,12},{12,14},{14,0},{1,3},{3,5},... | collective-permute-start | bytes 589832 | tf_op jit(solution)/shard_map/ppermute | solution.py:17
  7.8 4.0 %collective-permute-start.2 = (bf16[2,384,128]{2,1,0:T(8,128)(2,1)S(1)}, bf16[2,384,128]{2,1,0:T(8,128)(2,1)S(1)}, u32[]{:S(2)}, u32[]{:S(2)}) collective-permute-start(bf16[2,384,128]{2,1,0:T(8,128)(2,1)S(1)} %pad_maximum_fusion.refs_0_), channel_id=1, source_target_pairs={{0,14},{2,0},{4,2},{6,4},{8,6},{10,8},{12,10},{14,12},{1,15},{3,1}... | collective-permute-start | bytes 589832 | tf_op jit(solution)/shard_map/ppermute | solution.py:17
  11.9 3.6 %collective-permute-start.4 = (bf16[2,384,128]{2,1,0:T(8,128)(2,1)S(1)}, bf16[2,384,128]{2,1,0:T(8,128)(2,1)S(1)}, u32[]{:S(2)}, u32[]{:S(2)}) collective-permute-start(bf16[2,384,128]{2,1,0:T(8,128)(2,1)S(1)} %pad_maximum_fusion.refs_0_), channel_id=1, source_target_pairs={{0,12},{2,14},{4,0},{6,2},{8,4},{10,6},{12,8},{14,10},{1,13},{3,15... | collective-permute-start | bytes 589832 | tf_op jit(solution)/shard_map/ppermute | solution.py:17
  15.5 0.6 stack.23.pos
  16.1 3.6 %columns.1 = (bf16[8,192,256]{2,1,0:T(8,128)(2,1)}, bf16[8,192,256]{2,1,0:T(8,128)(2,1)}) custom-call(s32[5]{0:T(128)} %stack.23.pos, bf16[1,192,4096]{2,1,0:T(8,128)(2,1)} %gate.1, bf16[1,192,4096]{2,1,0:T(8,128)(2,1)} %up.1), custom_call_target="tpu_custom_call" | custom-call | tf_op jit(solution)/shard_map/columns/pallas_call | solution.py:141
  19.7 3.2 %collective-permute-done.3.refs_6_ = bf16[2,384,128]{2,1,0:T(8,128)(2,1)S(1)} collective-permute-done((bf16[2,384,128]{2,1,0:T(8,128)(2,1)S(1)}, bf16[2,384,128]{2,1,0:T(8,128)(2,1)S(1)}, u32[]{:S(2)}, u32[]{:S(2)}) %collective-permute-start.3) | collective-permute-done | bytes 196640 | tf_op jit(solution)/shard_map/ppermute | solution.py:17
  23.3 1.0 collective-permute-start.5
  24.8 5.8 %collective-permute-start.6 = (bf16[1,384,128]{2,1,0:T(8,128)(2,1)S(1)}, bf16[1,384,128]{2,1,0:T(8,128)(2,1)S(1)}, u32[]{:S(2)}, u32[]{:S(2)}) collective-permute-start(bf16[1,384,128]{2,1,0:T(8,128)(2,1)S(1)} %slice.18), channel_id=1, source_target_pairs={{0,4},{2,6},{4,8},{6,10},{8,12},{10,14},{12,0},{14,2},{1,5},{3,7},... | collective-permute-start | bytes 294920 | tf_op jit(solution)/shard_map/ppermute | solution.py:17
  30.6 4.1 %collective-permute-done.6 = bf16[1,384,128]{2,1,0:T(8,128)(2,1)S(1)} collective-permute-done((bf16[1,384,128]{2,1,0:T(8,128)(2,1)S(1)}, bf16[1,384,128]{2,1,0:T(8,128)(2,1)S(1)}, u32[]{:S(2)}, u32[]{:S(2)}) %collective-permute-start.6) | collective-permute-done | bytes 98336 | tf_op jit(solution)/shard_map/ppermute | solution.py:17
  34.7 2.2 %collective-permute-done.7 = bf16[1,384,128]{2,1,0:T(8,128)(2,1)S(1)} collective-permute-done((bf16[1,384,128]{2,1,0:T(8,128)(2,1)S(1)}, bf16[1,384,128]{2,1,0:T(8,128)(2,1)S(1)}, u32[]{:S(2)}, u32[]{:S(2)}) %collective-permute-start.7) | collective-permute-done | bytes 98336 | tf_op jit(solution)/shard_map/ppermute | solution.py:17
  36.9 3.8 %all-to-all-start = ((bf16[8,192,256]{2,1,0:T(8,128)(2,1)}), bf16[8,192,256]{2,1,0:T(8,128)(2,1)S(1)}, u32[]{:S(2)}, u32[]{:S(2)}) async-start(bf16[8,192,256]{2,1,0:T(8,128)(2,1)} %get-tuple-element.48), calls=%async_computation | async-start | bytes 1572864 | tf_op jit(solution)/shard_map/all_to_all | solution.py:152
  40.7 3.4 %dispatch.1 = (bf16[160,3200]{1,0:T(8,128)(2,1)S(1)}, bf16[160,3200]{1,0:T(8,128)(2,1)}, bf16[160,3200]{1,0:T(8,128)(2,1)S(1)}, bf16[160,3200]{1,0:T(8,128)(2,1)}) custom-call(s32[5]{0:T(128)S(1)} %copy-done, f32[4,4,128]{2,1,0:T(4,128)S(1)} %maximum_bitcast_fusion.meta, bf16[2,384,128]{2,1,0:T(8,128)(2,1)S(1)} %pad_maximum_fusion.refs_0_, ...), custom_call_target="tpu_custom_call" | custom-call | tf_op jit(solution)/shard_map/dispatch/pallas_call | solution.py:174
  44.1 1.0 copy-done.2
  45.1 1.3 collective-permute-start.10
  46.4 1.4 collective-permute-start.11
  47.8 5.3 %collective-permute-start.9 = (bf16[160,3200]{1,0:T(8,128)(2,1)S(1)}, bf16[160,3200]{1,0:T(8,128)(2,1)}, u32[]{:S(2)}, u32[]{:S(2)}) collective-permute-start(bf16[160,3200]{1,0:T(8,128)(2,1)S(1)} %get-tuple-element.57.refs_0_), channel_id=1, source_target_pairs={{0,16},{16,0},{1,17},{17,1},{2,18},{18,2},{3,19},{19,3},{4,20},{20... | collective-permute-start | bytes 3072008 | tf_op jit(solution)/shard_map/ppermute | solution.py:17
  53.1 7.5 %all-to-all-done.refs_8_ = bf16[8,192,256]{2,1,0:T(8,128)(2,1)S(1)} async-done(((bf16[8,192,256]{2,1,0:T(8,128)(2,1)}), bf16[8,192,256]{2,1,0:T(8,128)(2,1)S(1)}, u32[]{:S(2)}, u32[]{:S(2)}) %all-to-all-start) | async-done | bytes 786464 | tf_op jit(solution)/shard_map/all_to_all | solution.py:152
  60.6 1.2 collective-permute-start.13
  61.8 1.5 collective-permute-start.14
  63.3 4.2 %all-to-all-start.1 = ((bf16[8,192,256]{2,1,0:T(8,128)(2,1)}), bf16[8,192,256]{2,1,0:T(8,128)(2,1)}, u32[]{:S(2)}, u32[]{:S(2)}) async-start(bf16[8,192,256]{2,1,0:T(8,128)(2,1)} %get-tuple-element.49), calls=%async_computation.1 | async-start | bytes 1572864 | tf_op jit(solution)/shard_map/all_to_all | solution.py:152
  67.5 3.0 %collective-permute-start.12 = (bf16[160,3200]{1,0:T(8,128)(2,1)S(1)}, bf16[160,3200]{1,0:T(8,128)(2,1)}, u32[]{:S(2)}, u32[]{:S(2)}) collective-permute-start(bf16[160,3200]{1,0:T(8,128)(2,1)S(1)} %copy-done.3), channel_id=1, source_target_pairs={{0,64},{32,96},{64,0},{96,32},{1,65},{33,97},{65,1},{97,33},{2,66}... | collective-permute-start | bytes 3072008 | tf_op jit(solution)/shard_map/ppermute | solution.py:17
  70.6 6.3 %collective-permute-done.13.refs_9_ = bf16[8,192,256]{2,1,0:T(8,128)(2,1)} collective-permute-done((bf16[8,192,256]{2,1,0:T(8,128)(2,1)S(1)}, bf16[8,192,256]{2,1,0:T(8,128)(2,1)}, u32[]{:S(2)}, u32[]{:S(2)}) %collective-permute-start.13) | collective-permute-done | bytes 786464 | tf_op jit(solution)/shard_map/ppermute | solution.py:17
  76.8 5.1 %collective-permute-start.17 = (bf16[160,3200]{1,0:T(8,128)(2,1)}, bf16[160,3200]{1,0:T(8,128)(2,1)}, u32[]{:S(2)}, u32[]{:S(2)}) collective-permute-start(bf16[160,3200]{1,0:T(8,128)(2,1)} %collective-permute-done.10.refs_1_), channel_id=1, source_target_pairs={{0,16},{16,0},{1,17},{17,1},{2,18},{18,2},{3,19},{19,3},{4,20},{20... | collective-permute-start | bytes 3072008 | tf_op jit(solution)/shard_map/ppermute | solution.py:17
  81.9 1.0 slice.20
  82.9 1.3 collective-permute-start.15
  84.2 1.0 slice.21
  85.2 1.6 collective-permute-start.16
  86.8 3.0 %collective-permute-done.12.refs_2_ = bf16[160,3200]{1,0:T(8,128)(2,1)} collective-permute-done((bf16[160,3200]{1,0:T(8,128)(2,1)S(1)}, bf16[160,3200]{1,0:T(8,128)(2,1)}, u32[]{:S(2)}, u32[]{:S(2)}) %collective-permute-start.12) | collective-permute-done | bytes 1024032 | tf_op jit(solution)/shard_map/ppermute | solution.py:17
  89.7 4.7 %collective-permute-done.15.refs_11_ = bf16[4,192,256]{2,1,0:T(8,128)(2,1)S(1)} collective-permute-done((bf16[4,192,256]{2,1,0:T(8,128)(2,1)S(1)}, bf16[4,192,256]{2,1,0:T(8,128)(2,1)S(1)}, u32[]{:S(2)}, u32[]{:S(2)}) %collective-permute-start.15) | collective-permute-done | bytes 393248 | tf_op jit(solution)/shard_map/ppermute | solution.py:17
  94.4 0.8 copy-done.10
  95.3 1.8 %collective-permute-start.21 = (bf16[160,3200]{1,0:T(8,128)(2,1)}, bf16[160,3200]{1,0:T(8,128)(2,1)S(1)}, u32[]{:S(2)}, u32[]{:S(2)}) collective-permute-start(bf16[160,3200]{1,0:T(8,128)(2,1)} %collective-permute-done.12.refs_2_), channel_id=1, source_target_pairs={{0,16},{16,0},{1,17},{17,1},{2,18},{18,2},{3,19},{19,3},{4,20},{20... | collective-permute-start | bytes 3072008 | tf_op jit(solution)/shard_map/ppermute | solution.py:17
  97.0 0.9 collective-permute-start.19
  98.0 1.8 %collective-permute-start.20 = (bf16[8,192,256]{2,1,0:T(8,128)(2,1)}, bf16[8,192,256]{2,1,0:T(8,128)(2,1)S(1)}, u32[]{:S(2)}, u32[]{:S(2)}) collective-permute-start(bf16[8,192,256]{2,1,0:T(8,128)(2,1)} %all-to-all-done.1.refs_8_), channel_id=1, source_target_pairs={{0,129},{1,0},{128,1},{129,128},{2,131},{3,2},{130,3},{131,130},{4... | collective-permute-start | bytes 2359304 | tf_op jit(solution)/shard_map/ppermute | solution.py:17
  99.7 1.0 copy-done.9
  100.7 10.3 %expert.2 = bf16[4,2,2,160,128]{4,3,2,1,0:T(8,128)(2,1)} custom-call(s32[5]{0:T(128)} %stack.23.pos, bf16[160,3200]{1,0:T(8,128)(2,1)} %copy-done.1, bf16[160,3200]{1,0:T(8,128)(2,1)} %collective-permute-done.10.refs_1_, bf16[160,3200]{1,0:T(8,128)(2,1)} %collective-permute-done.12.refs_2_, bf16[160,3200]{1,0:T(8,128)(2,1)} %collective-permute-done.11.refs_3_, ...), custom_call_target="tpu_custom_call" | custom-call | flops 4026531840 | bytes 12582912 | tf_op jit(solution)/shard_map/expert/pallas_call | solution.py:199
  111.0 6.5 %collective-permute-done.19.refs_9_ = bf16[8,192,256]{2,1,0:T(8,128)(2,1)S(1)} collective-permute-done((bf16[8,192,256]{2,1,0:T(8,128)(2,1)}, bf16[8,192,256]{2,1,0:T(8,128)(2,1)S(1)}, u32[]{:S(2)}, u32[]{:S(2)}) %collective-permute-start.19) | collective-permute-done | bytes 786464 | tf_op jit(solution)/shard_map/ppermute | solution.py:17
  117.6 0.9 collective-permute-start.22
  118.5 2.0 %collective-permute-start.23 = (bf16[4,192,256]{2,1,0:T(8,128)(2,1)S(1)}, bf16[4,192,256]{2,1,0:T(8,128)(2,1)}, u32[]{:S(2)}, u32[]{:S(2)}) collective-permute-start(bf16[4,192,256]{2,1,0:T(8,128)(2,1)S(1)} %slice.23), channel_id=1, source_target_pairs={{0,129},{1,0},{128,1},{129,128},{2,131},{3,2},{130,3},{131,130},{4... | collective-permute-start | bytes 1179656 | tf_op jit(solution)/shard_map/ppermute | solution.py:17
  120.5 8.3 %all-to-all-start.2 = ((bf16[16,160,128]{2,1,0:T(8,128)(2,1)}), bf16[16,160,128]{2,1,0:T(8,128)(2,1)S(1)}, u32[]{:S(2)}, u32[]{:S(2)}) async-start(bf16[16,160,128]{2,1,0:T(8,128)(2,1)} %bitcast.11), calls=%async_computation.2 | async-start | bytes 1310720 | tf_op jit(solution)/shard_map/all_to_all | solution.py:218
  128.8 10.4 %expert.3 = bf16[4,2,2,160,128]{4,3,2,1,0:T(8,128)(2,1)} custom-call(s32[5]{0:T(128)} %stack.23.pos, bf16[160,3200]{1,0:T(8,128)(2,1)} %copy-done.1, bf16[160,3200]{1,0:T(8,128)(2,1)} %collective-permute-done.10.refs_1_, bf16[160,3200]{1,0:T(8,128)(2,1)} %collective-permute-done.12.refs_2_, bf16[160,3200]{1,0:T(8,128)(2,1)} %collective-permute-done.11.refs_3_, ...), custom_call_target="tpu_custom_call" | custom-call | flops 4026531840 | bytes 12582912 | tf_op jit(solution)/shard_map/expert/pallas_call | solution.py:199
  139.2 0.8 all-to-all-done.2
  140.0 20.6 %all_to_all.20 = bf16[16,160,128]{2,1,0:T(8,128)(2,1)S(1)} all-to-all(bf16[16,160,128]{2,1,0:T(8,128)(2,1)} %bitcast.21), channel_id=1, replica_groups=mesh['dp'=2,'y'=4,'c'=2,'z'=8,'xl'=2] {'y','c','xl'}, dimensions={0} | all-to-all | bytes 1310720 | tf_op jit(solution)/shard_map/all_to_all | solution.py:218
  160.6 1.5 combine.1
  162.0 1.6 reshape.23
  (48 shorter events, 1.1 us)
Async XLA Ops:
  0.9 4.0 %collective-permute-start = (bf16[2,192,128]{2,1,0:T(8,128)(2,1)S(1)}, bf16[2,192,128]{2,1,0:T(8,128)(2,1)S(1)}, u32[]{:S(2)}, u32[]{:S(2)}) collective-permute-start(bf16[2,192,128]{2,1,0:T(8,128)(2,1)S(1)} %dynamic-slice_bitcast_fusion), channel_id=1, source_target_pairs={{0,1},{1,0},{2,3},{3,2},{4,5},{5,4},{6,7},{7,6},{8,9},{9,8},{10,11... | collective-permute-start | bytes 294920 | tf_op jit(solution)/shard_map/ppermute | solution.py:17
  5.9 13.8 %collective-permute-start.1 = (bf16[2,384,128]{2,1,0:T(8,128)(2,1)S(1)}, bf16[2,384,128]{2,1,0:T(8,128)(2,1)S(1)}, u32[]{:S(2)}, u32[]{:S(2)}) collective-permute-start(bf16[2,384,128]{2,1,0:T(8,128)(2,1)S(1)} %pad_maximum_fusion.refs_0_), channel_id=1, source_target_pairs={{0,2},{2,4},{4,6},{6,8},{8,10},{10,12},{12,14},{14,0},{1,3},{3,5},... | collective-permute-start | bytes 589832 | tf_op jit(solution)/shard_map/ppermute | solution.py:17
  7.8 11.8 %collective-permute-start.2 = (bf16[2,384,128]{2,1,0:T(8,128)(2,1)S(1)}, bf16[2,384,128]{2,1,0:T(8,128)(2,1)S(1)}, u32[]{:S(2)}, u32[]{:S(2)}) collective-permute-start(bf16[2,384,128]{2,1,0:T(8,128)(2,1)S(1)} %pad_maximum_fusion.refs_0_), channel_id=1, source_target_pairs={{0,14},{2,0},{4,2},{6,4},{8,6},{10,8},{12,10},{14,12},{1,15},{3,1}... | collective-permute-start | bytes 589832 | tf_op jit(solution)/shard_map/ppermute | solution.py:17
  11.9 11.0 %collective-permute-start.3 = (bf16[2,384,128]{2,1,0:T(8,128)(2,1)S(1)}, bf16[2,384,128]{2,1,0:T(8,128)(2,1)S(1)}, u32[]{:S(2)}, u32[]{:S(2)}) collective-permute-start(bf16[2,384,128]{2,1,0:T(8,128)(2,1)S(1)} %pad_maximum_fusion.refs_0_), channel_id=1, source_target_pairs={{0,4},{2,6},{4,8},{6,10},{8,12},{10,14},{12,0},{14,2},{1,5},{3,7},... | collective-permute-start | bytes 589832 | tf_op jit(solution)/shard_map/ppermute | solution.py:17
  11.9 11.4 %collective-permute-start.4 = (bf16[2,384,128]{2,1,0:T(8,128)(2,1)S(1)}, bf16[2,384,128]{2,1,0:T(8,128)(2,1)S(1)}, u32[]{:S(2)}, u32[]{:S(2)}) collective-permute-start(bf16[2,384,128]{2,1,0:T(8,128)(2,1)S(1)} %pad_maximum_fusion.refs_0_), channel_id=1, source_target_pairs={{0,12},{2,14},{4,0},{6,2},{8,4},{10,6},{12,8},{14,10},{1,13},{3,15... | collective-permute-start | bytes 589832 | tf_op jit(solution)/shard_map/ppermute | solution.py:17
  19.6 21.0 %copy-start.7 = (s32[4,128,2]{1,2,0:T(2,128)S(1)}, s32[4,128,2]{1,2,0:T(2,128)}, u32[]{:S(2)}) copy-start(s32[4,128,2]{1,2,0:T(2,128)} %param.6) | copy-start | bytes 12292
  19.7 21.0 %copy-start.8 = (f32[4,128,2]{1,2,0:T(2,128)S(1)}, f32[4,128,2]{1,2,0:T(2,128)}, u32[]{:S(2)}) copy-start(f32[4,128,2]{1,2,0:T(2,128)} %param.7) | copy-start | bytes 12292
  19.7 21.0 %copy-start = (s32[5]{0:T(128)S(1)}, s32[5]{0:T(128)}, u32[]{:S(2)}) copy-start(s32[5]{0:T(128)} %stack.23.pos) | copy-start | bytes 64
  23.3 13.6 %collective-permute-start.5 = (bf16[2,384,128]{2,1,0:T(8,128)(2,1)S(1)}, bf16[2,384,128]{2,1,0:T(8,128)(2,1)S(1)}, u32[]{:S(2)}, u32[]{:S(2)}) collective-permute-start(bf16[2,384,128]{2,1,0:T(8,128)(2,1)S(1)} %collective-permute-done.4.refs_2_), channel_id=1, source_target_pairs={{0,14},{2,0},{4,2},{6,4},{8,6},{10,8},{12,10},{14,12},{1,15},{3,1}... | collective-permute-start | bytes 589832 | tf_op jit(solution)/shard_map/ppermute | solution.py:17
  24.3 12.5 %collective-permute-start.8 = (bf16[2,384,128]{2,1,0:T(8,128)(2,1)S(1)}, bf16[2,384,128]{2,1,0:T(8,128)(2,1)S(1)}, u32[]{:S(2)}, u32[]{:S(2)}) collective-permute-start(bf16[2,384,128]{2,1,0:T(8,128)(2,1)S(1)} %collective-permute-done.3.refs_6_), channel_id=1, source_target_pairs={{0,2},{2,4},{4,6},{6,8},{8,10},{10,12},{12,14},{14,0},{1,3},{3,5},... | collective-permute-start | bytes 589832 | tf_op jit(solution)/shard_map/ppermute | solution.py:17
  24.8 9.9 %collective-permute-start.6 = (bf16[1,384,128]{2,1,0:T(8,128)(2,1)S(1)}, bf16[1,384,128]{2,1,0:T(8,128)(2,1)S(1)}, u32[]{:S(2)}, u32[]{:S(2)}) collective-permute-start(bf16[1,384,128]{2,1,0:T(8,128)(2,1)S(1)} %slice.18), channel_id=1, source_target_pairs={{0,4},{2,6},{4,8},{6,10},{8,12},{10,14},{12,0},{14,2},{1,5},{3,7},... | collective-permute-start | bytes 294920 | tf_op jit(solution)/shard_map/ppermute | solution.py:17
  30.6 6.3 %collective-permute-start.7 = (bf16[1,384,128]{2,1,0:T(8,128)(2,1)S(1)}, bf16[1,384,128]{2,1,0:T(8,128)(2,1)S(1)}, u32[]{:S(2)}, u32[]{:S(2)}) collective-permute-start(bf16[1,384,128]{2,1,0:T(8,128)(2,1)S(1)} %slice.19), channel_id=1, source_target_pairs={{0,12},{2,14},{4,0},{6,2},{8,4},{10,6},{12,8},{14,10},{1,13},{3,15... | collective-permute-start | bytes 294920 | tf_op jit(solution)/shard_map/ppermute | solution.py:17
  36.9 23.7 %all-to-all-start = ((bf16[8,192,256]{2,1,0:T(8,128)(2,1)}), bf16[8,192,256]{2,1,0:T(8,128)(2,1)S(1)}, u32[]{:S(2)}, u32[]{:S(2)}) async-start(bf16[8,192,256]{2,1,0:T(8,128)(2,1)} %get-tuple-element.48), calls=%async_computation | async-start | bytes 1572864 | tf_op jit(solution)/shard_map/all_to_all | solution.py:152
  44.1 1.0 copy-start.2
  45.1 40.2 %copy-start.1 = (bf16[160,3200]{1,0:T(8,128)(2,1)}, bf16[160,3200]{1,0:T(8,128)(2,1)S(1)}, u32[]{:S(2)}) copy-start(bf16[160,3200]{1,0:T(8,128)(2,1)S(1)} %get-tuple-element.57.refs_0_) | copy-start | bytes 3072004
  45.1 22.5 %copy-start.3 = (bf16[160,3200]{1,0:T(8,128)(2,1)S(1)}, bf16[160,3200]{1,0:T(8,128)(2,1)}, u32[]{:S(2)}) copy-start(bf16[160,3200]{1,0:T(8,128)(2,1)} %copy-done.2) | copy-start | bytes 3072004
  45.1 22.4 %collective-permute-start.10 = (bf16[160,3200]{1,0:T(8,128)(2,1)}, bf16[160,3200]{1,0:T(8,128)(2,1)}, u32[]{:S(2)}, u32[]{:S(2)}) collective-permute-start(bf16[160,3200]{1,0:T(8,128)(2,1)} %get-tuple-element.58), channel_id=1, source_target_pairs={{0,32},{32,64},{64,96},{96,0},{1,33},{33,65},{65,97},{97,1},{2,34}... | collective-permute-start | bytes 3072008 | tf_op jit(solution)/shard_map/ppermute | solution.py:17
  46.4 21.2 %collective-permute-start.11 = (bf16[160,3200]{1,0:T(8,128)(2,1)}, bf16[160,3200]{1,0:T(8,128)(2,1)}, u32[]{:S(2)}, u32[]{:S(2)}) collective-permute-start(bf16[160,3200]{1,0:T(8,128)(2,1)} %get-tuple-element.59), channel_id=1, source_target_pairs={{0,96},{32,0},{64,32},{96,64},{1,97},{33,1},{65,33},{97,65},{2,98}... | collective-permute-start | bytes 3072008 | tf_op jit(solution)/shard_map/ppermute | solution.py:17
  47.8 19.7 %collective-permute-start.9 = (bf16[160,3200]{1,0:T(8,128)(2,1)S(1)}, bf16[160,3200]{1,0:T(8,128)(2,1)}, u32[]{:S(2)}, u32[]{:S(2)}) collective-permute-start(bf16[160,3200]{1,0:T(8,128)(2,1)S(1)} %get-tuple-element.57.refs_0_), channel_id=1, source_target_pairs={{0,16},{16,0},{1,17},{17,1},{2,18},{18,2},{3,19},{19,3},{4,20},{20... | collective-permute-start | bytes 3072008 | tf_op jit(solution)/shard_map/ppermute | solution.py:17
  60.6 24.6 %copy-start.4 = (bf16[8,192,256]{2,1,0:T(8,128)(2,1)}, bf16[8,192,256]{2,1,0:T(8,128)(2,1)S(1)}, u32[]{:S(2)}) copy-start(bf16[8,192,256]{2,1,0:T(8,128)(2,1)S(1)} %all-to-all-done.refs_8_) | copy-start | bytes 2359300
  60.6 16.2 %collective-permute-start.13 = (bf16[8,192,256]{2,1,0:T(8,128)(2,1)S(1)}, bf16[8,192,256]{2,1,0:T(8,128)(2,1)}, u32[]{:S(2)}, u32[]{:S(2)}) collective-permute-start(bf16[8,192,256]{2,1,0:T(8,128)(2,1)S(1)} %all-to-all-done.refs_8_), channel_id=1, source_target_pairs={{0,1},{1,128},{128,129},{129,0},{2,3},{3,130},{130,131},{131,2},{4... | collective-permute-start | bytes 2359304 | tf_op jit(solution)/shard_map/ppermute | solution.py:17
  61.8 15.0 %collective-permute-start.14 = (bf16[8,192,256]{2,1,0:T(8,128)(2,1)S(1)}, bf16[8,192,256]{2,1,0:T(8,128)(2,1)}, u32[]{:S(2)}, u32[]{:S(2)}) collective-permute-start(bf16[8,192,256]{2,1,0:T(8,128)(2,1)S(1)} %all-to-all-done.refs_8_), channel_id=1, source_target_pairs={{0,129},{1,0},{128,1},{129,128},{2,131},{3,2},{130,3},{131,130},{4... | collective-permute-start | bytes 2359304 | tf_op jit(solution)/shard_map/ppermute | solution.py:17
  63.3 32.0 %all-to-all-start.1 = ((bf16[8,192,256]{2,1,0:T(8,128)(2,1)}), bf16[8,192,256]{2,1,0:T(8,128)(2,1)}, u32[]{:S(2)}, u32[]{:S(2)}) async-start(bf16[8,192,256]{2,1,0:T(8,128)(2,1)} %get-tuple-element.49), calls=%async_computation.1 | async-start | bytes 1572864 | tf_op jit(solution)/shard_map/all_to_all | solution.py:152
  67.5 22.2 %collective-permute-start.12 = (bf16[160,3200]{1,0:T(8,128)(2,1)S(1)}, bf16[160,3200]{1,0:T(8,128)(2,1)}, u32[]{:S(2)}, u32[]{:S(2)}) collective-permute-start(bf16[160,3200]{1,0:T(8,128)(2,1)S(1)} %copy-done.3), channel_id=1, source_target_pairs={{0,64},{32,96},{64,0},{96,32},{1,65},{33,97},{65,1},{97,33},{2,66}... | collective-permute-start | bytes 3072008 | tf_op jit(solution)/shard_map/ppermute | solution.py:17
  76.8 18.5 %collective-permute-start.17 = (bf16[160,3200]{1,0:T(8,128)(2,1)}, bf16[160,3200]{1,0:T(8,128)(2,1)}, u32[]{:S(2)}, u32[]{:S(2)}) collective-permute-start(bf16[160,3200]{1,0:T(8,128)(2,1)} %collective-permute-done.10.refs_1_), channel_id=1, source_target_pairs={{0,16},{16,0},{1,17},{17,1},{2,18},{18,2},{3,19},{19,3},{4,20},{20... | collective-permute-start | bytes 3072008 | tf_op jit(solution)/shard_map/ppermute | solution.py:17
  81.9 13.4 %collective-permute-start.18 = (bf16[160,3200]{1,0:T(8,128)(2,1)}, bf16[160,3200]{1,0:T(8,128)(2,1)}, u32[]{:S(2)}, u32[]{:S(2)}) collective-permute-start(bf16[160,3200]{1,0:T(8,128)(2,1)} %collective-permute-done.11.refs_3_), channel_id=1, source_target_pairs={{0,16},{16,0},{1,17},{17,1},{2,18},{18,2},{3,19},{19,3},{4,20},{20... | collective-permute-start | bytes 3072008 | tf_op jit(solution)/shard_map/ppermute | solution.py:17
  82.9 11.5 %collective-permute-start.15 = (bf16[4,192,256]{2,1,0:T(8,128)(2,1)S(1)}, bf16[4,192,256]{2,1,0:T(8,128)(2,1)S(1)}, u32[]{:S(2)}, u32[]{:S(2)}) collective-permute-start(bf16[4,192,256]{2,1,0:T(8,128)(2,1)S(1)} %slice.20), channel_id=1, source_target_pairs={{0,1},{1,128},{128,129},{129,0},{2,3},{3,130},{130,131},{131,2},{4... | collective-permute-start | bytes 1179656 | tf_op jit(solution)/shard_map/ppermute | solution.py:17
  85.2 10.0 %collective-permute-start.16 = (bf16[4,192,256]{2,1,0:T(8,128)(2,1)S(1)}, bf16[4,192,256]{2,1,0:T(8,128)(2,1)}, u32[]{:S(2)}, u32[]{:S(2)}) collective-permute-start(bf16[4,192,256]{2,1,0:T(8,128)(2,1)S(1)} %slice.21), channel_id=1, source_target_pairs={{0,129},{1,0},{128,1},{129,128},{2,131},{3,2},{130,3},{131,130},{4... | collective-permute-start | bytes 1179656 | tf_op jit(solution)/shard_map/ppermute | solution.py:17
  94.4 0.8 copy-start.10
  95.3 4.5 %collective-permute-start.21 = (bf16[160,3200]{1,0:T(8,128)(2,1)}, bf16[160,3200]{1,0:T(8,128)(2,1)S(1)}, u32[]{:S(2)}, u32[]{:S(2)}) collective-permute-start(bf16[160,3200]{1,0:T(8,128)(2,1)} %collective-permute-done.12.refs_2_), channel_id=1, source_target_pairs={{0,16},{16,0},{1,17},{17,1},{2,18},{18,2},{3,19},{19,3},{4,20},{20... | collective-permute-start | bytes 3072008 | tf_op jit(solution)/shard_map/ppermute | solution.py:17
  97.0 20.5 %collective-permute-start.19 = (bf16[8,192,256]{2,1,0:T(8,128)(2,1)}, bf16[8,192,256]{2,1,0:T(8,128)(2,1)S(1)}, u32[]{:S(2)}, u32[]{:S(2)}) collective-permute-start(bf16[8,192,256]{2,1,0:T(8,128)(2,1)} %all-to-all-done.1.refs_8_), channel_id=1, source_target_pairs={{0,1},{1,128},{128,129},{129,0},{2,3},{3,130},{130,131},{131,2},{4... | collective-permute-start | bytes 2359304 | tf_op jit(solution)/shard_map/ppermute | solution.py:17
  98.0 19.6 %collective-permute-start.20 = (bf16[8,192,256]{2,1,0:T(8,128)(2,1)}, bf16[8,192,256]{2,1,0:T(8,128)(2,1)S(1)}, u32[]{:S(2)}, u32[]{:S(2)}) collective-permute-start(bf16[8,192,256]{2,1,0:T(8,128)(2,1)} %all-to-all-done.1.refs_8_), channel_id=1, source_target_pairs={{0,129},{1,0},{128,1},{129,128},{2,131},{3,2},{130,3},{131,130},{4... | collective-permute-start | bytes 2359304 | tf_op jit(solution)/shard_map/ppermute | solution.py:17
  99.7 1.0 copy-start.9
  117.6 11.3 %copy-start.5 = (bf16[8,192,256]{2,1,0:T(8,128)(2,1)}, bf16[8,192,256]{2,1,0:T(8,128)(2,1)S(1)}, u32[]{:S(2)}) copy-start(bf16[8,192,256]{2,1,0:T(8,128)(2,1)S(1)} %collective-permute-done.19.refs_9_) | copy-start | bytes 2359300
  117.6 11.3 %copy-start.6 = (bf16[8,192,256]{2,1,0:T(8,128)(2,1)}, bf16[8,192,256]{2,1,0:T(8,128)(2,1)S(1)}, u32[]{:S(2)}) copy-start(bf16[8,192,256]{2,1,0:T(8,128)(2,1)S(1)} %collective-permute-done.20.refs_10_) | copy-start | bytes 2359300
  117.6 11.2 %collective-permute-start.22 = (bf16[4,192,256]{2,1,0:T(8,128)(2,1)S(1)}, bf16[4,192,256]{2,1,0:T(8,128)(2,1)}, u32[]{:S(2)}, u32[]{:S(2)}) collective-permute-start(bf16[4,192,256]{2,1,0:T(8,128)(2,1)S(1)} %slice.22), channel_id=1, source_target_pairs={{0,1},{1,128},{128,129},{129,0},{2,3},{3,130},{130,131},{131,2},{4... | collective-permute-start | bytes 1179656 | tf_op jit(solution)/shard_map/ppermute | solution.py:17
  118.5 10.3 %collective-permute-start.23 = (bf16[4,192,256]{2,1,0:T(8,128)(2,1)S(1)}, bf16[4,192,256]{2,1,0:T(8,128)(2,1)}, u32[]{:S(2)}, u32[]{:S(2)}) collective-permute-start(bf16[4,192,256]{2,1,0:T(8,128)(2,1)S(1)} %slice.23), channel_id=1, source_target_pairs={{0,129},{1,0},{128,1},{129,128},{2,131},{3,2},{130,3},{131,130},{4... | collective-permute-start | bytes 1179656 | tf_op jit(solution)/shard_map/ppermute | solution.py:17
  120.5 19.5 %all-to-all-start.2 = ((bf16[16,160,128]{2,1,0:T(8,128)(2,1)}), bf16[16,160,128]{2,1,0:T(8,128)(2,1)S(1)}, u32[]{:S(2)}, u32[]{:S(2)}) async-start(bf16[16,160,128]{2,1,0:T(8,128)(2,1)} %bitcast.11), calls=%async_computation.2 | async-start | bytes 1310720 | tf_op jit(solution)/shard_map/all_to_all | solution.py:218

commit v15 on v10

--- a/solution.py
+++ b/solution.py
@@ -1,3 +1,5 @@
+import functools
+
 import jax
 import jax.numpy as jnp
 from jax import lax
@@ -76,8 +78,13 @@
                 out[z, :, t * 128 : (t + 1) * 128] = held[:, first : first + 128]
 
 
-def expert_kernel(pos, *refs):
-    xs, ws, (out, xbuf, wbuf, xsem, wsem) = refs[:8], refs[8:13], refs[13:]
+def expert_kernel(first, last, *refs):
+    pos, refs = refs[0], refs[1:]
+    count = last - first
+    xs, ws, refs = refs[:count], refs[count : count + 5], refs[count + 5 :]
+    if first:
+        kept, refs = refs[0], refs[1:]
+    out, xbuf, wbuf, xsem, wsem = refs
     y, c, xl, dp, z = (pos[i] for i in range(5))
     width = 16 * ws[0].shape[1]
     copies = []
@@ -86,16 +93,19 @@
         for k in range(src.shape[0]):
             place = wbuf.at[lax.div(j, 2), lax.rem(low + k + 8 - z, 8), lax.rem(j, 2)]
             copies.append(pltpu.make_async_copy(src.at[k], place, wsem.at[i, k]))
-    rows = [pltpu.make_async_copy(xs[g], xbuf.at[g], xsem.at[g]) for g in range(8)]
+    rows = [pltpu.make_async_copy(xs[g], xbuf.at[g], xsem.at[g]) for g in range(count)]
     for cp in copies:
         cp.start()
     rows[0].start()
+    if first:
+        for e in range(4):
+            out[e, c] = kept[e, c]
     for cp in copies:
         cp.wait()
     rows[1].start()
-    for g in range(8):
-        d, cc = g % 4, g // 4
-        if g < 6:
+    for g in range(count):
+        d, cc = (first + g) % 4, (first + g) // 4
+        if g < count - 2:
             rows[g + 2].start()
         rows[g].wait()
         rw = jnp.sum(xbuf[g, :, width:].astype(F32), axis=1, keepdims=True)
@@ -183,40 +193,40 @@
     opposite = ring(far_rows, "y", 4, 2)
     left_a, right_a, *near = barrier((left_a, right_a, *near))
     far_a = far(left_a, right_a)
-    other += [ring(h, "c", 2, 1) for h in near]
-    own_b, opposite, *rest = barrier((own_b, opposite, *far_a, *other))
-    far_a, other = rest[:2], rest[2:]
+    own_b, opposite, *rest = barrier((own_b, opposite, *near, *far_a))
+    near, ws_a = rest[:2], [own_a, left_a, right_a, *rest[2:]]
     left_b, right_b = sides(own_b)
     held = [sent[0], near[0], opposite, near[1]]
-    other = [other[0], other[1], ring(opposite, "c", 2, 1), other[2]]
-
-    def expert(*ws):
+
+    def expert(first, last, xs, ws, kept=()):
         return pl.pallas_call(
-            expert_kernel,
+            functools.partial(expert_kernel, first, last),
             out_shape=jax.ShapeDtypeStruct((4, 2, 2, 2 * MOST, wide), BF),
-            in_specs=[SM] + [ANY] * 13,
+            in_specs=[SM] + [ANY] * (len(xs) + 5) + [VM] * len(kept),
             out_specs=VM,
             scratch_shapes=[
-                pltpu.VMEM((8, 2 * MOST, 16 * width + 128), BF),
+                pltpu.VMEM((len(xs), 2 * MOST, 16 * width + 128), BF),
                 pltpu.VMEM((2, 8, 2, rows, 2 * wide), BF),
                 pltpu.SemaphoreType.DMA((8,)),
                 pltpu.SemaphoreType.DMA((5, 8)),
             ],
             compiler_params=pltpu.CompilerParams(vmem_limit_bytes=58 << 20),
             cost_estimate=pl.CostEstimate(
-                flops=16 * MOST * 16 * width * 8 * wide, bytes_accessed=12 << 20, transcendentals=16 * MOST * 2 * wide
+                flops=2 * len(xs) * MOST * 16 * width * 8 * wide, bytes_accessed=12 << 20, transcendentals=4 * len(xs) * MOST * wide
             ),
             name="expert",
-        )(pos, *held, *other, *ws)
-
+        )(pos, *xs, *ws, *kept)
+
+    act_a = expert(0, 4, held, ws_a)
+    act_a, left_b, right_b, *rest = barrier((act_a, left_b, right_b, *held[1:]))
+    other += [ring(h, "c", 2, 1) for h in rest]
+    act_a = expert(4, 8, other, ws_a, (act_a,))
     def give_back(act):
         back = lax.all_to_all(act.reshape(16, 2 * MOST, wide), ("y", "c", "xl"), split_axis=0, concat_axis=0, tiled=True)
         return back.reshape(4, 2, 2, 2 * MOST, wide)
 
-    act_a = expert(own_a, left_a, right_a, *far_a)
-    left_b, right_b, act_a = barrier((left_b, right_b, act_a))
     back_a = give_back(act_a)
-    back_b = give_back(expert(own_b, left_b, right_b, *far(left_b, right_b)))
+    back_b = give_back(expert(0, 8, held + other, [own_b, left_b, right_b, *far(left_b, right_b)]))
     out = pl.pallas_call(
         combine_kernel,
         out_shape=jax.ShapeDtypeStruct((steps, n, 1024), BF),

time: 162 us -> 175 us (1.080)
  waiting for transfers between devices: 34.9 us -> 54.8 us
  starting transfers between devices: 69.8 us -> 56.8 us
  Pallas kernels: 29.1 us -> 33.9 us
  local copies, waits for them, and re-layouts: 7.95 us -> 10 us
    ppermute x24, waiting for transfers between devices: 31.3 us -> 49.6 us  [ring(): return lax.ppermute(x, axis, [(i, (i + step) % size) for i in range(size)])]
    ppermute x24, starting transfers between devices: 54.4 us -> 42.1 us  [ring(): return lax.ppermute(x, axis, [(i, (i + step) % size) for i in range(size)])]
    pallas_call x2 -> x3, Pallas kernels: 20.7 us -> 25.6 us  [expert(): pl.pallas_call(functools.partial(expert_kernel, first, last), out_shape=j...]
    unnamed x22 -> x28, local copies, waits for them, and re-layouts: 2.76 us -> 4.05 us
  transfers between devices with their start and end apart: 27 -> 27, of which waited for: 10 -> 8; matrix products, arithmetic and copies ran while one was open for 2% -> 2% of each run, Pallas kernels for 17% -> 19%
where the time goes in v15:
time: 175 us; the launch traced here: 174 us
  starting transfers between devices  56.8 us (32%)
  waiting for transfers between devices  54.8 us (31%)
  Pallas kernels  33.9 us (19%)
  blocking collectives  17.6 us (10%)
  local copies, waits for them, and re-layouts  10 us (6%)
    ppermute x24, waiting for transfers between devices, ring(): return lax.ppermute(x, axis, [(i, (i + step) % size) for i in range(size)])  49.6 us
    ppermute x24, starting transfers between devices, ring(): return lax.ppermute(x, axis, [(i, (i + step) % size) for i in range(size)])  42.1 us
    pallas_call x3, Pallas kernels, expert(): pl.pallas_call(functools.partial(expert_kernel, first, last), out_shape=j...  25.6 us
    all_to_all x1, blocking collectives, give_back(): lax.all_to_all(act.reshape(16, 2 * MOST, wide), ('y', 'c', 'xl'), split_a...  17.6 us
    all_to_all x2, starting transfers between devices, exchange(): return lax.all_to_all(x, 'z', split_axis=0, concat_axis=0, tiled=True)  10 us
    all_to_all x2, waiting for transfers between devices, exchange(): return lax.all_to_all(x, 'z', split_axis=0, concat_axis=0, tiled=True)  5.21 us
    all_to_all x1, starting transfers between devices, give_back(): lax.all_to_all(act.reshape(16, 2 * MOST, wide), ('y', 'c', 'xl'), split_a...  4.66 us
    unnamed x28, local copies, waits for them, and re-layouts  4.05 us
  transfers between devices with their start and end apart: 27, of which 8 were waited for; matrix products, arithmetic and copies ran while one was open for 2% of the time, Pallas kernels for 19%

profile of v15, /device:TPU:1, one launch (start us, length us, event | category | flops | bytes accessed | tf_op | source)
XLA Modules:
  0.0 174.4 jit_solution(15006966268025520839)
XLA Ops:
  0.0 0.9 dynamic-slice_bitcast_fusion
  0.9 2.0 %collective-permute-start = (bf16[2,192,128]{2,1,0:T(8,128)(2,1)S(1)}, bf16[2,192,128]{2,1,0:T(8,128)(2,1)S(1)}, u32[]{:S(2)}, u32[]{:S(2)}) collective-permute-start(bf16[2,192,128]{2,1,0:T(8,128)(2,1)S(1)} %dynamic-slice_bitcast_fusion), channel_id=1, source_target_pairs={{0,1},{1,0},{2,3},{3,2},{4,5},{5,4},{6,7},{7,6},{8,9},{9,8},{10,11... | collective-permute-start | bytes 294920 | tf_op jit(solution)/shard_map/ppermute | solution.py:19
  2.9 2.0 %collective-permute-done = bf16[2,192,128]{2,1,0:T(8,128)(2,1)S(1)} collective-permute-done((bf16[2,192,128]{2,1,0:T(8,128)(2,1)S(1)}, bf16[2,192,128]{2,1,0:T(8,128)(2,1)S(1)}, u32[]{:S(2)}, u32[]{:S(2)}) %collective-permute-start) | collective-permute-done | bytes 98336 | tf_op jit(solution)/shard_map/ppermute | solution.py:19
  4.9 0.9 bitcast_select_fusion.1
  5.9 2.0 %collective-permute-start.2 = (bf16[2,384,128]{2,1,0:T(8,128)(2,1)S(1)}, bf16[2,384,128]{2,1,0:T(8,128)(2,1)S(1)}, u32[]{:S(2)}, u32[]{:S(2)}) collective-permute-start(bf16[2,384,128]{2,1,0:T(8,128)(2,1)S(1)} %pad_maximum_fusion.refs_0_), channel_id=1, source_target_pairs={{0,2},{2,4},{4,6},{6,8},{8,10},{10,12},{12,14},{14,0},{1,3},{3,5},... | collective-permute-start | bytes 589832 | tf_op jit(solution)/shard_map/ppermute | solution.py:19
  7.8 4.0 %collective-permute-start.1 = (bf16[2,384,128]{2,1,0:T(8,128)(2,1)S(1)}, bf16[2,384,128]{2,1,0:T(8,128)(2,1)S(1)}, u32[]{:S(2)}, u32[]{:S(2)}) collective-permute-start(bf16[2,384,128]{2,1,0:T(8,128)(2,1)S(1)} %pad_maximum_fusion.refs_0_), channel_id=1, source_target_pairs={{0,14},{2,0},{4,2},{6,4},{8,6},{10,8},{12,10},{14,12},{1,15},{3,1}... | collective-permute-start | bytes 589832 | tf_op jit(solution)/shard_map/ppermute | solution.py:19
  11.9 3.3 %collective-permute-done.2.refs_7_ = bf16[2,384,128]{2,1,0:T(8,128)(2,1)S(1)} collective-permute-done((bf16[2,384,128]{2,1,0:T(8,128)(2,1)S(1)}, bf16[2,384,128]{2,1,0:T(8,128)(2,1)S(1)}, u32[]{:S(2)}, u32[]{:S(2)}) %collective-permute-start.2) | collective-permute-done | bytes 196640 | tf_op jit(solution)/shard_map/ppermute | solution.py:19
  15.2 2.7 %collective-permute-start.4 = (bf16[2,384,128]{2,1,0:T(8,128)(2,1)S(1)}, bf16[2,384,128]{2,1,0:T(8,128)(2,1)S(1)}, u32[]{:S(2)}, u32[]{:S(2)}) collective-permute-start(bf16[2,384,128]{2,1,0:T(8,128)(2,1)S(1)} %collective-permute-done.1.refs_1_), channel_id=1, source_target_pairs={{0,14},{2,0},{4,2},{6,4},{8,6},{10,8},{12,10},{14,12},{1,15},{3,1}... | collective-permute-start | bytes 589832 | tf_op jit(solution)/shard_map/ppermute | solution.py:19
  17.9 0.6 stack.23.pos.refs_0_
  18.5 3.6 %columns.1 = (bf16[8,192,256]{2,1,0:T(8,128)(2,1)}, bf16[8,192,256]{2,1,0:T(8,128)(2,1)}) custom-call(s32[5]{0:T(128)} %stack.23.pos.refs_0_, bf16[1,192,4096]{2,1,0:T(8,128)(2,1)} %gate.1, bf16[1,192,4096]{2,1,0:T(8,128)(2,1)} %up.1), custom_call_target="tpu_custom_call" | custom-call | tf_op jit(solution)/shard_map/columns/pallas_call | solution.py:151
  22.2 2.7 %collective-permute-start.5 = (bf16[2,384,128]{2,1,0:T(8,128)(2,1)S(1)}, bf16[2,384,128]{2,1,0:T(8,128)(2,1)S(1)}, u32[]{:S(2)}, u32[]{:S(2)}) collective-permute-start(bf16[2,384,128]{2,1,0:T(8,128)(2,1)S(1)} %collective-permute-done.4.refs_2_), channel_id=1, source_target_pairs={{0,14},{2,0},{4,2},{6,4},{8,6},{10,8},{12,10},{14,12},{1,15},{3,1}... | collective-permute-start | bytes 589832 | tf_op jit(solution)/shard_map/ppermute | solution.py:19
  24.8 3.1 %collective-permute-done.6.refs_5_ = bf16[2,384,128]{2,1,0:T(8,128)(2,1)S(1)} collective-permute-done((bf16[2,384,128]{2,1,0:T(8,128)(2,1)S(1)}, bf16[2,384,128]{2,1,0:T(8,128)(2,1)S(1)}, u32[]{:S(2)}, u32[]{:S(2)}) %collective-permute-start.6) | collective-permute-done | bytes 196640 | tf_op jit(solution)/shard_map/ppermute | solution.py:19
  28.0 2.7 %collective-permute-start.8 = (bf16[1,384,128]{2,1,0:T(8,128)(2,1)S(1)}, bf16[1,384,128]{2,1,0:T(8,128)(2,1)S(1)}, u32[]{:S(2)}, u32[]{:S(2)}) collective-permute-start(bf16[1,384,128]{2,1,0:T(8,128)(2,1)S(1)} %slice.25), channel_id=1, source_target_pairs={{0,14},{2,0},{4,2},{6,4},{8,6},{10,8},{12,10},{14,12},{1,15},{3,1}... | collective-permute-start | bytes 294920 | tf_op jit(solution)/shard_map/ppermute | solution.py:19
  30.7 1.9 %collective-permute-done.7 = bf16[1,384,128]{2,1,0:T(8,128)(2,1)S(1)} collective-permute-done((bf16[1,384,128]{2,1,0:T(8,128)(2,1)S(1)}, bf16[1,384,128]{2,1,0:T(8,128)(2,1)S(1)}, u32[]{:S(2)}, u32[]{:S(2)}) %collective-permute-start.7) | collective-permute-done | bytes 98336 | tf_op jit(solution)/shard_map/ppermute | solution.py:19
  32.7 5.8 %all-to-all-start = ((bf16[8,192,256]{2,1,0:T(8,128)(2,1)}), bf16[8,192,256]{2,1,0:T(8,128)(2,1)}, u32[]{:S(2)}, u32[]{:S(2)}) async-start(bf16[8,192,256]{2,1,0:T(8,128)(2,1)} %get-tuple-element.53), calls=%async_computation | async-start | bytes 1572864 | tf_op jit(solution)/shard_map/all_to_all | solution.py:162
  38.5 3.3 %dispatch.1 = (bf16[160,3200]{1,0:T(8,128)(2,1)S(1)}, bf16[160,3200]{1,0:T(8,128)(2,1)}, bf16[160,3200]{1,0:T(8,128)(2,1)S(1)}, bf16[160,3200]{1,0:T(8,128)(2,1)}) custom-call(s32[5]{0:T(128)S(1)} %copy-done.1, f32[4,4,128]{2,1,0:T(4,128)S(1)} %maximum_bitcast_fusion.meta, bf16[2,384,128]{2,1,0:T(8,128)(2,1)S(1)} %pad_maximum_fusion.refs_0_, ...), custom_call_target="tpu_custom_call" | custom-call | tf_op jit(solution)/shard_map/dispatch/pallas_call | solution.py:179
  41.9 6.2 %collective-permute-start.9 = (bf16[160,3200]{1,0:T(8,128)(2,1)S(1)}, bf16[160,3200]{1,0:T(8,128)(2,1)}, u32[]{:S(2)}, u32[]{:S(2)}) collective-permute-start(bf16[160,3200]{1,0:T(8,128)(2,1)S(1)} %get-tuple-element.48.refs_1_), channel_id=1, source_target_pairs={{0,16},{16,0},{1,17},{17,1},{2,18},{18,2},{3,19},{19,3},{4,20},{20... | collective-permute-start | bytes 3072008 | tf_op jit(solution)/shard_map/ppermute | solution.py:19
  48.1 1.3 collective-permute-start.10
  49.4 1.4 collective-permute-start.11
  50.8 5.2 %all-to-all-done.refs_5_ = bf16[8,192,256]{2,1,0:T(8,128)(2,1)} async-done(((bf16[8,192,256]{2,1,0:T(8,128)(2,1)}), bf16[8,192,256]{2,1,0:T(8,128)(2,1)}, u32[]{:S(2)}, u32[]{:S(2)}) %all-to-all-start) | async-done | bytes 786464 | tf_op jit(solution)/shard_map/all_to_all | solution.py:162
  56.1 4.2 %all-to-all-start.1 = ((bf16[8,192,256]{2,1,0:T(8,128)(2,1)}), bf16[8,192,256]{2,1,0:T(8,128)(2,1)}, u32[]{:S(2)}, u32[]{:S(2)}) async-start(bf16[8,192,256]{2,1,0:T(8,128)(2,1)} %get-tuple-element.54), calls=%async_computation.1 | async-start | bytes 1572864 | tf_op jit(solution)/shard_map/all_to_all | solution.py:162
  60.3 1.3 collective-permute-start.13
  61.6 1.5 collective-permute-start.14
  63.1 10.9 %collective-permute-done.10.refs_2_ = bf16[160,3200]{1,0:T(8,128)(2,1)} collective-permute-done((bf16[160,3200]{1,0:T(8,128)(2,1)}, bf16[160,3200]{1,0:T(8,128)(2,1)}, u32[]{:S(2)}, u32[]{:S(2)}) %collective-permute-start.10) | collective-permute-done | bytes 1024032 | tf_op jit(solution)/shard_map/ppermute | solution.py:19
  74.0 2.3 %collective-permute-start.12 = (bf16[160,3200]{1,0:T(8,128)(2,1)S(1)}, bf16[160,3200]{1,0:T(8,128)(2,1)S(1)}, u32[]{:S(2)}, u32[]{:S(2)}) collective-permute-start(bf16[160,3200]{1,0:T(8,128)(2,1)S(1)} %get-tuple-element.55), channel_id=1, source_target_pairs={{0,64},{32,96},{64,0},{96,32},{1,65},{33,97},{65,1},{97,33},{2,66}... | collective-permute-start | bytes 3072008 | tf_op jit(solution)/shard_map/ppermute | solution.py:19
  76.3 1.3 collective-permute-start.15
  77.7 1.5 collective-permute-start.16
  79.2 19.7 %collective-permute-done.12.refs_3_ = bf16[160,3200]{1,0:T(8,128)(2,1)S(1)} collective-permute-done((bf16[160,3200]{1,0:T(8,128)(2,1)S(1)}, bf16[160,3200]{1,0:T(8,128)(2,1)S(1)}, u32[]{:S(2)}, u32[]{:S(2)}) %collective-permute-start.12) | collective-permute-done | bytes 1024032 | tf_op jit(solution)/shard_map/ppermute | solution.py:19
  99.0 1.0 copy-done.5
  100.0 1.2 collective-permute-start.17
  101.2 1.5 collective-permute-start.18
  102.7 7.5 %expert.3.refs_10_ = bf16[4,2,2,160,128]{4,3,2,1,0:T(8,128)(2,1)} custom-call(s32[5]{0:T(128)} %stack.23.pos.refs_0_, bf16[160,3200]{1,0:T(8,128)(2,1)} %copy-done, bf16[160,3200]{1,0:T(8,128)(2,1)} %collective-permute-done.10.refs_2_, bf16[160,3200]{1,0:T(8,128)(2,1)} %copy-done.5, bf16[160,3200]{1,0:T(8,128)(2,1)} %collective-permute-done.11.refs_4_, ...), custom_call_target="tpu_custom_call" | custom-call | flops 2013265920 | bytes 12582912 | tf_op jit(solution)/shard_map/expert/pallas_call | solution.py:202
  110.2 8.6 %collective-permute-done.17.refs_10_ = bf16[8,192,256]{2,1,0:T(8,128)(2,1)S(1)} collective-permute-done((bf16[8,192,256]{2,1,0:T(8,128)(2,1)}, bf16[8,192,256]{2,1,0:T(8,128)(2,1)S(1)}, u32[]{:S(2)}, u32[]{:S(2)}) %collective-permute-start.17) | collective-permute-done | bytes 786464 | tf_op jit(solution)/shard_map/ppermute | solution.py:19
  118.9 2.6 %collective-permute-start.19 = (bf16[160,3200]{1,0:T(8,128)(2,1)}, bf16[160,3200]{1,0:T(8,128)(2,1)S(1)}, u32[]{:S(2)}, u32[]{:S(2)}) collective-permute-start(bf16[160,3200]{1,0:T(8,128)(2,1)} %collective-permute-done.10.refs_2_), channel_id=1, source_target_pairs={{0,16},{16,0},{1,17},{17,1},{2,18},{18,2},{3,19},{19,3},{4,20},{20... | collective-permute-start | bytes 3072008 | tf_op jit(solution)/shard_map/ppermute | solution.py:19
  121.5 0.9 collective-permute-start.20
  122.3 1.0 slice.22
  123.4 1.0 collective-permute-start.22
  124.3 1.8 %slice.23 = bf16[4,192,256]{2,1,0:T(8,128)(2,1)} slice(bf16[8,192,256]{2,1,0:T(8,128)(2,1)} %collective-permute-done.18.refs_11_), slice={[4:8], [0:192], [0:256]} | slice | bytes 786432 | tf_op jit(solution)/shard_map/slice | solution.py:168
  126.1 1.8 %collective-permute-start.23 = (bf16[4,192,256]{2,1,0:T(8,128)(2,1)}, bf16[4,192,256]{2,1,0:T(8,128)(2,1)}, u32[]{:S(2)}, u32[]{:S(2)}) collective-permute-start(bf16[4,192,256]{2,1,0:T(8,128)(2,1)} %slice.23), channel_id=1, source_target_pairs={{0,129},{1,0},{128,1},{129,128},{2,131},{3,2},{130,3},{131,130},{4... | collective-permute-start | bytes 1179656 | tf_op jit(solution)/shard_map/ppermute | solution.py:19
  127.9 0.9 copy-done.7
  129.2 1.0 copy-done.9
  130.2 7.7 %expert.4 = bf16[4,2,2,160,128]{4,3,2,1,0:T(8,128)(2,1)} custom-call(s32[5]{0:T(128)} %stack.23.pos.refs_0_, bf16[160,3200]{1,0:T(8,128)(2,1)} %collective-permute-done.9.refs_1_.refs_5_, bf16[160,3200]{1,0:T(8,128)(2,1)} %copy-done.7, bf16[160,3200]{1,0:T(8,128)(2,1)} %copy-done.8, bf16[160,3200]{1,0:T(8,128)(2,1)} %copy-done.9, ...), custom_call_target="tpu_custom_call" | custom-call | flops 2013265920 | bytes 12582912 | tf_op jit(solution)/shard_map/expert/pallas_call | solution.py:202
  138.0 4.7 %all-to-all-start.2 = ((bf16[16,160,128]{2,1,0:T(8,128)(2,1)}), bf16[16,160,128]{2,1,0:T(8,128)(2,1)S(1)}, u32[]{:S(2)}, u32[]{:S(2)}) async-start(bf16[16,160,128]{2,1,0:T(8,128)(2,1)} %bitcast.21), calls=%async_computation.2 | async-start | bytes 1310720 | tf_op jit(solution)/shard_map/all_to_all | solution.py:225
  142.6 0.8 copy-done.13
  143.4 10.3 %expert.5 = bf16[4,2,2,160,128]{4,3,2,1,0:T(8,128)(2,1)} custom-call(s32[5]{0:T(128)} %stack.23.pos.refs_0_, bf16[160,3200]{1,0:T(8,128)(2,1)} %copy-done, bf16[160,3200]{1,0:T(8,128)(2,1)} %collective-permute-done.10.refs_2_, bf16[160,3200]{1,0:T(8,128)(2,1)} %copy-done.5, bf16[160,3200]{1,0:T(8,128)(2,1)} %collective-permute-done.11.refs_4_, ...), custom_call_target="tpu_custom_call" | custom-call | flops 4026531840 | bytes 12582912 | tf_op jit(solution)/shard_map/expert/pallas_call | solution.py:202
  153.7 17.6 %all_to_all.20 = bf16[16,160,128]{2,1,0:T(8,128)(2,1)S(1)} all-to-all(bf16[16,160,128]{2,1,0:T(8,128)(2,1)} %bitcast.22), channel_id=1, replica_groups=mesh['dp'=2,'y'=4,'c'=2,'z'=8,'xl'=2] {'y','c','xl'}, dimensions={0} | all-to-all | bytes 1310720 | tf_op jit(solution)/shard_map/all_to_all | solution.py:225
  171.4 1.4 combine.1
  172.8 1.6 reshape.23
  (55 shorter events, 0.8 us)
Async XLA Ops:
  0.9 4.0 %collective-permute-start = (bf16[2,192,128]{2,1,0:T(8,128)(2,1)S(1)}, bf16[2,192,128]{2,1,0:T(8,128)(2,1)S(1)}, u32[]{:S(2)}, u32[]{:S(2)}) collective-permute-start(bf16[2,192,128]{2,1,0:T(8,128)(2,1)S(1)} %dynamic-slice_bitcast_fusion), channel_id=1, source_target_pairs={{0,1},{1,0},{2,3},{3,2},{4,5},{5,4},{6,7},{7,6},{8,9},{9,8},{10,11... | collective-permute-start | bytes 294920 | tf_op jit(solution)/shard_map/ppermute | solution.py:19
  5.9 9.3 %collective-permute-start.2 = (bf16[2,384,128]{2,1,0:T(8,128)(2,1)S(1)}, bf16[2,384,128]{2,1,0:T(8,128)(2,1)S(1)}, u32[]{:S(2)}, u32[]{:S(2)}) collective-permute-start(bf16[2,384,128]{2,1,0:T(8,128)(2,1)S(1)} %pad_maximum_fusion.refs_0_), channel_id=1, source_target_pairs={{0,2},{2,4},{4,6},{6,8},{8,10},{10,12},{12,14},{14,0},{1,3},{3,5},... | collective-permute-start | bytes 589832 | tf_op jit(solution)/shard_map/ppermute | solution.py:19
  7.8 7.3 %collective-permute-start.1 = (bf16[2,384,128]{2,1,0:T(8,128)(2,1)S(1)}, bf16[2,384,128]{2,1,0:T(8,128)(2,1)S(1)}, u32[]{:S(2)}, u32[]{:S(2)}) collective-permute-start(bf16[2,384,128]{2,1,0:T(8,128)(2,1)S(1)} %pad_maximum_fusion.refs_0_), channel_id=1, source_target_pairs={{0,14},{2,0},{4,2},{6,4},{8,6},{10,8},{12,10},{14,12},{1,15},{3,1}... | collective-permute-start | bytes 589832 | tf_op jit(solution)/shard_map/ppermute | solution.py:19
  15.2 6.9 %collective-permute-start.3 = (bf16[2,384,128]{2,1,0:T(8,128)(2,1)S(1)}, bf16[2,384,128]{2,1,0:T(8,128)(2,1)S(1)}, u32[]{:S(2)}, u32[]{:S(2)}) collective-permute-start(bf16[2,384,128]{2,1,0:T(8,128)(2,1)S(1)} %collective-permute-done.2.refs_7_), channel_id=1, source_target_pairs={{0,2},{2,4},{4,6},{6,8},{8,10},{10,12},{12,14},{14,0},{1,3},{3,5},... | collective-permute-start | bytes 589832 | tf_op jit(solution)/shard_map/ppermute | solution.py:19
  15.2 6.9 %collective-permute-start.4 = (bf16[2,384,128]{2,1,0:T(8,128)(2,1)S(1)}, bf16[2,384,128]{2,1,0:T(8,128)(2,1)S(1)}, u32[]{:S(2)}, u32[]{:S(2)}) collective-permute-start(bf16[2,384,128]{2,1,0:T(8,128)(2,1)S(1)} %collective-permute-done.1.refs_1_), channel_id=1, source_target_pairs={{0,14},{2,0},{4,2},{6,4},{8,6},{10,8},{12,10},{14,12},{1,15},{3,1}... | collective-permute-start | bytes 589832 | tf_op jit(solution)/shard_map/ppermute | solution.py:19
  22.0 16.4 %copy-start.11 = (s32[4,128,2]{1,2,0:T(2,128)S(1)}, s32[4,128,2]{1,2,0:T(2,128)}, u32[]{:S(2)}) copy-start(s32[4,128,2]{1,2,0:T(2,128)} %param.6) | copy-start | bytes 12292
  22.0 16.4 %copy-start.12 = (f32[4,128,2]{1,2,0:T(2,128)S(1)}, f32[4,128,2]{1,2,0:T(2,128)}, u32[]{:S(2)}) copy-start(f32[4,128,2]{1,2,0:T(2,128)} %param.7) | copy-start | bytes 12292
  22.0 16.5 %copy-start.1 = (s32[5]{0:T(128)S(1)}, s32[5]{0:T(128)}, u32[]{:S(2)}) copy-start(s32[5]{0:T(128)} %stack.23.pos.refs_0_) | copy-start | bytes 64
  22.1 5.8 %collective-permute-start.6 = (bf16[2,384,128]{2,1,0:T(8,128)(2,1)S(1)}, bf16[2,384,128]{2,1,0:T(8,128)(2,1)S(1)}, u32[]{:S(2)}, u32[]{:S(2)}) collective-permute-start(bf16[2,384,128]{2,1,0:T(8,128)(2,1)S(1)} %collective-permute-done.3.refs_6_), channel_id=1, source_target_pairs={{0,2},{2,4},{4,6},{6,8},{8,10},{10,12},{12,14},{14,0},{1,3},{3,5},... | collective-permute-start | bytes 589832 | tf_op jit(solution)/shard_map/ppermute | solution.py:19
  22.2 5.8 %collective-permute-start.5 = (bf16[2,384,128]{2,1,0:T(8,128)(2,1)S(1)}, bf16[2,384,128]{2,1,0:T(8,128)(2,1)S(1)}, u32[]{:S(2)}, u32[]{:S(2)}) collective-permute-start(bf16[2,384,128]{2,1,0:T(8,128)(2,1)S(1)} %collective-permute-done.4.refs_2_), channel_id=1, source_target_pairs={{0,14},{2,0},{4,2},{6,4},{8,6},{10,8},{12,10},{14,12},{1,15},{3,1}... | collective-permute-start | bytes 589832 | tf_op jit(solution)/shard_map/ppermute | solution.py:19
  27.9 4.8 %collective-permute-start.7 = (bf16[1,384,128]{2,1,0:T(8,128)(2,1)S(1)}, bf16[1,384,128]{2,1,0:T(8,128)(2,1)S(1)}, u32[]{:S(2)}, u32[]{:S(2)}) collective-permute-start(bf16[1,384,128]{2,1,0:T(8,128)(2,1)S(1)} %slice.24), channel_id=1, source_target_pairs={{0,2},{2,4},{4,6},{6,8},{8,10},{10,12},{12,14},{14,0},{1,3},{3,5},... | collective-permute-start | bytes 294920 | tf_op jit(solution)/shard_map/ppermute | solution.py:19
  28.0 4.6 %collective-permute-start.8 = (bf16[1,384,128]{2,1,0:T(8,128)(2,1)S(1)}, bf16[1,384,128]{2,1,0:T(8,128)(2,1)S(1)}, u32[]{:S(2)}, u32[]{:S(2)}) collective-permute-start(bf16[1,384,128]{2,1,0:T(8,128)(2,1)S(1)} %slice.25), channel_id=1, source_target_pairs={{0,14},{2,0},{4,2},{6,4},{8,6},{10,8},{12,10},{14,12},{1,15},{3,1}... | collective-permute-start | bytes 294920 | tf_op jit(solution)/shard_map/ppermute | solution.py:19
  32.7 23.4 %all-to-all-start = ((bf16[8,192,256]{2,1,0:T(8,128)(2,1)}), bf16[8,192,256]{2,1,0:T(8,128)(2,1)}, u32[]{:S(2)}, u32[]{:S(2)}) async-start(bf16[8,192,256]{2,1,0:T(8,128)(2,1)} %get-tuple-element.53), calls=%async_computation | async-start | bytes 1572864 | tf_op jit(solution)/shard_map/all_to_all | solution.py:162
  41.9 35.8 %copy-start = (bf16[160,3200]{1,0:T(8,128)(2,1)}, bf16[160,3200]{1,0:T(8,128)(2,1)S(1)}, u32[]{:S(2)}) copy-start(bf16[160,3200]{1,0:T(8,128)(2,1)S(1)} %get-tuple-element.48.refs_1_) | copy-start | bytes 3072004
  41.9 21.2 %collective-permute-start.9 = (bf16[160,3200]{1,0:T(8,128)(2,1)S(1)}, bf16[160,3200]{1,0:T(8,128)(2,1)}, u32[]{:S(2)}, u32[]{:S(2)}) collective-permute-start(bf16[160,3200]{1,0:T(8,128)(2,1)S(1)} %get-tuple-element.48.refs_1_), channel_id=1, source_target_pairs={{0,16},{16,0},{1,17},{17,1},{2,18},{18,2},{3,19},{19,3},{4,20},{20... | collective-permute-start | bytes 3072008 | tf_op jit(solution)/shard_map/ppermute | solution.py:19
  48.1 25.9 %collective-permute-start.10 = (bf16[160,3200]{1,0:T(8,128)(2,1)}, bf16[160,3200]{1,0:T(8,128)(2,1)}, u32[]{:S(2)}, u32[]{:S(2)}) collective-permute-start(bf16[160,3200]{1,0:T(8,128)(2,1)} %get-tuple-element.49), channel_id=1, source_target_pairs={{0,32},{32,64},{64,96},{96,0},{1,33},{33,65},{65,97},{97,1},{2,34}... | collective-permute-start | bytes 3072008 | tf_op jit(solution)/shard_map/ppermute | solution.py:19
  49.4 24.6 %collective-permute-start.11 = (bf16[160,3200]{1,0:T(8,128)(2,1)}, bf16[160,3200]{1,0:T(8,128)(2,1)}, u32[]{:S(2)}, u32[]{:S(2)}) collective-permute-start(bf16[160,3200]{1,0:T(8,128)(2,1)} %get-tuple-element.50), channel_id=1, source_target_pairs={{0,96},{32,0},{64,32},{96,64},{1,97},{33,1},{65,33},{97,65},{2,98}... | collective-permute-start | bytes 3072008 | tf_op jit(solution)/shard_map/ppermute | solution.py:19
  56.1 43.9 %all-to-all-start.1 = ((bf16[8,192,256]{2,1,0:T(8,128)(2,1)}), bf16[8,192,256]{2,1,0:T(8,128)(2,1)}, u32[]{:S(2)}, u32[]{:S(2)}) async-start(bf16[8,192,256]{2,1,0:T(8,128)(2,1)} %get-tuple-element.54), calls=%async_computation.1 | async-start | bytes 1572864 | tf_op jit(solution)/shard_map/all_to_all | solution.py:162
  60.3 16.0 %collective-permute-start.13 = (bf16[8,192,256]{2,1,0:T(8,128)(2,1)}, bf16[8,192,256]{2,1,0:T(8,128)(2,1)S(1)}, u32[]{:S(2)}, u32[]{:S(2)}) collective-permute-start(bf16[8,192,256]{2,1,0:T(8,128)(2,1)} %all-to-all-done.refs_5_), channel_id=1, source_target_pairs={{0,1},{1,128},{128,129},{129,0},{2,3},{3,130},{130,131},{131,2},{4... | collective-permute-start | bytes 2359304 | tf_op jit(solution)/shard_map/ppermute | solution.py:19
  61.6 14.7 %collective-permute-start.14 = (bf16[8,192,256]{2,1,0:T(8,128)(2,1)}, bf16[8,192,256]{2,1,0:T(8,128)(2,1)S(1)}, u32[]{:S(2)}, u32[]{:S(2)}) collective-permute-start(bf16[8,192,256]{2,1,0:T(8,128)(2,1)} %all-to-all-done.refs_5_), channel_id=1, source_target_pairs={{0,129},{1,0},{128,1},{129,128},{2,131},{3,2},{130,3},{131,130},{4... | collective-permute-start | bytes 2359304 | tf_op jit(solution)/shard_map/ppermute | solution.py:19
  74.0 24.9 %collective-permute-start.12 = (bf16[160,3200]{1,0:T(8,128)(2,1)S(1)}, bf16[160,3200]{1,0:T(8,128)(2,1)S(1)}, u32[]{:S(2)}, u32[]{:S(2)}) collective-permute-start(bf16[160,3200]{1,0:T(8,128)(2,1)S(1)} %get-tuple-element.55), channel_id=1, source_target_pairs={{0,64},{32,96},{64,0},{96,32},{1,65},{33,97},{65,1},{97,33},{2,66}... | collective-permute-start | bytes 3072008 | tf_op jit(solution)/shard_map/ppermute | solution.py:19
  76.3 26.4 %copy-start.2 = (bf16[8,192,256]{2,1,0:T(8,128)(2,1)}, bf16[8,192,256]{2,1,0:T(8,128)(2,1)S(1)}, u32[]{:S(2)}) copy-start(bf16[8,192,256]{2,1,0:T(8,128)(2,1)S(1)} %collective-permute-done.13.refs_6_) | copy-start | bytes 2359300
  76.3 22.7 %copy-start.3 = (bf16[8,192,256]{2,1,0:T(8,128)(2,1)}, bf16[8,192,256]{2,1,0:T(8,128)(2,1)S(1)}, u32[]{:S(2)}) copy-start(bf16[8,192,256]{2,1,0:T(8,128)(2,1)S(1)} %collective-permute-done.14.refs_7_) | copy-start | bytes 2359300
  76.3 22.6 %collective-permute-start.15 = (bf16[4,192,256]{2,1,0:T(8,128)(2,1)S(1)}, bf16[4,192,256]{2,1,0:T(8,128)(2,1)S(1)}, u32[]{:S(2)}, u32[]{:S(2)}) collective-permute-start(bf16[4,192,256]{2,1,0:T(8,128)(2,1)S(1)} %slice.20), channel_id=1, source_target_pairs={{0,1},{1,128},{128,129},{129,0},{2,3},{3,130},{130,131},{131,2},{4... | collective-permute-start | bytes 1179656 | tf_op jit(solution)/shard_map/ppermute | solution.py:19
  77.7 22.3 %collective-permute-start.16 = (bf16[4,192,256]{2,1,0:T(8,128)(2,1)S(1)}, bf16[4,192,256]{2,1,0:T(8,128)(2,1)}, u32[]{:S(2)}, u32[]{:S(2)}) collective-permute-start(bf16[4,192,256]{2,1,0:T(8,128)(2,1)S(1)} %slice.21), channel_id=1, source_target_pairs={{0,129},{1,0},{128,1},{129,128},{2,131},{3,2},{130,3},{131,130},{4... | collective-permute-start | bytes 1179656 | tf_op jit(solution)/shard_map/ppermute | solution.py:19
  99.0 1.0 copy-start.5
  100.0 2.8 %copy-start.4 = (bf16[4,192,256]{2,1,0:T(8,128)(2,1)}, bf16[4,192,256]{2,1,0:T(8,128)(2,1)S(1)}, u32[]{:S(2)}) copy-start(bf16[4,192,256]{2,1,0:T(8,128)(2,1)S(1)} %collective-permute-done.15.refs_8_) | copy-start | bytes 1179652
  100.0 21.5 %copy-start.6 = (bf16[160,3200]{1,0:T(8,128)(2,1)S(1)}, bf16[160,3200]{1,0:T(8,128)(2,1)}, u32[]{:S(2)}) copy-start(bf16[160,3200]{1,0:T(8,128)(2,1)} %copy-done.5) | copy-start | bytes 3072004
  100.0 18.9 %collective-permute-start.17 = (bf16[8,192,256]{2,1,0:T(8,128)(2,1)}, bf16[8,192,256]{2,1,0:T(8,128)(2,1)S(1)}, u32[]{:S(2)}, u32[]{:S(2)}) collective-permute-start(bf16[8,192,256]{2,1,0:T(8,128)(2,1)} %all-to-all-done.1.refs_9_), channel_id=1, source_target_pairs={{0,1},{1,128},{128,129},{129,0},{2,3},{3,130},{130,131},{131,2},{4... | collective-permute-start | bytes 2359304 | tf_op jit(solution)/shard_map/ppermute | solution.py:19
  101.2 17.7 %collective-permute-start.18 = (bf16[8,192,256]{2,1,0:T(8,128)(2,1)}, bf16[8,192,256]{2,1,0:T(8,128)(2,1)}, u32[]{:S(2)}, u32[]{:S(2)}) collective-permute-start(bf16[8,192,256]{2,1,0:T(8,128)(2,1)} %all-to-all-done.1.refs_9_), channel_id=1, source_target_pairs={{0,129},{1,0},{128,1},{129,128},{2,131},{3,2},{130,3},{131,130},{4... | collective-permute-start | bytes 2359304 | tf_op jit(solution)/shard_map/ppermute | solution.py:19
  118.9 2.6 %copy-start.10 = (bf16[8,192,256]{2,1,0:T(8,128)(2,1)}, bf16[8,192,256]{2,1,0:T(8,128)(2,1)S(1)}, u32[]{:S(2)}) copy-start(bf16[8,192,256]{2,1,0:T(8,128)(2,1)S(1)} %collective-permute-done.17.refs_10_) | copy-start | bytes 2359300
  118.9 9.0 %collective-permute-start.19 = (bf16[160,3200]{1,0:T(8,128)(2,1)}, bf16[160,3200]{1,0:T(8,128)(2,1)S(1)}, u32[]{:S(2)}, u32[]{:S(2)}) collective-permute-start(bf16[160,3200]{1,0:T(8,128)(2,1)} %collective-permute-done.10.refs_2_), channel_id=1, source_target_pairs={{0,16},{16,0},{1,17},{17,1},{2,18},{18,2},{3,19},{19,3},{4,20},{20... | collective-permute-start | bytes 3072008 | tf_op jit(solution)/shard_map/ppermute | solution.py:19
  121.5 6.4 %collective-permute-start.20 = (bf16[160,3200]{1,0:T(8,128)(2,1)S(1)}, bf16[160,3200]{1,0:T(8,128)(2,1)S(1)}, u32[]{:S(2)}, u32[]{:S(2)}) collective-permute-start(bf16[160,3200]{1,0:T(8,128)(2,1)S(1)} %copy-done.6), channel_id=1, source_target_pairs={{0,16},{16,0},{1,17},{17,1},{2,18},{18,2},{3,19},{19,3},{4,20},{20... | collective-permute-start | bytes 3072008 | tf_op jit(solution)/shard_map/ppermute | solution.py:19
  122.3 5.6 %collective-permute-start.21 = (bf16[160,3200]{1,0:T(8,128)(2,1)}, bf16[160,3200]{1,0:T(8,128)(2,1)S(1)}, u32[]{:S(2)}, u32[]{:S(2)}) collective-permute-start(bf16[160,3200]{1,0:T(8,128)(2,1)} %collective-permute-done.11.refs_4_), channel_id=1, source_target_pairs={{0,16},{16,0},{1,17},{17,1},{2,18},{18,2},{3,19},{19,3},{4,20},{20... | collective-permute-start | bytes 3072008 | tf_op jit(solution)/shard_map/ppermute | solution.py:19
  123.4 19.2 %collective-permute-start.22 = (bf16[4,192,256]{2,1,0:T(8,128)(2,1)S(1)}, bf16[4,192,256]{2,1,0:T(8,128)(2,1)S(1)}, u32[]{:S(2)}, u32[]{:S(2)}) collective-permute-start(bf16[4,192,256]{2,1,0:T(8,128)(2,1)S(1)} %slice.22), channel_id=1, source_target_pairs={{0,1},{1,128},{128,129},{129,0},{2,3},{3,130},{130,131},{131,2},{4... | collective-permute-start | bytes 1179656 | tf_op jit(solution)/shard_map/ppermute | solution.py:19
  126.1 16.5 %collective-permute-start.23 = (bf16[4,192,256]{2,1,0:T(8,128)(2,1)}, bf16[4,192,256]{2,1,0:T(8,128)(2,1)}, u32[]{:S(2)}, u32[]{:S(2)}) collective-permute-start(bf16[4,192,256]{2,1,0:T(8,128)(2,1)} %slice.23), channel_id=1, source_target_pairs={{0,129},{1,0},{128,1},{129,128},{2,131},{3,2},{130,3},{131,130},{4... | collective-permute-start | bytes 1179656 | tf_op jit(solution)/shard_map/ppermute | solution.py:19
  127.9 1.0 copy-start.7
  127.9 1.3 copy-start.8
  129.2 1.0 copy-start.9
  138.0 15.8 %all-to-all-start.2 = ((bf16[16,160,128]{2,1,0:T(8,128)(2,1)}), bf16[16,160,128]{2,1,0:T(8,128)(2,1)S(1)}, u32[]{:S(2)}, u32[]{:S(2)}) async-start(bf16[16,160,128]{2,1,0:T(8,128)(2,1)} %bitcast.21), calls=%async_computation.2 | async-start | bytes 1310720 | tf_op jit(solution)/shard_map/all_to_all | solution.py:225
  142.6 0.8 copy-start.13

commit v16 on v12

--- a/solution.py
+++ b/solution.py
@@ -179,11 +179,12 @@
     opposite = ring(far_rows, "y", 4, 2)
     left_a, right_a, *near = barrier((left_a, right_a, *near))
     far_a = far(left_a, right_a)
-    own_b, opposite, *rest = barrier((own_b, opposite, *near, *far_a))
-    near, far_a = rest[:2], rest[2:]
+    other += [ring(h, "c", 2, 1) for h in near]
+    own_b, opposite, *rest = barrier((own_b, opposite, *far_a, *other))
+    far_a, other = rest[:2], rest[2:]
     left_b, right_b = sides(own_b)
     held = [sent[0], near[0], opposite, near[1]]
-    other += [ring(h, "c", 2, 1) for h in held[1:]]
+    other = [other[0], other[1], ring(opposite, "c", 2, 1), other[2]]
 
     def expert(*ws):
         return pl.pallas_call(

time: 166 us -> 165 us (level)
  waiting for transfers between devices: 38.3 us -> 34.8 us
  starting transfers between devices: 68.4 us -> 71.5 us
    ppermute x24, waiting for transfers between devices: 35 us -> 31.5 us  [ring(): return lax.ppermute(x, axis, [(i, (i + step) % size) for i in range(size)])]
    ppermute x24, starting transfers between devices: 51.6 us -> 54.6 us  [ring(): return lax.ppermute(x, axis, [(i, (i + step) % size) for i in range(size)])]
    unnamed x30 -> x26, local copies, waits for them, and re-layouts: 7.62 us -> 7.57 us
  transfers between devices with their start and end apart: 27 -> 27, of which waited for: 14 -> 11; matrix products, arithmetic and copies ran while one was open for 1% -> 1% of each run, Pallas kernels for 14% -> 14%
where the time goes in v16:
time: 165 us; the launch traced here: 164 us
  starting transfers between devices  71.5 us (43%)
  waiting for transfers between devices  34.8 us (21%)
  Pallas kernels  24.4 us (15%)
  blocking collectives  20.8 us (13%)
  local copies, waits for them, and re-layouts  11.8 us (7%)
    ppermute x24, starting transfers between devices, ring(): return lax.ppermute(x, axis, [(i, (i + step) % size) for i in range(size)])  54.6 us
    ppermute x24, waiting for transfers between devices, ring(): return lax.ppermute(x, axis, [(i, (i + step) % size) for i in range(size)])  31.5 us
    all_to_all x1, blocking collectives, give_back(): lax.all_to_all(act.reshape(16, 2 * MOST, wide), ('y', 'c', 'xl'), split_a...  20.8 us
    pallas_call x2, Pallas kernels, expert(): pl.pallas_call(expert_kernel, out_shape=pltpu.VMEM((4, 2, 2, 2 * MOST, wi...  15.9 us
    all_to_all x2, starting transfers between devices, exchange(): return lax.all_to_all(x, 'z', split_axis=0, concat_axis=0, tiled=True)  9.68 us
    unnamed x26, local copies, waits for them, and re-layouts  7.57 us
    all_to_all x1, starting transfers between devices, give_back(): lax.all_to_all(act.reshape(16, 2 * MOST, wide), ('y', 'c', 'xl'), split_a...  7.27 us
    pallas_call x1, Pallas kernels, body(): pl.pallas_call(dispatch_kernel, out_shape=[pltpu.VMEM((2 * MOST, 16 * wid...  3.67 us
  transfers between devices with their start and end apart: 27, of which 11 were waited for; matrix products, arithmetic and copies ran while one was open for 1% of the time, Pallas kernels for 14%

profile of v16, /device:TPU:1, one launch (start us, length us, event | category | flops | bytes accessed | tf_op | source)
XLA Modules:
  0.0 164.5 jit_solution(7647768396973940563)
XLA Ops:
  0.0 0.9 dynamic-slice_bitcast_fusion
  0.9 2.0 %collective-permute-start = (bf16[2,192,128]{2,1,0:T(8,128)(2,1)S(1)}, bf16[2,192,128]{2,1,0:T(8,128)(2,1)S(1)}, u32[]{:S(2)}, u32[]{:S(2)}) collective-permute-start(bf16[2,192,128]{2,1,0:T(8,128)(2,1)S(1)} %dynamic-slice_bitcast_fusion), channel_id=1, source_target_pairs={{0,1},{1,0},{2,3},{3,2},{4,5},{5,4},{6,7},{7,6},{8,9},{9,8},{10,11... | collective-permute-start | bytes 294920 | tf_op jit(solution)/shard_map/ppermute | solution.py:21
  2.9 2.0 %collective-permute-done = bf16[2,192,128]{2,1,0:T(8,128)(2,1)S(1)} collective-permute-done((bf16[2,192,128]{2,1,0:T(8,128)(2,1)S(1)}, bf16[2,192,128]{2,1,0:T(8,128)(2,1)S(1)}, u32[]{:S(2)}, u32[]{:S(2)}) %collective-permute-start) | collective-permute-done | bytes 98336 | tf_op jit(solution)/shard_map/ppermute | solution.py:21
  4.9 0.9 bitcast_select_fusion.1
  5.9 2.0 %collective-permute-start.1 = (bf16[2,384,128]{2,1,0:T(8,128)(2,1)S(1)}, bf16[2,384,128]{2,1,0:T(8,128)(2,1)S(1)}, u32[]{:S(2)}, u32[]{:S(2)}) collective-permute-start(bf16[2,384,128]{2,1,0:T(8,128)(2,1)S(1)} %pad_maximum_fusion.refs_0_), channel_id=1, source_target_pairs={{0,2},{2,4},{4,6},{6,8},{8,10},{10,12},{12,14},{14,0},{1,3},{3,5},... | collective-permute-start | bytes 589832 | tf_op jit(solution)/shard_map/ppermute | solution.py:21
  7.9 4.0 %collective-permute-start.3 = (bf16[2,384,128]{2,1,0:T(8,128)(2,1)S(1)}, bf16[2,384,128]{2,1,0:T(8,128)(2,1)S(1)}, u32[]{:S(2)}, u32[]{:S(2)}) collective-permute-start(bf16[2,384,128]{2,1,0:T(8,128)(2,1)S(1)} %pad_maximum_fusion.refs_0_), channel_id=1, source_target_pairs={{0,14},{2,0},{4,2},{6,4},{8,6},{10,8},{12,10},{14,12},{1,15},{3,1}... | collective-permute-start | bytes 589832 | tf_op jit(solution)/shard_map/ppermute | solution.py:21
  11.9 3.3 %collective-permute-done.1.refs_7_ = bf16[2,384,128]{2,1,0:T(8,128)(2,1)S(1)} collective-permute-done((bf16[2,384,128]{2,1,0:T(8,128)(2,1)S(1)}, bf16[2,384,128]{2,1,0:T(8,128)(2,1)S(1)}, u32[]{:S(2)}, u32[]{:S(2)}) %collective-permute-start.1) | collective-permute-done | bytes 196640 | tf_op jit(solution)/shard_map/ppermute | solution.py:21
  15.2 2.7 %collective-permute-start.4 = (bf16[2,384,128]{2,1,0:T(8,128)(2,1)S(1)}, bf16[2,384,128]{2,1,0:T(8,128)(2,1)S(1)}, u32[]{:S(2)}, u32[]{:S(2)}) collective-permute-start(bf16[2,384,128]{2,1,0:T(8,128)(2,1)S(1)} %collective-permute-done.3.refs_1_), channel_id=1, source_target_pairs={{0,14},{2,0},{4,2},{6,4},{8,6},{10,8},{12,10},{14,12},{1,15},{3,1}... | collective-permute-start | bytes 589832 | tf_op jit(solution)/shard_map/ppermute | solution.py:21
  17.9 3.4 %columns.1 = (bf16[8,192,256]{2,1,0:T(8,128)(2,1)}, bf16[8,192,256]{2,1,0:T(8,128)(2,1)}) custom-call(s32[5]{0:T(128)S(1)} %stack.23.pos, bf16[1,192,4096]{2,1,0:T(8,128)(2,1)} %gate.1, bf16[1,192,4096]{2,1,0:T(8,128)(2,1)} %up.1), custom_call_target="tpu_custom_call" | custom-call | tf_op jit(solution)/shard_map/columns/pallas_call | solution.py:137
  21.4 2.7 %collective-permute-start.7 = (bf16[2,384,128]{2,1,0:T(8,128)(2,1)S(1)}, bf16[2,384,128]{2,1,0:T(8,128)(2,1)S(1)}, u32[]{:S(2)}, u32[]{:S(2)}) collective-permute-start(bf16[2,384,128]{2,1,0:T(8,128)(2,1)S(1)} %collective-permute-done.4.refs_2_), channel_id=1, source_target_pairs={{0,14},{2,0},{4,2},{6,4},{8,6},{10,8},{12,10},{14,12},{1,15},{3,1}... | collective-permute-start | bytes 589832 | tf_op jit(solution)/shard_map/ppermute | solution.py:21
  24.1 3.1 %collective-permute-done.5.refs_5_ = bf16[2,384,128]{2,1,0:T(8,128)(2,1)S(1)} collective-permute-done((bf16[2,384,128]{2,1,0:T(8,128)(2,1)S(1)}, bf16[2,384,128]{2,1,0:T(8,128)(2,1)S(1)}, u32[]{:S(2)}, u32[]{:S(2)}) %collective-permute-start.5) | collective-permute-done | bytes 196640 | tf_op jit(solution)/shard_map/ppermute | solution.py:21
  27.3 2.7 %collective-permute-start.8 = (bf16[1,384,128]{2,1,0:T(8,128)(2,1)S(1)}, bf16[1,384,128]{2,1,0:T(8,128)(2,1)S(1)}, u32[]{:S(2)}, u32[]{:S(2)}) collective-permute-start(bf16[1,384,128]{2,1,0:T(8,128)(2,1)S(1)} %slice.25), channel_id=1, source_target_pairs={{0,14},{2,0},{4,2},{6,4},{8,6},{10,8},{12,10},{14,12},{1,15},{3,1}... | collective-permute-start | bytes 294920 | tf_op jit(solution)/shard_map/ppermute | solution.py:21
  30.0 1.9 %collective-permute-done.6 = bf16[1,384,128]{2,1,0:T(8,128)(2,1)S(1)} collective-permute-done((bf16[1,384,128]{2,1,0:T(8,128)(2,1)S(1)}, bf16[1,384,128]{2,1,0:T(8,128)(2,1)S(1)}, u32[]{:S(2)}, u32[]{:S(2)}) %collective-permute-start.6) | collective-permute-done | bytes 98336 | tf_op jit(solution)/shard_map/ppermute | solution.py:21
  31.9 5.9 %all-to-all-start = ((bf16[8,192,256]{2,1,0:T(8,128)(2,1)}), bf16[8,192,256]{2,1,0:T(8,128)(2,1)S(1)}, u32[]{:S(2)}, u32[]{:S(2)}) async-start(bf16[8,192,256]{2,1,0:T(8,128)(2,1)} %get-tuple-element.44), calls=%async_computation | async-start | bytes 1572864 | tf_op jit(solution)/shard_map/all_to_all | solution.py:148
  37.9 3.7 %dispatch.1 = (bf16[160,3200]{1,0:T(8,128)(2,1)}, bf16[160,3200]{1,0:T(8,128)(2,1)}, bf16[160,3200]{1,0:T(8,128)(2,1)S(1)}, bf16[160,3200]{1,0:T(8,128)(2,1)}) custom-call(s32[5]{0:T(128)S(1)} %stack.23.pos, f32[4,4,128]{2,1,0:T(4,128)S(1)} %maximum_bitcast_fusion.meta, bf16[2,384,128]{2,1,0:T(8,128)(2,1)S(1)} %pad_maximum_fusion.refs_0_, ...), custom_call_target="tpu_custom_call" | custom-call | tf_op jit(solution)/shard_map/dispatch/pallas_call | solution.py:165
  41.5 1.0 copy-done.4
  42.5 1.3 collective-permute-start.10
  43.8 1.5 collective-permute-start.11
  45.3 6.8 %collective-permute-start.9 = (bf16[160,3200]{1,0:T(8,128)(2,1)}, bf16[160,3200]{1,0:T(8,128)(2,1)}, u32[]{:S(2)}, u32[]{:S(2)}) collective-permute-start(bf16[160,3200]{1,0:T(8,128)(2,1)} %get-tuple-element.49.refs_0_), channel_id=1, source_target_pairs={{0,16},{16,0},{1,17},{17,1},{2,18},{18,2},{3,19},{19,3},{4,20},{20... | collective-permute-start | bytes 3072008 | tf_op jit(solution)/shard_map/ppermute | solution.py:21
  52.1 3.1 %all-to-all-done.refs_8_ = bf16[8,192,256]{2,1,0:T(8,128)(2,1)S(1)} async-done(((bf16[8,192,256]{2,1,0:T(8,128)(2,1)}), bf16[8,192,256]{2,1,0:T(8,128)(2,1)S(1)}, u32[]{:S(2)}, u32[]{:S(2)}) %all-to-all-start) | async-done | bytes 786464 | tf_op jit(solution)/shard_map/all_to_all | solution.py:148
  55.2 1.2 collective-permute-start.13
  56.4 1.5 collective-permute-start.14
  57.9 3.8 %all-to-all-start.1 = ((bf16[8,192,256]{2,1,0:T(8,128)(2,1)}), bf16[8,192,256]{2,1,0:T(8,128)(2,1)S(1)}, u32[]{:S(2)}, u32[]{:S(2)}) async-start(bf16[8,192,256]{2,1,0:T(8,128)(2,1)} %get-tuple-element.45), calls=%async_computation.1 | async-start | bytes 1572864 | tf_op jit(solution)/shard_map/all_to_all | solution.py:148
  62.0 2.4 %collective-permute-start.12 = (bf16[160,3200]{1,0:T(8,128)(2,1)}, bf16[160,3200]{1,0:T(8,128)(2,1)S(1)}, u32[]{:S(2)}, u32[]{:S(2)}) collective-permute-start(bf16[160,3200]{1,0:T(8,128)(2,1)} %copy-done.4), channel_id=1, source_target_pairs={{0,64},{32,96},{64,0},{96,32},{1,65},{33,97},{65,1},{97,33},{2,66}... | collective-permute-start | bytes 3072008 | tf_op jit(solution)/shard_map/ppermute | solution.py:21
  64.5 4.4 %collective-permute-done.13.refs_9_ = bf16[8,192,256]{2,1,0:T(8,128)(2,1)S(1)} collective-permute-done((bf16[8,192,256]{2,1,0:T(8,128)(2,1)S(1)}, bf16[8,192,256]{2,1,0:T(8,128)(2,1)S(1)}, u32[]{:S(2)}, u32[]{:S(2)}) %collective-permute-start.13) | collective-permute-done | bytes 786464 | tf_op jit(solution)/shard_map/ppermute | solution.py:21
  68.9 13.2 %collective-permute-start.17 = (bf16[160,3200]{1,0:T(8,128)(2,1)}, bf16[160,3200]{1,0:T(8,128)(2,1)}, u32[]{:S(2)}, u32[]{:S(2)}) collective-permute-start(bf16[160,3200]{1,0:T(8,128)(2,1)} %collective-permute-done.10.refs_1_), channel_id=1, source_target_pairs={{0,16},{16,0},{1,17},{17,1},{2,18},{18,2},{3,19},{19,3},{4,20},{20... | collective-permute-start | bytes 3072008 | tf_op jit(solution)/shard_map/ppermute | solution.py:21
  82.2 1.3 collective-permute-start.15
  83.5 1.6 collective-permute-start.16
  85.1 8.7 %collective-permute-done.15.refs_11_ = bf16[4,192,256]{2,1,0:T(8,128)(2,1)S(1)} collective-permute-done((bf16[4,192,256]{2,1,0:T(8,128)(2,1)S(1)}, bf16[4,192,256]{2,1,0:T(8,128)(2,1)S(1)}, u32[]{:S(2)}, u32[]{:S(2)}) %collective-permute-start.15) | collective-permute-done | bytes 393248 | tf_op jit(solution)/shard_map/ppermute | solution.py:21
  93.8 0.8 copy-done.5
  94.6 2.1 %collective-permute-start.21 = (bf16[160,3200]{1,0:T(8,128)(2,1)}, bf16[160,3200]{1,0:T(8,128)(2,1)S(1)}, u32[]{:S(2)}, u32[]{:S(2)}) collective-permute-start(bf16[160,3200]{1,0:T(8,128)(2,1)} %copy-done.11), channel_id=1, source_target_pairs={{0,16},{16,0},{1,17},{17,1},{2,18},{18,2},{3,19},{19,3},{4,20},{20... | collective-permute-start | bytes 3072008 | tf_op jit(solution)/shard_map/ppermute | solution.py:21
  96.7 1.2 collective-permute-start.19
  97.9 1.5 collective-permute-start.20
  99.4 0.9 copy-done.12
  100.3 1.0 copy-done.6
  101.3 8.4 %expert.2 = bf16[4,2,2,160,128]{4,3,2,1,0:T(8,128)(2,1)} custom-call(s32[5]{0:T(128)S(1)} %stack.23.pos, bf16[160,3200]{1,0:T(8,128)(2,1)} %get-tuple-element.49.refs_0_, bf16[160,3200]{1,0:T(8,128)(2,1)} %collective-permute-done.10.refs_1_, bf16[160,3200]{1,0:T(8,128)(2,1)} %copy-done.11, bf16[160,3200]{1,0:T(8,128)(2,1)} %collective-permute-done.11.refs_3_, ...), custom_call_target="tpu_custom_call" | custom-call | flops 4026531840 | bytes 12582912 | tf_op jit(solution)/shard_map/expert/pallas_call | solution.py:190
  109.7 7.3 %collective-permute-done.19.refs_9_ = bf16[8,192,256]{2,1,0:T(8,128)(2,1)S(1)} collective-permute-done((bf16[8,192,256]{2,1,0:T(8,128)(2,1)S(1)}, bf16[8,192,256]{2,1,0:T(8,128)(2,1)S(1)}, u32[]{:S(2)}, u32[]{:S(2)}) %collective-permute-start.19) | collective-permute-done | bytes 786464 | tf_op jit(solution)/shard_map/ppermute | solution.py:21
  117.0 0.8 slice.22
  117.8 1.0 copy-done
  119.5 0.8 slice.23
  120.3 2.0 %collective-permute-start.23 = (bf16[4,192,256]{2,1,0:T(8,128)(2,1)}, bf16[4,192,256]{2,1,0:T(8,128)(2,1)S(1)}, u32[]{:S(2)}, u32[]{:S(2)}) collective-permute-start(bf16[4,192,256]{2,1,0:T(8,128)(2,1)} %slice.23), channel_id=1, source_target_pairs={{0,129},{1,0},{128,1},{129,128},{2,131},{3,2},{130,3},{131,130},{4... | collective-permute-start | bytes 1179656 | tf_op jit(solution)/shard_map/ppermute | solution.py:21
  122.3 7.3 %all-to-all-start.2 = ((bf16[16,160,128]{2,1,0:T(8,128)(2,1)}), bf16[16,160,128]{2,1,0:T(8,128)(2,1)S(1)}, u32[]{:S(2)}, u32[]{:S(2)}) async-start(bf16[16,160,128]{2,1,0:T(8,128)(2,1)} %bitcast.11), calls=%async_computation.2 | async-start | bytes 1310720 | tf_op jit(solution)/shard_map/all_to_all | solution.py:208
  130.7 1.1 copy-done.3
  131.9 1.0 copy-done.8
  132.9 7.5 %expert.3 = bf16[4,2,2,160,128]{4,3,2,1,0:T(8,128)(2,1)S(1)} custom-call(s32[5]{0:T(128)S(1)} %stack.23.pos, bf16[160,3200]{1,0:T(8,128)(2,1)} %get-tuple-element.49.refs_0_, bf16[160,3200]{1,0:T(8,128)(2,1)} %collective-permute-done.10.refs_1_, bf16[160,3200]{1,0:T(8,128)(2,1)} %copy-done.11, bf16[160,3200]{1,0:T(8,128)(2,1)} %collective-permute-done.11.refs_3_, ...), custom_call_target="tpu_custom_call" | custom-call | flops 4026531840 | bytes 12582912 | tf_op jit(solution)/shard_map/expert/pallas_call | solution.py:190
  140.6 20.8 %all_to_all.20 = bf16[16,160,128]{2,1,0:T(8,128)(2,1)S(1)} all-to-all(bf16[16,160,128]{2,1,0:T(8,128)(2,1)S(1)} %bitcast.21), channel_id=1, replica_groups=mesh['dp'=2,'y'=4,'c'=2,'z'=8,'xl'=2] {'y','c','xl'}, dimensions={0} | all-to-all | bytes 1310720 | tf_op jit(solution)/shard_map/all_to_all | solution.py:208
  161.4 1.4 combine.1
  162.9 1.6 reshape.23
  (52 shorter events, 2.9 us)
Async XLA Ops:
  0.9 4.0 %collective-permute-start = (bf16[2,192,128]{2,1,0:T(8,128)(2,1)S(1)}, bf16[2,192,128]{2,1,0:T(8,128)(2,1)S(1)}, u32[]{:S(2)}, u32[]{:S(2)}) collective-permute-start(bf16[2,192,128]{2,1,0:T(8,128)(2,1)S(1)} %dynamic-slice_bitcast_fusion), channel_id=1, source_target_pairs={{0,1},{1,0},{2,3},{3,2},{4,5},{5,4},{6,7},{7,6},{8,9},{9,8},{10,11... | collective-permute-start | bytes 294920 | tf_op jit(solution)/shard_map/ppermute | solution.py:21
  5.9 9.3 %collective-permute-start.1 = (bf16[2,384,128]{2,1,0:T(8,128)(2,1)S(1)}, bf16[2,384,128]{2,1,0:T(8,128)(2,1)S(1)}, u32[]{:S(2)}, u32[]{:S(2)}) collective-permute-start(bf16[2,384,128]{2,1,0:T(8,128)(2,1)S(1)} %pad_maximum_fusion.refs_0_), channel_id=1, source_target_pairs={{0,2},{2,4},{4,6},{6,8},{8,10},{10,12},{12,14},{14,0},{1,3},{3,5},... | collective-permute-start | bytes 589832 | tf_op jit(solution)/shard_map/ppermute | solution.py:21
  7.9 7.3 %collective-permute-start.3 = (bf16[2,384,128]{2,1,0:T(8,128)(2,1)S(1)}, bf16[2,384,128]{2,1,0:T(8,128)(2,1)S(1)}, u32[]{:S(2)}, u32[]{:S(2)}) collective-permute-start(bf16[2,384,128]{2,1,0:T(8,128)(2,1)S(1)} %pad_maximum_fusion.refs_0_), channel_id=1, source_target_pairs={{0,14},{2,0},{4,2},{6,4},{8,6},{10,8},{12,10},{14,12},{1,15},{3,1}... | collective-permute-start | bytes 589832 | tf_op jit(solution)/shard_map/ppermute | solution.py:21
  15.2 6.2 %collective-permute-start.2 = (bf16[2,384,128]{2,1,0:T(8,128)(2,1)S(1)}, bf16[2,384,128]{2,1,0:T(8,128)(2,1)S(1)}, u32[]{:S(2)}, u32[]{:S(2)}) collective-permute-start(bf16[2,384,128]{2,1,0:T(8,128)(2,1)S(1)} %collective-permute-done.1.refs_7_), channel_id=1, source_target_pairs={{0,2},{2,4},{4,6},{6,8},{8,10},{10,12},{12,14},{14,0},{1,3},{3,5},... | collective-permute-start | bytes 589832 | tf_op jit(solution)/shard_map/ppermute | solution.py:21
  15.2 6.2 %collective-permute-start.4 = (bf16[2,384,128]{2,1,0:T(8,128)(2,1)S(1)}, bf16[2,384,128]{2,1,0:T(8,128)(2,1)S(1)}, u32[]{:S(2)}, u32[]{:S(2)}) collective-permute-start(bf16[2,384,128]{2,1,0:T(8,128)(2,1)S(1)} %collective-permute-done.3.refs_1_), channel_id=1, source_target_pairs={{0,14},{2,0},{4,2},{6,4},{8,6},{10,8},{12,10},{14,12},{1,15},{3,1}... | collective-permute-start | bytes 589832 | tf_op jit(solution)/shard_map/ppermute | solution.py:21
  21.3 16.5 %copy-start.9 = (s32[4,128,2]{1,2,0:T(2,128)S(1)}, s32[4,128,2]{1,2,0:T(2,128)}, u32[]{:S(2)}) copy-start(s32[4,128,2]{1,2,0:T(2,128)} %param.6) | copy-start | bytes 12292
  21.3 16.5 %copy-start.10 = (f32[4,128,2]{1,2,0:T(2,128)S(1)}, f32[4,128,2]{1,2,0:T(2,128)}, u32[]{:S(2)}) copy-start(f32[4,128,2]{1,2,0:T(2,128)} %param.7) | copy-start | bytes 12292
  21.4 5.8 %collective-permute-start.5 = (bf16[2,384,128]{2,1,0:T(8,128)(2,1)S(1)}, bf16[2,384,128]{2,1,0:T(8,128)(2,1)S(1)}, u32[]{:S(2)}, u32[]{:S(2)}) collective-permute-start(bf16[2,384,128]{2,1,0:T(8,128)(2,1)S(1)} %collective-permute-done.2.refs_6_), channel_id=1, source_target_pairs={{0,2},{2,4},{4,6},{6,8},{8,10},{10,12},{12,14},{14,0},{1,3},{3,5},... | collective-permute-start | bytes 589832 | tf_op jit(solution)/shard_map/ppermute | solution.py:21
  21.4 5.8 %collective-permute-start.7 = (bf16[2,384,128]{2,1,0:T(8,128)(2,1)S(1)}, bf16[2,384,128]{2,1,0:T(8,128)(2,1)S(1)}, u32[]{:S(2)}, u32[]{:S(2)}) collective-permute-start(bf16[2,384,128]{2,1,0:T(8,128)(2,1)S(1)} %collective-permute-done.4.refs_2_), channel_id=1, source_target_pairs={{0,14},{2,0},{4,2},{6,4},{8,6},{10,8},{12,10},{14,12},{1,15},{3,1}... | collective-permute-start | bytes 589832 | tf_op jit(solution)/shard_map/ppermute | solution.py:21
  27.2 4.8 %collective-permute-start.6 = (bf16[1,384,128]{2,1,0:T(8,128)(2,1)S(1)}, bf16[1,384,128]{2,1,0:T(8,128)(2,1)S(1)}, u32[]{:S(2)}, u32[]{:S(2)}) collective-permute-start(bf16[1,384,128]{2,1,0:T(8,128)(2,1)S(1)} %slice.24), channel_id=1, source_target_pairs={{0,2},{2,4},{4,6},{6,8},{8,10},{10,12},{12,14},{14,0},{1,3},{3,5},... | collective-permute-start | bytes 294920 | tf_op jit(solution)/shard_map/ppermute | solution.py:21
  27.3 4.6 %collective-permute-start.8 = (bf16[1,384,128]{2,1,0:T(8,128)(2,1)S(1)}, bf16[1,384,128]{2,1,0:T(8,128)(2,1)S(1)}, u32[]{:S(2)}, u32[]{:S(2)}) collective-permute-start(bf16[1,384,128]{2,1,0:T(8,128)(2,1)S(1)} %slice.25), channel_id=1, source_target_pairs={{0,14},{2,0},{4,2},{6,4},{8,6},{10,8},{12,10},{14,12},{1,15},{3,1}... | collective-permute-start | bytes 294920 | tf_op jit(solution)/shard_map/ppermute | solution.py:21
  31.9 23.3 %all-to-all-start = ((bf16[8,192,256]{2,1,0:T(8,128)(2,1)}), bf16[8,192,256]{2,1,0:T(8,128)(2,1)S(1)}, u32[]{:S(2)}, u32[]{:S(2)}) async-start(bf16[8,192,256]{2,1,0:T(8,128)(2,1)} %get-tuple-element.44), calls=%async_computation | async-start | bytes 1572864 | tf_op jit(solution)/shard_map/all_to_all | solution.py:148
  41.5 1.0 copy-start.4
  42.5 19.5 %collective-permute-start.10 = (bf16[160,3200]{1,0:T(8,128)(2,1)}, bf16[160,3200]{1,0:T(8,128)(2,1)}, u32[]{:S(2)}, u32[]{:S(2)}) collective-permute-start(bf16[160,3200]{1,0:T(8,128)(2,1)} %get-tuple-element.50), channel_id=1, source_target_pairs={{0,32},{32,64},{64,96},{96,0},{1,33},{33,65},{65,97},{97,1},{2,34}... | collective-permute-start | bytes 3072008 | tf_op jit(solution)/shard_map/ppermute | solution.py:21
  43.8 18.2 %collective-permute-start.11 = (bf16[160,3200]{1,0:T(8,128)(2,1)}, bf16[160,3200]{1,0:T(8,128)(2,1)}, u32[]{:S(2)}, u32[]{:S(2)}) collective-permute-start(bf16[160,3200]{1,0:T(8,128)(2,1)} %get-tuple-element.51), channel_id=1, source_target_pairs={{0,96},{32,0},{64,32},{96,64},{1,97},{33,1},{65,33},{97,65},{2,98}... | collective-permute-start | bytes 3072008 | tf_op jit(solution)/shard_map/ppermute | solution.py:21
  45.3 16.7 %collective-permute-start.9 = (bf16[160,3200]{1,0:T(8,128)(2,1)}, bf16[160,3200]{1,0:T(8,128)(2,1)}, u32[]{:S(2)}, u32[]{:S(2)}) collective-permute-start(bf16[160,3200]{1,0:T(8,128)(2,1)} %get-tuple-element.49.refs_0_), channel_id=1, source_target_pairs={{0,16},{16,0},{1,17},{17,1},{2,18},{18,2},{3,19},{19,3},{4,20},{20... | collective-permute-start | bytes 3072008 | tf_op jit(solution)/shard_map/ppermute | solution.py:21
  55.2 13.7 %collective-permute-start.13 = (bf16[8,192,256]{2,1,0:T(8,128)(2,1)S(1)}, bf16[8,192,256]{2,1,0:T(8,128)(2,1)S(1)}, u32[]{:S(2)}, u32[]{:S(2)}) collective-permute-start(bf16[8,192,256]{2,1,0:T(8,128)(2,1)S(1)} %all-to-all-done.refs_8_), channel_id=1, source_target_pairs={{0,1},{1,128},{128,129},{129,0},{2,3},{3,130},{130,131},{131,2},{4... | collective-permute-start | bytes 2359304 | tf_op jit(solution)/shard_map/ppermute | solution.py:21
  56.4 12.4 %collective-permute-start.14 = (bf16[8,192,256]{2,1,0:T(8,128)(2,1)S(1)}, bf16[8,192,256]{2,1,0:T(8,128)(2,1)S(1)}, u32[]{:S(2)}, u32[]{:S(2)}) collective-permute-start(bf16[8,192,256]{2,1,0:T(8,128)(2,1)S(1)} %all-to-all-done.refs_8_), channel_id=1, source_target_pairs={{0,129},{1,0},{128,1},{129,128},{2,131},{3,2},{130,3},{131,130},{4... | collective-permute-start | bytes 2359304 | tf_op jit(solution)/shard_map/ppermute | solution.py:21
  57.9 36.7 %all-to-all-start.1 = ((bf16[8,192,256]{2,1,0:T(8,128)(2,1)}), bf16[8,192,256]{2,1,0:T(8,128)(2,1)S(1)}, u32[]{:S(2)}, u32[]{:S(2)}) async-start(bf16[8,192,256]{2,1,0:T(8,128)(2,1)} %get-tuple-element.45), calls=%async_computation.1 | async-start | bytes 1572864 | tf_op jit(solution)/shard_map/all_to_all | solution.py:148
  62.0 23.1 %collective-permute-start.12 = (bf16[160,3200]{1,0:T(8,128)(2,1)}, bf16[160,3200]{1,0:T(8,128)(2,1)S(1)}, u32[]{:S(2)}, u32[]{:S(2)}) collective-permute-start(bf16[160,3200]{1,0:T(8,128)(2,1)} %copy-done.4), channel_id=1, source_target_pairs={{0,64},{32,96},{64,0},{96,32},{1,65},{33,97},{65,1},{97,33},{2,66}... | collective-permute-start | bytes 3072008 | tf_op jit(solution)/shard_map/ppermute | solution.py:21
  68.9 25.7 %collective-permute-start.17 = (bf16[160,3200]{1,0:T(8,128)(2,1)}, bf16[160,3200]{1,0:T(8,128)(2,1)}, u32[]{:S(2)}, u32[]{:S(2)}) collective-permute-start(bf16[160,3200]{1,0:T(8,128)(2,1)} %collective-permute-done.10.refs_1_), channel_id=1, source_target_pairs={{0,16},{16,0},{1,17},{17,1},{2,18},{18,2},{3,19},{19,3},{4,20},{20... | collective-permute-start | bytes 3072008 | tf_op jit(solution)/shard_map/ppermute | solution.py:21
  82.1 12.5 %collective-permute-start.18 = (bf16[160,3200]{1,0:T(8,128)(2,1)}, bf16[160,3200]{1,0:T(8,128)(2,1)}, u32[]{:S(2)}, u32[]{:S(2)}) collective-permute-start(bf16[160,3200]{1,0:T(8,128)(2,1)} %collective-permute-done.11.refs_3_), channel_id=1, source_target_pairs={{0,16},{16,0},{1,17},{17,1},{2,18},{18,2},{3,19},{19,3},{4,20},{20... | collective-permute-start | bytes 3072008 | tf_op jit(solution)/shard_map/ppermute | solution.py:21
  82.2 11.6 %collective-permute-start.15 = (bf16[4,192,256]{2,1,0:T(8,128)(2,1)S(1)}, bf16[4,192,256]{2,1,0:T(8,128)(2,1)S(1)}, u32[]{:S(2)}, u32[]{:S(2)}) collective-permute-start(bf16[4,192,256]{2,1,0:T(8,128)(2,1)S(1)} %slice.20), channel_id=1, source_target_pairs={{0,1},{1,128},{128,129},{129,0},{2,3},{3,130},{130,131},{131,2},{4... | collective-permute-start | bytes 1179656 | tf_op jit(solution)/shard_map/ppermute | solution.py:21
  83.5 10.3 %collective-permute-start.16 = (bf16[4,192,256]{2,1,0:T(8,128)(2,1)S(1)}, bf16[4,192,256]{2,1,0:T(8,128)(2,1)S(1)}, u32[]{:S(2)}, u32[]{:S(2)}) collective-permute-start(bf16[4,192,256]{2,1,0:T(8,128)(2,1)S(1)} %slice.21), channel_id=1, source_target_pairs={{0,129},{1,0},{128,1},{129,128},{2,131},{3,2},{130,3},{131,130},{4... | collective-permute-start | bytes 1179656 | tf_op jit(solution)/shard_map/ppermute | solution.py:21
  85.1 8.7 %copy-start.11 = (bf16[160,3200]{1,0:T(8,128)(2,1)}, bf16[160,3200]{1,0:T(8,128)(2,1)S(1)}, u32[]{:S(2)}) copy-start(bf16[160,3200]{1,0:T(8,128)(2,1)S(1)} %collective-permute-done.12.refs_2_) | copy-start | bytes 3072004
  93.8 0.8 copy-start.5
  94.6 4.8 %collective-permute-start.21 = (bf16[160,3200]{1,0:T(8,128)(2,1)}, bf16[160,3200]{1,0:T(8,128)(2,1)S(1)}, u32[]{:S(2)}, u32[]{:S(2)}) collective-permute-start(bf16[160,3200]{1,0:T(8,128)(2,1)} %copy-done.11), channel_id=1, source_target_pairs={{0,16},{16,0},{1,17},{17,1},{2,18},{18,2},{3,19},{19,3},{4,20},{20... | collective-permute-start | bytes 3072008 | tf_op jit(solution)/shard_map/ppermute | solution.py:21
  96.7 20.3 %collective-permute-start.19 = (bf16[8,192,256]{2,1,0:T(8,128)(2,1)S(1)}, bf16[8,192,256]{2,1,0:T(8,128)(2,1)S(1)}, u32[]{:S(2)}, u32[]{:S(2)}) collective-permute-start(bf16[8,192,256]{2,1,0:T(8,128)(2,1)S(1)} %all-to-all-done.1.refs_8_), channel_id=1, source_target_pairs={{0,1},{1,128},{128,129},{129,0},{2,3},{3,130},{130,131},{131,2},{4... | collective-permute-start | bytes 2359304 | tf_op jit(solution)/shard_map/ppermute | solution.py:21
  97.9 19.1 %collective-permute-start.20 = (bf16[8,192,256]{2,1,0:T(8,128)(2,1)S(1)}, bf16[8,192,256]{2,1,0:T(8,128)(2,1)S(1)}, u32[]{:S(2)}, u32[]{:S(2)}) collective-permute-start(bf16[8,192,256]{2,1,0:T(8,128)(2,1)S(1)} %all-to-all-done.1.refs_8_), channel_id=1, source_target_pairs={{0,129},{1,0},{128,1},{129,128},{2,131},{3,2},{130,3},{131,130},{4... | collective-permute-start | bytes 2359304 | tf_op jit(solution)/shard_map/ppermute | solution.py:21
  99.4 0.9 copy-start.12
  100.3 1.0 copy-start.6
  117.0 2.4 %copy-start.2 = (bf16[8,192,256]{2,1,0:T(8,128)(2,1)}, bf16[8,192,256]{2,1,0:T(8,128)(2,1)S(1)}, u32[]{:S(2)}) copy-start(bf16[8,192,256]{2,1,0:T(8,128)(2,1)S(1)} %collective-permute-done.20.refs_10_) | copy-start | bytes 2359300
  117.8 1.0 copy-start
  118.8 11.2 %collective-permute-start.22 = (bf16[4,192,256]{2,1,0:T(8,128)(2,1)}, bf16[4,192,256]{2,1,0:T(8,128)(2,1)S(1)}, u32[]{:S(2)}, u32[]{:S(2)}) collective-permute-start(bf16[4,192,256]{2,1,0:T(8,128)(2,1)} %slice.22), channel_id=1, source_target_pairs={{0,1},{1,128},{128,129},{129,0},{2,3},{3,130},{130,131},{131,2},{4... | collective-permute-start | bytes 1179656 | tf_op jit(solution)/shard_map/ppermute | solution.py:21
  119.5 11.3 %copy-start.1 = (bf16[8,192,256]{2,1,0:T(8,128)(2,1)S(1)}, bf16[8,192,256]{2,1,0:T(8,128)(2,1)}, u32[]{:S(2)}) copy-start(bf16[8,192,256]{2,1,0:T(8,128)(2,1)} %copy-done) | copy-start | bytes 2359300
  120.3 9.7 %collective-permute-start.23 = (bf16[4,192,256]{2,1,0:T(8,128)(2,1)}, bf16[4,192,256]{2,1,0:T(8,128)(2,1)S(1)}, u32[]{:S(2)}, u32[]{:S(2)}) collective-permute-start(bf16[4,192,256]{2,1,0:T(8,128)(2,1)} %slice.23), channel_id=1, source_target_pairs={{0,129},{1,0},{128,1},{129,128},{2,131},{3,2},{130,3},{131,130},{4... | collective-permute-start | bytes 1179656 | tf_op jit(solution)/shard_map/ppermute | solution.py:21
  122.3 18.4 %all-to-all-start.2 = ((bf16[16,160,128]{2,1,0:T(8,128)(2,1)}), bf16[16,160,128]{2,1,0:T(8,128)(2,1)S(1)}, u32[]{:S(2)}, u32[]{:S(2)}) async-start(bf16[16,160,128]{2,1,0:T(8,128)(2,1)} %bitcast.11), calls=%async_computation.2 | async-start | bytes 1310720 | tf_op jit(solution)/shard_map/all_to_all | solution.py:208
  130.0 0.7 copy-start.7
  130.7 1.1 copy-start.3
  131.9 1.0 copy-start.8

commit v17 on v10

--- a/solution.py
+++ b/solution.py
@@ -181,7 +181,6 @@
     left_a, right_a = sides(own_a)
     far_rows, other[0], *near = barrier((sent[2], other[0], *near))
     opposite = ring(far_rows, "y", 4, 2)
-    left_a, right_a, *near = barrier((left_a, right_a, *near))
     far_a = far(left_a, right_a)
     other += [ring(h, "c", 2, 1) for h in near]
     own_b, opposite, *rest = barrier((own_b, opposite, *far_a, *other))

time: 162 us -> 163 us (level)
  starting transfers between devices: 69.8 us -> 76.2 us
  waiting for transfers between devices: 34.9 us -> 29.9 us
  local copies, waits for them, and re-layouts: 7.95 us -> 6.04 us
  blocking collectives: 18.5 us -> 20.3 us
    ppermute x24, waiting for transfers between devices: 31.3 us -> 26.3 us  [ring(): return lax.ppermute(x, axis, [(i, (i + step) % size) for i in range(size)])]
    ppermute x24, starting transfers between devices: 54.4 us -> 59 us  [ring(): return lax.ppermute(x, axis, [(i, (i + step) % size) for i in range(size)])]
    slice x4, local copies, waits for them, and re-layouts: 2.09 us -> 0.11 us  [far(): return (ring(left[:4], X, 4, 1), ring(right[4:], X, 4, -1))]
    all_to_all x1, blocking collectives: 18.5 us -> 20.3 us  [give_back(): lax.all_to_all(act.reshape(16, 2 * MOST, wide), ('y', 'c', 'xl'), split_a...]
    all_to_all x1, starting transfers between devices: 5.42 us -> 7.19 us  [give_back(): lax.all_to_all(act.reshape(16, 2 * MOST, wide), ('y', 'c', 'xl'), split_a...]
  transfers between devices with their start and end apart: 27 -> 27, of which waited for: 10 -> 9; matrix products, arithmetic and copies ran while one was open for 2% -> 0% of each run, Pallas kernels for 17% -> 17%
where the time goes in v17:
time: 163 us
  starting transfers between devices  76.2 us (47%)
  waiting for transfers between devices  29.9 us (18%)
  Pallas kernels  29 us (18%)
  blocking collectives  20.3 us (12%)
  local copies, waits for them, and re-layouts  6.04 us (4%)
    ppermute x24, starting transfers between devices, ring(): return lax.ppermute(x, axis, [(i, (i + step) % size) for i in range(size)])  59 us
    ppermute x24, waiting for transfers between devices, ring(): return lax.ppermute(x, axis, [(i, (i + step) % size) for i in range(size)])  26.3 us
    pallas_call x2, Pallas kernels, expert(): pl.pallas_call(expert_kernel, out_shape=jax.ShapeDtypeStruct((4, 2, 2, 2...  20.7 us
    all_to_all x1, blocking collectives, give_back(): lax.all_to_all(act.reshape(16, 2 * MOST, wide), ('y', 'c', 'xl'), split_a...  20.3 us
    all_to_all x2, starting transfers between devices, exchange(): return lax.all_to_all(x, 'z', split_axis=0, concat_axis=0, tiled=True)  10 us
    all_to_all x1, starting transfers between devices, give_back(): lax.all_to_all(act.reshape(16, 2 * MOST, wide), ('y', 'c', 'xl'), split_a...  7.19 us
    all_to_all x2, waiting for transfers between devices, exchange(): return lax.all_to_all(x, 'z', split_axis=0, concat_axis=0, tiled=True)  3.61 us
    pallas_call x1, Pallas kernels, body(): pl.pallas_call(columns_kernel, out_shape=[jax.ShapeDtypeStruct((8, rows,...  3.5 us
  transfers between devices with their start and end apart: 27, of which 9 were waited for; matrix products, arithmetic and copies ran while one was open for 0% of the time, Pallas kernels for 17%

profile of v17, /device:TPU:1, one launch (start us, length us, event | category | flops | bytes accessed | tf_op | source)
XLA Modules:
  0.0 162.7 jit_solution(3457420854838986446)
XLA Ops:
  0.0 0.9 dynamic-slice_bitcast_fusion
  0.9 2.0 %collective-permute-start = (bf16[2,192,128]{2,1,0:T(8,128)(2,1)S(1)}, bf16[2,192,128]{2,1,0:T(8,128)(2,1)S(1)}, u32[]{:S(2)}, u32[]{:S(2)}) collective-permute-start(bf16[2,192,128]{2,1,0:T(8,128)(2,1)S(1)} %dynamic-slice_bitcast_fusion), channel_id=1, source_target_pairs={{0,1},{1,0},{2,3},{3,2},{4,5},{5,4},{6,7},{7,6},{8,9},{9,8},{10,11... | collective-permute-start | bytes 294920 | tf_op jit(solution)/shard_map/ppermute | solution.py:17
  2.9 2.0 %collective-permute-done = bf16[2,192,128]{2,1,0:T(8,128)(2,1)S(1)} collective-permute-done((bf16[2,192,128]{2,1,0:T(8,128)(2,1)S(1)}, bf16[2,192,128]{2,1,0:T(8,128)(2,1)S(1)}, u32[]{:S(2)}, u32[]{:S(2)}) %collective-permute-start) | collective-permute-done | bytes 98336 | tf_op jit(solution)/shard_map/ppermute | solution.py:17
  4.9 0.9 bitcast_select_fusion.1
  5.9 2.0 %collective-permute-start.1 = (bf16[2,384,128]{2,1,0:T(8,128)(2,1)S(1)}, bf16[2,384,128]{2,1,0:T(8,128)(2,1)S(1)}, u32[]{:S(2)}, u32[]{:S(2)}) collective-permute-start(bf16[2,384,128]{2,1,0:T(8,128)(2,1)S(1)} %pad_maximum_fusion.refs_0_), channel_id=1, source_target_pairs={{0,2},{2,4},{4,6},{6,8},{8,10},{10,12},{12,14},{14,0},{1,3},{3,5},... | collective-permute-start | bytes 589832 | tf_op jit(solution)/shard_map/ppermute | solution.py:17
  7.8 4.0 %collective-permute-start.3 = (bf16[2,384,128]{2,1,0:T(8,128)(2,1)S(1)}, bf16[2,384,128]{2,1,0:T(8,128)(2,1)S(1)}, u32[]{:S(2)}, u32[]{:S(2)}) collective-permute-start(bf16[2,384,128]{2,1,0:T(8,128)(2,1)S(1)} %pad_maximum_fusion.refs_0_), channel_id=1, source_target_pairs={{0,14},{2,0},{4,2},{6,4},{8,6},{10,8},{12,10},{14,12},{1,15},{3,1}... | collective-permute-start | bytes 589832 | tf_op jit(solution)/shard_map/ppermute | solution.py:17
  11.9 3.3 %collective-permute-done.1.refs_7_ = bf16[2,384,128]{2,1,0:T(8,128)(2,1)S(1)} collective-permute-done((bf16[2,384,128]{2,1,0:T(8,128)(2,1)S(1)}, bf16[2,384,128]{2,1,0:T(8,128)(2,1)S(1)}, u32[]{:S(2)}, u32[]{:S(2)}) %collective-permute-start.1) | collective-permute-done | bytes 196640 | tf_op jit(solution)/shard_map/ppermute | solution.py:17
  15.2 2.7 %collective-permute-start.4 = (bf16[2,384,128]{2,1,0:T(8,128)(2,1)S(1)}, bf16[2,384,128]{2,1,0:T(8,128)(2,1)S(1)}, u32[]{:S(2)}, u32[]{:S(2)}) collective-permute-start(bf16[2,384,128]{2,1,0:T(8,128)(2,1)S(1)} %collective-permute-done.3.refs_1_), channel_id=1, source_target_pairs={{0,14},{2,0},{4,2},{6,4},{8,6},{10,8},{12,10},{14,12},{1,15},{3,1}... | collective-permute-start | bytes 589832 | tf_op jit(solution)/shard_map/ppermute | solution.py:17
  17.9 0.7 stack.23.pos
  18.5 3.5 %columns.1 = (bf16[8,192,256]{2,1,0:T(8,128)(2,1)}, bf16[8,192,256]{2,1,0:T(8,128)(2,1)}) custom-call(s32[5]{0:T(128)} %stack.23.pos, bf16[1,192,4096]{2,1,0:T(8,128)(2,1)} %gate.1, bf16[1,192,4096]{2,1,0:T(8,128)(2,1)} %up.1), custom_call_target="tpu_custom_call" | custom-call | tf_op jit(solution)/shard_map/columns/pallas_call | solution.py:141
  22.0 0.0 copy-start.9
  22.1 0.1 collective-permute-start.5
  22.2 2.7 %collective-permute-start.7 = (bf16[2,384,128]{2,1,0:T(8,128)(2,1)S(1)}, bf16[2,384,128]{2,1,0:T(8,128)(2,1)S(1)}, u32[]{:S(2)}, u32[]{:S(2)}) collective-permute-start(bf16[2,384,128]{2,1,0:T(8,128)(2,1)S(1)} %collective-permute-done.4.refs_2_), channel_id=1, source_target_pairs={{0,14},{2,0},{4,2},{6,4},{8,6},{10,8},{12,10},{14,12},{1,15},{3,1}... | collective-permute-start | bytes 589832 | tf_op jit(solution)/shard_map/ppermute | solution.py:17
  24.8 3.1 %collective-permute-done.5.refs_5_ = bf16[2,384,128]{2,1,0:T(8,128)(2,1)S(1)} collective-permute-done((bf16[2,384,128]{2,1,0:T(8,128)(2,1)S(1)}, bf16[2,384,128]{2,1,0:T(8,128)(2,1)S(1)}, u32[]{:S(2)}, u32[]{:S(2)}) %collective-permute-start.5) | collective-permute-done | bytes 196640 | tf_op jit(solution)/shard_map/ppermute | solution.py:17
  27.9 0.1 collective-permute-start.6
  28.0 2.7 %collective-permute-start.8 = (bf16[1,384,128]{2,1,0:T(8,128)(2,1)S(1)}, bf16[1,384,128]{2,1,0:T(8,128)(2,1)S(1)}, u32[]{:S(2)}, u32[]{:S(2)}) collective-permute-start(bf16[1,384,128]{2,1,0:T(8,128)(2,1)S(1)} %slice.25), channel_id=1, source_target_pairs={{0,14},{2,0},{4,2},{6,4},{8,6},{10,8},{12,10},{14,12},{1,15},{3,1}... | collective-permute-start | bytes 294920 | tf_op jit(solution)/shard_map/ppermute | solution.py:17
  30.7 1.9 %collective-permute-done.6 = bf16[1,384,128]{2,1,0:T(8,128)(2,1)S(1)} collective-permute-done((bf16[1,384,128]{2,1,0:T(8,128)(2,1)S(1)}, bf16[1,384,128]{2,1,0:T(8,128)(2,1)S(1)}, u32[]{:S(2)}, u32[]{:S(2)}) %collective-permute-start.6) | collective-permute-done | bytes 98336 | tf_op jit(solution)/shard_map/ppermute | solution.py:17
  32.7 5.8 %all-to-all-start = ((bf16[8,192,256]{2,1,0:T(8,128)(2,1)}), bf16[8,192,256]{2,1,0:T(8,128)(2,1)S(1)}, u32[]{:S(2)}, u32[]{:S(2)}) async-start(bf16[8,192,256]{2,1,0:T(8,128)(2,1)} %get-tuple-element.40), calls=%async_computation | async-start | bytes 1572864 | tf_op jit(solution)/shard_map/all_to_all | solution.py:152
  38.5 3.4 %dispatch.1 = (bf16[160,3200]{1,0:T(8,128)(2,1)S(1)}, bf16[160,3200]{1,0:T(8,128)(2,1)}, bf16[160,3200]{1,0:T(8,128)(2,1)S(1)}, bf16[160,3200]{1,0:T(8,128)(2,1)}) custom-call(s32[5]{0:T(128)S(1)} %copy-done, f32[4,4,128]{2,1,0:T(4,128)S(1)} %maximum_bitcast_fusion.meta, bf16[2,384,128]{2,1,0:T(8,128)(2,1)S(1)} %pad_maximum_fusion.refs_0_, ...), custom_call_target="tpu_custom_call" | custom-call | tf_op jit(solution)/shard_map/dispatch/pallas_call | solution.py:169
  41.9 1.0 copy-done.2
  42.9 1.3 collective-permute-start.10
  44.2 1.4 collective-permute-start.11
  45.6 6.7 %collective-permute-start.9 = (bf16[160,3200]{1,0:T(8,128)(2,1)S(1)}, bf16[160,3200]{1,0:T(8,128)(2,1)}, u32[]{:S(2)}, u32[]{:S(2)}) collective-permute-start(bf16[160,3200]{1,0:T(8,128)(2,1)S(1)} %get-tuple-element.45.refs_0_), channel_id=1, source_target_pairs={{0,16},{16,0},{1,17},{17,1},{2,18},{18,2},{3,19},{19,3},{4,20},{20... | collective-permute-start | bytes 3072008 | tf_op jit(solution)/shard_map/ppermute | solution.py:17
  52.3 3.6 %all-to-all-done.refs_8_ = bf16[8,192,256]{2,1,0:T(8,128)(2,1)S(1)} async-done(((bf16[8,192,256]{2,1,0:T(8,128)(2,1)}), bf16[8,192,256]{2,1,0:T(8,128)(2,1)S(1)}, u32[]{:S(2)}, u32[]{:S(2)}) %all-to-all-start) | async-done | bytes 786464 | tf_op jit(solution)/shard_map/all_to_all | solution.py:152
  56.0 4.2 %all-to-all-start.1 = ((bf16[8,192,256]{2,1,0:T(8,128)(2,1)}), bf16[8,192,256]{2,1,0:T(8,128)(2,1)}, u32[]{:S(2)}, u32[]{:S(2)}) async-start(bf16[8,192,256]{2,1,0:T(8,128)(2,1)} %get-tuple-element.41), calls=%async_computation.1 | async-start | bytes 1572864 | tf_op jit(solution)/shard_map/all_to_all | solution.py:152
  60.2 1.3 collective-permute-start.13
  61.5 1.5 collective-permute-start.15
  63.0 3.0 %collective-permute-start.12 = (bf16[160,3200]{1,0:T(8,128)(2,1)S(1)}, bf16[160,3200]{1,0:T(8,128)(2,1)}, u32[]{:S(2)}, u32[]{:S(2)}) collective-permute-start(bf16[160,3200]{1,0:T(8,128)(2,1)S(1)} %copy-done.3), channel_id=1, source_target_pairs={{0,64},{32,96},{64,0},{96,32},{1,65},{33,97},{65,1},{97,33},{2,66}... | collective-permute-start | bytes 3072008 | tf_op jit(solution)/shard_map/ppermute | solution.py:17
  66.0 8.8 %collective-permute-start.17 = (bf16[160,3200]{1,0:T(8,128)(2,1)}, bf16[160,3200]{1,0:T(8,128)(2,1)S(1)}, u32[]{:S(2)}, u32[]{:S(2)}) collective-permute-start(bf16[160,3200]{1,0:T(8,128)(2,1)} %collective-permute-done.10.refs_1_), channel_id=1, source_target_pairs={{0,16},{16,0},{1,17},{17,1},{2,18},{18,2},{3,19},{19,3},{4,20},{20... | collective-permute-start | bytes 3072008 | tf_op jit(solution)/shard_map/ppermute | solution.py:17
  74.8 9.0 %collective-permute-start.14 = (bf16[4,192,256]{2,1,0:T(8,128)(2,1)S(1)}, bf16[4,192,256]{2,1,0:T(8,128)(2,1)S(1)}, u32[]{:S(2)}, u32[]{:S(2)}) collective-permute-start(bf16[4,192,256]{2,1,0:T(8,128)(2,1)S(1)} %slice.26), channel_id=1, source_target_pairs={{0,1},{1,128},{128,129},{129,0},{2,3},{3,130},{130,131},{131,2},{4... | collective-permute-start | bytes 1179656 | tf_op jit(solution)/shard_map/ppermute | solution.py:17
  83.9 2.1 %collective-permute-start.16 = (bf16[4,192,256]{2,1,0:T(8,128)(2,1)S(1)}, bf16[4,192,256]{2,1,0:T(8,128)(2,1)}, u32[]{:S(2)}, u32[]{:S(2)}) collective-permute-start(bf16[4,192,256]{2,1,0:T(8,128)(2,1)S(1)} %slice.27), channel_id=1, source_target_pairs={{0,129},{1,0},{128,1},{129,128},{2,131},{3,2},{130,3},{131,130},{4... | collective-permute-start | bytes 1179656 | tf_op jit(solution)/shard_map/ppermute | solution.py:17
  86.0 0.4 collective-permute-done.12.refs_2_
  86.4 7.7 %collective-permute-done.14.refs_11_ = bf16[4,192,256]{2,1,0:T(8,128)(2,1)S(1)} collective-permute-done((bf16[4,192,256]{2,1,0:T(8,128)(2,1)S(1)}, bf16[4,192,256]{2,1,0:T(8,128)(2,1)S(1)}, u32[]{:S(2)}, u32[]{:S(2)}) %collective-permute-start.14) | collective-permute-done | bytes 393248 | tf_op jit(solution)/shard_map/ppermute | solution.py:17
  94.2 0.8 copy-done.14
  94.9 1.0 collective-permute-start.21
  96.0 2.5 %collective-permute-start.19 = (bf16[8,192,256]{2,1,0:T(8,128)(2,1)}, bf16[8,192,256]{2,1,0:T(8,128)(2,1)S(1)}, u32[]{:S(2)}, u32[]{:S(2)}) collective-permute-start(bf16[8,192,256]{2,1,0:T(8,128)(2,1)} %all-to-all-done.1.refs_8_), channel_id=1, source_target_pairs={{0,1},{1,128},{128,129},{129,0},{2,3},{3,130},{130,131},{131,2},{4... | collective-permute-start | bytes 2359304 | tf_op jit(solution)/shard_map/ppermute | solution.py:17
  98.5 1.2 collective-permute-start.20
  99.7 1.0 copy-done.13
  100.7 10.3 %expert.2 = bf16[4,2,2,160,128]{4,3,2,1,0:T(8,128)(2,1)} custom-call(s32[5]{0:T(128)} %stack.23.pos, bf16[160,3200]{1,0:T(8,128)(2,1)} %copy-done.1, bf16[160,3200]{1,0:T(8,128)(2,1)} %collective-permute-done.10.refs_1_, bf16[160,3200]{1,0:T(8,128)(2,1)} %collective-permute-done.12.refs_2_, bf16[160,3200]{1,0:T(8,128)(2,1)} %collective-permute-done.11.refs_3_, ...), custom_call_target="tpu_custom_call" | custom-call | flops 4026531840 | bytes 12582912 | tf_op jit(solution)/shard_map/expert/pallas_call | solution.py:193
  111.0 6.7 %collective-permute-done.19.refs_9_ = bf16[8,192,256]{2,1,0:T(8,128)(2,1)S(1)} collective-permute-done((bf16[8,192,256]{2,1,0:T(8,128)(2,1)}, bf16[8,192,256]{2,1,0:T(8,128)(2,1)S(1)}, u32[]{:S(2)}, u32[]{:S(2)}) %collective-permute-start.19) | collective-permute-done | bytes 786464 | tf_op jit(solution)/shard_map/ppermute | solution.py:17
  117.8 1.0 collective-permute-start.22
  118.8 1.8 %collective-permute-start.23 = (bf16[4,192,256]{2,1,0:T(8,128)(2,1)S(1)}, bf16[4,192,256]{2,1,0:T(8,128)(2,1)}, u32[]{:S(2)}, u32[]{:S(2)}) collective-permute-start(bf16[4,192,256]{2,1,0:T(8,128)(2,1)S(1)} %slice.23), channel_id=1, source_target_pairs={{0,129},{1,0},{128,1},{129,128},{2,131},{3,2},{130,3},{131,130},{4... | collective-permute-start | bytes 1179656 | tf_op jit(solution)/shard_map/ppermute | solution.py:17
  120.7 7.2 %all-to-all-start.2 = ((bf16[16,160,128]{2,1,0:T(8,128)(2,1)}), bf16[16,160,128]{2,1,0:T(8,128)(2,1)S(1)}, u32[]{:S(2)}, u32[]{:S(2)}) async-start(bf16[16,160,128]{2,1,0:T(8,128)(2,1)} %bitcast.11), calls=%async_computation.2 | async-start | bytes 1310720 | tf_op jit(solution)/shard_map/all_to_all | solution.py:212
  127.9 1.1 collective-permute-done.22.refs_11_
  129.0 10.4 %expert.3 = bf16[4,2,2,160,128]{4,3,2,1,0:T(8,128)(2,1)} custom-call(s32[5]{0:T(128)} %stack.23.pos, bf16[160,3200]{1,0:T(8,128)(2,1)} %copy-done.1, bf16[160,3200]{1,0:T(8,128)(2,1)} %collective-permute-done.10.refs_1_, bf16[160,3200]{1,0:T(8,128)(2,1)} %collective-permute-done.12.refs_2_, bf16[160,3200]{1,0:T(8,128)(2,1)} %collective-permute-done.11.refs_3_, ...), custom_call_target="tpu_custom_call" | custom-call | flops 4026531840 | bytes 12582912 | tf_op jit(solution)/shard_map/expert/pallas_call | solution.py:193
  139.4 20.3 %all_to_all.20 = bf16[16,160,128]{2,1,0:T(8,128)(2,1)S(1)} all-to-all(bf16[16,160,128]{2,1,0:T(8,128)(2,1)} %bitcast.21), channel_id=1, replica_groups=mesh['dp'=2,'y'=4,'c'=2,'z'=8,'xl'=2] {'y','c','xl'}, dimensions={0} | all-to-all | bytes 1310720 | tf_op jit(solution)/shard_map/all_to_all | solution.py:212
  159.7 1.5 combine.1
  161.1 1.6 reshape.23
  (56 shorter events, 0.3 us)
Async XLA Ops:
  0.9 4.0 %collective-permute-start = (bf16[2,192,128]{2,1,0:T(8,128)(2,1)S(1)}, bf16[2,192,128]{2,1,0:T(8,128)(2,1)S(1)}, u32[]{:S(2)}, u32[]{:S(2)}) collective-permute-start(bf16[2,192,128]{2,1,0:T(8,128)(2,1)S(1)} %dynamic-slice_bitcast_fusion), channel_id=1, source_target_pairs={{0,1},{1,0},{2,3},{3,2},{4,5},{5,4},{6,7},{7,6},{8,9},{9,8},{10,11... | collective-permute-start | bytes 294920 | tf_op jit(solution)/shard_map/ppermute | solution.py:17
  5.9 9.3 %collective-permute-start.1 = (bf16[2,384,128]{2,1,0:T(8,128)(2,1)S(1)}, bf16[2,384,128]{2,1,0:T(8,128)(2,1)S(1)}, u32[]{:S(2)}, u32[]{:S(2)}) collective-permute-start(bf16[2,384,128]{2,1,0:T(8,128)(2,1)S(1)} %pad_maximum_fusion.refs_0_), channel_id=1, source_target_pairs={{0,2},{2,4},{4,6},{6,8},{8,10},{10,12},{12,14},{14,0},{1,3},{3,5},... | collective-permute-start | bytes 589832 | tf_op jit(solution)/shard_map/ppermute | solution.py:17
  7.8 7.3 %collective-permute-start.3 = (bf16[2,384,128]{2,1,0:T(8,128)(2,1)S(1)}, bf16[2,384,128]{2,1,0:T(8,128)(2,1)S(1)}, u32[]{:S(2)}, u32[]{:S(2)}) collective-permute-start(bf16[2,384,128]{2,1,0:T(8,128)(2,1)S(1)} %pad_maximum_fusion.refs_0_), channel_id=1, source_target_pairs={{0,14},{2,0},{4,2},{6,4},{8,6},{10,8},{12,10},{14,12},{1,15},{3,1}... | collective-permute-start | bytes 589832 | tf_op jit(solution)/shard_map/ppermute | solution.py:17
  15.2 6.9 %collective-permute-start.2 = (bf16[2,384,128]{2,1,0:T(8,128)(2,1)S(1)}, bf16[2,384,128]{2,1,0:T(8,128)(2,1)S(1)}, u32[]{:S(2)}, u32[]{:S(2)}) collective-permute-start(bf16[2,384,128]{2,1,0:T(8,128)(2,1)S(1)} %collective-permute-done.1.refs_7_), channel_id=1, source_target_pairs={{0,2},{2,4},{4,6},{6,8},{8,10},{10,12},{12,14},{14,0},{1,3},{3,5},... | collective-permute-start | bytes 589832 | tf_op jit(solution)/shard_map/ppermute | solution.py:17
  15.2 6.9 %collective-permute-start.4 = (bf16[2,384,128]{2,1,0:T(8,128)(2,1)S(1)}, bf16[2,384,128]{2,1,0:T(8,128)(2,1)S(1)}, u32[]{:S(2)}, u32[]{:S(2)}) collective-permute-start(bf16[2,384,128]{2,1,0:T(8,128)(2,1)S(1)} %collective-permute-done.3.refs_1_), channel_id=1, source_target_pairs={{0,14},{2,0},{4,2},{6,4},{8,6},{10,8},{12,10},{14,12},{1,15},{3,1}... | collective-permute-start | bytes 589832 | tf_op jit(solution)/shard_map/ppermute | solution.py:17
  22.0 16.4 %copy-start.9 = (s32[4,128,2]{1,2,0:T(2,128)S(1)}, s32[4,128,2]{1,2,0:T(2,128)}, u32[]{:S(2)}) copy-start(s32[4,128,2]{1,2,0:T(2,128)} %param.6) | copy-start | bytes 12292
  22.0 16.4 %copy-start.10 = (f32[4,128,2]{1,2,0:T(2,128)S(1)}, f32[4,128,2]{1,2,0:T(2,128)}, u32[]{:S(2)}) copy-start(f32[4,128,2]{1,2,0:T(2,128)} %param.7) | copy-start | bytes 12292
  22.1 16.5 %copy-start = (s32[5]{0:T(128)S(1)}, s32[5]{0:T(128)}, u32[]{:S(2)}) copy-start(s32[5]{0:T(128)} %stack.23.pos) | copy-start | bytes 64
  22.1 5.8 %collective-permute-start.5 = (bf16[2,384,128]{2,1,0:T(8,128)(2,1)S(1)}, bf16[2,384,128]{2,1,0:T(8,128)(2,1)S(1)}, u32[]{:S(2)}, u32[]{:S(2)}) collective-permute-start(bf16[2,384,128]{2,1,0:T(8,128)(2,1)S(1)} %collective-permute-done.2.refs_6_), channel_id=1, source_target_pairs={{0,2},{2,4},{4,6},{6,8},{8,10},{10,12},{12,14},{14,0},{1,3},{3,5},... | collective-permute-start | bytes 589832 | tf_op jit(solution)/shard_map/ppermute | solution.py:17
  22.2 5.8 %collective-permute-start.7 = (bf16[2,384,128]{2,1,0:T(8,128)(2,1)S(1)}, bf16[2,384,128]{2,1,0:T(8,128)(2,1)S(1)}, u32[]{:S(2)}, u32[]{:S(2)}) collective-permute-start(bf16[2,384,128]{2,1,0:T(8,128)(2,1)S(1)} %collective-permute-done.4.refs_2_), channel_id=1, source_target_pairs={{0,14},{2,0},{4,2},{6,4},{8,6},{10,8},{12,10},{14,12},{1,15},{3,1}... | collective-permute-start | bytes 589832 | tf_op jit(solution)/shard_map/ppermute | solution.py:17
  27.9 4.8 %collective-permute-start.6 = (bf16[1,384,128]{2,1,0:T(8,128)(2,1)S(1)}, bf16[1,384,128]{2,1,0:T(8,128)(2,1)S(1)}, u32[]{:S(2)}, u32[]{:S(2)}) collective-permute-start(bf16[1,384,128]{2,1,0:T(8,128)(2,1)S(1)} %slice.24), channel_id=1, source_target_pairs={{0,2},{2,4},{4,6},{6,8},{8,10},{10,12},{12,14},{14,0},{1,3},{3,5},... | collective-permute-start | bytes 294920 | tf_op jit(solution)/shard_map/ppermute | solution.py:17
  28.0 4.6 %collective-permute-start.8 = (bf16[1,384,128]{2,1,0:T(8,128)(2,1)S(1)}, bf16[1,384,128]{2,1,0:T(8,128)(2,1)S(1)}, u32[]{:S(2)}, u32[]{:S(2)}) collective-permute-start(bf16[1,384,128]{2,1,0:T(8,128)(2,1)S(1)} %slice.25), channel_id=1, source_target_pairs={{0,14},{2,0},{4,2},{6,4},{8,6},{10,8},{12,10},{14,12},{1,15},{3,1}... | collective-permute-start | bytes 294920 | tf_op jit(solution)/shard_map/ppermute | solution.py:17
  32.7 23.3 %all-to-all-start = ((bf16[8,192,256]{2,1,0:T(8,128)(2,1)}), bf16[8,192,256]{2,1,0:T(8,128)(2,1)S(1)}, u32[]{:S(2)}, u32[]{:S(2)}) async-start(bf16[8,192,256]{2,1,0:T(8,128)(2,1)} %get-tuple-element.40), calls=%async_computation | async-start | bytes 1572864 | tf_op jit(solution)/shard_map/all_to_all | solution.py:152
  41.9 1.0 copy-start.2
  42.9 41.0 %copy-start.1 = (bf16[160,3200]{1,0:T(8,128)(2,1)}, bf16[160,3200]{1,0:T(8,128)(2,1)S(1)}, u32[]{:S(2)}) copy-start(bf16[160,3200]{1,0:T(8,128)(2,1)S(1)} %get-tuple-element.45.refs_0_) | copy-start | bytes 3072004
  42.9 20.1 %copy-start.3 = (bf16[160,3200]{1,0:T(8,128)(2,1)S(1)}, bf16[160,3200]{1,0:T(8,128)(2,1)}, u32[]{:S(2)}) copy-start(bf16[160,3200]{1,0:T(8,128)(2,1)} %copy-done.2) | copy-start | bytes 3072004
  42.9 20.1 %collective-permute-start.10 = (bf16[160,3200]{1,0:T(8,128)(2,1)}, bf16[160,3200]{1,0:T(8,128)(2,1)}, u32[]{:S(2)}, u32[]{:S(2)}) collective-permute-start(bf16[160,3200]{1,0:T(8,128)(2,1)} %get-tuple-element.46), channel_id=1, source_target_pairs={{0,32},{32,64},{64,96},{96,0},{1,33},{33,65},{65,97},{97,1},{2,34}... | collective-permute-start | bytes 3072008 | tf_op jit(solution)/shard_map/ppermute | solution.py:17
  44.2 18.8 %collective-permute-start.11 = (bf16[160,3200]{1,0:T(8,128)(2,1)}, bf16[160,3200]{1,0:T(8,128)(2,1)}, u32[]{:S(2)}, u32[]{:S(2)}) collective-permute-start(bf16[160,3200]{1,0:T(8,128)(2,1)} %get-tuple-element.47), channel_id=1, source_target_pairs={{0,96},{32,0},{64,32},{96,64},{1,97},{33,1},{65,33},{97,65},{2,98}... | collective-permute-start | bytes 3072008 | tf_op jit(solution)/shard_map/ppermute | solution.py:17
  45.6 17.4 %collective-permute-start.9 = (bf16[160,3200]{1,0:T(8,128)(2,1)S(1)}, bf16[160,3200]{1,0:T(8,128)(2,1)}, u32[]{:S(2)}, u32[]{:S(2)}) collective-permute-start(bf16[160,3200]{1,0:T(8,128)(2,1)S(1)} %get-tuple-element.45.refs_0_), channel_id=1, source_target_pairs={{0,16},{16,0},{1,17},{17,1},{2,18},{18,2},{3,19},{19,3},{4,20},{20... | collective-permute-start | bytes 3072008 | tf_op jit(solution)/shard_map/ppermute | solution.py:17
  56.0 28.0 %copy-start.4 = (bf16[8,192,256]{2,1,0:T(8,128)(2,1)}, bf16[8,192,256]{2,1,0:T(8,128)(2,1)S(1)}, u32[]{:S(2)}) copy-start(bf16[8,192,256]{2,1,0:T(8,128)(2,1)S(1)} %all-to-all-done.refs_8_) | copy-start | bytes 2359300
  56.0 39.0 %all-to-all-start.1 = ((bf16[8,192,256]{2,1,0:T(8,128)(2,1)}), bf16[8,192,256]{2,1,0:T(8,128)(2,1)}, u32[]{:S(2)}, u32[]{:S(2)}) async-start(bf16[8,192,256]{2,1,0:T(8,128)(2,1)} %get-tuple-element.41), calls=%async_computation.1 | async-start | bytes 1572864 | tf_op jit(solution)/shard_map/all_to_all | solution.py:152
  60.2 14.6 %collective-permute-start.13 = (bf16[8,192,256]{2,1,0:T(8,128)(2,1)S(1)}, bf16[8,192,256]{2,1,0:T(8,128)(2,1)S(1)}, u32[]{:S(2)}, u32[]{:S(2)}) collective-permute-start(bf16[8,192,256]{2,1,0:T(8,128)(2,1)S(1)} %all-to-all-done.refs_8_), channel_id=1, source_target_pairs={{0,1},{1,128},{128,129},{129,0},{2,3},{3,130},{130,131},{131,2},{4... | collective-permute-start | bytes 2359304 | tf_op jit(solution)/shard_map/ppermute | solution.py:17
  61.5 22.4 %collective-permute-start.15 = (bf16[8,192,256]{2,1,0:T(8,128)(2,1)S(1)}, bf16[8,192,256]{2,1,0:T(8,128)(2,1)S(1)}, u32[]{:S(2)}, u32[]{:S(2)}) collective-permute-start(bf16[8,192,256]{2,1,0:T(8,128)(2,1)S(1)} %all-to-all-done.refs_8_), channel_id=1, source_target_pairs={{0,129},{1,0},{128,1},{129,128},{2,131},{3,2},{130,3},{131,130},{4... | collective-permute-start | bytes 2359304 | tf_op jit(solution)/shard_map/ppermute | solution.py:17
  63.0 23.4 %collective-permute-start.12 = (bf16[160,3200]{1,0:T(8,128)(2,1)S(1)}, bf16[160,3200]{1,0:T(8,128)(2,1)}, u32[]{:S(2)}, u32[]{:S(2)}) collective-permute-start(bf16[160,3200]{1,0:T(8,128)(2,1)S(1)} %copy-done.3), channel_id=1, source_target_pairs={{0,64},{32,96},{64,0},{96,32},{1,65},{33,97},{65,1},{97,33},{2,66}... | collective-permute-start | bytes 3072008 | tf_op jit(solution)/shard_map/ppermute | solution.py:17
  66.0 20.4 %collective-permute-start.17 = (bf16[160,3200]{1,0:T(8,128)(2,1)}, bf16[160,3200]{1,0:T(8,128)(2,1)S(1)}, u32[]{:S(2)}, u32[]{:S(2)}) collective-permute-start(bf16[160,3200]{1,0:T(8,128)(2,1)} %collective-permute-done.10.refs_1_), channel_id=1, source_target_pairs={{0,16},{16,0},{1,17},{17,1},{2,18},{18,2},{3,19},{19,3},{4,20},{20... | collective-permute-start | bytes 3072008 | tf_op jit(solution)/shard_map/ppermute | solution.py:17
  74.8 11.6 %collective-permute-start.18 = (bf16[160,3200]{1,0:T(8,128)(2,1)}, bf16[160,3200]{1,0:T(8,128)(2,1)S(1)}, u32[]{:S(2)}, u32[]{:S(2)}) collective-permute-start(bf16[160,3200]{1,0:T(8,128)(2,1)} %collective-permute-done.11.refs_3_), channel_id=1, source_target_pairs={{0,16},{16,0},{1,17},{17,1},{2,18},{18,2},{3,19},{19,3},{4,20},{20... | collective-permute-start | bytes 3072008 | tf_op jit(solution)/shard_map/ppermute | solution.py:17
  74.8 9.1 %copy-start.5 = (bf16[8,192,256]{2,1,0:T(8,128)(2,1)}, bf16[8,192,256]{2,1,0:T(8,128)(2,1)S(1)}, u32[]{:S(2)}) copy-start(bf16[8,192,256]{2,1,0:T(8,128)(2,1)S(1)} %collective-permute-done.13.refs_9_) | copy-start | bytes 2359300
  74.8 19.3 %collective-permute-start.14 = (bf16[4,192,256]{2,1,0:T(8,128)(2,1)S(1)}, bf16[4,192,256]{2,1,0:T(8,128)(2,1)S(1)}, u32[]{:S(2)}, u32[]{:S(2)}) collective-permute-start(bf16[4,192,256]{2,1,0:T(8,128)(2,1)S(1)} %slice.26), channel_id=1, source_target_pairs={{0,1},{1,128},{128,129},{129,0},{2,3},{3,130},{130,131},{131,2},{4... | collective-permute-start | bytes 1179656 | tf_op jit(solution)/shard_map/ppermute | solution.py:17
  83.9 10.3 %copy-start.6 = (bf16[8,192,256]{2,1,0:T(8,128)(2,1)}, bf16[8,192,256]{2,1,0:T(8,128)(2,1)S(1)}, u32[]{:S(2)}) copy-start(bf16[8,192,256]{2,1,0:T(8,128)(2,1)S(1)} %collective-permute-done.15.refs_10_) | copy-start | bytes 2359300
  83.9 11.0 %collective-permute-start.16 = (bf16[4,192,256]{2,1,0:T(8,128)(2,1)S(1)}, bf16[4,192,256]{2,1,0:T(8,128)(2,1)}, u32[]{:S(2)}, u32[]{:S(2)}) collective-permute-start(bf16[4,192,256]{2,1,0:T(8,128)(2,1)S(1)} %slice.27), channel_id=1, source_target_pairs={{0,129},{1,0},{128,1},{129,128},{2,131},{3,2},{130,3},{131,130},{4... | collective-permute-start | bytes 1179656 | tf_op jit(solution)/shard_map/ppermute | solution.py:17
  86.4 7.7 %copy-start.11 = (bf16[160,3200]{1,0:T(8,128)(2,1)}, bf16[160,3200]{1,0:T(8,128)(2,1)S(1)}, u32[]{:S(2)}) copy-start(bf16[160,3200]{1,0:T(8,128)(2,1)S(1)} %collective-permute-done.17.refs_5_) | copy-start | bytes 3072004
  86.4 7.7 %copy-start.12 = (bf16[160,3200]{1,0:T(8,128)(2,1)}, bf16[160,3200]{1,0:T(8,128)(2,1)S(1)}, u32[]{:S(2)}) copy-start(bf16[160,3200]{1,0:T(8,128)(2,1)S(1)} %collective-permute-done.18.refs_7_) | copy-start | bytes 3072004
  94.2 0.8 copy-start.14
  94.9 4.8 %collective-permute-start.21 = (bf16[160,3200]{1,0:T(8,128)(2,1)}, bf16[160,3200]{1,0:T(8,128)(2,1)S(1)}, u32[]{:S(2)}, u32[]{:S(2)}) collective-permute-start(bf16[160,3200]{1,0:T(8,128)(2,1)} %collective-permute-done.12.refs_2_), channel_id=1, source_target_pairs={{0,16},{16,0},{1,17},{17,1},{2,18},{18,2},{3,19},{19,3},{4,20},{20... | collective-permute-start | bytes 3072008 | tf_op jit(solution)/shard_map/ppermute | solution.py:17
  96.0 21.8 %collective-permute-start.19 = (bf16[8,192,256]{2,1,0:T(8,128)(2,1)}, bf16[8,192,256]{2,1,0:T(8,128)(2,1)S(1)}, u32[]{:S(2)}, u32[]{:S(2)}) collective-permute-start(bf16[8,192,256]{2,1,0:T(8,128)(2,1)} %all-to-all-done.1.refs_8_), channel_id=1, source_target_pairs={{0,1},{1,128},{128,129},{129,0},{2,3},{3,130},{130,131},{131,2},{4... | collective-permute-start | bytes 2359304 | tf_op jit(solution)/shard_map/ppermute | solution.py:17
  98.5 19.3 %collective-permute-start.20 = (bf16[8,192,256]{2,1,0:T(8,128)(2,1)}, bf16[8,192,256]{2,1,0:T(8,128)(2,1)S(1)}, u32[]{:S(2)}, u32[]{:S(2)}) collective-permute-start(bf16[8,192,256]{2,1,0:T(8,128)(2,1)} %all-to-all-done.1.refs_8_), channel_id=1, source_target_pairs={{0,129},{1,0},{128,1},{129,128},{2,131},{3,2},{130,3},{131,130},{4... | collective-permute-start | bytes 2359304 | tf_op jit(solution)/shard_map/ppermute | solution.py:17
  99.7 1.0 copy-start.13
  117.8 11.2 %copy-start.7 = (bf16[8,192,256]{2,1,0:T(8,128)(2,1)}, bf16[8,192,256]{2,1,0:T(8,128)(2,1)S(1)}, u32[]{:S(2)}) copy-start(bf16[8,192,256]{2,1,0:T(8,128)(2,1)S(1)} %collective-permute-done.19.refs_9_) | copy-start | bytes 2359300
  117.8 11.2 %copy-start.8 = (bf16[8,192,256]{2,1,0:T(8,128)(2,1)}, bf16[8,192,256]{2,1,0:T(8,128)(2,1)S(1)}, u32[]{:S(2)}) copy-start(bf16[8,192,256]{2,1,0:T(8,128)(2,1)S(1)} %collective-permute-done.20.refs_10_) | copy-start | bytes 2359300
  117.8 11.1 %collective-permute-start.22 = (bf16[4,192,256]{2,1,0:T(8,128)(2,1)S(1)}, bf16[4,192,256]{2,1,0:T(8,128)(2,1)}, u32[]{:S(2)}, u32[]{:S(2)}) collective-permute-start(bf16[4,192,256]{2,1,0:T(8,128)(2,1)S(1)} %slice.22), channel_id=1, source_target_pairs={{0,1},{1,128},{128,129},{129,0},{2,3},{3,130},{130,131},{131,2},{4... | collective-permute-start | bytes 1179656 | tf_op jit(solution)/shard_map/ppermute | solution.py:17
  118.8 10.1 %collective-permute-start.23 = (bf16[4,192,256]{2,1,0:T(8,128)(2,1)S(1)}, bf16[4,192,256]{2,1,0:T(8,128)(2,1)}, u32[]{:S(2)}, u32[]{:S(2)}) collective-permute-start(bf16[4,192,256]{2,1,0:T(8,128)(2,1)S(1)} %slice.23), channel_id=1, source_target_pairs={{0,129},{1,0},{128,1},{129,128},{2,131},{3,2},{130,3},{131,130},{4... | collective-permute-start | bytes 1179656 | tf_op jit(solution)/shard_map/ppermute | solution.py:17
  120.7 18.7 %all-to-all-start.2 = ((bf16[16,160,128]{2,1,0:T(8,128)(2,1)}), bf16[16,160,128]{2,1,0:T(8,128)(2,1)S(1)}, u32[]{:S(2)}, u32[]{:S(2)}) async-start(bf16[16,160,128]{2,1,0:T(8,128)(2,1)} %bitcast.11), calls=%async_computation.2 | async-start | bytes 1310720 | tf_op jit(solution)/shard_map/all_to_all | solution.py:212
